TPU v7x, 32 devices: a whole 2x2x4 slice. The times are simulated.
32 devices in a mesh: parts: 2 (over y), op: 4 (over z), sec: 2 (over x), sub: 2 (over core).
Axes of the slice: x: 2, y: 2, z: 4, core: 2. Of those that a mesh axis runs over, the one named last changes fastest.
Arguments:
- psi: float32 [32, 256, 256], P(('parts', 'sec', 'sub'), 'op'), parts along dimension 0, may hold values from -6 to 6
- left_ops: float32 [32, 256, 256], P('op'), may hold values from -0.09375 to 0.09375
- right_ops: float32 [32, 256, 256], P('op'), may hold values from -0.375 to 0.375
- shifts: int32 [32], P('op'), may hold values from -1 to 1
- allowed: int32 [32, 16], P('op'), may hold values 0 or 1
Outputs:
- sigma: float32 [32, 256, 256], P(('parts', 'sec', 'sub'), 'op'), parts along dimension 0
There are 2 independent parts, one for each index of `parts`. A program takes and returns all parts, laid end to end along the dimension named above; an argument that names none is the same for every part. Nothing has to cross between parts.
All inputs are finite; a program needn't handle non-finite values. No bound on the sum of `allowed` on one device may be relied on, other than what follows from the above.
Results may differ from a plain program's by a relative error of at most 0.0003.
Values sent between devices are 32-bit elements; how exact they have to be, the bound alone decides.
No kernel may reach another device: no remote copies, remote signals or barrier semaphores. Data moves between devices by JAX's collectives and lax.ppermute only.
A program may use at most 64 MiB of HBM per device.

v0:
```python
import functools

import jax
import jax.numpy as jnp
from jax import lax
from jax.experimental import pallas as pl
from jax.experimental.pallas import tpu as pltpu
from jax.sharding import PartitionSpec as P

F32, BF16 = jnp.float32, jnp.bfloat16
SMEM = pl.BlockSpec(memory_space=pltpu.SMEM)
VMEM = pl.BlockSpec(memory_space=pltpu.VMEM)


def shifted(block, axis, distance):
    devices = range(lax.axis_size(axis))
    route = [(i - distance, i) for i in devices if i - distance in devices]
    return lax.ppermute(block, axis, route)


def ring_route(n):
    order = [0] + [i for i in range(n) if i % 2] + [i for i in reversed(range(1, n)) if i % 2 == 0]
    return [(order[i], order[(i + 1) % n]) for i in range(n)]


def ring_place(n, steps_back):
    me = lax.axis_index("op")
    place = jnp.where(me == 0, 0, jnp.where(lax.rem(me, 2) == 1, (me + 1) // 2, n - me // 2))
    at = lax.rem(place - steps_back + 2 * n, n)
    return jnp.where(at == 0, 0, jnp.where(at <= n // 2, 2 * at - 1, 2 * (n - at)))


def split(x):
    hi = x.astype(BF16)
    return hi, (x - hi.astype(F32)).astype(BF16)


def dot3(a, b):
    one = functools.partial(jnp.dot, preferred_element_type=F32)
    return one(a[0], b[0]) + (one(a[0], b[1]) + one(a[1], b[0]))


def prepare(left_ref, right_ref, left_parts, right_hi, right_lo, zero):
    kops, width, _ = left_ref.shape
    zero[...] = jnp.zeros_like(zero)
    for k in range(kops):
        hi, lo = split(left_ref[k])
        left_parts[k] = jnp.concatenate([hi, hi, lo], axis=1)
        right_hi[k * width : (k + 1) * width, :], right_lo[k * width : (k + 1) * width, :] = split(right_ref[k].T)


def stacked(block):
    hi, lo = split(block)
    return jnp.concatenate([hi, lo, hi], axis=0)


def place_rows(n, target, blocks):
    for j, block in enumerate(blocks):
        rows = block.shape[-2]
        target[..., pl.ds(pl.multiple_of(ring_place(n, j) * rows, rows), rows), :] = block


def first_stage(n, nloc, sectors, allowed_ref, *refs):
    left_parts, middle, psi = refs[n:]
    kops, width, _ = left_parts.shape
    first = lax.axis_index(("sec", "sub")) * nloc
    place_rows(n, psi, [ref[...] for ref in refs[:n]])
    parts = [stacked(psi[i]) for i in range(len(sectors))]
    for k in range(kops):
        for i, s in enumerate(sectors):
            block = jnp.dot(left_parts[k], parts[i], preferred_element_type=F32)
            middle[i, :, k * width : (k + 1) * width] = block * allowed_ref[k, first + s].astype(F32)


def first_stage_outside(n, nloc, shifts_ref, allowed_ref, above, below, left_parts, middle, psi, parts):
    kops, width, _ = left_parts.shape
    first = lax.axis_index(("sec", "sub")) * nloc
    place_rows(n, psi.at[0], [above[j] for j in range(n)])
    place_rows(n, psi.at[1], [below[j] for j in range(n)])
    for i in range(2):
        parts[i] = stacked(psi[i])
    for k in range(kops):
        up = shifts_ref[k] == 1
        source = jnp.where(up, jnp.maximum(first - 1, 0), jnp.minimum(first + nloc, allowed_ref.shape[1] - 1))
        block = jnp.dot(left_parts[k], parts[jnp.where(up, 0, 1)], preferred_element_type=F32)
        middle[:, k * width : (k + 1) * width] = block * allowed_ref[k, source].astype(F32)


def second_stage(n, step, shifts_ref, outer, inner, outside, right_hi, right_lo, *outs):
    per, rows, width = outs[0].shape
    nloc = per * len(outs)
    at = pl.ds(pl.multiple_of(ring_place(n, step + 1) * rows, rows), rows)
    last = nloc - 1
    highs, lows = [], []
    for k in range(shifts_ref.shape[0]):
        shift = shifts_ref[k]
        columns = slice(k * width, (k + 1) * width)

        def source(t, shift=shift, columns=columns):
            s = t - shift
            block = inner[jnp.clip(s - 1, 0, nloc - 3), at, columns]
            if t <= 1:
                block = jnp.where(s == 0, outer[0, at, columns], block)
            if t >= last - 1:
                block = jnp.where(s == last, outer[1, at, columns], block)
            if t in (0, last):
                block = jnp.where((s < 0) | (s > last), outside[at, columns], block)
            return block

        hi, lo = split(jnp.concatenate([source(t) for t in range(nloc)]))
        highs.append(hi)
        lows.append(lo)
    high, low = jnp.concatenate(highs, axis=1), jnp.concatenate(lows, axis=1)
    total = dot3((high, low), (right_hi[...], right_lo[...])).reshape(nloc, rows, width)
    for i, out in enumerate(outs):
        out[...] = total[i * per : (i + 1) * per]


def call(body, name, flops, out_shape, in_specs, operands, scratch=()):
    return pl.pallas_call(
        body,
        name=name,
        out_shape=out_shape,
        in_specs=in_specs,
        out_specs=jax.tree.map(lambda _: VMEM, out_shape),
        scratch_shapes=list(scratch),
        compiler_params=pltpu.CompilerParams(vmem_limit_bytes=24 * 2**20),
        cost_estimate=pl.CostEstimate(flops=flops, bytes_accessed=2**20, transcendentals=0),
    )(*operands)


def shards(psi, left_ops, right_ops, shifts, allowed):
    nloc, rows, width = psi.shape
    kops = left_ops.shape[0]
    n = lax.axis_size("op")
    route = ring_route(n)
    one = 6 * width**3

    tall = jax.ShapeDtypeStruct((kops * width, width), BF16)
    parts = jax.ShapeDtypeStruct((kops, width, 3 * width), BF16)
    zero = jax.ShapeDtypeStruct((1, 128), F32)
    left_parts, right_hi, right_lo, zero = call(
        prepare, "prepare", 4 * kops * one, [parts, tall, tall, zero], [VMEM] * 2, [left_ops, right_ops]
    )

    outer, inner = [psi[:: nloc - 1]], [psi[1 : nloc - 1]]
    for step in range(n - 1):
        outer.append(lax.ppermute(outer[-1] + zero[0, 0] if step == 1 else outer[-1], "op", route))
        inner.append(lax.ppermute(inner[-1] + zero[0, 0] if step == 1 else inner[-1], "op", route))

    above = shifted(jnp.concatenate([b[1:] for b in outer]), ("sec", "sub"), 1)
    below = shifted(jnp.concatenate([b[:1] for b in outer]), ("sec", "sub"), -1)

    def stage(name, sectors, blocks):
        operands = [allowed, *blocks, left_parts]
        return call(
            functools.partial(first_stage, n, nloc, sectors), name, 2 * len(sectors) * kops * one,
            jax.ShapeDtypeStruct((len(sectors), width, kops * width), F32), [SMEM] + [VMEM] * (n + 1), operands,
            [pltpu.VMEM((len(sectors), width, width), F32)],
        )

    mid_outer = stage("outer", (0, nloc - 1), outer)
    mid_inner = stage("inner", tuple(range(1, nloc - 1)), inner)
    mid_outside = call(
        functools.partial(first_stage_outside, n, nloc), "outside", 2 * kops * one,
        jax.ShapeDtypeStruct((width, kops * width), F32), [SMEM] * 2 + [VMEM] * 3, [shifts, allowed, above, below, left_parts],
        [pltpu.VMEM((2, width, width), F32), pltpu.VMEM((2, 3 * width, width), BF16)],
    )
    chunk = [jax.ShapeDtypeStruct((nloc // 2, rows, width), F32)] * 2

    def own(step):
        return call(
            functools.partial(second_stage, n, step), "chunk", nloc * kops * one // n, chunk,
            [SMEM] + [VMEM] * 5, [shifts, mid_outer, mid_inner, mid_outside, right_hi, right_lo],
        )

    result = own(0)
    for step in range(1, n):
        result = [lax.ppermute(r, "op", route) + o for r, o in zip(result, own(step))]
    return jnp.concatenate(result)


def solution(mesh):
    return jax.shard_map(
        shards,
        mesh=mesh,
        in_specs=(
            P(("parts", "sec", "sub"), "op", None),
            P("op", None, None),
            P("op", None, None),
            P("op"),
            P("op", None),
        ),
        out_specs=P(("parts", "sec", "sub"), "op", None),
        check_vma=False,
    )
```

profile of v0, /device:TPU:1, one launch (start us, length us, event | category | flops | bytes accessed | tf_op | source)
XLA Modules:
  0.0 58.6 jit_solution(9265389318809782926)
XLA Ops:
  0.0 1.0 %fusion = (f32[2,64,256]{2,1,0:T(8,128)S(1)}, f32[2,64,256]{2,1,0:T(8,128)S(1)}) fusion(f32[4,64,256]{2,1,0:T(8,128)} %param.5), kind=kLoop, calls=%fused_computation.5 | loop fusion | bytes 524288 | tf_op jit(solution)/shard_map/slice | solution.py:146
  1.0 2.2 %collective-permute-start.3 = (f32[2,64,256]{2,1,0:T(8,128)S(1)}, f32[2,64,256]{2,1,0:T(8,128)S(1)}, u32[]{:S(2)}, u32[]{:S(2)}) collective-permute-start(f32[2,64,256]{2,1,0:T(8,128)S(1)} %get-tuple-element.29.refs_0_), channel_id=1, source_target_pairs={{0,4},{4,12},{12,8},{8,0},{1,5},{5,13},{13,9},{9,1},{2,6},{6,14},{... | collective-permute-start | bytes 393224 | tf_op jit(solution)/shard_map/ppermute | solution.py:149
  3.2 2.3 %collective-permute-start = (f32[2,64,256]{2,1,0:T(8,128)S(1)}, f32[2,64,256]{2,1,0:T(8,128)S(1)}, u32[]{:S(2)}, u32[]{:S(2)}) collective-permute-start(f32[2,64,256]{2,1,0:T(8,128)S(1)} %get-tuple-element.30.refs_0_), channel_id=1, source_target_pairs={{0,4},{4,12},{12,8},{8,0},{1,5},{5,13},{13,9},{9,1},{2,6},{6,14},{... | collective-permute-start | bytes 393224 | tf_op jit(solution)/shard_map/ppermute | solution.py:148
  5.5 0.0 copy-start.1
  5.5 1.6 %copy-done.1 = f32[8,256,256]{2,1,0:T(8,128)S(1)} copy-done((f32[8,256,256]{2,1,0:T(8,128)S(1)}, f32[8,256,256]{2,1,0:T(8,128)}, u32[]{:S(2)}) %copy-start.1) | copy-done | bytes 2097176
  7.1 0.0 copy-start.2
  7.1 1.6 %copy-done.2 = f32[8,256,256]{2,1,0:T(8,128)S(1)} copy-done((f32[8,256,256]{2,1,0:T(8,128)S(1)}, f32[8,256,256]{2,1,0:T(8,128)}, u32[]{:S(2)}) %copy-start.2) | copy-done | bytes 2097176
  8.7 0.0 copy-start.3
  8.7 1.1 %prepare.1 = (bf16[8,256,768]{2,1,0:T(8,128)(2,1)S(1)}, bf16[2048,256]{1,0:T(8,128)(2,1)S(1)}, bf16[2048,256]{1,0:T(8,128)(2,1)S(1)}, f32[1,128]{1,0:T(1,128)S(1)}) custom-call(f32[8,256,256]{2,1,0:T(8,128)S(1)} %copy-done.1, f32[8,256,256]{2,1,0:T(8,128)S(1)} %copy-done.2), custom_call_target="tpu_custom_call" | custom-call | flops 3221225472 | bytes 1048576 | tf_op jit(solution)/shard_map/prepare/pallas_call | solution.py:120
  9.8 0.5 collective-permute-done.refs_1_
  10.3 0.4 collective-permute-start.1
  10.6 0.0 collective-permute-done.3.refs_1_
  10.7 3.1 %collective-permute-start.4 = (f32[2,64,256]{2,1,0:T(8,128)S(1)}, f32[2,64,256]{2,1,0:T(8,128)S(1)}, u32[]{:S(2)}, u32[]{:S(2)}) collective-permute-start(f32[2,64,256]{2,1,0:T(8,128)S(1)} %broadcast_add_fusion), channel_id=1, source_target_pairs={{0,4},{4,12},{12,8},{8,0},{1,5},{5,13},{13,9},{9,1},{2,6},{6,14},{... | collective-permute-start | bytes 393224 | tf_op jit(solution)/shard_map/ppermute | solution.py:149
  13.8 1.3 %collective-permute-done.1.refs_2_ = f32[2,64,256]{2,1,0:T(8,128)S(1)} collective-permute-done((f32[2,64,256]{2,1,0:T(8,128)S(1)}, f32[2,64,256]{2,1,0:T(8,128)S(1)}, u32[]{:S(2)}, u32[]{:S(2)}) %collective-permute-start.1) | collective-permute-done | bytes 131104 | tf_op jit(solution)/shard_map/ppermute | solution.py:148
  15.0 0.6 collective-permute-start.2
  15.6 2.2 %collective-permute-done.4.refs_2_ = f32[2,64,256]{2,1,0:T(8,128)S(1)} collective-permute-done((f32[2,64,256]{2,1,0:T(8,128)S(1)}, f32[2,64,256]{2,1,0:T(8,128)S(1)}, u32[]{:S(2)}, u32[]{:S(2)}) %collective-permute-start.4) | collective-permute-done | bytes 131104 | tf_op jit(solution)/shard_map/ppermute | solution.py:149
  17.8 0.6 %collective-permute-start.5 = (f32[2,64,256]{2,1,0:T(8,128)S(1)}, f32[2,64,256]{2,1,0:T(8,128)S(1)}, u32[]{:S(2)}, u32[]{:S(2)}) collective-permute-start(f32[2,64,256]{2,1,0:T(8,128)S(1)} %collective-permute-done.4.refs_2_), channel_id=1, source_target_pairs={{0,4},{4,12},{12,8},{8,0},{1,5},{5,13},{13,9},{9,1},{2,6},{6,14},{... | collective-permute-start | bytes 393224 | tf_op jit(solution)/shard_map/ppermute | solution.py:149
  18.4 2.3 %collective-permute-done.2.refs_3_ = f32[2,64,256]{2,1,0:T(8,128)S(1)} collective-permute-done((f32[2,64,256]{2,1,0:T(8,128)S(1)}, f32[2,64,256]{2,1,0:T(8,128)S(1)}, u32[]{:S(2)}, u32[]{:S(2)}) %collective-permute-start.2) | collective-permute-done | bytes 131104 | tf_op jit(solution)/shard_map/ppermute | solution.py:148
  20.7 6.5 %collective-permute-start.6 = (f32[4,64,256]{2,1,0:T(8,128)S(1)}, f32[4,64,256]{2,1,0:T(8,128)S(1)}, u32[]{:S(2)}, u32[]{:S(2)}) collective-permute-start(f32[4,64,256]{2,1,0:T(8,128)S(1)} %pad_maximum_fusion), channel_id=1, source_target_pairs={{0,1},{1,2},{2,3},{4,5},{5,6},{6,7},{8,9},{9,10},{10,11},{12,13},{... | collective-permute-start | bytes 786440 | tf_op jit(solution)/shard_map/ppermute | solution.py:18
  27.2 1.9 %collective-permute-start.7 = (f32[4,64,256]{2,1,0:T(8,128)S(1)}, f32[4,64,256]{2,1,0:T(8,128)S(1)}, u32[]{:S(2)}, u32[]{:S(2)}) collective-permute-start(f32[4,64,256]{2,1,0:T(8,128)S(1)} %pad_maximum_fusion.1), channel_id=1, source_target_pairs={{1,0},{2,1},{3,2},{5,4},{6,5},{7,6},{9,8},{10,9},{11,10},{13,12},{... | collective-permute-start | bytes 786440 | tf_op jit(solution)/shard_map/ppermute | solution.py:18
  29.1 0.0 copy-done.3
  29.2 2.5 %outer.1 = f32[2,256,2048]{2,1,0:T(8,128)S(1)} custom-call(s32[8,16]{1,0:T(8,128)S(1)} %copy-done.3, f32[2,64,256]{2,1,0:T(8,128)S(1)} %get-tuple-element.30.refs_0_, f32[2,64,256]{2,1,0:T(8,128)S(1)} %collective-permute-done.refs_1_, f32[2,64,256]{2,1,0:T(8,128)S(1)} %collective-permute-done.1.refs_2_, f32[2,64,256]{2,1,0:T(8,128)S(1)} %collective-permute-done.2.refs_3_, ...), custom_call_target="tpu_custom_call" | custom-call | flops 3221225472 | bytes 1048576 | tf_op jit(solution)/shard_map/outer/pallas_call | solution.py:120
  31.6 0.0 copy-start
  31.6 0.0 collective-permute-done.5.refs_3_
  31.7 2.5 %inner.1 = f32[2,256,2048]{2,1,0:T(8,128)S(1)} custom-call(s32[8,16]{1,0:T(8,128)S(1)} %copy-done.3, f32[2,64,256]{2,1,0:T(8,128)S(1)} %get-tuple-element.29.refs_0_, f32[2,64,256]{2,1,0:T(8,128)S(1)} %collective-permute-done.3.refs_1_, f32[2,64,256]{2,1,0:T(8,128)S(1)} %collective-permute-done.4.refs_2_, f32[2,64,256]{2,1,0:T(8,128)S(1)} %collective-permute-done.5.refs_3_, ...), custom_call_target="tpu_custom_call" | custom-call | flops 3221225472 | bytes 1048576 | tf_op jit(solution)/shard_map/inner/pallas_call | solution.py:120
  34.1 0.0 collective-permute-done.6.above
  34.2 0.8 %collective-permute-done.7.below = f32[4,64,256]{2,1,0:T(8,128)S(1)} collective-permute-done((f32[4,64,256]{2,1,0:T(8,128)S(1)}, f32[4,64,256]{2,1,0:T(8,128)S(1)}, u32[]{:S(2)}, u32[]{:S(2)}) %collective-permute-start.7) | collective-permute-done | bytes 262176 | tf_op jit(solution)/shard_map/ppermute | solution.py:18
  34.9 0.0 copy-done
  34.9 1.8 %outside.1 = f32[256,2048]{1,0:T(8,128)S(1)} custom-call(s32[8]{0:T(128)S(1)} %copy-done, s32[8,16]{1,0:T(8,128)S(1)} %copy-done.3, f32[4,64,256]{2,1,0:T(8,128)S(1)} %collective-permute-done.6.above, f32[4,64,256]{2,1,0:T(8,128)S(1)} %collective-permute-done.7.below, bf16[8,256,768]{2,1,0:T(8,128)(2,1)S(1)} %get-tuple-element.18.refs_4_.left_parts), custom_call_target="tpu_custom_call" | custom-call | flops 1610612736 | bytes 1048576 | tf_op jit(solution)/shard_map/outside/pallas_call | solution.py:120
  36.7 1.6 %chunk.4 = (f32[2,64,256]{2,1,0:T(8,128)S(1)}, f32[2,64,256]{2,1,0:T(8,128)S(1)}) custom-call(s32[8]{0:T(128)S(1)} %copy-done, f32[2,256,2048]{2,1,0:T(8,128)S(1)} %outer.1, f32[2,256,2048]{2,1,0:T(8,128)S(1)} %inner.1, f32[256,2048]{1,0:T(8,128)S(1)} %outside.1, bf16[2048,256]{1,0:T(8,128)(2,1)S(1)} %get-tuple-element.19.right_hi, ...), custom_call_target="tpu_custom_call" | custom-call | flops 805306368 | bytes 1048576 | tf_op jit(solution)/shard_map/chunk/pallas_call | solution.py:120
  38.3 0.6 %collective-permute-start.8 = (f32[2,64,256]{2,1,0:T(8,128)S(1)}, f32[2,64,256]{2,1,0:T(8,128)S(1)}, u32[]{:S(2)}, u32[]{:S(2)}) collective-permute-start(f32[2,64,256]{2,1,0:T(8,128)S(1)} %get-tuple-element.21), channel_id=1, source_target_pairs={{0,4},{4,12},{12,8},{8,0},{1,5},{5,13},{13,9},{9,1},{2,6},{6,14},{... | collective-permute-start | bytes 393224 | tf_op jit(solution)/shard_map/ppermute | solution.py:179
  38.9 3.1 %collective-permute-start.11 = (f32[2,64,256]{2,1,0:T(8,128)S(1)}, f32[2,64,256]{2,1,0:T(8,128)S(1)}, u32[]{:S(2)}, u32[]{:S(2)}) collective-permute-start(f32[2,64,256]{2,1,0:T(8,128)S(1)} %get-tuple-element.25), channel_id=1, source_target_pairs={{0,4},{4,12},{12,8},{8,0},{1,5},{5,13},{13,9},{9,1},{2,6},{6,14},{... | collective-permute-start | bytes 393224 | tf_op jit(solution)/shard_map/ppermute | solution.py:179
  42.0 1.6 %chunk.5 = (f32[2,64,256]{2,1,0:T(8,128)S(1)}, f32[2,64,256]{2,1,0:T(8,128)S(1)}) custom-call(s32[8]{0:T(128)S(1)} %copy-done, f32[2,256,2048]{2,1,0:T(8,128)S(1)} %outer.1, f32[2,256,2048]{2,1,0:T(8,128)S(1)} %inner.1, f32[256,2048]{1,0:T(8,128)S(1)} %outside.1, bf16[2048,256]{1,0:T(8,128)(2,1)S(1)} %get-tuple-element.19.right_hi, ...), custom_call_target="tpu_custom_call" | custom-call | flops 805306368 | bytes 1048576 | tf_op jit(solution)/shard_map/chunk/pallas_call | solution.py:120
  43.6 0.1 collective-permute-done.8
  43.8 0.4 collective-permute-start.9
  44.2 1.0 %collective-permute-done.11 = f32[2,64,256]{2,1,0:T(8,128)S(1)} collective-permute-done((f32[2,64,256]{2,1,0:T(8,128)S(1)}, f32[2,64,256]{2,1,0:T(8,128)S(1)}, u32[]{:S(2)}, u32[]{:S(2)}) %collective-permute-start.11) | collective-permute-done | bytes 131104 | tf_op jit(solution)/shard_map/ppermute | solution.py:179
  45.2 2.1 %collective-permute-start.12 = (f32[2,64,256]{2,1,0:T(8,128)S(1)}, f32[2,64,256]{2,1,0:T(8,128)S(1)}, u32[]{:S(2)}, u32[]{:S(2)}) collective-permute-start(f32[2,64,256]{2,1,0:T(8,128)S(1)} %add.34), channel_id=1, source_target_pairs={{0,4},{4,12},{12,8},{8,0},{1,5},{5,13},{13,9},{9,1},{2,6},{6,14},{... | collective-permute-start | bytes 393224 | tf_op jit(solution)/shard_map/ppermute | solution.py:179
  47.3 1.6 %chunk.6 = (f32[2,64,256]{2,1,0:T(8,128)S(1)}, f32[2,64,256]{2,1,0:T(8,128)S(1)}) custom-call(s32[8]{0:T(128)S(1)} %copy-done, f32[2,256,2048]{2,1,0:T(8,128)S(1)} %outer.1, f32[2,256,2048]{2,1,0:T(8,128)S(1)} %inner.1, f32[256,2048]{1,0:T(8,128)S(1)} %outside.1, bf16[2048,256]{1,0:T(8,128)(2,1)S(1)} %get-tuple-element.19.right_hi, ...), custom_call_target="tpu_custom_call" | custom-call | flops 805306368 | bytes 1048576 | tf_op jit(solution)/shard_map/chunk/pallas_call | solution.py:120
  48.9 1.1 %collective-permute-done.9 = f32[2,64,256]{2,1,0:T(8,128)S(1)} collective-permute-done((f32[2,64,256]{2,1,0:T(8,128)S(1)}, f32[2,64,256]{2,1,0:T(8,128)S(1)}, u32[]{:S(2)}, u32[]{:S(2)}) %collective-permute-start.9) | collective-permute-done | bytes 131104 | tf_op jit(solution)/shard_map/ppermute | solution.py:179
  50.0 0.3 collective-permute-start.10
  50.3 1.1 %collective-permute-done.12 = f32[2,64,256]{2,1,0:T(8,128)S(1)} collective-permute-done((f32[2,64,256]{2,1,0:T(8,128)S(1)}, f32[2,64,256]{2,1,0:T(8,128)S(1)}, u32[]{:S(2)}, u32[]{:S(2)}) %collective-permute-start.12) | collective-permute-done | bytes 131104 | tf_op jit(solution)/shard_map/ppermute | solution.py:179
  51.4 1.9 %collective-permute-start.13 = (f32[2,64,256]{2,1,0:T(8,128)S(1)}, f32[2,64,256]{2,1,0:T(8,128)S(1)}, u32[]{:S(2)}, u32[]{:S(2)}) collective-permute-start(f32[2,64,256]{2,1,0:T(8,128)S(1)} %add.35), channel_id=1, source_target_pairs={{0,4},{4,12},{12,8},{8,0},{1,5},{5,13},{13,9},{9,1},{2,6},{6,14},{... | collective-permute-start | bytes 393224 | tf_op jit(solution)/shard_map/ppermute | solution.py:179
  53.3 1.6 %chunk.7 = (f32[2,64,256]{2,1,0:T(8,128)S(1)}, f32[2,64,256]{2,1,0:T(8,128)S(1)}) custom-call(s32[8]{0:T(128)S(1)} %copy-done, f32[2,256,2048]{2,1,0:T(8,128)S(1)} %outer.1, f32[2,256,2048]{2,1,0:T(8,128)S(1)} %inner.1, f32[256,2048]{1,0:T(8,128)S(1)} %outside.1, bf16[2048,256]{1,0:T(8,128)(2,1)S(1)} %get-tuple-element.19.right_hi, ...), custom_call_target="tpu_custom_call" | custom-call | flops 805306368 | bytes 1048576 | tf_op jit(solution)/shard_map/chunk/pallas_call | solution.py:120
  55.0 0.0 collective-permute-done.10
  55.0 2.9 %collective-permute-done.13 = f32[2,64,256]{2,1,0:T(8,128)S(1)} collective-permute-done((f32[2,64,256]{2,1,0:T(8,128)S(1)}, f32[2,64,256]{2,1,0:T(8,128)S(1)}, u32[]{:S(2)}, u32[]{:S(2)}) %collective-permute-start.13) | collective-permute-done | bytes 131104 | tf_op jit(solution)/shard_map/ppermute | solution.py:179
  57.9 0.7 %pad_maximum_fusion.2 = f32[4,64,256]{2,1,0:T(8,128)} fusion(f32[2,64,256]{2,1,0:T(8,128)S(1)} %add.36, f32[2,64,256]{2,1,0:T(8,128)S(1)} %add.33), kind=kLoop, calls=%fused_computation.2 | loop fusion | flops 65536 | bytes 524288 | tf_op jit(solution)/shard_map/concatenate | solution.py:180
  (14 shorter events, 0.3 us)
Async XLA Ops:
  1.0 9.6 %collective-permute-start.3 = (f32[2,64,256]{2,1,0:T(8,128)S(1)}, f32[2,64,256]{2,1,0:T(8,128)S(1)}, u32[]{:S(2)}, u32[]{:S(2)}) collective-permute-start(f32[2,64,256]{2,1,0:T(8,128)S(1)} %get-tuple-element.29.refs_0_), channel_id=1, source_target_pairs={{0,4},{4,12},{12,8},{8,0},{1,5},{5,13},{13,9},{9,1},{2,6},{6,14},{... | collective-permute-start | bytes 393224 | tf_op jit(solution)/shard_map/ppermute | solution.py:149
  3.2 7.0 %collective-permute-start = (f32[2,64,256]{2,1,0:T(8,128)S(1)}, f32[2,64,256]{2,1,0:T(8,128)S(1)}, u32[]{:S(2)}, u32[]{:S(2)}) collective-permute-start(f32[2,64,256]{2,1,0:T(8,128)S(1)} %get-tuple-element.30.refs_0_), channel_id=1, source_target_pairs={{0,4},{4,12},{12,8},{8,0},{1,5},{5,13},{13,9},{9,1},{2,6},{6,14},{... | collective-permute-start | bytes 393224 | tf_op jit(solution)/shard_map/ppermute | solution.py:148
  5.5 1.6 %copy-start.1 = (f32[8,256,256]{2,1,0:T(8,128)S(1)}, f32[8,256,256]{2,1,0:T(8,128)}, u32[]{:S(2)}) copy-start(f32[8,256,256]{2,1,0:T(8,128)} %left_ref.1) | copy-start | bytes 6291460
  7.1 1.6 %copy-start.2 = (f32[8,256,256]{2,1,0:T(8,128)S(1)}, f32[8,256,256]{2,1,0:T(8,128)}, u32[]{:S(2)}) copy-start(f32[8,256,256]{2,1,0:T(8,128)} %right_ref.1) | copy-start | bytes 6291460
  8.7 20.5 %copy-start.3 = (s32[8,16]{1,0:T(8,128)S(1)}, s32[8,16]{1,0:T(8,128)}, u32[]{:S(2)}) copy-start(s32[8,16]{1,0:T(8,128)} %allowed_ref.5) | copy-start | bytes 1540
  10.3 4.8 %collective-permute-start.1 = (f32[2,64,256]{2,1,0:T(8,128)S(1)}, f32[2,64,256]{2,1,0:T(8,128)S(1)}, u32[]{:S(2)}, u32[]{:S(2)}) collective-permute-start(f32[2,64,256]{2,1,0:T(8,128)S(1)} %broadcast_add_fusion.1), channel_id=1, source_target_pairs={{0,4},{4,12},{12,8},{8,0},{1,5},{5,13},{13,9},{9,1},{2,6},{6,14},{... | collective-permute-start | bytes 393224 | tf_op jit(solution)/shard_map/ppermute | solution.py:148
  10.7 7.1 %collective-permute-start.4 = (f32[2,64,256]{2,1,0:T(8,128)S(1)}, f32[2,64,256]{2,1,0:T(8,128)S(1)}, u32[]{:S(2)}, u32[]{:S(2)}) collective-permute-start(f32[2,64,256]{2,1,0:T(8,128)S(1)} %broadcast_add_fusion), channel_id=1, source_target_pairs={{0,4},{4,12},{12,8},{8,0},{1,5},{5,13},{13,9},{9,1},{2,6},{6,14},{... | collective-permute-start | bytes 393224 | tf_op jit(solution)/shard_map/ppermute | solution.py:149
  15.0 5.6 %collective-permute-start.2 = (f32[2,64,256]{2,1,0:T(8,128)S(1)}, f32[2,64,256]{2,1,0:T(8,128)S(1)}, u32[]{:S(2)}, u32[]{:S(2)}) collective-permute-start(f32[2,64,256]{2,1,0:T(8,128)S(1)} %collective-permute-done.1.refs_2_), channel_id=1, source_target_pairs={{0,4},{4,12},{12,8},{8,0},{1,5},{5,13},{13,9},{9,1},{2,6},{6,14},{... | collective-permute-start | bytes 393224 | tf_op jit(solution)/shard_map/ppermute | solution.py:148
  17.8 13.9 %collective-permute-start.5 = (f32[2,64,256]{2,1,0:T(8,128)S(1)}, f32[2,64,256]{2,1,0:T(8,128)S(1)}, u32[]{:S(2)}, u32[]{:S(2)}) collective-permute-start(f32[2,64,256]{2,1,0:T(8,128)S(1)} %collective-permute-done.4.refs_2_), channel_id=1, source_target_pairs={{0,4},{4,12},{12,8},{8,0},{1,5},{5,13},{13,9},{9,1},{2,6},{6,14},{... | collective-permute-start | bytes 393224 | tf_op jit(solution)/shard_map/ppermute | solution.py:149
  20.7 13.4 %collective-permute-start.6 = (f32[4,64,256]{2,1,0:T(8,128)S(1)}, f32[4,64,256]{2,1,0:T(8,128)S(1)}, u32[]{:S(2)}, u32[]{:S(2)}) collective-permute-start(f32[4,64,256]{2,1,0:T(8,128)S(1)} %pad_maximum_fusion), channel_id=1, source_target_pairs={{0,1},{1,2},{2,3},{4,5},{5,6},{6,7},{8,9},{9,10},{10,11},{12,13},{... | collective-permute-start | bytes 786440 | tf_op jit(solution)/shard_map/ppermute | solution.py:18
  27.2 7.7 %collective-permute-start.7 = (f32[4,64,256]{2,1,0:T(8,128)S(1)}, f32[4,64,256]{2,1,0:T(8,128)S(1)}, u32[]{:S(2)}, u32[]{:S(2)}) collective-permute-start(f32[4,64,256]{2,1,0:T(8,128)S(1)} %pad_maximum_fusion.1), channel_id=1, source_target_pairs={{1,0},{2,1},{3,2},{5,4},{6,5},{7,6},{9,8},{10,9},{11,10},{13,12},{... | collective-permute-start | bytes 786440 | tf_op jit(solution)/shard_map/ppermute | solution.py:18
  31.6 3.3 %copy-start = (s32[8]{0:T(128)S(1)}, s32[8]{0:T(128)}, u32[]{:S(2)}) copy-start(s32[8]{0:T(128)} %shifts_ref.9) | copy-start | bytes 100
  38.3 5.4 %collective-permute-start.8 = (f32[2,64,256]{2,1,0:T(8,128)S(1)}, f32[2,64,256]{2,1,0:T(8,128)S(1)}, u32[]{:S(2)}, u32[]{:S(2)}) collective-permute-start(f32[2,64,256]{2,1,0:T(8,128)S(1)} %get-tuple-element.21), channel_id=1, source_target_pairs={{0,4},{4,12},{12,8},{8,0},{1,5},{5,13},{13,9},{9,1},{2,6},{6,14},{... | collective-permute-start | bytes 393224 | tf_op jit(solution)/shard_map/ppermute | solution.py:179
  38.9 6.3 %collective-permute-start.11 = (f32[2,64,256]{2,1,0:T(8,128)S(1)}, f32[2,64,256]{2,1,0:T(8,128)S(1)}, u32[]{:S(2)}, u32[]{:S(2)}) collective-permute-start(f32[2,64,256]{2,1,0:T(8,128)S(1)} %get-tuple-element.25), channel_id=1, source_target_pairs={{0,4},{4,12},{12,8},{8,0},{1,5},{5,13},{13,9},{9,1},{2,6},{6,14},{... | collective-permute-start | bytes 393224 | tf_op jit(solution)/shard_map/ppermute | solution.py:179
  43.8 6.2 %collective-permute-start.9 = (f32[2,64,256]{2,1,0:T(8,128)S(1)}, f32[2,64,256]{2,1,0:T(8,128)S(1)}, u32[]{:S(2)}, u32[]{:S(2)}) collective-permute-start(f32[2,64,256]{2,1,0:T(8,128)S(1)} %add.31), channel_id=1, source_target_pairs={{0,4},{4,12},{12,8},{8,0},{1,5},{5,13},{13,9},{9,1},{2,6},{6,14},{... | collective-permute-start | bytes 393224 | tf_op jit(solution)/shard_map/ppermute | solution.py:179
  45.2 6.2 %collective-permute-start.12 = (f32[2,64,256]{2,1,0:T(8,128)S(1)}, f32[2,64,256]{2,1,0:T(8,128)S(1)}, u32[]{:S(2)}, u32[]{:S(2)}) collective-permute-start(f32[2,64,256]{2,1,0:T(8,128)S(1)} %add.34), channel_id=1, source_target_pairs={{0,4},{4,12},{12,8},{8,0},{1,5},{5,13},{13,9},{9,1},{2,6},{6,14},{... | collective-permute-start | bytes 393224 | tf_op jit(solution)/shard_map/ppermute | solution.py:179
  50.0 5.0 %collective-permute-start.10 = (f32[2,64,256]{2,1,0:T(8,128)S(1)}, f32[2,64,256]{2,1,0:T(8,128)S(1)}, u32[]{:S(2)}, u32[]{:S(2)}) collective-permute-start(f32[2,64,256]{2,1,0:T(8,128)S(1)} %add.32), channel_id=1, source_target_pairs={{0,4},{4,12},{12,8},{8,0},{1,5},{5,13},{13,9},{9,1},{2,6},{6,14},{... | collective-permute-start | bytes 393224 | tf_op jit(solution)/shard_map/ppermute | solution.py:179
  51.4 6.5 %collective-permute-start.13 = (f32[2,64,256]{2,1,0:T(8,128)S(1)}, f32[2,64,256]{2,1,0:T(8,128)S(1)}, u32[]{:S(2)}, u32[]{:S(2)}) collective-permute-start(f32[2,64,256]{2,1,0:T(8,128)S(1)} %add.35), channel_id=1, source_target_pairs={{0,4},{4,12},{12,8},{8,0},{1,5},{5,13},{13,9},{9,1},{2,6},{6,14},{... | collective-permute-start | bytes 393224 | tf_op jit(solution)/shard_map/ppermute | solution.py:179
where the time goes:
time: 59.6 us; the launch traced here: 58.6 us
  starting transfers between devices  25.9 us (43%)
  Pallas kernels  14.3 us (24%)
  waiting for transfers between devices  13 us (22%)
  local copies, waits for them, and re-layouts  4.22 us (7%)
  other arithmetic  0.96 us (2%)
    pallas_call x8, Pallas kernels, call(): pl.pallas_call(body, name=name, out_shape=out_shape, in_specs=in_specs, o...  14.3 us
    ppermute x2, starting transfers between devices, shifted(): return lax.ppermute(block, axis, route)  8.4 us
    ppermute x6, starting transfers between devices, shards(): lax.ppermute(r, 'op', route) + o  8.38 us
    ppermute x6, waiting for transfers between devices, shards(): lax.ppermute(r, 'op', route) + o  6.12 us
    ppermute x3, starting transfers between devices, shards(): lax.ppermute(inner[-1] + zero[0, 0] if step == 1 else inner[-1], 'op', ro...  5.85 us
    ppermute x3, waiting for transfers between devices, shards(): lax.ppermute(outer[-1] + zero[0, 0] if step == 1 else outer[-1], 'op', ro...  3.98 us
    ppermute x3, starting transfers between devices, shards(): lax.ppermute(outer[-1] + zero[0, 0] if step == 1 else outer[-1], 'op', ro...  3.24 us
    unnamed x8, local copies, waits for them, and re-layouts  3.19 us
  transfers between devices with their start and end apart: 14, of which 10 were waited for; matrix products, arithmetic and copies ran while one was open for 0% of the time, Pallas kernels for 19%

commit v1 on v0

v1 whole, which is shorter than its diff:
```python
import functools

import jax
import jax.numpy as jnp
from jax import lax
from jax.experimental import pallas as pl
from jax.experimental.pallas import tpu as pltpu
from jax.sharding import PartitionSpec as P

F32, BF16 = jnp.float32, jnp.bfloat16
SMEM = pl.BlockSpec(memory_space=pltpu.SMEM)
VMEM = pl.BlockSpec(memory_space=pltpu.VMEM)


def shifted(block, axis, distance):
    devices = range(lax.axis_size(axis))
    route = [(i - distance, i) for i in devices if i - distance in devices]
    return lax.ppermute(block, axis, route)


def ring_route(n):
    order = [0] + [i for i in range(n) if i % 2] + [i for i in reversed(range(1, n)) if i % 2 == 0]
    return [(order[i], order[(i + 1) % n]) for i in range(n)]


def ring_place(n, steps_back):
    me = lax.axis_index("op")
    place = jnp.where(me == 0, 0, jnp.where(lax.rem(me, 2) == 1, (me + 1) // 2, n - me // 2))
    at = lax.rem(place - steps_back + 2 * n, n)
    return jnp.where(at == 0, 0, jnp.where(at <= n // 2, 2 * at - 1, 2 * (n - at)))


def split(x):
    hi = x.astype(BF16)
    return hi, (x - hi.astype(F32)).astype(BF16)


def dot3(a, b):
    one = functools.partial(jnp.dot, preferred_element_type=F32)
    return one(a[0], b[0]) + (one(a[0], b[1]) + one(a[1], b[0]))


def prepare(left_ref, right_ref, left_parts, right_hi, right_lo, zero):
    n, kops, rows, _ = left_parts.shape
    width = left_ref.shape[1]
    zero[...] = jnp.zeros_like(zero)
    for k in range(kops):
        hi, lo = split(left_ref[k])
        parts = jnp.concatenate([hi, hi, lo], axis=1)
        for c in range(n):
            left_parts[c, k] = parts[c * rows : (c + 1) * rows]
        right_hi[k * width : (k + 1) * width, :], right_lo[k * width : (k + 1) * width, :] = split(right_ref[k].T)


def stacked(block):
    hi, lo = split(block)
    return jnp.concatenate([hi, lo, hi], axis=0)


def place_rows(n, target, blocks):
    for j, block in enumerate(blocks):
        rows = block.shape[-2]
        target[..., pl.ds(pl.multiple_of(ring_place(n, j) * rows, rows), rows), :] = block


def assemble(n, *refs):
    parts, psi = refs[n:]
    place_rows(n, psi, [ref[...] for ref in refs[:n]])
    for i in range(parts.shape[0]):
        parts[i] = stacked(psi[i])


def first_product(left, parts):
    return jnp.dot(left, parts, preferred_element_type=F32)


def chunk_left(n, step, left_parts):
    return left_parts[ring_place(n, step + 1)].reshape(-1, left_parts.shape[-1])


def own_sectors(n, *refs):
    (outer, left_parts), (inner, middle, psi) = refs[n : n + 2], refs[n + 2 :]
    assemble(n, *refs[:n], inner, psi)
    left = chunk_left(n, 0, left_parts)
    middle[0] = first_product(left, outer[0])
    for i in range(inner.shape[0]):
        middle[i + 1] = first_product(left, inner[i])
    middle[inner.shape[0] + 1] = first_product(left, outer[1])


def second_product(nloc, shifts_ref, allowed_ref, middle, right_hi, right_lo, outs):
    kops = shifts_ref.shape[0]
    rows, width = outs[0].shape[1:]
    first = lax.axis_index(("sec", "sub")) * nloc
    highs, lows = [], []
    for k in range(kops):
        shift = shifts_ref[k]
        blocks = []
        for t in range(nloc):
            below, same, above = [middle[t + d][k * rows : (k + 1) * rows] for d in range(3)]
            block = jnp.where(shift == 0, same, jnp.where(shift == 1, below, above))
            source = jnp.clip(first + t - shift, 0, allowed_ref.shape[1] - 1)
            blocks.append(block * allowed_ref[k, source].astype(F32))
        hi, lo = split(jnp.concatenate(blocks))
        highs.append(hi)
        lows.append(lo)
    high, low = jnp.concatenate(highs, axis=1), jnp.concatenate(lows, axis=1)
    total = dot3((high, low), (right_hi[...], right_lo[...])).reshape(nloc, rows, width)
    per = nloc // len(outs)
    for i, out in enumerate(outs):
        out[...] = total[i * per : (i + 1) * per]


def outside_sectors(n, above, below, left_parts, outside, middle, psi):
    place_rows(n, psi.at[0], [above[j] for j in range(n)])
    place_rows(n, psi.at[1], [below[j] for j in range(n)])
    left = chunk_left(n, 0, left_parts)
    for i in range(2):
        outside[i] = stacked(psi[i])
        middle[i] = first_product(left, outside[i])


def first_chunk(n, nloc, shifts_ref, allowed_ref, own, ends, right_hi, right_lo, *outs):
    middle = [ends[0], *[own[i] for i in range(nloc)], ends[1]]
    second_product(nloc, shifts_ref, allowed_ref, middle, right_hi, right_lo, outs)


def later_chunk(n, nloc, step, shifts_ref, allowed_ref, outer, inner, outside, left_parts, right_hi, right_lo, *outs):
    left = chunk_left(n, step, left_parts)
    sources = [outside.at[0], outer.at[0], *[inner.at[i] for i in range(nloc - 2)], outer.at[1], outside.at[1]]
    middle = [first_product(left, ref[...]) for ref in sources]
    second_product(nloc, shifts_ref, allowed_ref, middle, right_hi, right_lo, outs)


def call(body, name, flops, out_shape, in_specs, operands, scratch=()):
    return pl.pallas_call(
        body,
        name=name,
        out_shape=out_shape,
        in_specs=in_specs,
        out_specs=jax.tree.map(lambda _: VMEM, out_shape),
        scratch_shapes=list(scratch),
        compiler_params=pltpu.CompilerParams(vmem_limit_bytes=24 * 2**20),
        cost_estimate=pl.CostEstimate(flops=flops, bytes_accessed=2**20, transcendentals=0),
    )(*operands)


def shards(psi, left_ops, right_ops, shifts, allowed):
    nloc, rows, width = psi.shape
    kops = left_ops.shape[0]
    n = lax.axis_size("op")
    route = ring_route(n)
    one = 6 * width**3

    tall = jax.ShapeDtypeStruct((kops * width, width), BF16)
    parts = jax.ShapeDtypeStruct((n, kops, rows, 3 * width), BF16)
    zero = jax.ShapeDtypeStruct((1, 128), F32)
    left_parts, right_hi, right_lo, zero = call(
        prepare, "prepare", 4 * kops * one, [parts, tall, tall, zero], [VMEM] * 2, [left_ops, right_ops]
    )

    outer, inner = [psi[:: nloc - 1]], [psi[1 : nloc - 1]]
    for step in range(n - 1):
        inner.append(lax.ppermute(inner[-1] + zero[0, 0] if step == 1 else inner[-1], "op", route))
        outer.append(lax.ppermute(outer[-1] + zero[0, 0] if step == 1 else outer[-1], "op", route))

    above = shifted(jnp.concatenate([b[1:] for b in outer]), ("sec", "sub"), 1)
    below = shifted(jnp.concatenate([b[:1] for b in outer]), ("sec", "sub"), -1)

    def split_parts(sectors):
        return jax.ShapeDtypeStruct((sectors, 3 * width, width), BF16)

    def whole(sectors):
        return [pltpu.VMEM((sectors, width, width), F32)]

    parts_outer = call(functools.partial(assemble, n), "assemble", one // 2, split_parts(2), [VMEM] * n, outer, whole(2))
    parts_inner, own = call(
        functools.partial(own_sectors, n), "own", 4 * kops * one,
        [split_parts(nloc - 2), jax.ShapeDtypeStruct((nloc, kops * rows, width), F32)],
        [VMEM] * (n + 2), [*inner, parts_outer, left_parts], whole(nloc - 2),
    )
    parts_outside, ends = call(
        functools.partial(outside_sectors, n), "outside", 2 * kops * one,
        [split_parts(2), jax.ShapeDtypeStruct((2, kops * rows, width), F32)],
        [VMEM] * 3, [above, below, left_parts], whole(2),
    )
    chunk = [jax.ShapeDtypeStruct((nloc // 2, rows, width), F32)] * 2
    result = call(
        functools.partial(first_chunk, n, nloc), "first_chunk", nloc * kops * one // n, chunk,
        [SMEM] * 2 + [VMEM] * 4, [shifts, allowed, own, ends, right_hi, right_lo],
    )

    def mine(step):
        return call(
            functools.partial(later_chunk, n, nloc, step), "chunk", 4 * nloc * kops * one // n, chunk,
            [SMEM] * 2 + [VMEM] * 6,
            [shifts, allowed, parts_outer, parts_inner, parts_outside, left_parts, right_hi, right_lo],
        )

    for step in range(1, n):
        result = [lax.ppermute(r, "op", route) + o for r, o in zip(result, mine(step))]
    return jnp.concatenate(result)


def solution(mesh):
    return jax.shard_map(
        shards,
        mesh=mesh,
        in_specs=(
            P(("parts", "sec", "sub"), "op", None),
            P("op", None, None),
            P("op", None, None),
            P("op"),
            P("op", None),
        ),
        out_specs=P(("parts", "sec", "sub"), "op", None),
        check_vma=False,
    )
```

time: 59.6 us -> 62.5 us (1.049)
  the two profiles are of different devices: /device:TPU:1 before, /device:TPU:10 now
where the time goes in v1:
time: 62.5 us; the launch traced here: 62.3 us
  starting transfers between devices  29.9 us (48%)
  Pallas kernels  18 us (29%)
  waiting for transfers between devices  8.93 us (14%)
  local copies, waits for them, and re-layouts  4.22 us (7%)
  other arithmetic  0.97 us (2%)
    pallas_call x8, Pallas kernels, call(): pl.pallas_call(body, name=name, out_shape=out_shape, in_specs=in_specs, o...  18 us
    ppermute x6, starting transfers between devices, shards(): lax.ppermute(r, 'op', route) + o  11 us
    ppermute x3, starting transfers between devices, shards(): lax.ppermute(inner[-1] + zero[0, 0] if step == 1 else inner[-1], 'op', ro...  8.62 us
    ppermute x2, starting transfers between devices, shifted(): return lax.ppermute(block, axis, route)  5.56 us
    ppermute x3, starting transfers between devices, shards(): lax.ppermute(outer[-1] + zero[0, 0] if step == 1 else outer[-1], 'op', ro...  4.7 us
    unnamed x8, local copies, waits for them, and re-layouts  3.19 us
    ppermute x2, waiting for transfers between devices, shifted(): return lax.ppermute(block, axis, route)  2.57 us
    ppermute x3, waiting for transfers between devices, shards(): lax.ppermute(outer[-1] + zero[0, 0] if step == 1 else outer[-1], 'op', ro...  2.51 us
  transfers between devices with their start and end apart: 14, of which 5 were waited for; matrix products, arithmetic and copies ran while one was open for 0% of the time, Pallas kernels for 25%

profile of v1, /device:TPU:10, one launch (start us, length us, event | category | flops | bytes accessed | tf_op | source)
XLA Modules:
  0.0 62.3 jit_solution(8962501240599960573)
XLA Ops:
  0.0 1.0 %fusion = (f32[2,64,256]{2,1,0:T(8,128)S(1)}, f32[2,64,256]{2,1,0:T(8,128)S(1)}) fusion(f32[4,64,256]{2,1,0:T(8,128)} %param.5), kind=kLoop, calls=%fused_computation.5 | loop fusion | bytes 524288 | tf_op jit(solution)/shard_map/slice | solution.py:162
  1.0 2.6 %collective-permute-start = (f32[2,64,256]{2,1,0:T(8,128)S(1)}, f32[2,64,256]{2,1,0:T(8,128)S(1)}, u32[]{:S(2)}, u32[]{:S(2)}) collective-permute-start(f32[2,64,256]{2,1,0:T(8,128)S(1)} %get-tuple-element.38.refs_0_), channel_id=1, source_target_pairs={{0,4},{4,12},{12,8},{8,0},{1,5},{5,13},{13,9},{9,1},{2,6},{6,14},{... | collective-permute-start | bytes 393224 | tf_op jit(solution)/shard_map/ppermute | solution.py:164
  3.6 0.4 collective-permute-start.3
  4.1 0.0 copy-start.2
  4.1 1.6 %copy-done.2 = f32[8,256,256]{2,1,0:T(8,128)S(1)} copy-done((f32[8,256,256]{2,1,0:T(8,128)S(1)}, f32[8,256,256]{2,1,0:T(8,128)}, u32[]{:S(2)}) %copy-start.2) | copy-done | bytes 2097176
  5.7 0.0 copy-start.3
  5.7 1.6 %copy-done.3 = f32[8,256,256]{2,1,0:T(8,128)S(1)} copy-done((f32[8,256,256]{2,1,0:T(8,128)S(1)}, f32[8,256,256]{2,1,0:T(8,128)}, u32[]{:S(2)}) %copy-start.3) | copy-done | bytes 2097176
  7.3 1.1 %prepare.1 = (bf16[4,8,64,768]{3,2,1,0:T(8,128)(2,1)S(1)}, bf16[2048,256]{1,0:T(8,128)(2,1)S(1)}, bf16[2048,256]{1,0:T(8,128)(2,1)S(1)}, f32[1,128]{1,0:T(1,128)S(1)}) custom-call(f32[8,256,256]{2,1,0:T(8,128)S(1)} %copy-done.2, f32[8,256,256]{2,1,0:T(8,128)S(1)} %copy-done.3), custom_call_target="tpu_custom_call" | custom-call | flops 3221225472 | bytes 1048576 | tf_op jit(solution)/shard_map/prepare/pallas_call | solution.py:136
  8.4 0.0 collective-permute-done.refs_1_
  8.4 2.6 %collective-permute-start.1 = (f32[2,64,256]{2,1,0:T(8,128)S(1)}, f32[2,64,256]{2,1,0:T(8,128)S(1)}, u32[]{:S(2)}, u32[]{:S(2)}) collective-permute-start(f32[2,64,256]{2,1,0:T(8,128)S(1)} %broadcast_add_fusion.1), channel_id=1, source_target_pairs={{0,4},{4,12},{12,8},{8,0},{1,5},{5,13},{13,9},{9,1},{2,6},{6,14},{... | collective-permute-start | bytes 393224 | tf_op jit(solution)/shard_map/ppermute | solution.py:164
  11.0 0.0 collective-permute-done.3.refs_1_
  11.1 1.8 %collective-permute-start.4 = (f32[2,64,256]{2,1,0:T(8,128)S(1)}, f32[2,64,256]{2,1,0:T(8,128)S(1)}, u32[]{:S(2)}, u32[]{:S(2)}) collective-permute-start(f32[2,64,256]{2,1,0:T(8,128)S(1)} %broadcast_add_fusion), channel_id=1, source_target_pairs={{0,4},{4,12},{12,8},{8,0},{1,5},{5,13},{13,9},{9,1},{2,6},{6,14},{... | collective-permute-start | bytes 393224 | tf_op jit(solution)/shard_map/ppermute | solution.py:165
  12.9 2.0 %collective-permute-done.1.refs_2_ = f32[2,64,256]{2,1,0:T(8,128)S(1)} collective-permute-done((f32[2,64,256]{2,1,0:T(8,128)S(1)}, f32[2,64,256]{2,1,0:T(8,128)S(1)}, u32[]{:S(2)}, u32[]{:S(2)}) %collective-permute-start.1) | collective-permute-done | bytes 131104 | tf_op jit(solution)/shard_map/ppermute | solution.py:164
  14.9 3.4 %collective-permute-start.2 = (f32[2,64,256]{2,1,0:T(8,128)S(1)}, f32[2,64,256]{2,1,0:T(8,128)S(1)}, u32[]{:S(2)}, u32[]{:S(2)}) collective-permute-start(f32[2,64,256]{2,1,0:T(8,128)S(1)} %collective-permute-done.1.refs_2_), channel_id=1, source_target_pairs={{0,4},{4,12},{12,8},{8,0},{1,5},{5,13},{13,9},{9,1},{2,6},{6,14},{... | collective-permute-start | bytes 393224 | tf_op jit(solution)/shard_map/ppermute | solution.py:164
  18.3 0.0 collective-permute-done.4.refs_2_
  18.3 2.5 %collective-permute-start.5 = (f32[2,64,256]{2,1,0:T(8,128)S(1)}, f32[2,64,256]{2,1,0:T(8,128)S(1)}, u32[]{:S(2)}, u32[]{:S(2)}) collective-permute-start(f32[2,64,256]{2,1,0:T(8,128)S(1)} %collective-permute-done.4.refs_2_), channel_id=1, source_target_pairs={{0,4},{4,12},{12,8},{8,0},{1,5},{5,13},{13,9},{9,1},{2,6},{6,14},{... | collective-permute-start | bytes 393224 | tf_op jit(solution)/shard_map/ppermute | solution.py:165
  20.8 2.5 %collective-permute-done.5.refs_3_ = f32[2,64,256]{2,1,0:T(8,128)S(1)} collective-permute-done((f32[2,64,256]{2,1,0:T(8,128)S(1)}, f32[2,64,256]{2,1,0:T(8,128)S(1)}, u32[]{:S(2)}, u32[]{:S(2)}) %collective-permute-start.5) | collective-permute-done | bytes 131104 | tf_op jit(solution)/shard_map/ppermute | solution.py:165
  23.3 1.9 %collective-permute-start.6 = (f32[4,64,256]{2,1,0:T(8,128)S(1)}, f32[4,64,256]{2,1,0:T(8,128)S(1)}, u32[]{:S(2)}, u32[]{:S(2)}) collective-permute-start(f32[4,64,256]{2,1,0:T(8,128)S(1)} %pad_maximum_fusion), channel_id=1, source_target_pairs={{0,1},{1,2},{2,3},{4,5},{5,6},{6,7},{8,9},{9,10},{10,11},{12,13},{... | collective-permute-start | bytes 786440 | tf_op jit(solution)/shard_map/ppermute | solution.py:18
  25.3 3.6 %collective-permute-start.7 = (f32[4,64,256]{2,1,0:T(8,128)S(1)}, f32[4,64,256]{2,1,0:T(8,128)S(1)}, u32[]{:S(2)}, u32[]{:S(2)}) collective-permute-start(f32[4,64,256]{2,1,0:T(8,128)S(1)} %pad_maximum_fusion.1), channel_id=1, source_target_pairs={{1,0},{2,1},{3,2},{5,4},{6,5},{7,6},{9,8},{10,9},{11,10},{13,12},{... | collective-permute-start | bytes 786440 | tf_op jit(solution)/shard_map/ppermute | solution.py:18
  28.9 0.2 assemble.1.refs_4_.outer
  29.1 0.0 collective-permute-done.2.refs_3_
  29.1 1.1 %own.1 = (bf16[2,768,256]{2,1,0:T(8,128)(2,1)S(1)}, f32[4,512,256]{2,1,0:T(8,128)S(1)}) custom-call(f32[2,64,256]{2,1,0:T(8,128)S(1)} %get-tuple-element.38.refs_0_, f32[2,64,256]{2,1,0:T(8,128)S(1)} %collective-permute-done.refs_1_, f32[2,64,256]{2,1,0:T(8,128)S(1)} %collective-permute-done.1.refs_2_, f32[2,64,256]{2,1,0:T(8,128)S(1)} %collective-permute-done.2.refs_3_, ...), custom_call_target="tpu_custom_call" | custom-call | flops 3221225472 | bytes 1048576 | tf_op jit(solution)/shard_map/own/pallas_call | solution.py:136
  30.2 0.0 copy-start
  30.2 0.0 copy-start.1
  30.2 0.8 %collective-permute-done.6.above = f32[4,64,256]{2,1,0:T(8,128)S(1)} collective-permute-done((f32[4,64,256]{2,1,0:T(8,128)S(1)}, f32[4,64,256]{2,1,0:T(8,128)S(1)}, u32[]{:S(2)}, u32[]{:S(2)}) %collective-permute-start.6) | collective-permute-done | bytes 262176 | tf_op jit(solution)/shard_map/ppermute | solution.py:18
  31.0 1.8 %collective-permute-done.7.below = f32[4,64,256]{2,1,0:T(8,128)S(1)} collective-permute-done((f32[4,64,256]{2,1,0:T(8,128)S(1)}, f32[4,64,256]{2,1,0:T(8,128)S(1)}, u32[]{:S(2)}, u32[]{:S(2)}) %collective-permute-start.7) | collective-permute-done | bytes 262176 | tf_op jit(solution)/shard_map/ppermute | solution.py:18
  32.8 0.7 %outside.1 = (bf16[2,768,256]{2,1,0:T(8,128)(2,1)S(1)}, f32[2,512,256]{2,1,0:T(8,128)S(1)}) custom-call(f32[4,64,256]{2,1,0:T(8,128)S(1)} %collective-permute-done.6.above, f32[4,64,256]{2,1,0:T(8,128)S(1)} %collective-permute-done.7.below, bf16[4,8,64,768]{3,2,1,0:T(8,128)(2,1)S(1)} %get-tuple-element.22.refs_5_.left_parts), custom_call_target="tpu_custom_call" | custom-call | flops 1610612736 | bytes 1048576 | tf_op jit(solution)/shard_map/outside/pallas_call | solution.py:136
  33.5 0.0 copy-done
  33.5 0.0 copy-done.1
  33.5 1.8 %first_chunk.1 = (f32[2,64,256]{2,1,0:T(8,128)S(1)}, f32[2,64,256]{2,1,0:T(8,128)S(1)}) custom-call(s32[8]{0:T(128)S(1)} %copy-done.1, s32[8,16]{1,0:T(8,128)S(1)} %copy-done, f32[4,512,256]{2,1,0:T(8,128)S(1)} %get-tuple-element.23.own, f32[2,512,256]{2,1,0:T(8,128)S(1)} %get-tuple-element.24.ends, bf16[2048,256]{1,0:T(8,128)(2,1)S(1)} %get-tuple-element.25.right_hi, ...), custom_call_target="tpu_custom_call" | custom-call | flops 805306368 | bytes 1048576 | tf_op jit(solution)/shard_map/first_chunk/pallas_call | solution.py:136
  35.3 3.4 %collective-permute-start.8 = (f32[2,64,256]{2,1,0:T(8,128)S(1)}, f32[2,64,256]{2,1,0:T(8,128)S(1)}, u32[]{:S(2)}, u32[]{:S(2)}) collective-permute-start(f32[2,64,256]{2,1,0:T(8,128)S(1)} %get-tuple-element.27), channel_id=1, source_target_pairs={{0,4},{4,12},{12,8},{8,0},{1,5},{5,13},{13,9},{9,1},{2,6},{6,14},{... | collective-permute-start | bytes 393224 | tf_op jit(solution)/shard_map/ppermute | solution.py:201
  38.7 0.1 collective-permute-start.11
  38.7 4.4 %chunk.3 = (f32[2,64,256]{2,1,0:T(8,128)S(1)}, f32[2,64,256]{2,1,0:T(8,128)S(1)}) custom-call(s32[8]{0:T(128)S(1)} %copy-done.1, s32[8,16]{1,0:T(8,128)S(1)} %copy-done, bf16[2,768,256]{2,1,0:T(8,128)(2,1)S(1)} %assemble.1.refs_4_.outer, bf16[2,768,256]{2,1,0:T(8,128)(2,1)S(1)} %get-tuple-element.28.inner, ...), custom_call_target="tpu_custom_call" | custom-call | flops 3221225472 | bytes 1048576 | tf_op jit(solution)/shard_map/chunk/pallas_call | solution.py:136
  43.2 1.8 %collective-permute-done.11 = f32[2,64,256]{2,1,0:T(8,128)S(1)} collective-permute-done((f32[2,64,256]{2,1,0:T(8,128)S(1)}, f32[2,64,256]{2,1,0:T(8,128)S(1)}, u32[]{:S(2)}, u32[]{:S(2)}) %collective-permute-start.11) | collective-permute-done | bytes 131104 | tf_op jit(solution)/shard_map/ppermute | solution.py:201
  45.0 2.3 %collective-permute-start.12 = (f32[2,64,256]{2,1,0:T(8,128)S(1)}, f32[2,64,256]{2,1,0:T(8,128)S(1)}, u32[]{:S(2)}, u32[]{:S(2)}) collective-permute-start(f32[2,64,256]{2,1,0:T(8,128)S(1)} %add.34), channel_id=1, source_target_pairs={{0,4},{4,12},{12,8},{8,0},{1,5},{5,13},{13,9},{9,1},{2,6},{6,14},{... | collective-permute-start | bytes 393224 | tf_op jit(solution)/shard_map/ppermute | solution.py:201
  47.3 0.0 collective-permute-done.8
  47.3 0.1 collective-permute-start.9
  47.4 4.4 %chunk.4 = (f32[2,64,256]{2,1,0:T(8,128)S(1)}, f32[2,64,256]{2,1,0:T(8,128)S(1)}) custom-call(s32[8]{0:T(128)S(1)} %copy-done.1, s32[8,16]{1,0:T(8,128)S(1)} %copy-done, bf16[2,768,256]{2,1,0:T(8,128)(2,1)S(1)} %assemble.1.refs_4_.outer, bf16[2,768,256]{2,1,0:T(8,128)(2,1)S(1)} %get-tuple-element.28.inner, ...), custom_call_target="tpu_custom_call" | custom-call | flops 3221225472 | bytes 1048576 | tf_op jit(solution)/shard_map/chunk/pallas_call | solution.py:136
  51.8 0.0 collective-permute-done.12
  51.9 2.7 %collective-permute-start.13 = (f32[2,64,256]{2,1,0:T(8,128)S(1)}, f32[2,64,256]{2,1,0:T(8,128)S(1)}, u32[]{:S(2)}, u32[]{:S(2)}) collective-permute-start(f32[2,64,256]{2,1,0:T(8,128)S(1)} %add.35), channel_id=1, source_target_pairs={{0,4},{4,12},{12,8},{8,0},{1,5},{5,13},{13,9},{9,1},{2,6},{6,14},{... | collective-permute-start | bytes 393224 | tf_op jit(solution)/shard_map/ppermute | solution.py:201
  54.6 0.0 collective-permute-done.9
  54.6 2.5 %collective-permute-start.10 = (f32[2,64,256]{2,1,0:T(8,128)S(1)}, f32[2,64,256]{2,1,0:T(8,128)S(1)}, u32[]{:S(2)}, u32[]{:S(2)}) collective-permute-start(f32[2,64,256]{2,1,0:T(8,128)S(1)} %add.32), channel_id=1, source_target_pairs={{0,4},{4,12},{12,8},{8,0},{1,5},{5,13},{13,9},{9,1},{2,6},{6,14},{... | collective-permute-start | bytes 393224 | tf_op jit(solution)/shard_map/ppermute | solution.py:201
  57.0 4.4 %chunk.5 = (f32[2,64,256]{2,1,0:T(8,128)S(1)}, f32[2,64,256]{2,1,0:T(8,128)S(1)}) custom-call(s32[8]{0:T(128)S(1)} %copy-done.1, s32[8,16]{1,0:T(8,128)S(1)} %copy-done, bf16[2,768,256]{2,1,0:T(8,128)(2,1)S(1)} %assemble.1.refs_4_.outer, bf16[2,768,256]{2,1,0:T(8,128)(2,1)S(1)} %get-tuple-element.28.inner, ...), custom_call_target="tpu_custom_call" | custom-call | flops 3221225472 | bytes 1048576 | tf_op jit(solution)/shard_map/chunk/pallas_call | solution.py:136
  61.5 0.0 collective-permute-done.13
  61.5 0.0 collective-permute-done.10
  61.6 0.7 %pad_maximum_fusion.2 = f32[4,64,256]{2,1,0:T(8,128)} fusion(f32[2,64,256]{2,1,0:T(8,128)S(1)} %add.36, f32[2,64,256]{2,1,0:T(8,128)S(1)} %add.33), kind=kLoop, calls=%fused_computation.2 | loop fusion | flops 65536 | bytes 524288 | tf_op jit(solution)/shard_map/concatenate | solution.py:202
  (14 shorter events, 0.3 us)
Async XLA Ops:
  1.0 7.4 %collective-permute-start = (f32[2,64,256]{2,1,0:T(8,128)S(1)}, f32[2,64,256]{2,1,0:T(8,128)S(1)}, u32[]{:S(2)}, u32[]{:S(2)}) collective-permute-start(f32[2,64,256]{2,1,0:T(8,128)S(1)} %get-tuple-element.38.refs_0_), channel_id=1, source_target_pairs={{0,4},{4,12},{12,8},{8,0},{1,5},{5,13},{13,9},{9,1},{2,6},{6,14},{... | collective-permute-start | bytes 393224 | tf_op jit(solution)/shard_map/ppermute | solution.py:164
  3.6 7.4 %collective-permute-start.3 = (f32[2,64,256]{2,1,0:T(8,128)S(1)}, f32[2,64,256]{2,1,0:T(8,128)S(1)}, u32[]{:S(2)}, u32[]{:S(2)}) collective-permute-start(f32[2,64,256]{2,1,0:T(8,128)S(1)} %get-tuple-element.37.refs_0_), channel_id=1, source_target_pairs={{0,4},{4,12},{12,8},{8,0},{1,5},{5,13},{13,9},{9,1},{2,6},{6,14},{... | collective-permute-start | bytes 393224 | tf_op jit(solution)/shard_map/ppermute | solution.py:165
  4.1 1.6 %copy-start.2 = (f32[8,256,256]{2,1,0:T(8,128)S(1)}, f32[8,256,256]{2,1,0:T(8,128)}, u32[]{:S(2)}) copy-start(f32[8,256,256]{2,1,0:T(8,128)} %left_ref.1) | copy-start | bytes 6291460
  5.7 1.6 %copy-start.3 = (f32[8,256,256]{2,1,0:T(8,128)S(1)}, f32[8,256,256]{2,1,0:T(8,128)}, u32[]{:S(2)}) copy-start(f32[8,256,256]{2,1,0:T(8,128)} %right_ref.1) | copy-start | bytes 6291460
  8.4 6.5 %collective-permute-start.1 = (f32[2,64,256]{2,1,0:T(8,128)S(1)}, f32[2,64,256]{2,1,0:T(8,128)S(1)}, u32[]{:S(2)}, u32[]{:S(2)}) collective-permute-start(f32[2,64,256]{2,1,0:T(8,128)S(1)} %broadcast_add_fusion.1), channel_id=1, source_target_pairs={{0,4},{4,12},{12,8},{8,0},{1,5},{5,13},{13,9},{9,1},{2,6},{6,14},{... | collective-permute-start | bytes 393224 | tf_op jit(solution)/shard_map/ppermute | solution.py:164
  11.1 7.2 %collective-permute-start.4 = (f32[2,64,256]{2,1,0:T(8,128)S(1)}, f32[2,64,256]{2,1,0:T(8,128)S(1)}, u32[]{:S(2)}, u32[]{:S(2)}) collective-permute-start(f32[2,64,256]{2,1,0:T(8,128)S(1)} %broadcast_add_fusion), channel_id=1, source_target_pairs={{0,4},{4,12},{12,8},{8,0},{1,5},{5,13},{13,9},{9,1},{2,6},{6,14},{... | collective-permute-start | bytes 393224 | tf_op jit(solution)/shard_map/ppermute | solution.py:165
  14.9 14.2 %collective-permute-start.2 = (f32[2,64,256]{2,1,0:T(8,128)S(1)}, f32[2,64,256]{2,1,0:T(8,128)S(1)}, u32[]{:S(2)}, u32[]{:S(2)}) collective-permute-start(f32[2,64,256]{2,1,0:T(8,128)S(1)} %collective-permute-done.1.refs_2_), channel_id=1, source_target_pairs={{0,4},{4,12},{12,8},{8,0},{1,5},{5,13},{13,9},{9,1},{2,6},{6,14},{... | collective-permute-start | bytes 393224 | tf_op jit(solution)/shard_map/ppermute | solution.py:164
  18.3 5.0 %collective-permute-start.5 = (f32[2,64,256]{2,1,0:T(8,128)S(1)}, f32[2,64,256]{2,1,0:T(8,128)S(1)}, u32[]{:S(2)}, u32[]{:S(2)}) collective-permute-start(f32[2,64,256]{2,1,0:T(8,128)S(1)} %collective-permute-done.4.refs_2_), channel_id=1, source_target_pairs={{0,4},{4,12},{12,8},{8,0},{1,5},{5,13},{13,9},{9,1},{2,6},{6,14},{... | collective-permute-start | bytes 393224 | tf_op jit(solution)/shard_map/ppermute | solution.py:165
  23.3 7.7 %collective-permute-start.6 = (f32[4,64,256]{2,1,0:T(8,128)S(1)}, f32[4,64,256]{2,1,0:T(8,128)S(1)}, u32[]{:S(2)}, u32[]{:S(2)}) collective-permute-start(f32[4,64,256]{2,1,0:T(8,128)S(1)} %pad_maximum_fusion), channel_id=1, source_target_pairs={{0,1},{1,2},{2,3},{4,5},{5,6},{6,7},{8,9},{9,10},{10,11},{12,13},{... | collective-permute-start | bytes 786440 | tf_op jit(solution)/shard_map/ppermute | solution.py:18
  25.3 7.5 %collective-permute-start.7 = (f32[4,64,256]{2,1,0:T(8,128)S(1)}, f32[4,64,256]{2,1,0:T(8,128)S(1)}, u32[]{:S(2)}, u32[]{:S(2)}) collective-permute-start(f32[4,64,256]{2,1,0:T(8,128)S(1)} %pad_maximum_fusion.1), channel_id=1, source_target_pairs={{1,0},{2,1},{3,2},{5,4},{6,5},{7,6},{9,8},{10,9},{11,10},{13,12},{... | collective-permute-start | bytes 786440 | tf_op jit(solution)/shard_map/ppermute | solution.py:18
  30.2 3.3 %copy-start = (s32[8,16]{1,0:T(8,128)S(1)}, s32[8,16]{1,0:T(8,128)}, u32[]{:S(2)}) copy-start(s32[8,16]{1,0:T(8,128)} %allowed_ref.7) | copy-start | bytes 1540
  30.2 3.3 %copy-start.1 = (s32[8]{0:T(128)S(1)}, s32[8]{0:T(128)}, u32[]{:S(2)}) copy-start(s32[8]{0:T(128)} %shifts_ref.7) | copy-start | bytes 100
  35.3 12.0 %collective-permute-start.8 = (f32[2,64,256]{2,1,0:T(8,128)S(1)}, f32[2,64,256]{2,1,0:T(8,128)S(1)}, u32[]{:S(2)}, u32[]{:S(2)}) collective-permute-start(f32[2,64,256]{2,1,0:T(8,128)S(1)} %get-tuple-element.27), channel_id=1, source_target_pairs={{0,4},{4,12},{12,8},{8,0},{1,5},{5,13},{13,9},{9,1},{2,6},{6,14},{... | collective-permute-start | bytes 393224 | tf_op jit(solution)/shard_map/ppermute | solution.py:201
  38.7 6.3 %collective-permute-start.11 = (f32[2,64,256]{2,1,0:T(8,128)S(1)}, f32[2,64,256]{2,1,0:T(8,128)S(1)}, u32[]{:S(2)}, u32[]{:S(2)}) collective-permute-start(f32[2,64,256]{2,1,0:T(8,128)S(1)} %get-tuple-element.33), channel_id=1, source_target_pairs={{0,4},{4,12},{12,8},{8,0},{1,5},{5,13},{13,9},{9,1},{2,6},{6,14},{... | collective-permute-start | bytes 393224 | tf_op jit(solution)/shard_map/ppermute | solution.py:201
  45.0 6.8 %collective-permute-start.12 = (f32[2,64,256]{2,1,0:T(8,128)S(1)}, f32[2,64,256]{2,1,0:T(8,128)S(1)}, u32[]{:S(2)}, u32[]{:S(2)}) collective-permute-start(f32[2,64,256]{2,1,0:T(8,128)S(1)} %add.34), channel_id=1, source_target_pairs={{0,4},{4,12},{12,8},{8,0},{1,5},{5,13},{13,9},{9,1},{2,6},{6,14},{... | collective-permute-start | bytes 393224 | tf_op jit(solution)/shard_map/ppermute | solution.py:201
  47.3 7.2 %collective-permute-start.9 = (f32[2,64,256]{2,1,0:T(8,128)S(1)}, f32[2,64,256]{2,1,0:T(8,128)S(1)}, u32[]{:S(2)}, u32[]{:S(2)}) collective-permute-start(f32[2,64,256]{2,1,0:T(8,128)S(1)} %add.31), channel_id=1, source_target_pairs={{0,4},{4,12},{12,8},{8,0},{1,5},{5,13},{13,9},{9,1},{2,6},{6,14},{... | collective-permute-start | bytes 393224 | tf_op jit(solution)/shard_map/ppermute | solution.py:201
  51.9 9.6 %collective-permute-start.13 = (f32[2,64,256]{2,1,0:T(8,128)S(1)}, f32[2,64,256]{2,1,0:T(8,128)S(1)}, u32[]{:S(2)}, u32[]{:S(2)}) collective-permute-start(f32[2,64,256]{2,1,0:T(8,128)S(1)} %add.35), channel_id=1, source_target_pairs={{0,4},{4,12},{12,8},{8,0},{1,5},{5,13},{13,9},{9,1},{2,6},{6,14},{... | collective-permute-start | bytes 393224 | tf_op jit(solution)/shard_map/ppermute | solution.py:201
  54.6 6.9 %collective-permute-start.10 = (f32[2,64,256]{2,1,0:T(8,128)S(1)}, f32[2,64,256]{2,1,0:T(8,128)S(1)}, u32[]{:S(2)}, u32[]{:S(2)}) collective-permute-start(f32[2,64,256]{2,1,0:T(8,128)S(1)} %add.32), channel_id=1, source_target_pairs={{0,4},{4,12},{12,8},{8,0},{1,5},{5,13},{13,9},{9,1},{2,6},{6,14},{... | collective-permute-start | bytes 393224 | tf_op jit(solution)/shard_map/ppermute | solution.py:201

commit v2 on v1

v2 whole, which is shorter than its diff:
```python
import functools

import jax
import jax.numpy as jnp
from jax import lax
from jax.experimental import pallas as pl
from jax.experimental.pallas import tpu as pltpu
from jax.sharding import PartitionSpec as P

F32, BF16 = jnp.float32, jnp.bfloat16
SMEM = pl.BlockSpec(memory_space=pltpu.SMEM)
VMEM = pl.BlockSpec(memory_space=pltpu.VMEM)


def shifted(block, axis, distance):
    devices = range(lax.axis_size(axis))
    route = [(i - distance, i) for i in devices if i - distance in devices]
    return lax.ppermute(block, axis, route)


def ring_route(n):
    order = [0] + [i for i in range(n) if i % 2] + [i for i in reversed(range(1, n)) if i % 2 == 0]
    return [(order[i], order[(i + 1) % n]) for i in range(n)]


def ring_place(n, steps_back):
    me = lax.axis_index("op")
    place = jnp.where(me == 0, 0, jnp.where(lax.rem(me, 2) == 1, (me + 1) // 2, n - me // 2))
    at = lax.rem(place - steps_back + 2 * n, n)
    return jnp.where(at == 0, 0, jnp.where(at <= n // 2, 2 * at - 1, 2 * (n - at)))


def exchanged(n):
    return n == 4


def block_owner(n, j):
    return jnp.bitwise_xor(lax.axis_index("op"), j) if exchanged(n) else ring_place(n, j)


def chunk_target(n, step):
    return jnp.bitwise_xor(lax.axis_index("op"), n - 1 - step) if exchanged(n) else ring_place(n, step + 1)


def split(x):
    hi = x.astype(BF16)
    return hi, (x - hi.astype(F32)).astype(BF16)


def dot3(a, b):
    one = functools.partial(jnp.dot, preferred_element_type=F32)
    return one(a[0], b[0]) + (one(a[0], b[1]) + one(a[1], b[0]))


def prepare(left_ref, right_ref, left_parts, right_hi, right_lo, zero):
    n, kops, rows, _ = left_parts.shape
    width = left_ref.shape[1]
    zero[...] = jnp.zeros_like(zero)
    for k in range(kops):
        hi, lo = split(left_ref[k])
        parts = jnp.concatenate([hi, hi, lo], axis=1)
        for c in range(n):
            left_parts[c, k] = parts[c * rows : (c + 1) * rows]
        right_hi[k * width : (k + 1) * width, :], right_lo[k * width : (k + 1) * width, :] = split(right_ref[k].T)


def stacked(block):
    hi, lo = split(block)
    return jnp.concatenate([hi, lo, hi], axis=0)


def place_rows(n, target, blocks):
    for j, block in enumerate(blocks):
        rows = block.shape[-2]
        target[..., pl.ds(pl.multiple_of(block_owner(n, j) * rows, rows), rows), :] = block


def assemble(n, *refs):
    parts, psi = refs[n:]
    place_rows(n, psi, [ref[...] for ref in refs[:n]])
    for i in range(parts.shape[0]):
        parts[i] = stacked(psi[i])


def first_product(left, parts):
    return jnp.dot(left, parts, preferred_element_type=F32)


def chunk_left(n, step, left_parts):
    return left_parts[chunk_target(n, step)].reshape(-1, left_parts.shape[-1])


def own_sectors(n, *refs):
    (outer, left_parts), (inner, middle, psi) = refs[n : n + 2], refs[n + 2 :]
    assemble(n, *refs[:n], inner, psi)
    left = chunk_left(n, 0, left_parts)
    middle[0] = first_product(left, outer[0])
    for i in range(inner.shape[0]):
        middle[i + 1] = first_product(left, inner[i])
    middle[inner.shape[0] + 1] = first_product(left, outer[1])


def second_product(nloc, shifts_ref, allowed_ref, middle, right_hi, right_lo, out):
    kops = shifts_ref.shape[0]
    rows, width = out.shape[1:]
    first = lax.axis_index(("sec", "sub")) * nloc
    highs, lows = [], []
    for k in range(kops):
        shift = shifts_ref[k]
        blocks = []
        for t in range(nloc):
            source = jnp.clip(first + t - shift, 0, allowed_ref.shape[1] - 1)
            block = middle[t + 1 - shift, k * rows : (k + 1) * rows]
            blocks.append(block * allowed_ref[k, source].astype(F32))
        hi, lo = split(jnp.concatenate(blocks))
        highs.append(hi)
        lows.append(lo)
    high, low = jnp.concatenate(highs, axis=1), jnp.concatenate(lows, axis=1)
    out[...] = dot3((high, low), (right_hi[...], right_lo[...])).reshape(nloc, rows, width)


def first_chunk(n, nloc, shifts_ref, allowed_ref, own, above, below, left_parts, right_hi, right_lo, out, outside, psi, middle):
    place_rows(n, psi.at[0], [above[j] for j in range(n)])
    place_rows(n, psi.at[1], [below[j] for j in range(n)])
    left = chunk_left(n, 0, left_parts)
    for i in range(2):
        outside[i] = stacked(psi[i])
        middle[i * (nloc + 1)] = first_product(left, outside[i])
    for i in range(nloc):
        middle[i + 1] = own[i]
    second_product(nloc, shifts_ref, allowed_ref, middle, right_hi, right_lo, out)


def later_chunk(n, nloc, step, shifts_ref, allowed_ref, outer, inner, outside, left_parts, right_hi, right_lo, out, middle):
    left = chunk_left(n, step, left_parts)
    sources = [outside.at[0], outer.at[0], *[inner.at[i] for i in range(nloc - 2)], outer.at[1], outside.at[1]]
    for i, ref in enumerate(sources):
        middle[i] = first_product(left, ref[...])
    second_product(nloc, shifts_ref, allowed_ref, middle, right_hi, right_lo, out)


def call(body, name, flops, out_shape, in_specs, operands, scratch=()):
    return pl.pallas_call(
        body,
        name=name,
        out_shape=out_shape,
        in_specs=in_specs,
        out_specs=jax.tree.map(lambda _: VMEM, out_shape),
        scratch_shapes=list(scratch),
        compiler_params=pltpu.CompilerParams(vmem_limit_bytes=24 * 2**20),
        cost_estimate=pl.CostEstimate(flops=flops, bytes_accessed=2**20, transcendentals=0),
    )(*operands)


def gather(n, psi, zero):
    nloc = psi.shape[0]
    halves = [lambda b: b[:: nloc - 1], lambda b: b[1 : nloc - 1]]
    if not exchanged(n):
        blocks = [[part(psi)] for part in halves]
        for _ in range(n - 1):
            for held in blocks:
                held.append(lax.ppermute(held[-1], "op", ring_route(n)))
        return blocks
    two = lax.ppermute(psi, "op", [(z, z ^ 2) for z in range(n)])
    one = lax.ppermute(psi, "op", [(z, z ^ 1) for z in range(n)])
    late = 0 * two + zero[0, 0]
    blocks = []
    for part in halves:
        passed = lax.ppermute(part(two), "op", [(1, 0), (2, 3)])
        direct = lax.ppermute(part(psi) + part(late), "op", [(1, 2), (2, 1)])
        blocks.append([part(psi), part(one), part(two), passed + direct])
    return blocks


def scatter(n, mine):
    result = mine(0)
    if not exchanged(n):
        for step in range(1, n):
            result = lax.ppermute(result, "op", ring_route(n)) + mine(step)
        return result
    passed = lax.ppermute(result, "op", [(0, 1), (3, 2)])
    direct = lax.ppermute(result, "op", [(1, 2), (2, 1)])
    far = mine(1) + passed
    two = lax.ppermute(far, "op", [(z, z ^ 2) for z in range(n)])
    one = lax.ppermute(mine(2), "op", [(z, z ^ 1) for z in range(n)])
    return mine(3) + direct + two + one


def shards(psi, left_ops, right_ops, shifts, allowed):
    nloc, rows, width = psi.shape
    kops = left_ops.shape[0]
    n = lax.axis_size("op")
    one = 6 * width**3

    tall = jax.ShapeDtypeStruct((kops * width, width), BF16)
    parts = jax.ShapeDtypeStruct((n, kops, rows, 3 * width), BF16)
    zero = jax.ShapeDtypeStruct((1, 128), F32)
    left_parts, right_hi, right_lo, zero = call(
        prepare, "prepare", 4 * kops * one, [parts, tall, tall, zero], [VMEM] * 2, [left_ops, right_ops]
    )
    outer, inner = gather(n, psi, zero)
    above = shifted(jnp.concatenate([b[1:] for b in outer]), ("sec", "sub"), 1)
    below = shifted(jnp.concatenate([b[:1] for b in outer]), ("sec", "sub"), -1)

    def split_parts(sectors):
        return jax.ShapeDtypeStruct((sectors, 3 * width, width), BF16)

    def whole(sectors):
        return pltpu.VMEM((sectors, width, width), F32)

    parts_outer = call(functools.partial(assemble, n), "assemble", one // 2, split_parts(2), [VMEM] * n, outer, [whole(2)])
    parts_inner, own = call(
        functools.partial(own_sectors, n), "own", 4 * kops * one,
        [split_parts(nloc - 2), jax.ShapeDtypeStruct((nloc, kops * rows, width), F32)],
        [VMEM] * (n + 2), [*inner, parts_outer, left_parts], [whole(nloc - 2)],
    )
    chunk = jax.ShapeDtypeStruct((nloc, rows, width), F32)
    middle = pltpu.VMEM((nloc + 2, kops * rows, width), F32)
    first, parts_outside = call(
        functools.partial(first_chunk, n, nloc), "first_chunk", 2 * nloc * kops * one // n, [chunk, split_parts(2)],
        [SMEM] * 2 + [VMEM] * 6, [shifts, allowed, own, above, below, left_parts, right_hi, right_lo], [whole(2), middle],
    )

    def mine(step):
        if step == 0:
            return first
        return call(
            functools.partial(later_chunk, n, nloc, step), "chunk", 4 * nloc * kops * one // n, chunk,
            [SMEM] * 2 + [VMEM] * 6,
            [shifts, allowed, parts_outer, parts_inner, parts_outside, left_parts, right_hi, right_lo], [middle],
        )

    return scatter(n, mine)


def solution(mesh):
    return jax.shard_map(
        shards,
        mesh=mesh,
        in_specs=(
            P(("parts", "sec", "sub"), "op", None),
            P("op", None, None),
            P("op", None, None),
            P("op"),
            P("op", None),
        ),
        out_specs=P(("parts", "sec", "sub"), "op", None),
        check_vma=False,
    )
```

time: 62.5 us -> 72.3 us (1.16)
  the two profiles are of different devices: /device:TPU:10 before, /device:TPU:1 now
where the time goes in v2:
time: 72.3 us; the launch traced here: 72 us
  starting transfers between devices  31.3 us (43%)
  Pallas kernels  18.9 us (26%)
  waiting for transfers between devices  17.2 us (24%)
  local copies, waits for them, and re-layouts  3.28 us (5%)
  other arithmetic  0.98 us (1%)
    pallas_call x7, Pallas kernels, call(): pl.pallas_call(body, name=name, out_shape=out_shape, in_specs=in_specs, o...  18.9 us
    ppermute x1, starting transfers between devices, scatter(): passed = lax.ppermute(result, 'op', [(0, 1), (3, 2)])  10.6 us
    ppermute x2, starting transfers between devices, shifted(): return lax.ppermute(block, axis, route)  9.61 us
    ppermute x1, waiting for transfers between devices, scatter(): two = lax.ppermute(far, 'op', [(z, z ^ 2) for z in range(n)])  5.74 us
    ppermute x2, waiting for transfers between devices, shifted(): return lax.ppermute(block, axis, route)  4.48 us
    ppermute x1, waiting for transfers between devices, gather(): two = lax.ppermute(psi, 'op', [(z, z ^ 2) for z in range(n)])  4.38 us
    unnamed x10, local copies, waits for them, and re-layouts  3.2 us
    ppermute x2, starting transfers between devices, gather(): passed = lax.ppermute(part(two), 'op', [(1, 0), (2, 3)])  2.58 us
  transfers between devices with their start and end apart: 12, of which 5 were waited for; matrix products, arithmetic and copies ran while one was open for 0% of the time, Pallas kernels for 22%

profile of v2, /device:TPU:1, one launch (start us, length us, event | category | flops | bytes accessed | tf_op | source)
XLA Modules:
  0.0 72.0 jit_solution(13400149208159653103)
XLA Ops:
  0.0 2.1 %collective-permute-start = (f32[4,64,256]{2,1,0:T(8,128)}, f32[4,64,256]{2,1,0:T(8,128)S(1)}, u32[]{:S(2)}, u32[]{:S(2)}) collective-permute-start(f32[4,64,256]{2,1,0:T(8,128)} %param.5), channel_id=1, source_target_pairs={{0,4},{4,0},{8,12},{12,8},{1,5},{5,1},{9,13},{13,9},{2,6},{6,2},{1... | collective-permute-start | bytes 786440 | tf_op jit(solution)/shard_map/ppermute | solution.py:165
  2.1 2.3 %collective-permute-start.1 = (f32[4,64,256]{2,1,0:T(8,128)}, f32[4,64,256]{2,1,0:T(8,128)S(1)}, u32[]{:S(2)}, u32[]{:S(2)}) collective-permute-start(f32[4,64,256]{2,1,0:T(8,128)} %param.5), channel_id=1, source_target_pairs={{0,8},{4,12},{8,0},{12,4},{1,9},{5,13},{9,1},{13,5},{2,10},{6,14},... | collective-permute-start | bytes 786440 | tf_op jit(solution)/shard_map/ppermute | solution.py:164
  4.4 0.0 copy-start.2
  4.4 1.6 %copy-done.2 = f32[8,256,256]{2,1,0:T(8,128)S(1)} copy-done((f32[8,256,256]{2,1,0:T(8,128)S(1)}, f32[8,256,256]{2,1,0:T(8,128)}, u32[]{:S(2)}) %copy-start.2) | copy-done | bytes 2097176
  6.0 0.0 copy-start.3
  6.0 1.6 %copy-done.3 = f32[8,256,256]{2,1,0:T(8,128)S(1)} copy-done((f32[8,256,256]{2,1,0:T(8,128)S(1)}, f32[8,256,256]{2,1,0:T(8,128)}, u32[]{:S(2)}) %copy-start.3) | copy-done | bytes 2097176
  7.6 1.1 %prepare.1 = (bf16[4,8,64,768]{3,2,1,0:T(8,128)(2,1)S(1)}, bf16[2048,256]{1,0:T(8,128)(2,1)S(1)}, bf16[2048,256]{1,0:T(8,128)(2,1)S(1)}, f32[1,128]{1,0:T(1,128)S(1)}) custom-call(f32[8,256,256]{2,1,0:T(8,128)S(1)} %copy-done.2, f32[8,256,256]{2,1,0:T(8,128)S(1)} %copy-done.3), custom_call_target="tpu_custom_call" | custom-call | flops 3221225472 | bytes 1048576 | tf_op jit(solution)/shard_map/prepare/pallas_call | solution.py:143
  8.7 0.0 copy-start.4
  8.7 4.4 %collective-permute-done.1 = f32[4,64,256]{2,1,0:T(8,128)S(1)} collective-permute-done((f32[4,64,256]{2,1,0:T(8,128)}, f32[4,64,256]{2,1,0:T(8,128)S(1)}, u32[]{:S(2)}, u32[]{:S(2)}) %collective-permute-start.1) | collective-permute-done | bytes 262176 | tf_op jit(solution)/shard_map/ppermute | solution.py:164
  13.1 1.3 %collective-permute-start.2 = (f32[2,64,256]{2,1,0:T(8,128)S(1)}, f32[2,64,256]{2,1,0:T(8,128)S(1)}, u32[]{:S(2)}, u32[]{:S(2)}) collective-permute-start(f32[2,64,256]{2,1,0:T(8,128)S(1)} %get-tuple-element.26.refs_2_), channel_id=1, source_target_pairs={{4,0},{8,12},{5,1},{9,13},{6,2},{10,14},{7,3},{11,15},{20,16},{24,... | collective-permute-start | bytes 393224 | tf_op jit(solution)/shard_map/ppermute | solution.py:169
  14.4 0.0 collective-permute-done
  14.5 1.3 %collective-permute-start.4 = (f32[2,64,256]{2,1,0:T(8,128)S(1)}, f32[2,64,256]{2,1,0:T(8,128)S(1)}, u32[]{:S(2)}, u32[]{:S(2)}) collective-permute-start(f32[2,64,256]{2,1,0:T(8,128)S(1)} %get-tuple-element.25.refs_2_), channel_id=1, source_target_pairs={{4,0},{8,12},{5,1},{9,13},{6,2},{10,14},{7,3},{11,15},{20,16},{24,... | collective-permute-start | bytes 393224 | tf_op jit(solution)/shard_map/ppermute | solution.py:169
  15.8 0.1 multiply_add_fusion
  15.8 0.0 copy-done.4
  15.9 0.7 collective-permute-start.5
  16.6 0.7 collective-permute-start.3
  17.3 2.6 %collective-permute-done.2 = f32[2,64,256]{2,1,0:T(8,128)S(1)} collective-permute-done((f32[2,64,256]{2,1,0:T(8,128)S(1)}, f32[2,64,256]{2,1,0:T(8,128)S(1)}, u32[]{:S(2)}, u32[]{:S(2)}) %collective-permute-start.2) | collective-permute-done | bytes 131104 | tf_op jit(solution)/shard_map/ppermute | solution.py:169
  19.8 0.0 collective-permute-done.3
  19.9 7.7 %collective-permute-start.6 = (f32[4,64,256]{2,1,0:T(8,128)S(1)}, f32[4,64,256]{2,1,0:T(8,128)S(1)}, u32[]{:S(2)}, u32[]{:S(2)}) collective-permute-start(f32[4,64,256]{2,1,0:T(8,128)S(1)} %pad_maximum_fusion), channel_id=1, source_target_pairs={{0,1},{1,2},{2,3},{4,5},{5,6},{6,7},{8,9},{9,10},{10,11},{12,13},{... | collective-permute-start | bytes 786440 | tf_op jit(solution)/shard_map/ppermute | solution.py:18
  27.6 1.9 %collective-permute-start.7 = (f32[4,64,256]{2,1,0:T(8,128)S(1)}, f32[4,64,256]{2,1,0:T(8,128)S(1)}, u32[]{:S(2)}, u32[]{:S(2)}) collective-permute-start(f32[4,64,256]{2,1,0:T(8,128)S(1)} %pad_maximum_fusion.1), channel_id=1, source_target_pairs={{1,0},{2,1},{3,2},{5,4},{6,5},{7,6},{9,8},{10,9},{11,10},{13,12},{... | collective-permute-start | bytes 786440 | tf_op jit(solution)/shard_map/ppermute | solution.py:18
  29.6 0.2 assemble.1.refs_4_.outer
  29.7 0.0 collective-permute-done.4
  29.8 0.0 collective-permute-done.5
  29.8 0.0 copy-start
  29.8 0.0 copy-start.1
  29.8 1.0 %own.1 = (bf16[2,768,256]{2,1,0:T(8,128)(2,1)S(1)}, f32[4,512,256]{2,1,0:T(8,128)S(1)}) custom-call(f32[2,64,256]{2,1,0:T(8,128)S(1)} %get-tuple-element.24.refs_0_, f32[2,64,256]{2,1,0:T(8,128)S(1)} %get-tuple-element.27.refs_1_, f32[2,64,256]{2,1,0:T(8,128)S(1)} %get-tuple-element.25.refs_2_, f32[2,64,256]{2,1,0:T(8,128)S(1)} %add.35.refs_3_, ...), custom_call_target="tpu_custom_call" | custom-call | flops 3221225472 | bytes 1048576 | tf_op jit(solution)/shard_map/own/pallas_call | solution.py:143
  30.8 0.1 collective-permute-done.6.above
  30.9 4.4 %collective-permute-done.7.below = f32[4,64,256]{2,1,0:T(8,128)S(1)} collective-permute-done((f32[4,64,256]{2,1,0:T(8,128)S(1)}, f32[4,64,256]{2,1,0:T(8,128)S(1)}, u32[]{:S(2)}, u32[]{:S(2)}) %collective-permute-start.7) | collective-permute-done | bytes 262176 | tf_op jit(solution)/shard_map/ppermute | solution.py:18
  35.3 0.0 copy-done
  35.3 0.0 copy-done.1
  35.3 3.1 %first_chunk.1 = (f32[4,64,256]{2,1,0:T(8,128)S(1)}, bf16[2,768,256]{2,1,0:T(8,128)(2,1)S(1)}) custom-call(s32[8]{0:T(128)S(1)} %copy-done.1, s32[8,16]{1,0:T(8,128)S(1)} %copy-done, f32[4,512,256]{2,1,0:T(8,128)S(1)} %get-tuple-element.16.own, f32[4,64,256]{2,1,0:T(8,128)S(1)} %collective-permute-done.6.above, ...), custom_call_target="tpu_custom_call" | custom-call | flops 1610612736 | bytes 1048576 | tf_op jit(solution)/shard_map/first_chunk/pallas_call | solution.py:143
  38.4 10.6 %collective-permute-start.9 = (f32[4,64,256]{2,1,0:T(8,128)S(1)}, f32[4,64,256]{2,1,0:T(8,128)S(1)}, u32[]{:S(2)}, u32[]{:S(2)}) collective-permute-start(f32[4,64,256]{2,1,0:T(8,128)S(1)} %get-tuple-element.20), channel_id=1, source_target_pairs={{0,4},{12,8},{1,5},{13,9},{2,6},{14,10},{3,7},{15,11},{16,20},{28,... | collective-permute-start | bytes 786440 | tf_op jit(solution)/shard_map/ppermute | solution.py:181
  49.0 0.9 %collective-permute-start.8 = (f32[4,64,256]{2,1,0:T(8,128)S(1)}, f32[4,64,256]{2,1,0:T(8,128)S(1)}, u32[]{:S(2)}, u32[]{:S(2)}) collective-permute-start(f32[4,64,256]{2,1,0:T(8,128)S(1)} %get-tuple-element.20), channel_id=1, source_target_pairs={{4,8},{8,4},{5,9},{9,5},{6,10},{10,6},{7,11},{11,7},{20,24},{24,20... | collective-permute-start | bytes 786440 | tf_op jit(solution)/shard_map/ppermute | solution.py:182
  49.8 4.5 %chunk.5 = f32[4,64,256]{2,1,0:T(8,128)S(1)} custom-call(s32[8]{0:T(128)S(1)} %copy-done.1, s32[8,16]{1,0:T(8,128)S(1)} %copy-done, bf16[2,768,256]{2,1,0:T(8,128)(2,1)S(1)} %assemble.1.refs_4_.outer, bf16[2,768,256]{2,1,0:T(8,128)(2,1)S(1)} %get-tuple-element.15.inner, bf16[2,768,256]{2,1,0:T(8,128)(2,1)S(1)} %get-tuple-element.19.outside, ...), custom_call_target="tpu_custom_call" | custom-call | flops 3221225472 | bytes 1048576 | tf_op jit(solution)/shard_map/chunk/pallas_call | solution.py:143
  54.4 0.9 %collective-permute-start.11 = (f32[4,64,256]{2,1,0:T(8,128)S(1)}, f32[4,64,256]{2,1,0:T(8,128)S(1)}, u32[]{:S(2)}, u32[]{:S(2)}) collective-permute-start(f32[4,64,256]{2,1,0:T(8,128)S(1)} %chunk.5), channel_id=1, source_target_pairs={{0,4},{4,0},{8,12},{12,8},{1,5},{5,1},{9,13},{13,9},{2,6},{6,2},{1... | collective-permute-start | bytes 786440 | tf_op jit(solution)/shard_map/ppermute | solution.py:185
  55.2 4.5 %chunk.4 = f32[4,64,256]{2,1,0:T(8,128)S(1)} custom-call(s32[8]{0:T(128)S(1)} %copy-done.1, s32[8,16]{1,0:T(8,128)S(1)} %copy-done, bf16[2,768,256]{2,1,0:T(8,128)(2,1)S(1)} %assemble.1.refs_4_.outer, bf16[2,768,256]{2,1,0:T(8,128)(2,1)S(1)} %get-tuple-element.15.inner, bf16[2,768,256]{2,1,0:T(8,128)(2,1)S(1)} %get-tuple-element.19.outside, ...), custom_call_target="tpu_custom_call" | custom-call | flops 3221225472 | bytes 1048576 | tf_op jit(solution)/shard_map/chunk/pallas_call | solution.py:143
  59.8 0.0 collective-permute-done.9
  59.8 1.1 %collective-permute-start.10 = (f32[4,64,256]{2,1,0:T(8,128)S(1)}, f32[4,64,256]{2,1,0:T(8,128)S(1)}, u32[]{:S(2)}, u32[]{:S(2)}) collective-permute-start(f32[4,64,256]{2,1,0:T(8,128)S(1)} %add.37), channel_id=1, source_target_pairs={{0,8},{4,12},{8,0},{12,4},{1,9},{5,13},{9,1},{13,5},{2,10},{6,14},... | collective-permute-start | bytes 786440 | tf_op jit(solution)/shard_map/ppermute | solution.py:184
  60.9 4.5 %chunk.3 = f32[4,64,256]{2,1,0:T(8,128)S(1)} custom-call(s32[8]{0:T(128)S(1)} %copy-done.1, s32[8,16]{1,0:T(8,128)S(1)} %copy-done, bf16[2,768,256]{2,1,0:T(8,128)(2,1)S(1)} %assemble.1.refs_4_.outer, bf16[2,768,256]{2,1,0:T(8,128)(2,1)S(1)} %get-tuple-element.15.inner, bf16[2,768,256]{2,1,0:T(8,128)(2,1)S(1)} %get-tuple-element.19.outside, ...), custom_call_target="tpu_custom_call" | custom-call | flops 3221225472 | bytes 1048576 | tf_op jit(solution)/shard_map/chunk/pallas_call | solution.py:143
  65.4 0.0 collective-permute-done.11
  65.4 0.0 collective-permute-done.8
  65.5 5.7 %collective-permute-done.10 = f32[4,64,256]{2,1,0:T(8,128)S(1)} collective-permute-done((f32[4,64,256]{2,1,0:T(8,128)S(1)}, f32[4,64,256]{2,1,0:T(8,128)S(1)}, u32[]{:S(2)}, u32[]{:S(2)}) %collective-permute-start.10) | collective-permute-done | bytes 262176 | tf_op jit(solution)/shard_map/ppermute | solution.py:184
  71.2 0.8 %add_add_fusion = f32[4,64,256]{2,1,0:T(8,128)} fusion(f32[4,64,256]{2,1,0:T(8,128)S(1)} %collective-permute-done.11, f32[4,64,256]{2,1,0:T(8,128)S(1)} %collective-permute-done.10, f32[4,64,256]{2,1,0:T(8,128)S(1)} %chunk.3, f32[4,64,256]{2,1,0:T(8,128)S(1)} %collective-permute-done.8), kind=kLoop, calls=%fused_computation.2 | loop fusion | flops 196608 | bytes 1310720 | tf_op jit(solution)/shard_map/add | solution.py:186
  (12 shorter events, 0.2 us)
Async XLA Ops:
  0.0 14.4 %collective-permute-start = (f32[4,64,256]{2,1,0:T(8,128)}, f32[4,64,256]{2,1,0:T(8,128)S(1)}, u32[]{:S(2)}, u32[]{:S(2)}) collective-permute-start(f32[4,64,256]{2,1,0:T(8,128)} %param.5), channel_id=1, source_target_pairs={{0,4},{4,0},{8,12},{12,8},{1,5},{5,1},{9,13},{13,9},{2,6},{6,2},{1... | collective-permute-start | bytes 786440 | tf_op jit(solution)/shard_map/ppermute | solution.py:165
  2.1 11.0 %collective-permute-start.1 = (f32[4,64,256]{2,1,0:T(8,128)}, f32[4,64,256]{2,1,0:T(8,128)S(1)}, u32[]{:S(2)}, u32[]{:S(2)}) collective-permute-start(f32[4,64,256]{2,1,0:T(8,128)} %param.5), channel_id=1, source_target_pairs={{0,8},{4,12},{8,0},{12,4},{1,9},{5,13},{9,1},{13,5},{2,10},{6,14},... | collective-permute-start | bytes 786440 | tf_op jit(solution)/shard_map/ppermute | solution.py:164
  4.4 1.6 %copy-start.2 = (f32[8,256,256]{2,1,0:T(8,128)S(1)}, f32[8,256,256]{2,1,0:T(8,128)}, u32[]{:S(2)}) copy-start(f32[8,256,256]{2,1,0:T(8,128)} %left_ref.1) | copy-start | bytes 6291460
  6.0 1.6 %copy-start.3 = (f32[8,256,256]{2,1,0:T(8,128)S(1)}, f32[8,256,256]{2,1,0:T(8,128)}, u32[]{:S(2)}) copy-start(f32[8,256,256]{2,1,0:T(8,128)} %right_ref.1) | copy-start | bytes 6291460
  8.7 7.2 %copy-start.4 = (f32[4,64,256]{2,1,0:T(8,128)S(1)}, f32[4,64,256]{2,1,0:T(8,128)}, u32[]{:S(2)}) copy-start(f32[4,64,256]{2,1,0:T(8,128)} %param.5) | copy-start | bytes 786436
  13.1 6.7 %collective-permute-start.2 = (f32[2,64,256]{2,1,0:T(8,128)S(1)}, f32[2,64,256]{2,1,0:T(8,128)S(1)}, u32[]{:S(2)}, u32[]{:S(2)}) collective-permute-start(f32[2,64,256]{2,1,0:T(8,128)S(1)} %get-tuple-element.26.refs_2_), channel_id=1, source_target_pairs={{4,0},{8,12},{5,1},{9,13},{6,2},{10,14},{7,3},{11,15},{20,16},{24,... | collective-permute-start | bytes 393224 | tf_op jit(solution)/shard_map/ppermute | solution.py:169
  14.5 15.3 %collective-permute-start.4 = (f32[2,64,256]{2,1,0:T(8,128)S(1)}, f32[2,64,256]{2,1,0:T(8,128)S(1)}, u32[]{:S(2)}, u32[]{:S(2)}) collective-permute-start(f32[2,64,256]{2,1,0:T(8,128)S(1)} %get-tuple-element.25.refs_2_), channel_id=1, source_target_pairs={{4,0},{8,12},{5,1},{9,13},{6,2},{10,14},{7,3},{11,15},{20,16},{24,... | collective-permute-start | bytes 393224 | tf_op jit(solution)/shard_map/ppermute | solution.py:169
  15.9 13.9 %collective-permute-start.5 = (f32[2,64,256]{2,1,0:T(8,128)S(1)}, f32[2,64,256]{2,1,0:T(8,128)S(1)}, u32[]{:S(2)}, u32[]{:S(2)}) collective-permute-start(f32[2,64,256]{2,1,0:T(8,128)S(1)} %get-tuple-element.21), channel_id=1, source_target_pairs={{4,8},{8,4},{5,9},{9,5},{6,10},{10,6},{7,11},{11,7},{20,24},{24,20... | collective-permute-start | bytes 393224 | tf_op jit(solution)/shard_map/ppermute | solution.py:170
  16.6 3.3 %collective-permute-start.3 = (f32[2,64,256]{2,1,0:T(8,128)S(1)}, f32[2,64,256]{2,1,0:T(8,128)S(1)}, u32[]{:S(2)}, u32[]{:S(2)}) collective-permute-start(f32[2,64,256]{2,1,0:T(8,128)S(1)} %get-tuple-element.22), channel_id=1, source_target_pairs={{4,8},{8,4},{5,9},{9,5},{6,10},{10,6},{7,11},{11,7},{20,24},{24,20... | collective-permute-start | bytes 393224 | tf_op jit(solution)/shard_map/ppermute | solution.py:170
  19.9 11.0 %collective-permute-start.6 = (f32[4,64,256]{2,1,0:T(8,128)S(1)}, f32[4,64,256]{2,1,0:T(8,128)S(1)}, u32[]{:S(2)}, u32[]{:S(2)}) collective-permute-start(f32[4,64,256]{2,1,0:T(8,128)S(1)} %pad_maximum_fusion), channel_id=1, source_target_pairs={{0,1},{1,2},{2,3},{4,5},{5,6},{6,7},{8,9},{9,10},{10,11},{12,13},{... | collective-permute-start | bytes 786440 | tf_op jit(solution)/shard_map/ppermute | solution.py:18
  27.6 7.7 %collective-permute-start.7 = (f32[4,64,256]{2,1,0:T(8,128)S(1)}, f32[4,64,256]{2,1,0:T(8,128)S(1)}, u32[]{:S(2)}, u32[]{:S(2)}) collective-permute-start(f32[4,64,256]{2,1,0:T(8,128)S(1)} %pad_maximum_fusion.1), channel_id=1, source_target_pairs={{1,0},{2,1},{3,2},{5,4},{6,5},{7,6},{9,8},{10,9},{11,10},{13,12},{... | collective-permute-start | bytes 786440 | tf_op jit(solution)/shard_map/ppermute | solution.py:18
  29.8 5.5 %copy-start = (s32[8,16]{1,0:T(8,128)S(1)}, s32[8,16]{1,0:T(8,128)}, u32[]{:S(2)}) copy-start(s32[8,16]{1,0:T(8,128)} %allowed_ref.7) | copy-start | bytes 1540
  29.8 5.5 %copy-start.1 = (s32[8]{0:T(128)S(1)}, s32[8]{0:T(128)}, u32[]{:S(2)}) copy-start(s32[8]{0:T(128)} %shifts_ref.7) | copy-start | bytes 100
  38.4 21.4 %collective-permute-start.9 = (f32[4,64,256]{2,1,0:T(8,128)S(1)}, f32[4,64,256]{2,1,0:T(8,128)S(1)}, u32[]{:S(2)}, u32[]{:S(2)}) collective-permute-start(f32[4,64,256]{2,1,0:T(8,128)S(1)} %get-tuple-element.20), channel_id=1, source_target_pairs={{0,4},{12,8},{1,5},{13,9},{2,6},{14,10},{3,7},{15,11},{16,20},{28,... | collective-permute-start | bytes 786440 | tf_op jit(solution)/shard_map/ppermute | solution.py:181
  49.0 16.5 %collective-permute-start.8 = (f32[4,64,256]{2,1,0:T(8,128)S(1)}, f32[4,64,256]{2,1,0:T(8,128)S(1)}, u32[]{:S(2)}, u32[]{:S(2)}) collective-permute-start(f32[4,64,256]{2,1,0:T(8,128)S(1)} %get-tuple-element.20), channel_id=1, source_target_pairs={{4,8},{8,4},{5,9},{9,5},{6,10},{10,6},{7,11},{11,7},{20,24},{24,20... | collective-permute-start | bytes 786440 | tf_op jit(solution)/shard_map/ppermute | solution.py:182
  54.4 11.1 %collective-permute-start.11 = (f32[4,64,256]{2,1,0:T(8,128)S(1)}, f32[4,64,256]{2,1,0:T(8,128)S(1)}, u32[]{:S(2)}, u32[]{:S(2)}) collective-permute-start(f32[4,64,256]{2,1,0:T(8,128)S(1)} %chunk.5), channel_id=1, source_target_pairs={{0,4},{4,0},{8,12},{12,8},{1,5},{5,1},{9,13},{13,9},{2,6},{6,2},{1... | collective-permute-start | bytes 786440 | tf_op jit(solution)/shard_map/ppermute | solution.py:185
  59.8 11.4 %collective-permute-start.10 = (f32[4,64,256]{2,1,0:T(8,128)S(1)}, f32[4,64,256]{2,1,0:T(8,128)S(1)}, u32[]{:S(2)}, u32[]{:S(2)}) collective-permute-start(f32[4,64,256]{2,1,0:T(8,128)S(1)} %add.37), channel_id=1, source_target_pairs={{0,8},{4,12},{8,0},{12,4},{1,9},{5,13},{9,1},{13,5},{2,10},{6,14},... | collective-permute-start | bytes 786440 | tf_op jit(solution)/shard_map/ppermute | solution.py:184

commit v3 on v1

--- a/solution.py
+++ b/solution.py
@@ -70,66 +70,79 @@
         parts[i] = stacked(psi[i])
 
 
-def first_product(left, parts):
-    return jnp.dot(left, parts, preferred_element_type=F32)
+def first_product(left, parts, allowed_ref, source, high, low):
+    kops, sectors = allowed_ref.shape
+    block = jnp.dot(left, parts, preferred_element_type=F32)
+    rows = block.shape[0] // kops
+    source = jnp.clip(source, 0, sectors - 1)
+    for k in range(kops):
+        at = slice(k * rows, (k + 1) * rows)
+        high[at], low[at] = split(block[at] * allowed_ref[k, source].astype(F32))
 
 
 def chunk_left(n, step, left_parts):
     return left_parts[ring_place(n, step + 1)].reshape(-1, left_parts.shape[-1])
 
 
-def own_sectors(n, *refs):
-    (outer, left_parts), (inner, middle, psi) = refs[n : n + 2], refs[n + 2 :]
+def own_sectors(n, allowed_ref, *refs):
+    (outer, left_parts), (inner, high, low, psi) = refs[n : n + 2], refs[n + 2 :]
     assemble(n, *refs[:n], inner, psi)
     left = chunk_left(n, 0, left_parts)
-    middle[0] = first_product(left, outer[0])
-    for i in range(inner.shape[0]):
-        middle[i + 1] = first_product(left, inner[i])
-    middle[inner.shape[0] + 1] = first_product(left, outer[1])
-
-
-def second_product(nloc, shifts_ref, allowed_ref, middle, right_hi, right_lo, outs):
-    kops = shifts_ref.shape[0]
-    rows, width = outs[0].shape[1:]
+    nloc = high.shape[0]
     first = lax.axis_index(("sec", "sub")) * nloc
-    highs, lows = [], []
-    for k in range(kops):
-        shift = shifts_ref[k]
-        blocks = []
-        for t in range(nloc):
-            below, same, above = [middle[t + d][k * rows : (k + 1) * rows] for d in range(3)]
-            block = jnp.where(shift == 0, same, jnp.where(shift == 1, below, above))
-            source = jnp.clip(first + t - shift, 0, allowed_ref.shape[1] - 1)
-            blocks.append(block * allowed_ref[k, source].astype(F32))
-        hi, lo = split(jnp.concatenate(blocks))
-        highs.append(hi)
-        lows.append(lo)
-    high, low = jnp.concatenate(highs, axis=1), jnp.concatenate(lows, axis=1)
-    total = dot3((high, low), (right_hi[...], right_lo[...])).reshape(nloc, rows, width)
-    per = nloc // len(outs)
-    for i, out in enumerate(outs):
-        out[...] = total[i * per : (i + 1) * per]
-
-
-def outside_sectors(n, above, below, left_parts, outside, middle, psi):
+    sources = [outer.at[0], *[inner.at[i] for i in range(nloc - 2)], outer.at[1]]
+    for i, ref in enumerate(sources):
+        first_product(left, ref[...], allowed_ref, first + i, high.at[i], low.at[i])
+
+
+def outside_sectors(n, nloc, allowed_ref, above, below, left_parts, outside, high, low, psi):
     place_rows(n, psi.at[0], [above[j] for j in range(n)])
     place_rows(n, psi.at[1], [below[j] for j in range(n)])
     left = chunk_left(n, 0, left_parts)
+    first = lax.axis_index(("sec", "sub")) * nloc
     for i in range(2):
         outside[i] = stacked(psi[i])
-        middle[i] = first_product(left, outside[i])
-
-
-def first_chunk(n, nloc, shifts_ref, allowed_ref, own, ends, right_hi, right_lo, *outs):
-    middle = [ends[0], *[own[i] for i in range(nloc)], ends[1]]
-    second_product(nloc, shifts_ref, allowed_ref, middle, right_hi, right_lo, outs)
-
-
-def later_chunk(n, nloc, step, shifts_ref, allowed_ref, outer, inner, outside, left_parts, right_hi, right_lo, *outs):
+        first_product(left, outside[i], allowed_ref, first - 1 + i * (nloc + 1), high.at[i], low.at[i])
+
+
+def second_product(targets, shifts_ref, high, low, right_hi, right_lo, out):
+    kops = shifts_ref.shape[0]
+    _, rows, width = out.shape
+
+    def left(parts):
+        columns = []
+        for k in range(kops):
+            shift, at = shifts_ref[k], slice(k * rows, (k + 1) * rows)
+            blocks = []
+            for t in targets:
+                below, same, above = [parts[t + d][at] for d in range(3)]
+                blocks.append(jnp.where(shift == 0, same, jnp.where(shift == 1, below, above)))
+            columns.append(jnp.concatenate(blocks))
+        return jnp.concatenate(columns, axis=1)
+
+    out[...] = dot3((left(high), left(low)), (right_hi[...], right_lo[...])).reshape(len(targets), rows, width)
+
+
+def first_inner(nloc, shifts_ref, high, low, right_hi, right_lo, out):
+    own = [[None, *[ref.at[i] for i in range(nloc)], None] for ref in (high, low)]
+    second_product(range(1, nloc - 1), shifts_ref, *own, right_hi, right_lo, out)
+
+
+def first_outer(nloc, shifts_ref, high, low, end_high, end_low, right_hi, right_lo, out):
+    pairs = ((high, end_high), (low, end_low))
+    held = [[ends.at[0], *[ref.at[i] for i in range(nloc)], ends.at[1]] for ref, ends in pairs]
+    second_product((0, nloc - 1), shifts_ref, *held, right_hi, right_lo, out)
+
+
+def later_chunk(n, nloc, step, shifts_ref, allowed_ref, outer, inner, outside, left_parts, right_hi, right_lo, outer_out, inner_out, high, low):
     left = chunk_left(n, step, left_parts)
+    first = lax.axis_index(("sec", "sub")) * nloc
     sources = [outside.at[0], outer.at[0], *[inner.at[i] for i in range(nloc - 2)], outer.at[1], outside.at[1]]
-    middle = [first_product(left, ref[...]) for ref in sources]
-    second_product(nloc, shifts_ref, allowed_ref, middle, right_hi, right_lo, outs)
+    for i, ref in enumerate(sources):
+        first_product(left, ref[...], allowed_ref, first - 1 + i, high.at[i], low.at[i])
+    held = [[ref.at[i] for i in range(nloc + 2)] for ref in (high, low)]
+    second_product(range(1, nloc - 1), shifts_ref, *held, right_hi, right_lo, inner_out)
+    second_product((0, nloc - 1), shifts_ref, *held, right_hi, right_lo, outer_out)
 
 
 def call(body, name, flops, out_shape, in_specs, operands, scratch=()):
@@ -173,33 +186,42 @@
     def whole(sectors):
         return [pltpu.VMEM((sectors, width, width), F32)]
 
-    parts_outer = call(functools.partial(assemble, n), "assemble", one // 2, split_parts(2), [VMEM] * n, outer, whole(2))
-    parts_inner, own = call(
-        functools.partial(own_sectors, n), "own", 4 * kops * one,
-        [split_parts(nloc - 2), jax.ShapeDtypeStruct((nloc, kops * rows, width), F32)],
-        [VMEM] * (n + 2), [*inner, parts_outer, left_parts], whole(nloc - 2),
-    )
-    parts_outside, ends = call(
-        functools.partial(outside_sectors, n), "outside", 2 * kops * one,
-        [split_parts(2), jax.ShapeDtypeStruct((2, kops * rows, width), F32)],
-        [VMEM] * 3, [above, below, left_parts], whole(2),
-    )
-    chunk = [jax.ShapeDtypeStruct((nloc // 2, rows, width), F32)] * 2
-    result = call(
-        functools.partial(first_chunk, n, nloc), "first_chunk", nloc * kops * one // n, chunk,
-        [SMEM] * 2 + [VMEM] * 4, [shifts, allowed, own, ends, right_hi, right_lo],
+    parts_outer = call(functools.partial(assemble, n), "assemble", 4 * kops * one, split_parts(2), [VMEM] * n, outer, whole(2))
+    def products(sectors):
+        return [jax.ShapeDtypeStruct((sectors, kops * rows, width), BF16)] * 2
+
+    chunk = jax.ShapeDtypeStruct((2, rows, width), F32)
+    chunk_inner = jax.ShapeDtypeStruct((nloc - 2, rows, width), F32)
+    parts_inner, *own = call(
+        functools.partial(own_sectors, n), "own", 4 * kops * one, [split_parts(nloc - 2), *products(nloc)],
+        [SMEM] + [VMEM] * (n + 2), [allowed, *inner, parts_outer, left_parts], whole(nloc - 2),
+    )
+    result_inner = call(
+        functools.partial(first_inner, nloc), "first_inner", nloc * kops * one // n, chunk_inner,
+        [SMEM] + [VMEM] * 4, [shifts, *own, right_hi, right_lo],
+    )
+    parts_outside, *ends = call(
+        functools.partial(outside_sectors, n, nloc), "outside", 2 * kops * one, [split_parts(2), *products(2)],
+        [SMEM] + [VMEM] * 3, [allowed, above, below, left_parts], whole(2),
+    )
+    result_outer = call(
+        functools.partial(first_outer, nloc), "first_outer", nloc * kops * one // n, chunk,
+        [SMEM] + [VMEM] * 6, [shifts, *own, *ends, right_hi, right_lo],
     )
 
     def mine(step):
         return call(
-            functools.partial(later_chunk, n, nloc, step), "chunk", 4 * nloc * kops * one // n, chunk,
+            functools.partial(later_chunk, n, nloc, step), "chunk", 4 * nloc * kops * one // n, [chunk, chunk_inner],
             [SMEM] * 2 + [VMEM] * 6,
             [shifts, allowed, parts_outer, parts_inner, parts_outside, left_parts, right_hi, right_lo],
+            [pltpu.VMEM((nloc + 2, kops * rows, width), BF16)] * 2,
         )
 
     for step in range(1, n):
-        result = [lax.ppermute(r, "op", route) + o for r, o in zip(result, mine(step))]
-    return jnp.concatenate(result)
+        next_outer, next_inner = mine(step)
+        result_inner = lax.ppermute(result_inner, "op", route) + next_inner
+        result_outer = lax.ppermute(result_outer, "op", route) + next_outer
+    return jnp.concatenate([result_outer[:1], result_inner, result_outer[1:]])
 
 
 def solution(mesh):

time: 62.5 us -> 58.3 us (0.933)
  the two profiles are of different devices: /device:TPU:10 before, /device:TPU:1 now
where the time goes in v3:
time: 58.3 us; the launch traced here: 58 us
  starting transfers between devices  20.2 us (35%)
  waiting for transfers between devices  16.3 us (28%)
  Pallas kernels  16 us (27%)
  local copies, waits for them, and re-layouts  4.23 us (7%)
  other arithmetic  0.96 us (2%)
    pallas_call x9, Pallas kernels, call(): pl.pallas_call(body, name=name, out_shape=out_shape, in_specs=in_specs, o...  16 us
    ppermute x2, starting transfers between devices, shifted(): return lax.ppermute(block, axis, route)  8.62 us
    ppermute x3, waiting for transfers between devices, shards(): lax.ppermute(outer[-1] + zero[0, 0] if step == 1 else outer[-1], 'op', ro...  8.07 us
    ppermute x3, starting transfers between devices, shards(): result_inner = lax.ppermute(result_inner, 'op', route) + next_inner  5.91 us
    ppermute x3, waiting for transfers between devices, shards(): lax.ppermute(inner[-1] + zero[0, 0] if step == 1 else inner[-1], 'op', ro...  3.62 us
    unnamed x8, local copies, waits for them, and re-layouts  3.19 us
    ppermute x3, starting transfers between devices, shards(): lax.ppermute(outer[-1] + zero[0, 0] if step == 1 else outer[-1], 'op', ro...  3 us
    ppermute x2, waiting for transfers between devices, shifted(): return lax.ppermute(block, axis, route)  2.88 us
  transfers between devices with their start and end apart: 14, of which 7 were waited for; matrix products, arithmetic and copies ran while one was open for 0% of the time, Pallas kernels for 28%

profile of v3, /device:TPU:1, one launch (start us, length us, event | category | flops | bytes accessed | tf_op | source)
XLA Modules:
  0.0 58.0 jit_solution(2821706103006844740)
XLA Ops:
  0.0 1.0 %fusion = (f32[2,64,256]{2,1,0:T(8,128)S(1)}, f32[2,64,256]{2,1,0:T(8,128)S(1)}) fusion(f32[4,64,256]{2,1,0:T(8,128)} %param.5), kind=kLoop, calls=%fused_computation.5 | loop fusion | bytes 524288 | tf_op jit(solution)/shard_map/slice | solution.py:175
  1.0 2.2 %collective-permute-start = (f32[2,64,256]{2,1,0:T(8,128)S(1)}, f32[2,64,256]{2,1,0:T(8,128)S(1)}, u32[]{:S(2)}, u32[]{:S(2)}) collective-permute-start(f32[2,64,256]{2,1,0:T(8,128)S(1)} %get-tuple-element.38.refs_0_), channel_id=1, source_target_pairs={{0,4},{4,12},{12,8},{8,0},{1,5},{5,13},{13,9},{9,1},{2,6},{6,14},{... | collective-permute-start | bytes 393224 | tf_op jit(solution)/shard_map/ppermute | solution.py:177
  3.2 2.3 %collective-permute-start.3 = (f32[2,64,256]{2,1,0:T(8,128)S(1)}, f32[2,64,256]{2,1,0:T(8,128)S(1)}, u32[]{:S(2)}, u32[]{:S(2)}) collective-permute-start(f32[2,64,256]{2,1,0:T(8,128)S(1)} %get-tuple-element.37.refs_0_), channel_id=1, source_target_pairs={{0,4},{4,12},{12,8},{8,0},{1,5},{5,13},{13,9},{9,1},{2,6},{6,14},{... | collective-permute-start | bytes 393224 | tf_op jit(solution)/shard_map/ppermute | solution.py:178
  5.5 0.0 copy-start.1
  5.5 1.6 %copy-done.1 = f32[8,256,256]{2,1,0:T(8,128)S(1)} copy-done((f32[8,256,256]{2,1,0:T(8,128)S(1)}, f32[8,256,256]{2,1,0:T(8,128)}, u32[]{:S(2)}) %copy-start.1) | copy-done | bytes 2097176
  7.1 0.0 copy-start.2
  7.1 1.6 %copy-done.2 = f32[8,256,256]{2,1,0:T(8,128)S(1)} copy-done((f32[8,256,256]{2,1,0:T(8,128)S(1)}, f32[8,256,256]{2,1,0:T(8,128)}, u32[]{:S(2)}) %copy-start.2) | copy-done | bytes 2097176
  8.7 1.1 %prepare.1 = (bf16[4,8,64,768]{3,2,1,0:T(8,128)(2,1)S(1)}, bf16[2048,256]{1,0:T(8,128)(2,1)S(1)}, bf16[2048,256]{1,0:T(8,128)(2,1)S(1)}, f32[1,128]{1,0:T(1,128)S(1)}) custom-call(f32[8,256,256]{2,1,0:T(8,128)S(1)} %copy-done.1, f32[8,256,256]{2,1,0:T(8,128)S(1)} %copy-done.2), custom_call_target="tpu_custom_call" | custom-call | flops 3221225472 | bytes 1048576 | tf_op jit(solution)/shard_map/prepare/pallas_call | solution.py:149
  9.8 0.0 collective-permute-done.refs_1_
  9.8 0.2 collective-permute-start.1
  10.0 0.2 collective-permute-done.3.refs_1_
  10.3 0.7 %collective-permute-start.4 = (f32[2,64,256]{2,1,0:T(8,128)S(1)}, f32[2,64,256]{2,1,0:T(8,128)S(1)}, u32[]{:S(2)}, u32[]{:S(2)}) collective-permute-start(f32[2,64,256]{2,1,0:T(8,128)S(1)} %broadcast_add_fusion), channel_id=1, source_target_pairs={{0,4},{4,12},{12,8},{8,0},{1,5},{5,13},{13,9},{9,1},{2,6},{6,14},{... | collective-permute-start | bytes 393224 | tf_op jit(solution)/shard_map/ppermute | solution.py:178
  11.0 3.6 %collective-permute-done.1.refs_2_ = f32[2,64,256]{2,1,0:T(8,128)S(1)} collective-permute-done((f32[2,64,256]{2,1,0:T(8,128)S(1)}, f32[2,64,256]{2,1,0:T(8,128)S(1)}, u32[]{:S(2)}, u32[]{:S(2)}) %collective-permute-start.1) | collective-permute-done | bytes 131104 | tf_op jit(solution)/shard_map/ppermute | solution.py:177
  14.6 0.0 collective-permute-start.2
  14.6 2.7 %collective-permute-done.4.refs_2_ = f32[2,64,256]{2,1,0:T(8,128)S(1)} collective-permute-done((f32[2,64,256]{2,1,0:T(8,128)S(1)}, f32[2,64,256]{2,1,0:T(8,128)S(1)}, u32[]{:S(2)}, u32[]{:S(2)}) %collective-permute-start.4) | collective-permute-done | bytes 131104 | tf_op jit(solution)/shard_map/ppermute | solution.py:178
  17.3 0.0 collective-permute-start.5
  17.3 5.2 %collective-permute-done.5.refs_3_ = f32[2,64,256]{2,1,0:T(8,128)S(1)} collective-permute-done((f32[2,64,256]{2,1,0:T(8,128)S(1)}, f32[2,64,256]{2,1,0:T(8,128)S(1)}, u32[]{:S(2)}, u32[]{:S(2)}) %collective-permute-start.5) | collective-permute-done | bytes 131104 | tf_op jit(solution)/shard_map/ppermute | solution.py:178
  22.5 6.7 %collective-permute-start.6 = (f32[4,64,256]{2,1,0:T(8,128)S(1)}, f32[4,64,256]{2,1,0:T(8,128)S(1)}, u32[]{:S(2)}, u32[]{:S(2)}) collective-permute-start(f32[4,64,256]{2,1,0:T(8,128)S(1)} %pad_maximum_fusion), channel_id=1, source_target_pairs={{0,1},{1,2},{2,3},{4,5},{5,6},{6,7},{8,9},{9,10},{10,11},{12,13},{... | collective-permute-start | bytes 786440 | tf_op jit(solution)/shard_map/ppermute | solution.py:18
  29.3 0.0 copy-start.3
  29.3 1.9 %collective-permute-start.7 = (f32[4,64,256]{2,1,0:T(8,128)S(1)}, f32[4,64,256]{2,1,0:T(8,128)S(1)}, u32[]{:S(2)}, u32[]{:S(2)}) collective-permute-start(f32[4,64,256]{2,1,0:T(8,128)S(1)} %pad_maximum_fusion.1), channel_id=1, source_target_pairs={{1,0},{2,1},{3,2},{5,4},{6,5},{7,6},{9,8},{10,9},{11,10},{13,12},{... | collective-permute-start | bytes 786440 | tf_op jit(solution)/shard_map/ppermute | solution.py:18
  31.2 0.2 assemble.1.refs_4_.outer
  31.4 0.0 collective-permute-done.2.refs_3_
  31.4 0.0 copy-done.3
  31.4 0.0 copy-start
  31.4 1.7 %own.1 = (bf16[2,768,256]{2,1,0:T(8,128)(2,1)S(1)}, bf16[4,512,256]{2,1,0:T(8,128)(2,1)S(1)}, bf16[4,512,256]{2,1,0:T(8,128)(2,1)S(1)}) custom-call(s32[8,16]{1,0:T(8,128)S(1)} %copy-done.3, f32[2,64,256]{2,1,0:T(8,128)S(1)} %get-tuple-element.38.refs_0_, f32[2,64,256]{2,1,0:T(8,128)S(1)} %collective-permute-done.refs_1_, ...), custom_call_target="tpu_custom_call" | custom-call | flops 3221225472 | bytes 1048576 | tf_op jit(solution)/shard_map/own/pallas_call | solution.py:149
  33.1 0.0 copy-done
  33.1 1.2 %first_inner.1 = f32[2,64,256]{2,1,0:T(8,128)S(1)} custom-call(s32[8]{0:T(128)S(1)} %copy-done, bf16[4,512,256]{2,1,0:T(8,128)(2,1)S(1)} %get-tuple-element.23.high, bf16[4,512,256]{2,1,0:T(8,128)(2,1)S(1)} %get-tuple-element.24.low, bf16[2048,256]{1,0:T(8,128)(2,1)S(1)} %get-tuple-element.27.right_hi, bf16[2048,256]{1,0:T(8,128)(2,1)S(1)} %get-tuple-element.28.right_lo), custom_call_target="tpu_custom_call" | custom-call | flops 805306368 | bytes 1048576 | tf_op jit(solution)/shard_map/first_inner/pallas_call | solution.py:149
  34.3 0.1 collective-permute-start.11
  34.4 0.0 collective-permute-done.6.above
  34.4 2.9 %collective-permute-done.7.below = f32[4,64,256]{2,1,0:T(8,128)S(1)} collective-permute-done((f32[4,64,256]{2,1,0:T(8,128)S(1)}, f32[4,64,256]{2,1,0:T(8,128)S(1)}, u32[]{:S(2)}, u32[]{:S(2)}) %collective-permute-start.7) | collective-permute-done | bytes 262176 | tf_op jit(solution)/shard_map/ppermute | solution.py:18
  37.3 1.3 %outside.1 = (bf16[2,768,256]{2,1,0:T(8,128)(2,1)S(1)}, bf16[2,512,256]{2,1,0:T(8,128)(2,1)S(1)}, bf16[2,512,256]{2,1,0:T(8,128)(2,1)S(1)}) custom-call(s32[8,16]{1,0:T(8,128)S(1)} %copy-done.3, f32[4,64,256]{2,1,0:T(8,128)S(1)} %collective-permute-done.6.above, f32[4,64,256]{2,1,0:T(8,128)S(1)} %collective-permute-done.7.below, ...), custom_call_target="tpu_custom_call" | custom-call | flops 1610612736 | bytes 1048576 | tf_op jit(solution)/shard_map/outside/pallas_call | solution.py:149
  38.6 1.2 %first_outer.1 = f32[2,64,256]{2,1,0:T(8,128)S(1)} custom-call(s32[8]{0:T(128)S(1)} %copy-done, bf16[4,512,256]{2,1,0:T(8,128)(2,1)S(1)} %get-tuple-element.23.high, bf16[4,512,256]{2,1,0:T(8,128)(2,1)S(1)} %get-tuple-element.24.low, bf16[2,512,256]{2,1,0:T(8,128)(2,1)S(1)} %get-tuple-element.25.end_high, ...), custom_call_target="tpu_custom_call" | custom-call | flops 805306368 | bytes 1048576 | tf_op jit(solution)/shard_map/first_outer/pallas_call | solution.py:149
  39.7 0.1 collective-permute-start.8
  39.9 3.2 %chunk.3 = (f32[2,64,256]{2,1,0:T(8,128)S(1)}, f32[2,64,256]{2,1,0:T(8,128)S(1)}) custom-call(s32[8]{0:T(128)S(1)} %copy-done, s32[8,16]{1,0:T(8,128)S(1)} %copy-done.3, bf16[2,768,256]{2,1,0:T(8,128)(2,1)S(1)} %assemble.1.refs_4_.outer, bf16[2,768,256]{2,1,0:T(8,128)(2,1)S(1)} %get-tuple-element.29.inner, ...), custom_call_target="tpu_custom_call" | custom-call | flops 3221225472 | bytes 1048576 | tf_op jit(solution)/shard_map/chunk/pallas_call | solution.py:149
  43.0 0.0 collective-permute-done.11
  43.1 3.0 %collective-permute-start.12 = (f32[2,64,256]{2,1,0:T(8,128)S(1)}, f32[2,64,256]{2,1,0:T(8,128)S(1)}, u32[]{:S(2)}, u32[]{:S(2)}) collective-permute-start(f32[2,64,256]{2,1,0:T(8,128)S(1)} %add.34), channel_id=1, source_target_pairs={{0,4},{4,12},{12,8},{8,0},{1,5},{5,13},{13,9},{9,1},{2,6},{6,14},{... | collective-permute-start | bytes 393224 | tf_op jit(solution)/shard_map/ppermute | solution.py:222
  46.0 0.0 collective-permute-done.8
  46.0 0.1 collective-permute-start.9
  46.1 3.1 %chunk.4 = (f32[2,64,256]{2,1,0:T(8,128)S(1)}, f32[2,64,256]{2,1,0:T(8,128)S(1)}) custom-call(s32[8]{0:T(128)S(1)} %copy-done, s32[8,16]{1,0:T(8,128)S(1)} %copy-done.3, bf16[2,768,256]{2,1,0:T(8,128)(2,1)S(1)} %assemble.1.refs_4_.outer, bf16[2,768,256]{2,1,0:T(8,128)(2,1)S(1)} %get-tuple-element.29.inner, ...), custom_call_target="tpu_custom_call" | custom-call | flops 3221225472 | bytes 1048576 | tf_op jit(solution)/shard_map/chunk/pallas_call | solution.py:149
  49.3 0.3 collective-permute-done.12
  49.6 2.9 %collective-permute-start.13 = (f32[2,64,256]{2,1,0:T(8,128)S(1)}, f32[2,64,256]{2,1,0:T(8,128)S(1)}, u32[]{:S(2)}, u32[]{:S(2)}) collective-permute-start(f32[2,64,256]{2,1,0:T(8,128)S(1)} %add.35), channel_id=1, source_target_pairs={{0,4},{4,12},{12,8},{8,0},{1,5},{5,13},{13,9},{9,1},{2,6},{6,14},{... | collective-permute-start | bytes 393224 | tf_op jit(solution)/shard_map/ppermute | solution.py:222
  52.5 0.0 collective-permute-done.9
  52.5 0.1 collective-permute-start.10
  52.6 3.1 %chunk.5 = (f32[2,64,256]{2,1,0:T(8,128)S(1)}, f32[2,64,256]{2,1,0:T(8,128)S(1)}) custom-call(s32[8]{0:T(128)S(1)} %copy-done, s32[8,16]{1,0:T(8,128)S(1)} %copy-done.3, bf16[2,768,256]{2,1,0:T(8,128)(2,1)S(1)} %assemble.1.refs_4_.outer, bf16[2,768,256]{2,1,0:T(8,128)(2,1)S(1)} %get-tuple-element.29.inner, ...), custom_call_target="tpu_custom_call" | custom-call | flops 3221225472 | bytes 1048576 | tf_op jit(solution)/shard_map/chunk/pallas_call | solution.py:149
  55.8 0.0 collective-permute-done.13
  55.8 1.5 %collective-permute-done.10 = f32[2,64,256]{2,1,0:T(8,128)S(1)} collective-permute-done((f32[2,64,256]{2,1,0:T(8,128)S(1)}, f32[2,64,256]{2,1,0:T(8,128)S(1)}, u32[]{:S(2)}, u32[]{:S(2)}) %collective-permute-start.10) | collective-permute-done | bytes 131104 | tf_op jit(solution)/shard_map/ppermute | solution.py:223
  57.3 0.7 %pad_maximum_fusion.2 = f32[4,64,256]{2,1,0:T(8,128)} fusion(f32[1,64,256]{2,1,0:T(8,128)S(1)} %get-tuple-element.40, f32[2,64,256]{2,1,0:T(8,128)S(1)} %add.36, f32[1,64,256]{2,1,0:T(8,128)S(1)} %get-tuple-element.39), kind=kLoop, calls=%fused_computation.2 | loop fusion | flops 131072 | bytes 524288 | tf_op jit(solution)/shard_map/concatenate | solution.py:224
  (15 shorter events, 0.3 us)
Async XLA Ops:
  1.0 8.8 %collective-permute-start = (f32[2,64,256]{2,1,0:T(8,128)S(1)}, f32[2,64,256]{2,1,0:T(8,128)S(1)}, u32[]{:S(2)}, u32[]{:S(2)}) collective-permute-start(f32[2,64,256]{2,1,0:T(8,128)S(1)} %get-tuple-element.38.refs_0_), channel_id=1, source_target_pairs={{0,4},{4,12},{12,8},{8,0},{1,5},{5,13},{13,9},{9,1},{2,6},{6,14},{... | collective-permute-start | bytes 393224 | tf_op jit(solution)/shard_map/ppermute | solution.py:177
  3.2 7.0 %collective-permute-start.3 = (f32[2,64,256]{2,1,0:T(8,128)S(1)}, f32[2,64,256]{2,1,0:T(8,128)S(1)}, u32[]{:S(2)}, u32[]{:S(2)}) collective-permute-start(f32[2,64,256]{2,1,0:T(8,128)S(1)} %get-tuple-element.37.refs_0_), channel_id=1, source_target_pairs={{0,4},{4,12},{12,8},{8,0},{1,5},{5,13},{13,9},{9,1},{2,6},{6,14},{... | collective-permute-start | bytes 393224 | tf_op jit(solution)/shard_map/ppermute | solution.py:178
  5.5 1.6 %copy-start.1 = (f32[8,256,256]{2,1,0:T(8,128)S(1)}, f32[8,256,256]{2,1,0:T(8,128)}, u32[]{:S(2)}) copy-start(f32[8,256,256]{2,1,0:T(8,128)} %left_ref.1) | copy-start | bytes 6291460
  7.1 1.6 %copy-start.2 = (f32[8,256,256]{2,1,0:T(8,128)S(1)}, f32[8,256,256]{2,1,0:T(8,128)}, u32[]{:S(2)}) copy-start(f32[8,256,256]{2,1,0:T(8,128)} %right_ref.1) | copy-start | bytes 6291460
  9.8 4.8 %collective-permute-start.1 = (f32[2,64,256]{2,1,0:T(8,128)S(1)}, f32[2,64,256]{2,1,0:T(8,128)S(1)}, u32[]{:S(2)}, u32[]{:S(2)}) collective-permute-start(f32[2,64,256]{2,1,0:T(8,128)S(1)} %broadcast_add_fusion.1), channel_id=1, source_target_pairs={{0,4},{4,12},{12,8},{8,0},{1,5},{5,13},{13,9},{9,1},{2,6},{6,14},{... | collective-permute-start | bytes 393224 | tf_op jit(solution)/shard_map/ppermute | solution.py:177
  10.3 7.1 %collective-permute-start.4 = (f32[2,64,256]{2,1,0:T(8,128)S(1)}, f32[2,64,256]{2,1,0:T(8,128)S(1)}, u32[]{:S(2)}, u32[]{:S(2)}) collective-permute-start(f32[2,64,256]{2,1,0:T(8,128)S(1)} %broadcast_add_fusion), channel_id=1, source_target_pairs={{0,4},{4,12},{12,8},{8,0},{1,5},{5,13},{13,9},{9,1},{2,6},{6,14},{... | collective-permute-start | bytes 393224 | tf_op jit(solution)/shard_map/ppermute | solution.py:178
  14.6 16.8 %collective-permute-start.2 = (f32[2,64,256]{2,1,0:T(8,128)S(1)}, f32[2,64,256]{2,1,0:T(8,128)S(1)}, u32[]{:S(2)}, u32[]{:S(2)}) collective-permute-start(f32[2,64,256]{2,1,0:T(8,128)S(1)} %collective-permute-done.1.refs_2_), channel_id=1, source_target_pairs={{0,4},{4,12},{12,8},{8,0},{1,5},{5,13},{13,9},{9,1},{2,6},{6,14},{... | collective-permute-start | bytes 393224 | tf_op jit(solution)/shard_map/ppermute | solution.py:177
  17.3 5.2 %collective-permute-start.5 = (f32[2,64,256]{2,1,0:T(8,128)S(1)}, f32[2,64,256]{2,1,0:T(8,128)S(1)}, u32[]{:S(2)}, u32[]{:S(2)}) collective-permute-start(f32[2,64,256]{2,1,0:T(8,128)S(1)} %collective-permute-done.4.refs_2_), channel_id=1, source_target_pairs={{0,4},{4,12},{12,8},{8,0},{1,5},{5,13},{13,9},{9,1},{2,6},{6,14},{... | collective-permute-start | bytes 393224 | tf_op jit(solution)/shard_map/ppermute | solution.py:178
  22.5 11.8 %collective-permute-start.6 = (f32[4,64,256]{2,1,0:T(8,128)S(1)}, f32[4,64,256]{2,1,0:T(8,128)S(1)}, u32[]{:S(2)}, u32[]{:S(2)}) collective-permute-start(f32[4,64,256]{2,1,0:T(8,128)S(1)} %pad_maximum_fusion), channel_id=1, source_target_pairs={{0,1},{1,2},{2,3},{4,5},{5,6},{6,7},{8,9},{9,10},{10,11},{12,13},{... | collective-permute-start | bytes 786440 | tf_op jit(solution)/shard_map/ppermute | solution.py:18
  29.3 2.1 %copy-start.3 = (s32[8,16]{1,0:T(8,128)S(1)}, s32[8,16]{1,0:T(8,128)}, u32[]{:S(2)}) copy-start(s32[8,16]{1,0:T(8,128)} %allowed_ref.9) | copy-start | bytes 1540
  29.3 8.0 %collective-permute-start.7 = (f32[4,64,256]{2,1,0:T(8,128)S(1)}, f32[4,64,256]{2,1,0:T(8,128)S(1)}, u32[]{:S(2)}, u32[]{:S(2)}) collective-permute-start(f32[4,64,256]{2,1,0:T(8,128)S(1)} %pad_maximum_fusion.1), channel_id=1, source_target_pairs={{1,0},{2,1},{3,2},{5,4},{6,5},{7,6},{9,8},{10,9},{11,10},{13,12},{... | collective-permute-start | bytes 786440 | tf_op jit(solution)/shard_map/ppermute | solution.py:18
  31.4 1.7 %copy-start = (s32[8]{0:T(128)S(1)}, s32[8]{0:T(128)}, u32[]{:S(2)}) copy-start(s32[8]{0:T(128)} %shifts_ref.9) | copy-start | bytes 100
  34.3 8.7 %collective-permute-start.11 = (f32[2,64,256]{2,1,0:T(8,128)S(1)}, f32[2,64,256]{2,1,0:T(8,128)S(1)}, u32[]{:S(2)}, u32[]{:S(2)}) collective-permute-start(f32[2,64,256]{2,1,0:T(8,128)S(1)} %first_inner.1), channel_id=1, source_target_pairs={{0,4},{4,12},{12,8},{8,0},{1,5},{5,13},{13,9},{9,1},{2,6},{6,14},{... | collective-permute-start | bytes 393224 | tf_op jit(solution)/shard_map/ppermute | solution.py:222
  39.7 6.3 %collective-permute-start.8 = (f32[2,64,256]{2,1,0:T(8,128)S(1)}, f32[2,64,256]{2,1,0:T(8,128)S(1)}, u32[]{:S(2)}, u32[]{:S(2)}) collective-permute-start(f32[2,64,256]{2,1,0:T(8,128)S(1)} %first_outer.1), channel_id=1, source_target_pairs={{0,4},{4,12},{12,8},{8,0},{1,5},{5,13},{13,9},{9,1},{2,6},{6,14},{... | collective-permute-start | bytes 393224 | tf_op jit(solution)/shard_map/ppermute | solution.py:223
  43.1 6.5 %collective-permute-start.12 = (f32[2,64,256]{2,1,0:T(8,128)S(1)}, f32[2,64,256]{2,1,0:T(8,128)S(1)}, u32[]{:S(2)}, u32[]{:S(2)}) collective-permute-start(f32[2,64,256]{2,1,0:T(8,128)S(1)} %add.34), channel_id=1, source_target_pairs={{0,4},{4,12},{12,8},{8,0},{1,5},{5,13},{13,9},{9,1},{2,6},{6,14},{... | collective-permute-start | bytes 393224 | tf_op jit(solution)/shard_map/ppermute | solution.py:222
  46.0 6.4 %collective-permute-start.9 = (f32[2,64,256]{2,1,0:T(8,128)S(1)}, f32[2,64,256]{2,1,0:T(8,128)S(1)}, u32[]{:S(2)}, u32[]{:S(2)}) collective-permute-start(f32[2,64,256]{2,1,0:T(8,128)S(1)} %add.31), channel_id=1, source_target_pairs={{0,4},{4,12},{12,8},{8,0},{1,5},{5,13},{13,9},{9,1},{2,6},{6,14},{... | collective-permute-start | bytes 393224 | tf_op jit(solution)/shard_map/ppermute | solution.py:223
  49.6 6.2 %collective-permute-start.13 = (f32[2,64,256]{2,1,0:T(8,128)S(1)}, f32[2,64,256]{2,1,0:T(8,128)S(1)}, u32[]{:S(2)}, u32[]{:S(2)}) collective-permute-start(f32[2,64,256]{2,1,0:T(8,128)S(1)} %add.35), channel_id=1, source_target_pairs={{0,4},{4,12},{12,8},{8,0},{1,5},{5,13},{13,9},{9,1},{2,6},{6,14},{... | collective-permute-start | bytes 393224 | tf_op jit(solution)/shard_map/ppermute | solution.py:222
  52.5 4.8 %collective-permute-start.10 = (f32[2,64,256]{2,1,0:T(8,128)S(1)}, f32[2,64,256]{2,1,0:T(8,128)S(1)}, u32[]{:S(2)}, u32[]{:S(2)}) collective-permute-start(f32[2,64,256]{2,1,0:T(8,128)S(1)} %add.32), channel_id=1, source_target_pairs={{0,4},{4,12},{12,8},{8,0},{1,5},{5,13},{13,9},{9,1},{2,6},{6,14},{... | collective-permute-start | bytes 393224 | tf_op jit(solution)/shard_map/ppermute | solution.py:223

commit v4 on v3

--- a/solution.py
+++ b/solution.py
@@ -33,11 +33,6 @@
 def split(x):
     hi = x.astype(BF16)
     return hi, (x - hi.astype(F32)).astype(BF16)
-
-
-def dot3(a, b):
-    one = functools.partial(jnp.dot, preferred_element_type=F32)
-    return one(a[0], b[0]) + (one(a[0], b[1]) + one(a[1], b[0]))
 
 
 def prepare(left_ref, right_ref, left_parts, right_hi, right_lo, zero):
@@ -84,8 +79,8 @@
     return left_parts[ring_place(n, step + 1)].reshape(-1, left_parts.shape[-1])
 
 
-def own_sectors(n, allowed_ref, *refs):
-    (outer, left_parts), (inner, high, low, psi) = refs[n : n + 2], refs[n + 2 :]
+def own_sectors(n, allowed_ref, outer, *refs):
+    left_parts, inner, high, low, psi = refs[n:]
     assemble(n, *refs[:n], inner, psi)
     left = chunk_left(n, 0, left_parts)
     nloc = high.shape[0]
@@ -105,9 +100,8 @@
         first_product(left, outside[i], allowed_ref, first - 1 + i * (nloc + 1), high.at[i], low.at[i])
 
 
-def second_product(targets, shifts_ref, high, low, right_hi, right_lo, out):
-    kops = shifts_ref.shape[0]
-    _, rows, width = out.shape
+def second_product(targets, shifts_ref, high, low, right_hi, right_lo, rows):
+    kops, width = shifts_ref.shape[0], right_hi.shape[1]
 
     def left(parts):
         columns = []
@@ -120,18 +114,21 @@
             columns.append(jnp.concatenate(blocks))
         return jnp.concatenate(columns, axis=1)
 
-    out[...] = dot3((left(high), left(low)), (right_hi[...], right_lo[...])).reshape(len(targets), rows, width)
+    hi, lo = left(high), left(low)
+    main = jnp.dot(jnp.concatenate([hi, lo]), right_hi[...], preferred_element_type=F32)
+    total = main[: hi.shape[0]] + (main[hi.shape[0] :] + jnp.dot(hi, right_lo[...], preferred_element_type=F32))
+    return total.reshape(len(targets), rows, width)
 
 
 def first_inner(nloc, shifts_ref, high, low, right_hi, right_lo, out):
     own = [[None, *[ref.at[i] for i in range(nloc)], None] for ref in (high, low)]
-    second_product(range(1, nloc - 1), shifts_ref, *own, right_hi, right_lo, out)
+    out[...] = second_product(range(1, nloc - 1), shifts_ref, *own, right_hi, right_lo, out.shape[1])
 
 
 def first_outer(nloc, shifts_ref, high, low, end_high, end_low, right_hi, right_lo, out):
     pairs = ((high, end_high), (low, end_low))
     held = [[ends.at[0], *[ref.at[i] for i in range(nloc)], ends.at[1]] for ref, ends in pairs]
-    second_product((0, nloc - 1), shifts_ref, *held, right_hi, right_lo, out)
+    out[...] = second_product((0, nloc - 1), shifts_ref, *held, right_hi, right_lo, out.shape[1])
 
 
 def later_chunk(n, nloc, step, shifts_ref, allowed_ref, outer, inner, outside, left_parts, right_hi, right_lo, outer_out, inner_out, high, low):
@@ -141,8 +138,9 @@
     for i, ref in enumerate(sources):
         first_product(left, ref[...], allowed_ref, first - 1 + i, high.at[i], low.at[i])
     held = [[ref.at[i] for i in range(nloc + 2)] for ref in (high, low)]
-    second_product(range(1, nloc - 1), shifts_ref, *held, right_hi, right_lo, inner_out)
-    second_product((0, nloc - 1), shifts_ref, *held, right_hi, right_lo, outer_out)
+    total = second_product((0, nloc - 1, *range(1, nloc - 1)), shifts_ref, *held, right_hi, right_lo, outer_out.shape[1])
+    outer_out[...] = total[:2]
+    inner_out[...] = total[2:]
 
 
 def call(body, name, flops, out_shape, in_specs, operands, scratch=()):
@@ -194,7 +192,7 @@
     chunk_inner = jax.ShapeDtypeStruct((nloc - 2, rows, width), F32)
     parts_inner, *own = call(
         functools.partial(own_sectors, n), "own", 4 * kops * one, [split_parts(nloc - 2), *products(nloc)],
-        [SMEM] + [VMEM] * (n + 2), [allowed, *inner, parts_outer, left_parts], whole(nloc - 2),
+        [SMEM] + [VMEM] * (n + 2), [allowed, parts_outer, *inner, left_parts], whole(nloc - 2),
     )
     result_inner = call(
         functools.partial(first_inner, nloc), "first_inner", nloc * kops * one // n, chunk_inner,

time: 58.3 us -> 59 us (1.012)
  waiting for transfers between devices: 16.3 us -> 9.95 us
  Pallas kernels: 16 us -> 20 us
  starting transfers between devices: 20.2 us -> 23.4 us
    ppermute x3, waiting for transfers between devices: 8.07 us -> 3.98 us  [shards(): lax.ppermute(outer[-1] + zero[0, 0] if step == 1 else outer[-1], 'op', ro...]
    pallas_call x9, Pallas kernels: 16 us -> 20 us  [call(): pl.pallas_call(body, name=name, out_shape=out_shape, in_specs=in_specs, o...]
    ppermute x3, starting transfers between devices: 2.4 us -> 5.85 us  [shards(): lax.ppermute(inner[-1] + zero[0, 0] if step == 1 else inner[-1], 'op', ro...]
    ppermute x3, starting transfers between devices: 5.91 us -> 4.34 us  [shards(): result_inner = lax.ppermute(result_inner, 'op', route) + next_inner]
    ppermute x3, waiting for transfers between devices: 3.62 us -> 2.19 us  [shards(): lax.ppermute(inner[-1] + zero[0, 0] if step == 1 else inner[-1], 'op', ro...]
    ppermute x3, starting transfers between devices: 0.3 us -> 1.53 us  [shards(): result_outer = lax.ppermute(result_outer, 'op', route) + next_outer]
  transfers between devices with their start and end apart: 14 -> 14, of which waited for: 7 -> 7; matrix products, arithmetic and copies ran while one was open for 0% -> 0% of each run, Pallas kernels for 28% -> 34%
where the time goes in v4:
time: 59 us; the launch traced here: 58.7 us
  starting transfers between devices  23.4 us (40%)
  Pallas kernels  20 us (34%)
  waiting for transfers between devices  9.95 us (17%)
  local copies, waits for them, and re-layouts  4.23 us (7%)
  other arithmetic  0.96 us (2%)
    pallas_call x9, Pallas kernels, call(): pl.pallas_call(body, name=name, out_shape=out_shape, in_specs=in_specs, o...  20 us
    ppermute x2, starting transfers between devices, shifted(): return lax.ppermute(block, axis, route)  8.4 us
    ppermute x3, starting transfers between devices, shards(): lax.ppermute(inner[-1] + zero[0, 0] if step == 1 else inner[-1], 'op', ro...  5.85 us
    ppermute x3, starting transfers between devices, shards(): result_inner = lax.ppermute(result_inner, 'op', route) + next_inner  4.34 us
    ppermute x3, waiting for transfers between devices, shards(): lax.ppermute(outer[-1] + zero[0, 0] if step == 1 else outer[-1], 'op', ro...  3.98 us
    ppermute x3, starting transfers between devices, shards(): lax.ppermute(outer[-1] + zero[0, 0] if step == 1 else outer[-1], 'op', ro...  3.24 us
    unnamed x8, local copies, waits for them, and re-layouts  3.19 us
    ppermute x2, waiting for transfers between devices, shifted(): return lax.ppermute(block, axis, route)  2.38 us
  transfers between devices with their start and end apart: 14, of which 7 were waited for; matrix products, arithmetic and copies ran while one was open for 0% of the time, Pallas kernels for 34%

profile of v4, /device:TPU:1, one launch (start us, length us, event | category | flops | bytes accessed | tf_op | source)
XLA Modules:
  0.0 58.7 jit_solution(4072378601769071145)
XLA Ops:
  0.0 1.0 %fusion = (f32[2,64,256]{2,1,0:T(8,128)S(1)}, f32[2,64,256]{2,1,0:T(8,128)S(1)}) fusion(f32[4,64,256]{2,1,0:T(8,128)} %param.5), kind=kLoop, calls=%fused_computation.5 | loop fusion | bytes 524288 | tf_op jit(solution)/shard_map/slice | solution.py:173
  1.0 2.2 %collective-permute-start.3 = (f32[2,64,256]{2,1,0:T(8,128)S(1)}, f32[2,64,256]{2,1,0:T(8,128)S(1)}, u32[]{:S(2)}, u32[]{:S(2)}) collective-permute-start(f32[2,64,256]{2,1,0:T(8,128)S(1)} %get-tuple-element.37.refs_0_), channel_id=1, source_target_pairs={{0,4},{4,12},{12,8},{8,0},{1,5},{5,13},{13,9},{9,1},{2,6},{6,14},{... | collective-permute-start | bytes 393224 | tf_op jit(solution)/shard_map/ppermute | solution.py:175
  3.2 2.3 %collective-permute-start = (f32[2,64,256]{2,1,0:T(8,128)S(1)}, f32[2,64,256]{2,1,0:T(8,128)S(1)}, u32[]{:S(2)}, u32[]{:S(2)}) collective-permute-start(f32[2,64,256]{2,1,0:T(8,128)S(1)} %get-tuple-element.38.refs_0_), channel_id=1, source_target_pairs={{0,4},{4,12},{12,8},{8,0},{1,5},{5,13},{13,9},{9,1},{2,6},{6,14},{... | collective-permute-start | bytes 393224 | tf_op jit(solution)/shard_map/ppermute | solution.py:176
  5.5 0.0 copy-start.1
  5.5 1.6 %copy-done.1 = f32[8,256,256]{2,1,0:T(8,128)S(1)} copy-done((f32[8,256,256]{2,1,0:T(8,128)S(1)}, f32[8,256,256]{2,1,0:T(8,128)}, u32[]{:S(2)}) %copy-start.1) | copy-done | bytes 2097176
  7.1 0.0 copy-start.2
  7.1 1.6 %copy-done.2 = f32[8,256,256]{2,1,0:T(8,128)S(1)} copy-done((f32[8,256,256]{2,1,0:T(8,128)S(1)}, f32[8,256,256]{2,1,0:T(8,128)}, u32[]{:S(2)}) %copy-start.2) | copy-done | bytes 2097176
  8.7 1.1 %prepare.1 = (bf16[4,8,64,768]{3,2,1,0:T(8,128)(2,1)S(1)}, bf16[2048,256]{1,0:T(8,128)(2,1)S(1)}, bf16[2048,256]{1,0:T(8,128)(2,1)S(1)}, f32[1,128]{1,0:T(1,128)S(1)}) custom-call(f32[8,256,256]{2,1,0:T(8,128)S(1)} %copy-done.1, f32[8,256,256]{2,1,0:T(8,128)S(1)} %copy-done.2), custom_call_target="tpu_custom_call" | custom-call | flops 3221225472 | bytes 1048576 | tf_op jit(solution)/shard_map/prepare/pallas_call | solution.py:147
  9.8 0.5 collective-permute-done.refs_1_
  10.3 0.4 collective-permute-start.1
  10.6 0.0 collective-permute-done.3.refs_1_
  10.7 3.1 %collective-permute-start.4 = (f32[2,64,256]{2,1,0:T(8,128)S(1)}, f32[2,64,256]{2,1,0:T(8,128)S(1)}, u32[]{:S(2)}, u32[]{:S(2)}) collective-permute-start(f32[2,64,256]{2,1,0:T(8,128)S(1)} %broadcast_add_fusion), channel_id=1, source_target_pairs={{0,4},{4,12},{12,8},{8,0},{1,5},{5,13},{13,9},{9,1},{2,6},{6,14},{... | collective-permute-start | bytes 393224 | tf_op jit(solution)/shard_map/ppermute | solution.py:175
  13.8 1.3 %collective-permute-done.1.refs_2_ = f32[2,64,256]{2,1,0:T(8,128)S(1)} collective-permute-done((f32[2,64,256]{2,1,0:T(8,128)S(1)}, f32[2,64,256]{2,1,0:T(8,128)S(1)}, u32[]{:S(2)}, u32[]{:S(2)}) %collective-permute-start.1) | collective-permute-done | bytes 131104 | tf_op jit(solution)/shard_map/ppermute | solution.py:176
  15.0 0.6 collective-permute-start.2
  15.6 2.2 %collective-permute-done.4.refs_2_ = f32[2,64,256]{2,1,0:T(8,128)S(1)} collective-permute-done((f32[2,64,256]{2,1,0:T(8,128)S(1)}, f32[2,64,256]{2,1,0:T(8,128)S(1)}, u32[]{:S(2)}, u32[]{:S(2)}) %collective-permute-start.4) | collective-permute-done | bytes 131104 | tf_op jit(solution)/shard_map/ppermute | solution.py:175
  17.8 0.6 %collective-permute-start.5 = (f32[2,64,256]{2,1,0:T(8,128)S(1)}, f32[2,64,256]{2,1,0:T(8,128)S(1)}, u32[]{:S(2)}, u32[]{:S(2)}) collective-permute-start(f32[2,64,256]{2,1,0:T(8,128)S(1)} %collective-permute-done.4.refs_2_), channel_id=1, source_target_pairs={{0,4},{4,12},{12,8},{8,0},{1,5},{5,13},{13,9},{9,1},{2,6},{6,14},{... | collective-permute-start | bytes 393224 | tf_op jit(solution)/shard_map/ppermute | solution.py:175
  18.4 2.3 %collective-permute-done.2.refs_3_ = f32[2,64,256]{2,1,0:T(8,128)S(1)} collective-permute-done((f32[2,64,256]{2,1,0:T(8,128)S(1)}, f32[2,64,256]{2,1,0:T(8,128)S(1)}, u32[]{:S(2)}, u32[]{:S(2)}) %collective-permute-start.2) | collective-permute-done | bytes 131104 | tf_op jit(solution)/shard_map/ppermute | solution.py:176
  20.7 6.5 %collective-permute-start.6 = (f32[4,64,256]{2,1,0:T(8,128)S(1)}, f32[4,64,256]{2,1,0:T(8,128)S(1)}, u32[]{:S(2)}, u32[]{:S(2)}) collective-permute-start(f32[4,64,256]{2,1,0:T(8,128)S(1)} %pad_maximum_fusion), channel_id=1, source_target_pairs={{0,1},{1,2},{2,3},{4,5},{5,6},{6,7},{8,9},{9,10},{10,11},{12,13},{... | collective-permute-start | bytes 786440 | tf_op jit(solution)/shard_map/ppermute | solution.py:18
  27.2 0.0 copy-start.3
  27.2 1.9 %collective-permute-start.7 = (f32[4,64,256]{2,1,0:T(8,128)S(1)}, f32[4,64,256]{2,1,0:T(8,128)S(1)}, u32[]{:S(2)}, u32[]{:S(2)}) collective-permute-start(f32[4,64,256]{2,1,0:T(8,128)S(1)} %pad_maximum_fusion.1), channel_id=1, source_target_pairs={{1,0},{2,1},{3,2},{5,4},{6,5},{7,6},{9,8},{10,9},{11,10},{13,12},{... | collective-permute-start | bytes 786440 | tf_op jit(solution)/shard_map/ppermute | solution.py:18
  29.2 0.2 assemble.1.outer
  29.4 0.0 collective-permute-done.5.refs_3_
  29.4 0.0 copy-done.3
  29.4 0.0 copy-start
  29.4 1.7 %own.1 = (bf16[2,768,256]{2,1,0:T(8,128)(2,1)S(1)}, bf16[4,512,256]{2,1,0:T(8,128)(2,1)S(1)}, bf16[4,512,256]{2,1,0:T(8,128)(2,1)S(1)}) custom-call(s32[8,16]{1,0:T(8,128)S(1)} %copy-done.3, bf16[2,768,256]{2,1,0:T(8,128)(2,1)S(1)} %assemble.1.outer, f32[2,64,256]{2,1,0:T(8,128)S(1)} %get-tuple-element.37.refs_0_, ...), custom_call_target="tpu_custom_call" | custom-call | flops 3221225472 | bytes 1048576 | tf_op jit(solution)/shard_map/own/pallas_call | solution.py:147
  31.1 0.0 copy-done
  31.1 1.1 %first_inner.1 = f32[2,64,256]{2,1,0:T(8,128)S(1)} custom-call(s32[8]{0:T(128)S(1)} %copy-done, bf16[4,512,256]{2,1,0:T(8,128)(2,1)S(1)} %get-tuple-element.23.high, bf16[4,512,256]{2,1,0:T(8,128)(2,1)S(1)} %get-tuple-element.24.low, bf16[2048,256]{1,0:T(8,128)(2,1)S(1)} %get-tuple-element.27.right_hi, bf16[2048,256]{1,0:T(8,128)(2,1)S(1)} %get-tuple-element.28.right_lo), custom_call_target="tpu_custom_call" | custom-call | flops 805306368 | bytes 1048576 | tf_op jit(solution)/shard_map/first_inner/pallas_call | solution.py:147
  32.2 0.6 %collective-permute-start.11 = (f32[2,64,256]{2,1,0:T(8,128)S(1)}, f32[2,64,256]{2,1,0:T(8,128)S(1)}, u32[]{:S(2)}, u32[]{:S(2)}) collective-permute-start(f32[2,64,256]{2,1,0:T(8,128)S(1)} %first_inner.1), channel_id=1, source_target_pairs={{0,4},{4,12},{12,8},{8,0},{1,5},{5,13},{13,9},{9,1},{2,6},{6,14},{... | collective-permute-start | bytes 393224 | tf_op jit(solution)/shard_map/ppermute | solution.py:220
  32.8 0.0 collective-permute-done.6.above
  32.8 2.4 %collective-permute-done.7.below = f32[4,64,256]{2,1,0:T(8,128)S(1)} collective-permute-done((f32[4,64,256]{2,1,0:T(8,128)S(1)}, f32[4,64,256]{2,1,0:T(8,128)S(1)}, u32[]{:S(2)}, u32[]{:S(2)}) %collective-permute-start.7) | collective-permute-done | bytes 262176 | tf_op jit(solution)/shard_map/ppermute | solution.py:18
  35.2 1.3 %outside.1 = (bf16[2,768,256]{2,1,0:T(8,128)(2,1)S(1)}, bf16[2,512,256]{2,1,0:T(8,128)(2,1)S(1)}, bf16[2,512,256]{2,1,0:T(8,128)(2,1)S(1)}) custom-call(s32[8,16]{1,0:T(8,128)S(1)} %copy-done.3, f32[4,64,256]{2,1,0:T(8,128)S(1)} %collective-permute-done.6.above, f32[4,64,256]{2,1,0:T(8,128)S(1)} %collective-permute-done.7.below, ...), custom_call_target="tpu_custom_call" | custom-call | flops 1610612736 | bytes 1048576 | tf_op jit(solution)/shard_map/outside/pallas_call | solution.py:147
  36.5 1.1 %first_outer.1 = f32[2,64,256]{2,1,0:T(8,128)S(1)} custom-call(s32[8]{0:T(128)S(1)} %copy-done, bf16[4,512,256]{2,1,0:T(8,128)(2,1)S(1)} %get-tuple-element.23.high, bf16[4,512,256]{2,1,0:T(8,128)(2,1)S(1)} %get-tuple-element.24.low, bf16[2,512,256]{2,1,0:T(8,128)(2,1)S(1)} %get-tuple-element.25.end_high, ...), custom_call_target="tpu_custom_call" | custom-call | flops 805306368 | bytes 1048576 | tf_op jit(solution)/shard_map/first_outer/pallas_call | solution.py:147
  37.7 0.8 %collective-permute-start.8 = (f32[2,64,256]{2,1,0:T(8,128)S(1)}, f32[2,64,256]{2,1,0:T(8,128)S(1)}, u32[]{:S(2)}, u32[]{:S(2)}) collective-permute-start(f32[2,64,256]{2,1,0:T(8,128)S(1)} %first_outer.1), channel_id=1, source_target_pairs={{0,4},{4,12},{12,8},{8,0},{1,5},{5,13},{13,9},{9,1},{2,6},{6,14},{... | collective-permute-start | bytes 393224 | tf_op jit(solution)/shard_map/ppermute | solution.py:221
  38.4 4.5 %chunk.3 = (f32[2,64,256]{2,1,0:T(8,128)S(1)}, f32[2,64,256]{2,1,0:T(8,128)S(1)}) custom-call(s32[8]{0:T(128)S(1)} %copy-done, s32[8,16]{1,0:T(8,128)S(1)} %copy-done.3, bf16[2,768,256]{2,1,0:T(8,128)(2,1)S(1)} %assemble.1.outer, bf16[2,768,256]{2,1,0:T(8,128)(2,1)S(1)} %get-tuple-element.29.inner, bf16[2,768,256]{2,1,0:T(8,128)(2,1)S(1)} %get-tuple-element.30.outside, ...), custom_call_target="tpu_custom_call" | custom-call | flops 3221225472 | bytes 1048576 | tf_op jit(solution)/shard_map/chunk/pallas_call | solution.py:147
  42.9 0.0 collective-permute-done.11
  43.0 3.0 %collective-permute-start.12 = (f32[2,64,256]{2,1,0:T(8,128)S(1)}, f32[2,64,256]{2,1,0:T(8,128)S(1)}, u32[]{:S(2)}, u32[]{:S(2)}) collective-permute-start(f32[2,64,256]{2,1,0:T(8,128)S(1)} %add.34), channel_id=1, source_target_pairs={{0,4},{4,12},{12,8},{8,0},{1,5},{5,13},{13,9},{9,1},{2,6},{6,14},{... | collective-permute-start | bytes 393224 | tf_op jit(solution)/shard_map/ppermute | solution.py:220
  45.9 0.0 collective-permute-done.8
  46.0 0.1 collective-permute-start.9
  46.0 4.5 %chunk.4 = (f32[2,64,256]{2,1,0:T(8,128)S(1)}, f32[2,64,256]{2,1,0:T(8,128)S(1)}) custom-call(s32[8]{0:T(128)S(1)} %copy-done, s32[8,16]{1,0:T(8,128)S(1)} %copy-done.3, bf16[2,768,256]{2,1,0:T(8,128)(2,1)S(1)} %assemble.1.outer, bf16[2,768,256]{2,1,0:T(8,128)(2,1)S(1)} %get-tuple-element.29.inner, bf16[2,768,256]{2,1,0:T(8,128)(2,1)S(1)} %get-tuple-element.30.outside, ...), custom_call_target="tpu_custom_call" | custom-call | flops 3221225472 | bytes 1048576 | tf_op jit(solution)/shard_map/chunk/pallas_call | solution.py:147
  50.5 0.0 collective-permute-done.12
  50.6 0.8 %collective-permute-start.13 = (f32[2,64,256]{2,1,0:T(8,128)S(1)}, f32[2,64,256]{2,1,0:T(8,128)S(1)}, u32[]{:S(2)}, u32[]{:S(2)}) collective-permute-start(f32[2,64,256]{2,1,0:T(8,128)S(1)} %add.35), channel_id=1, source_target_pairs={{0,4},{4,12},{12,8},{8,0},{1,5},{5,13},{13,9},{9,1},{2,6},{6,14},{... | collective-permute-start | bytes 393224 | tf_op jit(solution)/shard_map/ppermute | solution.py:220
  51.4 0.0 collective-permute-done.9
  51.4 0.7 %collective-permute-start.10 = (f32[2,64,256]{2,1,0:T(8,128)S(1)}, f32[2,64,256]{2,1,0:T(8,128)S(1)}, u32[]{:S(2)}, u32[]{:S(2)}) collective-permute-start(f32[2,64,256]{2,1,0:T(8,128)S(1)} %add.32), channel_id=1, source_target_pairs={{0,4},{4,12},{12,8},{8,0},{1,5},{5,13},{13,9},{9,1},{2,6},{6,14},{... | collective-permute-start | bytes 393224 | tf_op jit(solution)/shard_map/ppermute | solution.py:221
  52.1 4.5 %chunk.5 = (f32[2,64,256]{2,1,0:T(8,128)S(1)}, f32[2,64,256]{2,1,0:T(8,128)S(1)}) custom-call(s32[8]{0:T(128)S(1)} %copy-done, s32[8,16]{1,0:T(8,128)S(1)} %copy-done.3, bf16[2,768,256]{2,1,0:T(8,128)(2,1)S(1)} %assemble.1.outer, bf16[2,768,256]{2,1,0:T(8,128)(2,1)S(1)} %get-tuple-element.29.inner, bf16[2,768,256]{2,1,0:T(8,128)(2,1)S(1)} %get-tuple-element.30.outside, ...), custom_call_target="tpu_custom_call" | custom-call | flops 3221225472 | bytes 1048576 | tf_op jit(solution)/shard_map/chunk/pallas_call | solution.py:147
  56.6 0.1 collective-permute-done.13
  56.7 1.3 %collective-permute-done.10 = f32[2,64,256]{2,1,0:T(8,128)S(1)} collective-permute-done((f32[2,64,256]{2,1,0:T(8,128)S(1)}, f32[2,64,256]{2,1,0:T(8,128)S(1)}, u32[]{:S(2)}, u32[]{:S(2)}) %collective-permute-start.10) | collective-permute-done | bytes 131104 | tf_op jit(solution)/shard_map/ppermute | solution.py:221
  58.0 0.7 %pad_maximum_fusion.2 = f32[4,64,256]{2,1,0:T(8,128)} fusion(f32[1,64,256]{2,1,0:T(8,128)S(1)} %get-tuple-element.40, f32[2,64,256]{2,1,0:T(8,128)S(1)} %add.36, f32[1,64,256]{2,1,0:T(8,128)S(1)} %get-tuple-element.39), kind=kLoop, calls=%fused_computation.2 | loop fusion | flops 131072 | bytes 524288 | tf_op jit(solution)/shard_map/concatenate | solution.py:222
  (15 shorter events, 0.3 us)
Async XLA Ops:
  1.0 9.6 %collective-permute-start.3 = (f32[2,64,256]{2,1,0:T(8,128)S(1)}, f32[2,64,256]{2,1,0:T(8,128)S(1)}, u32[]{:S(2)}, u32[]{:S(2)}) collective-permute-start(f32[2,64,256]{2,1,0:T(8,128)S(1)} %get-tuple-element.37.refs_0_), channel_id=1, source_target_pairs={{0,4},{4,12},{12,8},{8,0},{1,5},{5,13},{13,9},{9,1},{2,6},{6,14},{... | collective-permute-start | bytes 393224 | tf_op jit(solution)/shard_map/ppermute | solution.py:175
  3.2 7.0 %collective-permute-start = (f32[2,64,256]{2,1,0:T(8,128)S(1)}, f32[2,64,256]{2,1,0:T(8,128)S(1)}, u32[]{:S(2)}, u32[]{:S(2)}) collective-permute-start(f32[2,64,256]{2,1,0:T(8,128)S(1)} %get-tuple-element.38.refs_0_), channel_id=1, source_target_pairs={{0,4},{4,12},{12,8},{8,0},{1,5},{5,13},{13,9},{9,1},{2,6},{6,14},{... | collective-permute-start | bytes 393224 | tf_op jit(solution)/shard_map/ppermute | solution.py:176
  5.5 1.6 %copy-start.1 = (f32[8,256,256]{2,1,0:T(8,128)S(1)}, f32[8,256,256]{2,1,0:T(8,128)}, u32[]{:S(2)}) copy-start(f32[8,256,256]{2,1,0:T(8,128)} %left_ref.1) | copy-start | bytes 6291460
  7.1 1.6 %copy-start.2 = (f32[8,256,256]{2,1,0:T(8,128)S(1)}, f32[8,256,256]{2,1,0:T(8,128)}, u32[]{:S(2)}) copy-start(f32[8,256,256]{2,1,0:T(8,128)} %right_ref.1) | copy-start | bytes 6291460
  10.3 4.8 %collective-permute-start.1 = (f32[2,64,256]{2,1,0:T(8,128)S(1)}, f32[2,64,256]{2,1,0:T(8,128)S(1)}, u32[]{:S(2)}, u32[]{:S(2)}) collective-permute-start(f32[2,64,256]{2,1,0:T(8,128)S(1)} %broadcast_add_fusion.1), channel_id=1, source_target_pairs={{0,4},{4,12},{12,8},{8,0},{1,5},{5,13},{13,9},{9,1},{2,6},{6,14},{... | collective-permute-start | bytes 393224 | tf_op jit(solution)/shard_map/ppermute | solution.py:176
  10.7 7.1 %collective-permute-start.4 = (f32[2,64,256]{2,1,0:T(8,128)S(1)}, f32[2,64,256]{2,1,0:T(8,128)S(1)}, u32[]{:S(2)}, u32[]{:S(2)}) collective-permute-start(f32[2,64,256]{2,1,0:T(8,128)S(1)} %broadcast_add_fusion), channel_id=1, source_target_pairs={{0,4},{4,12},{12,8},{8,0},{1,5},{5,13},{13,9},{9,1},{2,6},{6,14},{... | collective-permute-start | bytes 393224 | tf_op jit(solution)/shard_map/ppermute | solution.py:175
  15.0 5.6 %collective-permute-start.2 = (f32[2,64,256]{2,1,0:T(8,128)S(1)}, f32[2,64,256]{2,1,0:T(8,128)S(1)}, u32[]{:S(2)}, u32[]{:S(2)}) collective-permute-start(f32[2,64,256]{2,1,0:T(8,128)S(1)} %collective-permute-done.1.refs_2_), channel_id=1, source_target_pairs={{0,4},{4,12},{12,8},{8,0},{1,5},{5,13},{13,9},{9,1},{2,6},{6,14},{... | collective-permute-start | bytes 393224 | tf_op jit(solution)/shard_map/ppermute | solution.py:176
  17.8 11.6 %collective-permute-start.5 = (f32[2,64,256]{2,1,0:T(8,128)S(1)}, f32[2,64,256]{2,1,0:T(8,128)S(1)}, u32[]{:S(2)}, u32[]{:S(2)}) collective-permute-start(f32[2,64,256]{2,1,0:T(8,128)S(1)} %collective-permute-done.4.refs_2_), channel_id=1, source_target_pairs={{0,4},{4,12},{12,8},{8,0},{1,5},{5,13},{13,9},{9,1},{2,6},{6,14},{... | collective-permute-start | bytes 393224 | tf_op jit(solution)/shard_map/ppermute | solution.py:175
  20.7 12.1 %collective-permute-start.6 = (f32[4,64,256]{2,1,0:T(8,128)S(1)}, f32[4,64,256]{2,1,0:T(8,128)S(1)}, u32[]{:S(2)}, u32[]{:S(2)}) collective-permute-start(f32[4,64,256]{2,1,0:T(8,128)S(1)} %pad_maximum_fusion), channel_id=1, source_target_pairs={{0,1},{1,2},{2,3},{4,5},{5,6},{6,7},{8,9},{9,10},{10,11},{12,13},{... | collective-permute-start | bytes 786440 | tf_op jit(solution)/shard_map/ppermute | solution.py:18
  27.2 2.1 %copy-start.3 = (s32[8,16]{1,0:T(8,128)S(1)}, s32[8,16]{1,0:T(8,128)}, u32[]{:S(2)}) copy-start(s32[8,16]{1,0:T(8,128)} %allowed_ref.9) | copy-start | bytes 1540
  27.2 8.0 %collective-permute-start.7 = (f32[4,64,256]{2,1,0:T(8,128)S(1)}, f32[4,64,256]{2,1,0:T(8,128)S(1)}, u32[]{:S(2)}, u32[]{:S(2)}) collective-permute-start(f32[4,64,256]{2,1,0:T(8,128)S(1)} %pad_maximum_fusion.1), channel_id=1, source_target_pairs={{1,0},{2,1},{3,2},{5,4},{6,5},{7,6},{9,8},{10,9},{11,10},{13,12},{... | collective-permute-start | bytes 786440 | tf_op jit(solution)/shard_map/ppermute | solution.py:18
  29.4 1.7 %copy-start = (s32[8]{0:T(128)S(1)}, s32[8]{0:T(128)}, u32[]{:S(2)}) copy-start(s32[8]{0:T(128)} %shifts_ref.9) | copy-start | bytes 100
  32.2 10.7 %collective-permute-start.11 = (f32[2,64,256]{2,1,0:T(8,128)S(1)}, f32[2,64,256]{2,1,0:T(8,128)S(1)}, u32[]{:S(2)}, u32[]{:S(2)}) collective-permute-start(f32[2,64,256]{2,1,0:T(8,128)S(1)} %first_inner.1), channel_id=1, source_target_pairs={{0,4},{4,12},{12,8},{8,0},{1,5},{5,13},{13,9},{9,1},{2,6},{6,14},{... | collective-permute-start | bytes 393224 | tf_op jit(solution)/shard_map/ppermute | solution.py:220
  37.7 8.3 %collective-permute-start.8 = (f32[2,64,256]{2,1,0:T(8,128)S(1)}, f32[2,64,256]{2,1,0:T(8,128)S(1)}, u32[]{:S(2)}, u32[]{:S(2)}) collective-permute-start(f32[2,64,256]{2,1,0:T(8,128)S(1)} %first_outer.1), channel_id=1, source_target_pairs={{0,4},{4,12},{12,8},{8,0},{1,5},{5,13},{13,9},{9,1},{2,6},{6,14},{... | collective-permute-start | bytes 393224 | tf_op jit(solution)/shard_map/ppermute | solution.py:221
  43.0 7.6 %collective-permute-start.12 = (f32[2,64,256]{2,1,0:T(8,128)S(1)}, f32[2,64,256]{2,1,0:T(8,128)S(1)}, u32[]{:S(2)}, u32[]{:S(2)}) collective-permute-start(f32[2,64,256]{2,1,0:T(8,128)S(1)} %add.34), channel_id=1, source_target_pairs={{0,4},{4,12},{12,8},{8,0},{1,5},{5,13},{13,9},{9,1},{2,6},{6,14},{... | collective-permute-start | bytes 393224 | tf_op jit(solution)/shard_map/ppermute | solution.py:220
  46.0 5.4 %collective-permute-start.9 = (f32[2,64,256]{2,1,0:T(8,128)S(1)}, f32[2,64,256]{2,1,0:T(8,128)S(1)}, u32[]{:S(2)}, u32[]{:S(2)}) collective-permute-start(f32[2,64,256]{2,1,0:T(8,128)S(1)} %add.31), channel_id=1, source_target_pairs={{0,4},{4,12},{12,8},{8,0},{1,5},{5,13},{13,9},{9,1},{2,6},{6,14},{... | collective-permute-start | bytes 393224 | tf_op jit(solution)/shard_map/ppermute | solution.py:221
  50.6 6.1 %collective-permute-start.13 = (f32[2,64,256]{2,1,0:T(8,128)S(1)}, f32[2,64,256]{2,1,0:T(8,128)S(1)}, u32[]{:S(2)}, u32[]{:S(2)}) collective-permute-start(f32[2,64,256]{2,1,0:T(8,128)S(1)} %add.35), channel_id=1, source_target_pairs={{0,4},{4,12},{12,8},{8,0},{1,5},{5,13},{13,9},{9,1},{2,6},{6,14},{... | collective-permute-start | bytes 393224 | tf_op jit(solution)/shard_map/ppermute | solution.py:220
  51.4 6.6 %collective-permute-start.10 = (f32[2,64,256]{2,1,0:T(8,128)S(1)}, f32[2,64,256]{2,1,0:T(8,128)S(1)}, u32[]{:S(2)}, u32[]{:S(2)}) collective-permute-start(f32[2,64,256]{2,1,0:T(8,128)S(1)} %add.32), channel_id=1, source_target_pairs={{0,4},{4,12},{12,8},{8,0},{1,5},{5,13},{13,9},{9,1},{2,6},{6,14},{... | collective-permute-start | bytes 393224 | tf_op jit(solution)/shard_map/ppermute | solution.py:221

commit v5 on v3

--- a/solution.py
+++ b/solution.py
@@ -57,15 +57,15 @@
     return jnp.concatenate([hi, lo, hi], axis=0)
 
 
-def place_rows(n, target, blocks):
+def place_rows(n, target, blocks, way=1):
     for j, block in enumerate(blocks):
         rows = block.shape[-2]
-        target[..., pl.ds(pl.multiple_of(ring_place(n, j) * rows, rows), rows), :] = block
-
-
-def assemble(n, *refs):
+        target[..., pl.ds(pl.multiple_of(ring_place(n, way * j) * rows, rows), rows), :] = block
+
+
+def assemble(n, way, *refs):
     parts, psi = refs[n:]
-    place_rows(n, psi, [ref[...] for ref in refs[:n]])
+    place_rows(n, psi, [ref[...] for ref in refs[:n]], way)
     for i in range(parts.shape[0]):
         parts[i] = stacked(psi[i])
 
@@ -84,9 +84,9 @@
     return left_parts[ring_place(n, step + 1)].reshape(-1, left_parts.shape[-1])
 
 
-def own_sectors(n, allowed_ref, *refs):
-    (outer, left_parts), (inner, high, low, psi) = refs[n : n + 2], refs[n + 2 :]
-    assemble(n, *refs[:n], inner, psi)
+def own_sectors(n, allowed_ref, outer, *refs):
+    left_parts, inner, high, low, psi = refs[n:]
+    assemble(n, -1, *refs[:n], inner, psi)
     left = chunk_left(n, 0, left_parts)
     nloc = high.shape[0]
     first = lax.axis_index(("sec", "sub")) * nloc
@@ -163,6 +163,7 @@
     kops = left_ops.shape[0]
     n = lax.axis_size("op")
     route = ring_route(n)
+    back = [(target, source) for source, target in route]
     one = 6 * width**3
 
     tall = jax.ShapeDtypeStruct((kops * width, width), BF16)
@@ -174,7 +175,7 @@
 
     outer, inner = [psi[:: nloc - 1]], [psi[1 : nloc - 1]]
     for step in range(n - 1):
-        inner.append(lax.ppermute(inner[-1] + zero[0, 0] if step == 1 else inner[-1], "op", route))
+        inner.append(lax.ppermute(inner[-1] + zero[0, 0] if step == 1 else inner[-1], "op", back))
         outer.append(lax.ppermute(outer[-1] + zero[0, 0] if step == 1 else outer[-1], "op", route))
 
     above = shifted(jnp.concatenate([b[1:] for b in outer]), ("sec", "sub"), 1)
@@ -186,7 +187,7 @@
     def whole(sectors):
         return [pltpu.VMEM((sectors, width, width), F32)]
 
-    parts_outer = call(functools.partial(assemble, n), "assemble", 4 * kops * one, split_parts(2), [VMEM] * n, outer, whole(2))
+    parts_outer = call(functools.partial(assemble, n, 1), "assemble", 4 * kops * one, split_parts(2), [VMEM] * n, outer, whole(2))
     def products(sectors):
         return [jax.ShapeDtypeStruct((sectors, kops * rows, width), BF16)] * 2
 
@@ -194,7 +195,7 @@
     chunk_inner = jax.ShapeDtypeStruct((nloc - 2, rows, width), F32)
     parts_inner, *own = call(
         functools.partial(own_sectors, n), "own", 4 * kops * one, [split_parts(nloc - 2), *products(nloc)],
-        [SMEM] + [VMEM] * (n + 2), [allowed, *inner, parts_outer, left_parts], whole(nloc - 2),
+        [SMEM] + [VMEM] * (n + 2), [allowed, parts_outer, *inner, left_parts], whole(nloc - 2),
     )
     result_inner = call(
         functools.partial(first_inner, nloc), "first_inner", nloc * kops * one // n, chunk_inner,

time: 58.3 us -> 61.1 us (1.048)
  starting transfers between devices: 20.2 us -> 29.5 us
  waiting for transfers between devices: 16.3 us -> 9.93 us
    ppermute x3, starting transfers between devices: 0.3 us -> 3.68 us  [shards(): result_outer = lax.ppermute(result_outer, 'op', route) + next_outer]
    ppermute x3, starting transfers between devices: 5.91 us -> 9.23 us  [shards(): result_inner = lax.ppermute(result_inner, 'op', route) + next_inner]
    ppermute x3, starting transfers between devices: 2.4 us -> 5.59 us  [shards(): lax.ppermute(inner[-1] + zero[0, 0] if step == 1 else inner[-1], 'op', back)]
    ppermute x2, waiting for transfers between devices: 2.88 us -> 0.01 us  [shifted(): return lax.ppermute(block, axis, route)]
    ppermute x3, waiting for transfers between devices: 3.62 us -> 1.05 us  [shards(): lax.ppermute(inner[-1] + zero[0, 0] if step == 1 else inner[-1], 'op', back)]
    ppermute x3, waiting for transfers between devices: 8.07 us -> 6.8 us  [shards(): lax.ppermute(outer[-1] + zero[0, 0] if step == 1 else outer[-1], 'op', ro...]
    ppermute x2, starting transfers between devices: 8.62 us -> 7.55 us  [shifted(): return lax.ppermute(block, axis, route)]
  transfers between devices with their start and end apart: 14 -> 14, of which waited for: 7 -> 6; matrix products, arithmetic and copies ran while one was open for 0% -> 0% of each run, Pallas kernels for 28% -> 26%
where the time goes in v5:
time: 61.1 us; the launch traced here: 60.9 us
  starting transfers between devices  29.5 us (48%)
  Pallas kernels  16 us (26%)
  waiting for transfers between devices  9.93 us (16%)
  local copies, waits for them, and re-layouts  4.23 us (7%)
  other arithmetic  0.96 us (2%)
    pallas_call x9, Pallas kernels, call(): pl.pallas_call(body, name=name, out_shape=out_shape, in_specs=in_specs, o...  16 us
    ppermute x3, starting transfers between devices, shards(): result_inner = lax.ppermute(result_inner, 'op', route) + next_inner  9.23 us
    ppermute x2, starting transfers between devices, shifted(): return lax.ppermute(block, axis, route)  7.55 us
    ppermute x3, waiting for transfers between devices, shards(): lax.ppermute(outer[-1] + zero[0, 0] if step == 1 else outer[-1], 'op', ro...  6.8 us
    ppermute x3, starting transfers between devices, shards(): lax.ppermute(inner[-1] + zero[0, 0] if step == 1 else inner[-1], 'op', back)  5.59 us
    ppermute x3, starting transfers between devices, shards(): result_outer = lax.ppermute(result_outer, 'op', route) + next_outer  3.68 us
    ppermute x3, starting transfers between devices, shards(): lax.ppermute(outer[-1] + zero[0, 0] if step == 1 else outer[-1], 'op', ro...  3.43 us
    unnamed x8, local copies, waits for them, and re-layouts  3.19 us
  transfers between devices with their start and end apart: 14, of which 6 were waited for; matrix products, arithmetic and copies ran while one was open for 0% of the time, Pallas kernels for 26%

profile of v5, /device:TPU:1, one launch (start us, length us, event | category | flops | bytes accessed | tf_op | source)
XLA Modules:
  0.0 60.9 jit_solution(2103432492935655075)
XLA Ops:
  0.0 1.0 %fusion = (f32[2,64,256]{2,1,0:T(8,128)S(1)}, f32[2,64,256]{2,1,0:T(8,128)S(1)}) fusion(f32[4,64,256]{2,1,0:T(8,128)} %param.5), kind=kLoop, calls=%fused_computation.5 | loop fusion | bytes 524288 | tf_op jit(solution)/shard_map/slice | solution.py:176
  1.0 3.2 %collective-permute-start.3 = (f32[2,64,256]{2,1,0:T(8,128)S(1)}, f32[2,64,256]{2,1,0:T(8,128)S(1)}, u32[]{:S(2)}, u32[]{:S(2)}) collective-permute-start(f32[2,64,256]{2,1,0:T(8,128)S(1)} %get-tuple-element.37.refs_0_), channel_id=1, source_target_pairs={{4,0},{12,4},{8,12},{0,8},{5,1},{13,5},{9,13},{1,9},{6,2},{14,6},{... | collective-permute-start | bytes 393224 | tf_op jit(solution)/shard_map/ppermute | solution.py:178
  4.2 0.0 collective-permute-start
  4.2 0.0 copy-start.1
  4.2 1.6 %copy-done.1 = f32[8,256,256]{2,1,0:T(8,128)S(1)} copy-done((f32[8,256,256]{2,1,0:T(8,128)S(1)}, f32[8,256,256]{2,1,0:T(8,128)}, u32[]{:S(2)}) %copy-start.1) | copy-done | bytes 2097176
  5.8 0.0 copy-start.2
  5.8 1.6 %copy-done.2 = f32[8,256,256]{2,1,0:T(8,128)S(1)} copy-done((f32[8,256,256]{2,1,0:T(8,128)S(1)}, f32[8,256,256]{2,1,0:T(8,128)}, u32[]{:S(2)}) %copy-start.2) | copy-done | bytes 2097176
  7.4 1.1 %prepare.1 = (bf16[4,8,64,768]{3,2,1,0:T(8,128)(2,1)S(1)}, bf16[2048,256]{1,0:T(8,128)(2,1)S(1)}, bf16[2048,256]{1,0:T(8,128)(2,1)S(1)}, f32[1,128]{1,0:T(1,128)S(1)}) custom-call(f32[8,256,256]{2,1,0:T(8,128)S(1)} %copy-done.1, f32[8,256,256]{2,1,0:T(8,128)S(1)} %copy-done.2), custom_call_target="tpu_custom_call" | custom-call | flops 3221225472 | bytes 1048576 | tf_op jit(solution)/shard_map/prepare/pallas_call | solution.py:149
  8.5 3.1 %collective-permute-done.refs_1_ = f32[2,64,256]{2,1,0:T(8,128)S(1)} collective-permute-done((f32[2,64,256]{2,1,0:T(8,128)S(1)}, f32[2,64,256]{2,1,0:T(8,128)S(1)}, u32[]{:S(2)}, u32[]{:S(2)}) %collective-permute-start) | collective-permute-done | bytes 131104 | tf_op jit(solution)/shard_map/ppermute | solution.py:179
  11.6 0.1 collective-permute-start.1
  11.6 0.0 collective-permute-done.3.refs_1_
  11.7 2.4 %collective-permute-start.4 = (f32[2,64,256]{2,1,0:T(8,128)S(1)}, f32[2,64,256]{2,1,0:T(8,128)S(1)}, u32[]{:S(2)}, u32[]{:S(2)}) collective-permute-start(f32[2,64,256]{2,1,0:T(8,128)S(1)} %broadcast_add_fusion), channel_id=1, source_target_pairs={{4,0},{12,4},{8,12},{0,8},{5,1},{13,5},{9,13},{1,9},{6,2},{14,6},{... | collective-permute-start | bytes 393224 | tf_op jit(solution)/shard_map/ppermute | solution.py:178
  14.1 2.3 %collective-permute-done.1.refs_2_ = f32[2,64,256]{2,1,0:T(8,128)S(1)} collective-permute-done((f32[2,64,256]{2,1,0:T(8,128)S(1)}, f32[2,64,256]{2,1,0:T(8,128)S(1)}, u32[]{:S(2)}, u32[]{:S(2)}) %collective-permute-start.1) | collective-permute-done | bytes 131104 | tf_op jit(solution)/shard_map/ppermute | solution.py:179
  16.4 3.4 %collective-permute-start.2 = (f32[2,64,256]{2,1,0:T(8,128)S(1)}, f32[2,64,256]{2,1,0:T(8,128)S(1)}, u32[]{:S(2)}, u32[]{:S(2)}) collective-permute-start(f32[2,64,256]{2,1,0:T(8,128)S(1)} %collective-permute-done.1.refs_2_), channel_id=1, source_target_pairs={{0,4},{4,12},{12,8},{8,0},{1,5},{5,13},{13,9},{9,1},{2,6},{6,14},{... | collective-permute-start | bytes 393224 | tf_op jit(solution)/shard_map/ppermute | solution.py:179
  19.8 1.0 %collective-permute-done.4.refs_2_ = f32[2,64,256]{2,1,0:T(8,128)S(1)} collective-permute-done((f32[2,64,256]{2,1,0:T(8,128)S(1)}, f32[2,64,256]{2,1,0:T(8,128)S(1)}, u32[]{:S(2)}, u32[]{:S(2)}) %collective-permute-start.4) | collective-permute-done | bytes 131104 | tf_op jit(solution)/shard_map/ppermute | solution.py:178
  20.8 0.0 collective-permute-start.5
  20.9 1.4 %collective-permute-done.2.refs_3_ = f32[2,64,256]{2,1,0:T(8,128)S(1)} collective-permute-done((f32[2,64,256]{2,1,0:T(8,128)S(1)}, f32[2,64,256]{2,1,0:T(8,128)S(1)}, u32[]{:S(2)}, u32[]{:S(2)}) %collective-permute-start.2) | collective-permute-done | bytes 131104 | tf_op jit(solution)/shard_map/ppermute | solution.py:179
  22.3 5.6 %collective-permute-start.6 = (f32[4,64,256]{2,1,0:T(8,128)S(1)}, f32[4,64,256]{2,1,0:T(8,128)S(1)}, u32[]{:S(2)}, u32[]{:S(2)}) collective-permute-start(f32[4,64,256]{2,1,0:T(8,128)S(1)} %pad_maximum_fusion), channel_id=1, source_target_pairs={{0,1},{1,2},{2,3},{4,5},{5,6},{6,7},{8,9},{9,10},{10,11},{12,13},{... | collective-permute-start | bytes 786440 | tf_op jit(solution)/shard_map/ppermute | solution.py:18
  28.0 0.0 copy-start.3
  28.0 1.9 %collective-permute-start.7 = (f32[4,64,256]{2,1,0:T(8,128)S(1)}, f32[4,64,256]{2,1,0:T(8,128)S(1)}, u32[]{:S(2)}, u32[]{:S(2)}) collective-permute-start(f32[4,64,256]{2,1,0:T(8,128)S(1)} %pad_maximum_fusion.1), channel_id=1, source_target_pairs={{1,0},{2,1},{3,2},{5,4},{6,5},{7,6},{9,8},{10,9},{11,10},{13,12},{... | collective-permute-start | bytes 786440 | tf_op jit(solution)/shard_map/ppermute | solution.py:18
  29.9 0.2 assemble.1.outer
  30.1 0.0 collective-permute-done.5.refs_3_
  30.1 0.0 copy-done.3
  30.2 0.0 copy-start
  30.2 1.7 %own.1 = (bf16[2,768,256]{2,1,0:T(8,128)(2,1)S(1)}, bf16[4,512,256]{2,1,0:T(8,128)(2,1)S(1)}, bf16[4,512,256]{2,1,0:T(8,128)(2,1)S(1)}) custom-call(s32[8,16]{1,0:T(8,128)S(1)} %copy-done.3, bf16[2,768,256]{2,1,0:T(8,128)(2,1)S(1)} %assemble.1.outer, f32[2,64,256]{2,1,0:T(8,128)S(1)} %get-tuple-element.37.refs_0_, ...), custom_call_target="tpu_custom_call" | custom-call | flops 3221225472 | bytes 1048576 | tf_op jit(solution)/shard_map/own/pallas_call | solution.py:149
  31.9 0.0 copy-done
  31.9 1.2 %first_inner.1 = f32[2,64,256]{2,1,0:T(8,128)S(1)} custom-call(s32[8]{0:T(128)S(1)} %copy-done, bf16[4,512,256]{2,1,0:T(8,128)(2,1)S(1)} %get-tuple-element.23.high, bf16[4,512,256]{2,1,0:T(8,128)(2,1)S(1)} %get-tuple-element.24.low, bf16[2048,256]{1,0:T(8,128)(2,1)S(1)} %get-tuple-element.27.right_hi, bf16[2048,256]{1,0:T(8,128)(2,1)S(1)} %get-tuple-element.28.right_lo), custom_call_target="tpu_custom_call" | custom-call | flops 805306368 | bytes 1048576 | tf_op jit(solution)/shard_map/first_inner/pallas_call | solution.py:149
  33.0 4.1 %collective-permute-start.11 = (f32[2,64,256]{2,1,0:T(8,128)S(1)}, f32[2,64,256]{2,1,0:T(8,128)S(1)}, u32[]{:S(2)}, u32[]{:S(2)}) collective-permute-start(f32[2,64,256]{2,1,0:T(8,128)S(1)} %first_inner.1), channel_id=1, source_target_pairs={{0,4},{4,12},{12,8},{8,0},{1,5},{5,13},{13,9},{9,1},{2,6},{6,14},{... | collective-permute-start | bytes 393224 | tf_op jit(solution)/shard_map/ppermute | solution.py:223
  37.2 0.0 collective-permute-done.6.above
  37.2 0.0 collective-permute-done.7.below
  37.2 1.3 %outside.1 = (bf16[2,768,256]{2,1,0:T(8,128)(2,1)S(1)}, bf16[2,512,256]{2,1,0:T(8,128)(2,1)S(1)}, bf16[2,512,256]{2,1,0:T(8,128)(2,1)S(1)}) custom-call(s32[8,16]{1,0:T(8,128)S(1)} %copy-done.3, f32[4,64,256]{2,1,0:T(8,128)S(1)} %collective-permute-done.6.above, f32[4,64,256]{2,1,0:T(8,128)S(1)} %collective-permute-done.7.below, ...), custom_call_target="tpu_custom_call" | custom-call | flops 1610612736 | bytes 1048576 | tf_op jit(solution)/shard_map/outside/pallas_call | solution.py:149
  38.5 1.2 %first_outer.1 = f32[2,64,256]{2,1,0:T(8,128)S(1)} custom-call(s32[8]{0:T(128)S(1)} %copy-done, bf16[4,512,256]{2,1,0:T(8,128)(2,1)S(1)} %get-tuple-element.23.high, bf16[4,512,256]{2,1,0:T(8,128)(2,1)S(1)} %get-tuple-element.24.low, bf16[2,512,256]{2,1,0:T(8,128)(2,1)S(1)} %get-tuple-element.25.end_high, ...), custom_call_target="tpu_custom_call" | custom-call | flops 805306368 | bytes 1048576 | tf_op jit(solution)/shard_map/first_outer/pallas_call | solution.py:149
  39.7 3.2 %collective-permute-start.8 = (f32[2,64,256]{2,1,0:T(8,128)S(1)}, f32[2,64,256]{2,1,0:T(8,128)S(1)}, u32[]{:S(2)}, u32[]{:S(2)}) collective-permute-start(f32[2,64,256]{2,1,0:T(8,128)S(1)} %first_outer.1), channel_id=1, source_target_pairs={{0,4},{4,12},{12,8},{8,0},{1,5},{5,13},{13,9},{9,1},{2,6},{6,14},{... | collective-permute-start | bytes 393224 | tf_op jit(solution)/shard_map/ppermute | solution.py:224
  42.8 3.2 %chunk.3 = (f32[2,64,256]{2,1,0:T(8,128)S(1)}, f32[2,64,256]{2,1,0:T(8,128)S(1)}) custom-call(s32[8]{0:T(128)S(1)} %copy-done, s32[8,16]{1,0:T(8,128)S(1)} %copy-done.3, bf16[2,768,256]{2,1,0:T(8,128)(2,1)S(1)} %assemble.1.outer, bf16[2,768,256]{2,1,0:T(8,128)(2,1)S(1)} %get-tuple-element.29.inner, bf16[2,768,256]{2,1,0:T(8,128)(2,1)S(1)} %get-tuple-element.30.outside, ...), custom_call_target="tpu_custom_call" | custom-call | flops 3221225472 | bytes 1048576 | tf_op jit(solution)/shard_map/chunk/pallas_call | solution.py:149
  46.0 0.0 collective-permute-done.11
  46.0 3.0 %collective-permute-start.12 = (f32[2,64,256]{2,1,0:T(8,128)S(1)}, f32[2,64,256]{2,1,0:T(8,128)S(1)}, u32[]{:S(2)}, u32[]{:S(2)}) collective-permute-start(f32[2,64,256]{2,1,0:T(8,128)S(1)} %add.34), channel_id=1, source_target_pairs={{0,4},{4,12},{12,8},{8,0},{1,5},{5,13},{13,9},{9,1},{2,6},{6,14},{... | collective-permute-start | bytes 393224 | tf_op jit(solution)/shard_map/ppermute | solution.py:223
  49.0 0.0 collective-permute-done.8
  49.0 0.1 collective-permute-start.9
  49.1 3.2 %chunk.4 = (f32[2,64,256]{2,1,0:T(8,128)S(1)}, f32[2,64,256]{2,1,0:T(8,128)S(1)}) custom-call(s32[8]{0:T(128)S(1)} %copy-done, s32[8,16]{1,0:T(8,128)S(1)} %copy-done.3, bf16[2,768,256]{2,1,0:T(8,128)(2,1)S(1)} %assemble.1.outer, bf16[2,768,256]{2,1,0:T(8,128)(2,1)S(1)} %get-tuple-element.29.inner, bf16[2,768,256]{2,1,0:T(8,128)(2,1)S(1)} %get-tuple-element.30.outside, ...), custom_call_target="tpu_custom_call" | custom-call | flops 3221225472 | bytes 1048576 | tf_op jit(solution)/shard_map/chunk/pallas_call | solution.py:149
  52.3 0.3 collective-permute-done.12
  52.5 2.1 %collective-permute-start.13 = (f32[2,64,256]{2,1,0:T(8,128)S(1)}, f32[2,64,256]{2,1,0:T(8,128)S(1)}, u32[]{:S(2)}, u32[]{:S(2)}) collective-permute-start(f32[2,64,256]{2,1,0:T(8,128)S(1)} %add.35), channel_id=1, source_target_pairs={{0,4},{4,12},{12,8},{8,0},{1,5},{5,13},{13,9},{9,1},{2,6},{6,14},{... | collective-permute-start | bytes 393224 | tf_op jit(solution)/shard_map/ppermute | solution.py:223
  54.7 0.0 collective-permute-done.9
  54.7 0.4 collective-permute-start.10
  55.1 3.1 %chunk.5 = (f32[2,64,256]{2,1,0:T(8,128)S(1)}, f32[2,64,256]{2,1,0:T(8,128)S(1)}) custom-call(s32[8]{0:T(128)S(1)} %copy-done, s32[8,16]{1,0:T(8,128)S(1)} %copy-done.3, bf16[2,768,256]{2,1,0:T(8,128)(2,1)S(1)} %assemble.1.outer, bf16[2,768,256]{2,1,0:T(8,128)(2,1)S(1)} %get-tuple-element.29.inner, bf16[2,768,256]{2,1,0:T(8,128)(2,1)S(1)} %get-tuple-element.30.outside, ...), custom_call_target="tpu_custom_call" | custom-call | flops 3221225472 | bytes 1048576 | tf_op jit(solution)/shard_map/chunk/pallas_call | solution.py:149
  58.3 0.0 collective-permute-done.13
  58.3 1.8 %collective-permute-done.10 = f32[2,64,256]{2,1,0:T(8,128)S(1)} collective-permute-done((f32[2,64,256]{2,1,0:T(8,128)S(1)}, f32[2,64,256]{2,1,0:T(8,128)S(1)}, u32[]{:S(2)}, u32[]{:S(2)}) %collective-permute-start.10) | collective-permute-done | bytes 131104 | tf_op jit(solution)/shard_map/ppermute | solution.py:224
  60.2 0.7 %pad_maximum_fusion.2 = f32[4,64,256]{2,1,0:T(8,128)} fusion(f32[1,64,256]{2,1,0:T(8,128)S(1)} %get-tuple-element.40, f32[2,64,256]{2,1,0:T(8,128)S(1)} %add.36, f32[1,64,256]{2,1,0:T(8,128)S(1)} %get-tuple-element.39), kind=kLoop, calls=%fused_computation.2 | loop fusion | flops 131072 | bytes 524288 | tf_op jit(solution)/shard_map/concatenate | solution.py:225
  (15 shorter events, 0.3 us)
Async XLA Ops:
  1.0 10.7 %collective-permute-start.3 = (f32[2,64,256]{2,1,0:T(8,128)S(1)}, f32[2,64,256]{2,1,0:T(8,128)S(1)}, u32[]{:S(2)}, u32[]{:S(2)}) collective-permute-start(f32[2,64,256]{2,1,0:T(8,128)S(1)} %get-tuple-element.37.refs_0_), channel_id=1, source_target_pairs={{4,0},{12,4},{8,12},{0,8},{5,1},{13,5},{9,13},{1,9},{6,2},{14,6},{... | collective-permute-start | bytes 393224 | tf_op jit(solution)/shard_map/ppermute | solution.py:178
  4.2 7.3 %collective-permute-start = (f32[2,64,256]{2,1,0:T(8,128)S(1)}, f32[2,64,256]{2,1,0:T(8,128)S(1)}, u32[]{:S(2)}, u32[]{:S(2)}) collective-permute-start(f32[2,64,256]{2,1,0:T(8,128)S(1)} %get-tuple-element.38.refs_0_), channel_id=1, source_target_pairs={{0,4},{4,12},{12,8},{8,0},{1,5},{5,13},{13,9},{9,1},{2,6},{6,14},{... | collective-permute-start | bytes 393224 | tf_op jit(solution)/shard_map/ppermute | solution.py:179
  4.2 1.6 %copy-start.1 = (f32[8,256,256]{2,1,0:T(8,128)S(1)}, f32[8,256,256]{2,1,0:T(8,128)}, u32[]{:S(2)}) copy-start(f32[8,256,256]{2,1,0:T(8,128)} %left_ref.1) | copy-start | bytes 6291460
  5.8 1.6 %copy-start.2 = (f32[8,256,256]{2,1,0:T(8,128)S(1)}, f32[8,256,256]{2,1,0:T(8,128)}, u32[]{:S(2)}) copy-start(f32[8,256,256]{2,1,0:T(8,128)} %right_ref.1) | copy-start | bytes 6291460
  11.6 4.8 %collective-permute-start.1 = (f32[2,64,256]{2,1,0:T(8,128)S(1)}, f32[2,64,256]{2,1,0:T(8,128)S(1)}, u32[]{:S(2)}, u32[]{:S(2)}) collective-permute-start(f32[2,64,256]{2,1,0:T(8,128)S(1)} %broadcast_add_fusion.1), channel_id=1, source_target_pairs={{0,4},{4,12},{12,8},{8,0},{1,5},{5,13},{13,9},{9,1},{2,6},{6,14},{... | collective-permute-start | bytes 393224 | tf_op jit(solution)/shard_map/ppermute | solution.py:179
  11.7 9.1 %collective-permute-start.4 = (f32[2,64,256]{2,1,0:T(8,128)S(1)}, f32[2,64,256]{2,1,0:T(8,128)S(1)}, u32[]{:S(2)}, u32[]{:S(2)}) collective-permute-start(f32[2,64,256]{2,1,0:T(8,128)S(1)} %broadcast_add_fusion), channel_id=1, source_target_pairs={{4,0},{12,4},{8,12},{0,8},{5,1},{13,5},{9,13},{1,9},{6,2},{14,6},{... | collective-permute-start | bytes 393224 | tf_op jit(solution)/shard_map/ppermute | solution.py:178
  16.4 5.9 %collective-permute-start.2 = (f32[2,64,256]{2,1,0:T(8,128)S(1)}, f32[2,64,256]{2,1,0:T(8,128)S(1)}, u32[]{:S(2)}, u32[]{:S(2)}) collective-permute-start(f32[2,64,256]{2,1,0:T(8,128)S(1)} %collective-permute-done.1.refs_2_), channel_id=1, source_target_pairs={{0,4},{4,12},{12,8},{8,0},{1,5},{5,13},{13,9},{9,1},{2,6},{6,14},{... | collective-permute-start | bytes 393224 | tf_op jit(solution)/shard_map/ppermute | solution.py:179
  20.8 9.3 %collective-permute-start.5 = (f32[2,64,256]{2,1,0:T(8,128)S(1)}, f32[2,64,256]{2,1,0:T(8,128)S(1)}, u32[]{:S(2)}, u32[]{:S(2)}) collective-permute-start(f32[2,64,256]{2,1,0:T(8,128)S(1)} %collective-permute-done.4.refs_2_), channel_id=1, source_target_pairs={{4,0},{12,4},{8,12},{0,8},{5,1},{13,5},{9,13},{1,9},{6,2},{14,6},{... | collective-permute-start | bytes 393224 | tf_op jit(solution)/shard_map/ppermute | solution.py:178
  22.3 14.9 %collective-permute-start.6 = (f32[4,64,256]{2,1,0:T(8,128)S(1)}, f32[4,64,256]{2,1,0:T(8,128)S(1)}, u32[]{:S(2)}, u32[]{:S(2)}) collective-permute-start(f32[4,64,256]{2,1,0:T(8,128)S(1)} %pad_maximum_fusion), channel_id=1, source_target_pairs={{0,1},{1,2},{2,3},{4,5},{5,6},{6,7},{8,9},{9,10},{10,11},{12,13},{... | collective-permute-start | bytes 786440 | tf_op jit(solution)/shard_map/ppermute | solution.py:18
  28.0 2.1 %copy-start.3 = (s32[8,16]{1,0:T(8,128)S(1)}, s32[8,16]{1,0:T(8,128)}, u32[]{:S(2)}) copy-start(s32[8,16]{1,0:T(8,128)} %allowed_ref.9) | copy-start | bytes 1540
  28.0 9.2 %collective-permute-start.7 = (f32[4,64,256]{2,1,0:T(8,128)S(1)}, f32[4,64,256]{2,1,0:T(8,128)S(1)}, u32[]{:S(2)}, u32[]{:S(2)}) collective-permute-start(f32[4,64,256]{2,1,0:T(8,128)S(1)} %pad_maximum_fusion.1), channel_id=1, source_target_pairs={{1,0},{2,1},{3,2},{5,4},{6,5},{7,6},{9,8},{10,9},{11,10},{13,12},{... | collective-permute-start | bytes 786440 | tf_op jit(solution)/shard_map/ppermute | solution.py:18
  30.2 1.7 %copy-start = (s32[8]{0:T(128)S(1)}, s32[8]{0:T(128)}, u32[]{:S(2)}) copy-start(s32[8]{0:T(128)} %shifts_ref.9) | copy-start | bytes 100
  33.0 13.0 %collective-permute-start.11 = (f32[2,64,256]{2,1,0:T(8,128)S(1)}, f32[2,64,256]{2,1,0:T(8,128)S(1)}, u32[]{:S(2)}, u32[]{:S(2)}) collective-permute-start(f32[2,64,256]{2,1,0:T(8,128)S(1)} %first_inner.1), channel_id=1, source_target_pairs={{0,4},{4,12},{12,8},{8,0},{1,5},{5,13},{13,9},{9,1},{2,6},{6,14},{... | collective-permute-start | bytes 393224 | tf_op jit(solution)/shard_map/ppermute | solution.py:223
  39.7 9.3 %collective-permute-start.8 = (f32[2,64,256]{2,1,0:T(8,128)S(1)}, f32[2,64,256]{2,1,0:T(8,128)S(1)}, u32[]{:S(2)}, u32[]{:S(2)}) collective-permute-start(f32[2,64,256]{2,1,0:T(8,128)S(1)} %first_outer.1), channel_id=1, source_target_pairs={{0,4},{4,12},{12,8},{8,0},{1,5},{5,13},{13,9},{9,1},{2,6},{6,14},{... | collective-permute-start | bytes 393224 | tf_op jit(solution)/shard_map/ppermute | solution.py:224
  46.0 6.5 %collective-permute-start.12 = (f32[2,64,256]{2,1,0:T(8,128)S(1)}, f32[2,64,256]{2,1,0:T(8,128)S(1)}, u32[]{:S(2)}, u32[]{:S(2)}) collective-permute-start(f32[2,64,256]{2,1,0:T(8,128)S(1)} %add.34), channel_id=1, source_target_pairs={{0,4},{4,12},{12,8},{8,0},{1,5},{5,13},{13,9},{9,1},{2,6},{6,14},{... | collective-permute-start | bytes 393224 | tf_op jit(solution)/shard_map/ppermute | solution.py:223
  49.0 5.7 %collective-permute-start.9 = (f32[2,64,256]{2,1,0:T(8,128)S(1)}, f32[2,64,256]{2,1,0:T(8,128)S(1)}, u32[]{:S(2)}, u32[]{:S(2)}) collective-permute-start(f32[2,64,256]{2,1,0:T(8,128)S(1)} %add.31), channel_id=1, source_target_pairs={{0,4},{4,12},{12,8},{8,0},{1,5},{5,13},{13,9},{9,1},{2,6},{6,14},{... | collective-permute-start | bytes 393224 | tf_op jit(solution)/shard_map/ppermute | solution.py:224
  52.5 5.7 %collective-permute-start.13 = (f32[2,64,256]{2,1,0:T(8,128)S(1)}, f32[2,64,256]{2,1,0:T(8,128)S(1)}, u32[]{:S(2)}, u32[]{:S(2)}) collective-permute-start(f32[2,64,256]{2,1,0:T(8,128)S(1)} %add.35), channel_id=1, source_target_pairs={{0,4},{4,12},{12,8},{8,0},{1,5},{5,13},{13,9},{9,1},{2,6},{6,14},{... | collective-permute-start | bytes 393224 | tf_op jit(solution)/shard_map/ppermute | solution.py:223
  54.7 5.4 %collective-permute-start.10 = (f32[2,64,256]{2,1,0:T(8,128)S(1)}, f32[2,64,256]{2,1,0:T(8,128)S(1)}, u32[]{:S(2)}, u32[]{:S(2)}) collective-permute-start(f32[2,64,256]{2,1,0:T(8,128)S(1)} %add.32), channel_id=1, source_target_pairs={{0,4},{4,12},{12,8},{8,0},{1,5},{5,13},{13,9},{9,1},{2,6},{6,14},{... | collective-permute-start | bytes 393224 | tf_op jit(solution)/shard_map/ppermute | solution.py:224

commit v6 on v3

--- a/solution.py
+++ b/solution.py
@@ -84,8 +84,8 @@
     return left_parts[ring_place(n, step + 1)].reshape(-1, left_parts.shape[-1])
 
 
-def own_sectors(n, allowed_ref, *refs):
-    (outer, left_parts), (inner, high, low, psi) = refs[n : n + 2], refs[n + 2 :]
+def own_sectors(n, allowed_ref, outer, *refs):
+    left_parts, inner, high, low, psi = refs[n:]
     assemble(n, *refs[:n], inner, psi)
     left = chunk_left(n, 0, left_parts)
     nloc = high.shape[0]
@@ -194,7 +194,7 @@
     chunk_inner = jax.ShapeDtypeStruct((nloc - 2, rows, width), F32)
     parts_inner, *own = call(
         functools.partial(own_sectors, n), "own", 4 * kops * one, [split_parts(nloc - 2), *products(nloc)],
-        [SMEM] + [VMEM] * (n + 2), [allowed, *inner, parts_outer, left_parts], whole(nloc - 2),
+        [SMEM] + [VMEM] * (n + 2), [allowed, parts_outer, *inner, left_parts], whole(nloc - 2),
     )
     result_inner = call(
         functools.partial(first_inner, nloc), "first_inner", nloc * kops * one // n, chunk_inner,

time: 58.3 us -> 56.9 us (0.976)
  waiting for transfers between devices: 16.3 us -> 10.3 us
  starting transfers between devices: 20.2 us -> 24.9 us
    ppermute x3, waiting for transfers between devices: 8.07 us -> 3.98 us  [shards(): lax.ppermute(outer[-1] + zero[0, 0] if step == 1 else outer[-1], 'op', ro...]
    ppermute x3, starting transfers between devices: 2.4 us -> 5.85 us  [shards(): lax.ppermute(inner[-1] + zero[0, 0] if step == 1 else inner[-1], 'op', ro...]
    ppermute x3, waiting for transfers between devices: 3.62 us -> 2.19 us  [shards(): lax.ppermute(inner[-1] + zero[0, 0] if step == 1 else inner[-1], 'op', ro...]
    ppermute x3, starting transfers between devices: 0.3 us -> 0.95 us  [shards(): result_outer = lax.ppermute(result_outer, 'op', route) + next_outer]
where the time goes in v6:
time: 56.9 us; the launch traced here: 56.6 us
  starting transfers between devices  24.9 us (44%)
  Pallas kernels  16 us (28%)
  waiting for transfers between devices  10.3 us (18%)
  local copies, waits for them, and re-layouts  4.23 us (7%)
  other arithmetic  0.96 us (2%)
    pallas_call x9, Pallas kernels, call(): pl.pallas_call(body, name=name, out_shape=out_shape, in_specs=in_specs, o...  16 us
    ppermute x2, starting transfers between devices, shifted(): return lax.ppermute(block, axis, route)  8.4 us
    ppermute x3, starting transfers between devices, shards(): result_inner = lax.ppermute(result_inner, 'op', route) + next_inner  6.46 us
    ppermute x3, starting transfers between devices, shards(): lax.ppermute(inner[-1] + zero[0, 0] if step == 1 else inner[-1], 'op', ro...  5.85 us
    ppermute x3, waiting for transfers between devices, shards(): lax.ppermute(outer[-1] + zero[0, 0] if step == 1 else outer[-1], 'op', ro...  3.98 us
    ppermute x3, starting transfers between devices, shards(): lax.ppermute(outer[-1] + zero[0, 0] if step == 1 else outer[-1], 'op', ro...  3.24 us
    unnamed x8, local copies, waits for them, and re-layouts  3.19 us
    ppermute x2, waiting for transfers between devices, shifted(): return lax.ppermute(block, axis, route)  2.36 us
  transfers between devices with their start and end apart: 14, of which 7 were waited for; matrix products, arithmetic and copies ran while one was open for 0% of the time, Pallas kernels for 28%

profile of v6, /device:TPU:1, one launch (start us, length us, event | category | flops | bytes accessed | tf_op | source)
XLA Modules:
  0.0 56.6 jit_solution(12472956686731420865)
XLA Ops:
  0.0 1.0 %fusion = (f32[2,64,256]{2,1,0:T(8,128)S(1)}, f32[2,64,256]{2,1,0:T(8,128)S(1)}) fusion(f32[4,64,256]{2,1,0:T(8,128)} %param.5), kind=kLoop, calls=%fused_computation.5 | loop fusion | bytes 524288 | tf_op jit(solution)/shard_map/slice | solution.py:175
  1.0 2.2 %collective-permute-start.3 = (f32[2,64,256]{2,1,0:T(8,128)S(1)}, f32[2,64,256]{2,1,0:T(8,128)S(1)}, u32[]{:S(2)}, u32[]{:S(2)}) collective-permute-start(f32[2,64,256]{2,1,0:T(8,128)S(1)} %get-tuple-element.37.refs_0_), channel_id=1, source_target_pairs={{0,4},{4,12},{12,8},{8,0},{1,5},{5,13},{13,9},{9,1},{2,6},{6,14},{... | collective-permute-start | bytes 393224 | tf_op jit(solution)/shard_map/ppermute | solution.py:177
  3.2 2.3 %collective-permute-start = (f32[2,64,256]{2,1,0:T(8,128)S(1)}, f32[2,64,256]{2,1,0:T(8,128)S(1)}, u32[]{:S(2)}, u32[]{:S(2)}) collective-permute-start(f32[2,64,256]{2,1,0:T(8,128)S(1)} %get-tuple-element.38.refs_0_), channel_id=1, source_target_pairs={{0,4},{4,12},{12,8},{8,0},{1,5},{5,13},{13,9},{9,1},{2,6},{6,14},{... | collective-permute-start | bytes 393224 | tf_op jit(solution)/shard_map/ppermute | solution.py:178
  5.5 0.0 copy-start.1
  5.5 1.6 %copy-done.1 = f32[8,256,256]{2,1,0:T(8,128)S(1)} copy-done((f32[8,256,256]{2,1,0:T(8,128)S(1)}, f32[8,256,256]{2,1,0:T(8,128)}, u32[]{:S(2)}) %copy-start.1) | copy-done | bytes 2097176
  7.1 0.0 copy-start.2
  7.1 1.6 %copy-done.2 = f32[8,256,256]{2,1,0:T(8,128)S(1)} copy-done((f32[8,256,256]{2,1,0:T(8,128)S(1)}, f32[8,256,256]{2,1,0:T(8,128)}, u32[]{:S(2)}) %copy-start.2) | copy-done | bytes 2097176
  8.7 1.1 %prepare.1 = (bf16[4,8,64,768]{3,2,1,0:T(8,128)(2,1)S(1)}, bf16[2048,256]{1,0:T(8,128)(2,1)S(1)}, bf16[2048,256]{1,0:T(8,128)(2,1)S(1)}, f32[1,128]{1,0:T(1,128)S(1)}) custom-call(f32[8,256,256]{2,1,0:T(8,128)S(1)} %copy-done.1, f32[8,256,256]{2,1,0:T(8,128)S(1)} %copy-done.2), custom_call_target="tpu_custom_call" | custom-call | flops 3221225472 | bytes 1048576 | tf_op jit(solution)/shard_map/prepare/pallas_call | solution.py:149
  9.8 0.5 collective-permute-done.refs_1_
  10.3 0.4 collective-permute-start.1
  10.6 0.0 collective-permute-done.3.refs_1_
  10.7 3.1 %collective-permute-start.4 = (f32[2,64,256]{2,1,0:T(8,128)S(1)}, f32[2,64,256]{2,1,0:T(8,128)S(1)}, u32[]{:S(2)}, u32[]{:S(2)}) collective-permute-start(f32[2,64,256]{2,1,0:T(8,128)S(1)} %broadcast_add_fusion), channel_id=1, source_target_pairs={{0,4},{4,12},{12,8},{8,0},{1,5},{5,13},{13,9},{9,1},{2,6},{6,14},{... | collective-permute-start | bytes 393224 | tf_op jit(solution)/shard_map/ppermute | solution.py:177
  13.8 1.3 %collective-permute-done.1.refs_2_ = f32[2,64,256]{2,1,0:T(8,128)S(1)} collective-permute-done((f32[2,64,256]{2,1,0:T(8,128)S(1)}, f32[2,64,256]{2,1,0:T(8,128)S(1)}, u32[]{:S(2)}, u32[]{:S(2)}) %collective-permute-start.1) | collective-permute-done | bytes 131104 | tf_op jit(solution)/shard_map/ppermute | solution.py:178
  15.0 0.6 %collective-permute-start.2 = (f32[2,64,256]{2,1,0:T(8,128)S(1)}, f32[2,64,256]{2,1,0:T(8,128)S(1)}, u32[]{:S(2)}, u32[]{:S(2)}) collective-permute-start(f32[2,64,256]{2,1,0:T(8,128)S(1)} %collective-permute-done.1.refs_2_), channel_id=1, source_target_pairs={{0,4},{4,12},{12,8},{8,0},{1,5},{5,13},{13,9},{9,1},{2,6},{6,14},{... | collective-permute-start | bytes 393224 | tf_op jit(solution)/shard_map/ppermute | solution.py:178
  15.6 2.2 %collective-permute-done.4.refs_2_ = f32[2,64,256]{2,1,0:T(8,128)S(1)} collective-permute-done((f32[2,64,256]{2,1,0:T(8,128)S(1)}, f32[2,64,256]{2,1,0:T(8,128)S(1)}, u32[]{:S(2)}, u32[]{:S(2)}) %collective-permute-start.4) | collective-permute-done | bytes 131104 | tf_op jit(solution)/shard_map/ppermute | solution.py:177
  17.8 0.6 %collective-permute-start.5 = (f32[2,64,256]{2,1,0:T(8,128)S(1)}, f32[2,64,256]{2,1,0:T(8,128)S(1)}, u32[]{:S(2)}, u32[]{:S(2)}) collective-permute-start(f32[2,64,256]{2,1,0:T(8,128)S(1)} %collective-permute-done.4.refs_2_), channel_id=1, source_target_pairs={{0,4},{4,12},{12,8},{8,0},{1,5},{5,13},{13,9},{9,1},{2,6},{6,14},{... | collective-permute-start | bytes 393224 | tf_op jit(solution)/shard_map/ppermute | solution.py:177
  18.4 2.3 %collective-permute-done.2.refs_3_ = f32[2,64,256]{2,1,0:T(8,128)S(1)} collective-permute-done((f32[2,64,256]{2,1,0:T(8,128)S(1)}, f32[2,64,256]{2,1,0:T(8,128)S(1)}, u32[]{:S(2)}, u32[]{:S(2)}) %collective-permute-start.2) | collective-permute-done | bytes 131104 | tf_op jit(solution)/shard_map/ppermute | solution.py:178
  20.7 6.5 %collective-permute-start.6 = (f32[4,64,256]{2,1,0:T(8,128)S(1)}, f32[4,64,256]{2,1,0:T(8,128)S(1)}, u32[]{:S(2)}, u32[]{:S(2)}) collective-permute-start(f32[4,64,256]{2,1,0:T(8,128)S(1)} %pad_maximum_fusion), channel_id=1, source_target_pairs={{0,1},{1,2},{2,3},{4,5},{5,6},{6,7},{8,9},{9,10},{10,11},{12,13},{... | collective-permute-start | bytes 786440 | tf_op jit(solution)/shard_map/ppermute | solution.py:18
  27.2 0.0 copy-start.3
  27.2 1.9 %collective-permute-start.7 = (f32[4,64,256]{2,1,0:T(8,128)S(1)}, f32[4,64,256]{2,1,0:T(8,128)S(1)}, u32[]{:S(2)}, u32[]{:S(2)}) collective-permute-start(f32[4,64,256]{2,1,0:T(8,128)S(1)} %pad_maximum_fusion.1), channel_id=1, source_target_pairs={{1,0},{2,1},{3,2},{5,4},{6,5},{7,6},{9,8},{10,9},{11,10},{13,12},{... | collective-permute-start | bytes 786440 | tf_op jit(solution)/shard_map/ppermute | solution.py:18
  29.2 0.2 assemble.1.outer
  29.4 0.0 collective-permute-done.5.refs_3_
  29.4 0.0 copy-done.3
  29.4 0.0 copy-start
  29.4 1.7 %own.1 = (bf16[2,768,256]{2,1,0:T(8,128)(2,1)S(1)}, bf16[4,512,256]{2,1,0:T(8,128)(2,1)S(1)}, bf16[4,512,256]{2,1,0:T(8,128)(2,1)S(1)}) custom-call(s32[8,16]{1,0:T(8,128)S(1)} %copy-done.3, bf16[2,768,256]{2,1,0:T(8,128)(2,1)S(1)} %assemble.1.outer, f32[2,64,256]{2,1,0:T(8,128)S(1)} %get-tuple-element.37.refs_0_, ...), custom_call_target="tpu_custom_call" | custom-call | flops 3221225472 | bytes 1048576 | tf_op jit(solution)/shard_map/own/pallas_call | solution.py:149
  31.1 0.0 copy-done
  31.1 1.2 %first_inner.1 = f32[2,64,256]{2,1,0:T(8,128)S(1)} custom-call(s32[8]{0:T(128)S(1)} %copy-done, bf16[4,512,256]{2,1,0:T(8,128)(2,1)S(1)} %get-tuple-element.23.high, bf16[4,512,256]{2,1,0:T(8,128)(2,1)S(1)} %get-tuple-element.24.low, bf16[2048,256]{1,0:T(8,128)(2,1)S(1)} %get-tuple-element.27.right_hi, bf16[2048,256]{1,0:T(8,128)(2,1)S(1)} %get-tuple-element.28.right_lo), custom_call_target="tpu_custom_call" | custom-call | flops 805306368 | bytes 1048576 | tf_op jit(solution)/shard_map/first_inner/pallas_call | solution.py:149
  32.3 0.6 %collective-permute-start.11 = (f32[2,64,256]{2,1,0:T(8,128)S(1)}, f32[2,64,256]{2,1,0:T(8,128)S(1)}, u32[]{:S(2)}, u32[]{:S(2)}) collective-permute-start(f32[2,64,256]{2,1,0:T(8,128)S(1)} %first_inner.1), channel_id=1, source_target_pairs={{0,4},{4,12},{12,8},{8,0},{1,5},{5,13},{13,9},{9,1},{2,6},{6,14},{... | collective-permute-start | bytes 393224 | tf_op jit(solution)/shard_map/ppermute | solution.py:222
  32.9 0.0 collective-permute-done.6.above
  32.9 2.4 %collective-permute-done.7.below = f32[4,64,256]{2,1,0:T(8,128)S(1)} collective-permute-done((f32[4,64,256]{2,1,0:T(8,128)S(1)}, f32[4,64,256]{2,1,0:T(8,128)S(1)}, u32[]{:S(2)}, u32[]{:S(2)}) %collective-permute-start.7) | collective-permute-done | bytes 262176 | tf_op jit(solution)/shard_map/ppermute | solution.py:18
  35.2 1.3 %outside.1 = (bf16[2,768,256]{2,1,0:T(8,128)(2,1)S(1)}, bf16[2,512,256]{2,1,0:T(8,128)(2,1)S(1)}, bf16[2,512,256]{2,1,0:T(8,128)(2,1)S(1)}) custom-call(s32[8,16]{1,0:T(8,128)S(1)} %copy-done.3, f32[4,64,256]{2,1,0:T(8,128)S(1)} %collective-permute-done.6.above, f32[4,64,256]{2,1,0:T(8,128)S(1)} %collective-permute-done.7.below, ...), custom_call_target="tpu_custom_call" | custom-call | flops 1610612736 | bytes 1048576 | tf_op jit(solution)/shard_map/outside/pallas_call | solution.py:149
  36.5 1.2 %first_outer.1 = f32[2,64,256]{2,1,0:T(8,128)S(1)} custom-call(s32[8]{0:T(128)S(1)} %copy-done, bf16[4,512,256]{2,1,0:T(8,128)(2,1)S(1)} %get-tuple-element.23.high, bf16[4,512,256]{2,1,0:T(8,128)(2,1)S(1)} %get-tuple-element.24.low, bf16[2,512,256]{2,1,0:T(8,128)(2,1)S(1)} %get-tuple-element.25.end_high, ...), custom_call_target="tpu_custom_call" | custom-call | flops 805306368 | bytes 1048576 | tf_op jit(solution)/shard_map/first_outer/pallas_call | solution.py:149
  37.7 0.8 %collective-permute-start.8 = (f32[2,64,256]{2,1,0:T(8,128)S(1)}, f32[2,64,256]{2,1,0:T(8,128)S(1)}, u32[]{:S(2)}, u32[]{:S(2)}) collective-permute-start(f32[2,64,256]{2,1,0:T(8,128)S(1)} %first_outer.1), channel_id=1, source_target_pairs={{0,4},{4,12},{12,8},{8,0},{1,5},{5,13},{13,9},{9,1},{2,6},{6,14},{... | collective-permute-start | bytes 393224 | tf_op jit(solution)/shard_map/ppermute | solution.py:223
  38.5 3.1 %chunk.3 = (f32[2,64,256]{2,1,0:T(8,128)S(1)}, f32[2,64,256]{2,1,0:T(8,128)S(1)}) custom-call(s32[8]{0:T(128)S(1)} %copy-done, s32[8,16]{1,0:T(8,128)S(1)} %copy-done.3, bf16[2,768,256]{2,1,0:T(8,128)(2,1)S(1)} %assemble.1.outer, bf16[2,768,256]{2,1,0:T(8,128)(2,1)S(1)} %get-tuple-element.29.inner, bf16[2,768,256]{2,1,0:T(8,128)(2,1)S(1)} %get-tuple-element.30.outside, ...), custom_call_target="tpu_custom_call" | custom-call | flops 3221225472 | bytes 1048576 | tf_op jit(solution)/shard_map/chunk/pallas_call | solution.py:149
  41.6 0.0 collective-permute-done.11
  41.7 3.0 %collective-permute-start.12 = (f32[2,64,256]{2,1,0:T(8,128)S(1)}, f32[2,64,256]{2,1,0:T(8,128)S(1)}, u32[]{:S(2)}, u32[]{:S(2)}) collective-permute-start(f32[2,64,256]{2,1,0:T(8,128)S(1)} %add.34), channel_id=1, source_target_pairs={{0,4},{4,12},{12,8},{8,0},{1,5},{5,13},{13,9},{9,1},{2,6},{6,14},{... | collective-permute-start | bytes 393224 | tf_op jit(solution)/shard_map/ppermute | solution.py:222
  44.6 0.0 collective-permute-done.8
  44.6 0.1 collective-permute-start.9
  44.7 3.2 %chunk.4 = (f32[2,64,256]{2,1,0:T(8,128)S(1)}, f32[2,64,256]{2,1,0:T(8,128)S(1)}) custom-call(s32[8]{0:T(128)S(1)} %copy-done, s32[8,16]{1,0:T(8,128)S(1)} %copy-done.3, bf16[2,768,256]{2,1,0:T(8,128)(2,1)S(1)} %assemble.1.outer, bf16[2,768,256]{2,1,0:T(8,128)(2,1)S(1)} %get-tuple-element.29.inner, bf16[2,768,256]{2,1,0:T(8,128)(2,1)S(1)} %get-tuple-element.30.outside, ...), custom_call_target="tpu_custom_call" | custom-call | flops 3221225472 | bytes 1048576 | tf_op jit(solution)/shard_map/chunk/pallas_call | solution.py:149
  47.9 0.3 collective-permute-done.12
  48.2 2.9 %collective-permute-start.13 = (f32[2,64,256]{2,1,0:T(8,128)S(1)}, f32[2,64,256]{2,1,0:T(8,128)S(1)}, u32[]{:S(2)}, u32[]{:S(2)}) collective-permute-start(f32[2,64,256]{2,1,0:T(8,128)S(1)} %add.35), channel_id=1, source_target_pairs={{0,4},{4,12},{12,8},{8,0},{1,5},{5,13},{13,9},{9,1},{2,6},{6,14},{... | collective-permute-start | bytes 393224 | tf_op jit(solution)/shard_map/ppermute | solution.py:222
  51.1 0.0 collective-permute-done.9
  51.1 0.1 collective-permute-start.10
  51.2 3.2 %chunk.5 = (f32[2,64,256]{2,1,0:T(8,128)S(1)}, f32[2,64,256]{2,1,0:T(8,128)S(1)}) custom-call(s32[8]{0:T(128)S(1)} %copy-done, s32[8,16]{1,0:T(8,128)S(1)} %copy-done.3, bf16[2,768,256]{2,1,0:T(8,128)(2,1)S(1)} %assemble.1.outer, bf16[2,768,256]{2,1,0:T(8,128)(2,1)S(1)} %get-tuple-element.29.inner, bf16[2,768,256]{2,1,0:T(8,128)(2,1)S(1)} %get-tuple-element.30.outside, ...), custom_call_target="tpu_custom_call" | custom-call | flops 3221225472 | bytes 1048576 | tf_op jit(solution)/shard_map/chunk/pallas_call | solution.py:149
  54.4 0.0 collective-permute-done.13
  54.4 1.5 %collective-permute-done.10 = f32[2,64,256]{2,1,0:T(8,128)S(1)} collective-permute-done((f32[2,64,256]{2,1,0:T(8,128)S(1)}, f32[2,64,256]{2,1,0:T(8,128)S(1)}, u32[]{:S(2)}, u32[]{:S(2)}) %collective-permute-start.10) | collective-permute-done | bytes 131104 | tf_op jit(solution)/shard_map/ppermute | solution.py:223
  55.9 0.7 %pad_maximum_fusion.2 = f32[4,64,256]{2,1,0:T(8,128)} fusion(f32[1,64,256]{2,1,0:T(8,128)S(1)} %get-tuple-element.40, f32[2,64,256]{2,1,0:T(8,128)S(1)} %add.36, f32[1,64,256]{2,1,0:T(8,128)S(1)} %get-tuple-element.39), kind=kLoop, calls=%fused_computation.2 | loop fusion | flops 131072 | bytes 524288 | tf_op jit(solution)/shard_map/concatenate | solution.py:224
  (15 shorter events, 0.3 us)
Async XLA Ops:
  1.0 9.6 %collective-permute-start.3 = (f32[2,64,256]{2,1,0:T(8,128)S(1)}, f32[2,64,256]{2,1,0:T(8,128)S(1)}, u32[]{:S(2)}, u32[]{:S(2)}) collective-permute-start(f32[2,64,256]{2,1,0:T(8,128)S(1)} %get-tuple-element.37.refs_0_), channel_id=1, source_target_pairs={{0,4},{4,12},{12,8},{8,0},{1,5},{5,13},{13,9},{9,1},{2,6},{6,14},{... | collective-permute-start | bytes 393224 | tf_op jit(solution)/shard_map/ppermute | solution.py:177
  3.2 7.0 %collective-permute-start = (f32[2,64,256]{2,1,0:T(8,128)S(1)}, f32[2,64,256]{2,1,0:T(8,128)S(1)}, u32[]{:S(2)}, u32[]{:S(2)}) collective-permute-start(f32[2,64,256]{2,1,0:T(8,128)S(1)} %get-tuple-element.38.refs_0_), channel_id=1, source_target_pairs={{0,4},{4,12},{12,8},{8,0},{1,5},{5,13},{13,9},{9,1},{2,6},{6,14},{... | collective-permute-start | bytes 393224 | tf_op jit(solution)/shard_map/ppermute | solution.py:178
  5.5 1.6 %copy-start.1 = (f32[8,256,256]{2,1,0:T(8,128)S(1)}, f32[8,256,256]{2,1,0:T(8,128)}, u32[]{:S(2)}) copy-start(f32[8,256,256]{2,1,0:T(8,128)} %left_ref.1) | copy-start | bytes 6291460
  7.1 1.6 %copy-start.2 = (f32[8,256,256]{2,1,0:T(8,128)S(1)}, f32[8,256,256]{2,1,0:T(8,128)}, u32[]{:S(2)}) copy-start(f32[8,256,256]{2,1,0:T(8,128)} %right_ref.1) | copy-start | bytes 6291460
  10.3 4.8 %collective-permute-start.1 = (f32[2,64,256]{2,1,0:T(8,128)S(1)}, f32[2,64,256]{2,1,0:T(8,128)S(1)}, u32[]{:S(2)}, u32[]{:S(2)}) collective-permute-start(f32[2,64,256]{2,1,0:T(8,128)S(1)} %broadcast_add_fusion.1), channel_id=1, source_target_pairs={{0,4},{4,12},{12,8},{8,0},{1,5},{5,13},{13,9},{9,1},{2,6},{6,14},{... | collective-permute-start | bytes 393224 | tf_op jit(solution)/shard_map/ppermute | solution.py:178
  10.7 7.1 %collective-permute-start.4 = (f32[2,64,256]{2,1,0:T(8,128)S(1)}, f32[2,64,256]{2,1,0:T(8,128)S(1)}, u32[]{:S(2)}, u32[]{:S(2)}) collective-permute-start(f32[2,64,256]{2,1,0:T(8,128)S(1)} %broadcast_add_fusion), channel_id=1, source_target_pairs={{0,4},{4,12},{12,8},{8,0},{1,5},{5,13},{13,9},{9,1},{2,6},{6,14},{... | collective-permute-start | bytes 393224 | tf_op jit(solution)/shard_map/ppermute | solution.py:177
  15.0 5.6 %collective-permute-start.2 = (f32[2,64,256]{2,1,0:T(8,128)S(1)}, f32[2,64,256]{2,1,0:T(8,128)S(1)}, u32[]{:S(2)}, u32[]{:S(2)}) collective-permute-start(f32[2,64,256]{2,1,0:T(8,128)S(1)} %collective-permute-done.1.refs_2_), channel_id=1, source_target_pairs={{0,4},{4,12},{12,8},{8,0},{1,5},{5,13},{13,9},{9,1},{2,6},{6,14},{... | collective-permute-start | bytes 393224 | tf_op jit(solution)/shard_map/ppermute | solution.py:178
  17.8 11.6 %collective-permute-start.5 = (f32[2,64,256]{2,1,0:T(8,128)S(1)}, f32[2,64,256]{2,1,0:T(8,128)S(1)}, u32[]{:S(2)}, u32[]{:S(2)}) collective-permute-start(f32[2,64,256]{2,1,0:T(8,128)S(1)} %collective-permute-done.4.refs_2_), channel_id=1, source_target_pairs={{0,4},{4,12},{12,8},{8,0},{1,5},{5,13},{13,9},{9,1},{2,6},{6,14},{... | collective-permute-start | bytes 393224 | tf_op jit(solution)/shard_map/ppermute | solution.py:177
  20.7 12.2 %collective-permute-start.6 = (f32[4,64,256]{2,1,0:T(8,128)S(1)}, f32[4,64,256]{2,1,0:T(8,128)S(1)}, u32[]{:S(2)}, u32[]{:S(2)}) collective-permute-start(f32[4,64,256]{2,1,0:T(8,128)S(1)} %pad_maximum_fusion), channel_id=1, source_target_pairs={{0,1},{1,2},{2,3},{4,5},{5,6},{6,7},{8,9},{9,10},{10,11},{12,13},{... | collective-permute-start | bytes 786440 | tf_op jit(solution)/shard_map/ppermute | solution.py:18
  27.2 2.1 %copy-start.3 = (s32[8,16]{1,0:T(8,128)S(1)}, s32[8,16]{1,0:T(8,128)}, u32[]{:S(2)}) copy-start(s32[8,16]{1,0:T(8,128)} %allowed_ref.9) | copy-start | bytes 1540
  27.2 8.0 %collective-permute-start.7 = (f32[4,64,256]{2,1,0:T(8,128)S(1)}, f32[4,64,256]{2,1,0:T(8,128)S(1)}, u32[]{:S(2)}, u32[]{:S(2)}) collective-permute-start(f32[4,64,256]{2,1,0:T(8,128)S(1)} %pad_maximum_fusion.1), channel_id=1, source_target_pairs={{1,0},{2,1},{3,2},{5,4},{6,5},{7,6},{9,8},{10,9},{11,10},{13,12},{... | collective-permute-start | bytes 786440 | tf_op jit(solution)/shard_map/ppermute | solution.py:18
  29.4 1.7 %copy-start = (s32[8]{0:T(128)S(1)}, s32[8]{0:T(128)}, u32[]{:S(2)}) copy-start(s32[8]{0:T(128)} %shifts_ref.9) | copy-start | bytes 100
  32.3 9.4 %collective-permute-start.11 = (f32[2,64,256]{2,1,0:T(8,128)S(1)}, f32[2,64,256]{2,1,0:T(8,128)S(1)}, u32[]{:S(2)}, u32[]{:S(2)}) collective-permute-start(f32[2,64,256]{2,1,0:T(8,128)S(1)} %first_inner.1), channel_id=1, source_target_pairs={{0,4},{4,12},{12,8},{8,0},{1,5},{5,13},{13,9},{9,1},{2,6},{6,14},{... | collective-permute-start | bytes 393224 | tf_op jit(solution)/shard_map/ppermute | solution.py:222
  37.7 6.9 %collective-permute-start.8 = (f32[2,64,256]{2,1,0:T(8,128)S(1)}, f32[2,64,256]{2,1,0:T(8,128)S(1)}, u32[]{:S(2)}, u32[]{:S(2)}) collective-permute-start(f32[2,64,256]{2,1,0:T(8,128)S(1)} %first_outer.1), channel_id=1, source_target_pairs={{0,4},{4,12},{12,8},{8,0},{1,5},{5,13},{13,9},{9,1},{2,6},{6,14},{... | collective-permute-start | bytes 393224 | tf_op jit(solution)/shard_map/ppermute | solution.py:223
  41.7 6.5 %collective-permute-start.12 = (f32[2,64,256]{2,1,0:T(8,128)S(1)}, f32[2,64,256]{2,1,0:T(8,128)S(1)}, u32[]{:S(2)}, u32[]{:S(2)}) collective-permute-start(f32[2,64,256]{2,1,0:T(8,128)S(1)} %add.34), channel_id=1, source_target_pairs={{0,4},{4,12},{12,8},{8,0},{1,5},{5,13},{13,9},{9,1},{2,6},{6,14},{... | collective-permute-start | bytes 393224 | tf_op jit(solution)/shard_map/ppermute | solution.py:222
  44.6 6.5 %collective-permute-start.9 = (f32[2,64,256]{2,1,0:T(8,128)S(1)}, f32[2,64,256]{2,1,0:T(8,128)S(1)}, u32[]{:S(2)}, u32[]{:S(2)}) collective-permute-start(f32[2,64,256]{2,1,0:T(8,128)S(1)} %add.31), channel_id=1, source_target_pairs={{0,4},{4,12},{12,8},{8,0},{1,5},{5,13},{13,9},{9,1},{2,6},{6,14},{... | collective-permute-start | bytes 393224 | tf_op jit(solution)/shard_map/ppermute | solution.py:223
  48.2 6.2 %collective-permute-start.13 = (f32[2,64,256]{2,1,0:T(8,128)S(1)}, f32[2,64,256]{2,1,0:T(8,128)S(1)}, u32[]{:S(2)}, u32[]{:S(2)}) collective-permute-start(f32[2,64,256]{2,1,0:T(8,128)S(1)} %add.35), channel_id=1, source_target_pairs={{0,4},{4,12},{12,8},{8,0},{1,5},{5,13},{13,9},{9,1},{2,6},{6,14},{... | collective-permute-start | bytes 393224 | tf_op jit(solution)/shard_map/ppermute | solution.py:222
  51.1 4.8 %collective-permute-start.10 = (f32[2,64,256]{2,1,0:T(8,128)S(1)}, f32[2,64,256]{2,1,0:T(8,128)S(1)}, u32[]{:S(2)}, u32[]{:S(2)}) collective-permute-start(f32[2,64,256]{2,1,0:T(8,128)S(1)} %add.32), channel_id=1, source_target_pairs={{0,4},{4,12},{12,8},{8,0},{1,5},{5,13},{13,9},{9,1},{2,6},{6,14},{... | collective-permute-start | bytes 393224 | tf_op jit(solution)/shard_map/ppermute | solution.py:223

commit v7 on v4

--- a/solution.py
+++ b/solution.py
@@ -35,7 +35,7 @@
     return hi, (x - hi.astype(F32)).astype(BF16)
 
 
-def prepare(left_ref, right_ref, left_parts, right_hi, right_lo, zero):
+def prepare(left_ref, right_ref, left_parts, right_parts, zero):
     n, kops, rows, _ = left_parts.shape
     width = left_ref.shape[1]
     zero[...] = jnp.zeros_like(zero)
@@ -44,7 +44,8 @@
         parts = jnp.concatenate([hi, hi, lo], axis=1)
         for c in range(n):
             left_parts[c, k] = parts[c * rows : (c + 1) * rows]
-        right_hi[k * width : (k + 1) * width, :], right_lo[k * width : (k + 1) * width, :] = split(right_ref[k].T)
+        hi, lo = split(right_ref[k].T)
+        right_parts[k] = jnp.concatenate([hi, hi, lo], axis=0)
 
 
 def stacked(block):
@@ -100,45 +101,43 @@
         first_product(left, outside[i], allowed_ref, first - 1 + i * (nloc + 1), high.at[i], low.at[i])
 
 
-def second_product(targets, shifts_ref, high, low, right_hi, right_lo, rows):
-    kops, width = shifts_ref.shape[0], right_hi.shape[1]
-
-    def left(parts):
-        columns = []
-        for k in range(kops):
-            shift, at = shifts_ref[k], slice(k * rows, (k + 1) * rows)
+def second_product(targets, shifts_ref, high, low, right_parts, rows):
+    total = None
+    for k in range(shifts_ref.shape[0]):
+        shift, at = shifts_ref[k], slice(k * rows, (k + 1) * rows)
+
+        def left(parts):
             blocks = []
             for t in targets:
                 below, same, above = [parts[t + d][at] for d in range(3)]
                 blocks.append(jnp.where(shift == 0, same, jnp.where(shift == 1, below, above)))
-            columns.append(jnp.concatenate(blocks))
-        return jnp.concatenate(columns, axis=1)
-
-    hi, lo = left(high), left(low)
-    main = jnp.dot(jnp.concatenate([hi, lo]), right_hi[...], preferred_element_type=F32)
-    total = main[: hi.shape[0]] + (main[hi.shape[0] :] + jnp.dot(hi, right_lo[...], preferred_element_type=F32))
-    return total.reshape(len(targets), rows, width)
-
-
-def first_inner(nloc, shifts_ref, high, low, right_hi, right_lo, out):
+            return jnp.concatenate(blocks)
+
+        hi, lo = left(high), left(low)
+        part = jnp.dot(jnp.concatenate([hi, lo, hi], axis=1), right_parts[k], preferred_element_type=F32)
+        total = part if total is None else total + part
+    return total.reshape(len(targets), rows, -1)
+
+
+def first_inner(nloc, shifts_ref, high, low, right_parts, out):
     own = [[None, *[ref.at[i] for i in range(nloc)], None] for ref in (high, low)]
-    out[...] = second_product(range(1, nloc - 1), shifts_ref, *own, right_hi, right_lo, out.shape[1])
-
-
-def first_outer(nloc, shifts_ref, high, low, end_high, end_low, right_hi, right_lo, out):
+    out[...] = second_product(range(1, nloc - 1), shifts_ref, *own, right_parts, out.shape[1])
+
+
+def first_outer(nloc, shifts_ref, high, low, end_high, end_low, right_parts, out):
     pairs = ((high, end_high), (low, end_low))
     held = [[ends.at[0], *[ref.at[i] for i in range(nloc)], ends.at[1]] for ref, ends in pairs]
-    out[...] = second_product((0, nloc - 1), shifts_ref, *held, right_hi, right_lo, out.shape[1])
-
-
-def later_chunk(n, nloc, step, shifts_ref, allowed_ref, outer, inner, outside, left_parts, right_hi, right_lo, outer_out, inner_out, high, low):
+    out[...] = second_product((0, nloc - 1), shifts_ref, *held, right_parts, out.shape[1])
+
+
+def later_chunk(n, nloc, step, shifts_ref, allowed_ref, outer, inner, outside, left_parts, right_parts, outer_out, inner_out, high, low):
     left = chunk_left(n, step, left_parts)
     first = lax.axis_index(("sec", "sub")) * nloc
     sources = [outside.at[0], outer.at[0], *[inner.at[i] for i in range(nloc - 2)], outer.at[1], outside.at[1]]
     for i, ref in enumerate(sources):
         first_product(left, ref[...], allowed_ref, first - 1 + i, high.at[i], low.at[i])
     held = [[ref.at[i] for i in range(nloc + 2)] for ref in (high, low)]
-    total = second_product((0, nloc - 1, *range(1, nloc - 1)), shifts_ref, *held, right_hi, right_lo, outer_out.shape[1])
+    total = second_product((0, nloc - 1, *range(1, nloc - 1)), shifts_ref, *held, right_parts, outer_out.shape[1])
     outer_out[...] = total[:2]
     inner_out[...] = total[2:]
 
@@ -163,11 +162,11 @@
     route = ring_route(n)
     one = 6 * width**3
 
-    tall = jax.ShapeDtypeStruct((kops * width, width), BF16)
+    tall = jax.ShapeDtypeStruct((kops, 3 * width, width), BF16)
     parts = jax.ShapeDtypeStruct((n, kops, rows, 3 * width), BF16)
     zero = jax.ShapeDtypeStruct((1, 128), F32)
-    left_parts, right_hi, right_lo, zero = call(
-        prepare, "prepare", 4 * kops * one, [parts, tall, tall, zero], [VMEM] * 2, [left_ops, right_ops]
+    left_parts, right_parts, zero = call(
+        prepare, "prepare", 4 * kops * one, [parts, tall, zero], [VMEM] * 2, [left_ops, right_ops]
     )
 
     outer, inner = [psi[:: nloc - 1]], [psi[1 : nloc - 1]]
@@ -196,7 +195,7 @@
     )
     result_inner = call(
         functools.partial(first_inner, nloc), "first_inner", nloc * kops * one // n, chunk_inner,
-        [SMEM] + [VMEM] * 4, [shifts, *own, right_hi, right_lo],
+        [SMEM] + [VMEM] * 3, [shifts, *own, right_parts],
     )
     parts_outside, *ends = call(
         functools.partial(outside_sectors, n, nloc), "outside", 2 * kops * one, [split_parts(2), *products(2)],
@@ -204,14 +203,14 @@
     )
     result_outer = call(
         functools.partial(first_outer, nloc), "first_outer", nloc * kops * one // n, chunk,
-        [SMEM] + [VMEM] * 6, [shifts, *own, *ends, right_hi, right_lo],
+        [SMEM] + [VMEM] * 5, [shifts, *own, *ends, right_parts],
     )
 
     def mine(step):
         return call(
             functools.partial(later_chunk, n, nloc, step), "chunk", 4 * nloc * kops * one // n, [chunk, chunk_inner],
-            [SMEM] * 2 + [VMEM] * 6,
-            [shifts, allowed, parts_outer, parts_inner, parts_outside, left_parts, right_hi, right_lo],
+            [SMEM] * 2 + [VMEM] * 5,
+            [shifts, allowed, parts_outer, parts_inner, parts_outside, left_parts, right_parts],
             [pltpu.VMEM((nloc + 2, kops * rows, width), BF16)] * 2,
         )
 

time: 59 us -> 59.1 us (level)
  no operation moved by 1% of the time
where the time goes in v7:
time: 59.1 us; the launch traced here: 58.9 us
  starting transfers between devices  23.5 us (40%)
  Pallas kernels  20 us (34%)
  waiting for transfers between devices  9.93 us (17%)
  local copies, waits for them, and re-layouts  4.23 us (7%)
  other arithmetic  0.97 us (2%)
    pallas_call x9, Pallas kernels, call(): pl.pallas_call(body, name=name, out_shape=out_shape, in_specs=in_specs, o...  20 us
    ppermute x2, starting transfers between devices, shifted(): return lax.ppermute(block, axis, route)  8.4 us
    ppermute x3, starting transfers between devices, shards(): lax.ppermute(inner[-1] + zero[0, 0] if step == 1 else inner[-1], 'op', ro...  5.85 us
    ppermute x3, starting transfers between devices, shards(): result_inner = lax.ppermute(result_inner, 'op', route) + next_inner  4.32 us
    ppermute x3, waiting for transfers between devices, shards(): lax.ppermute(outer[-1] + zero[0, 0] if step == 1 else outer[-1], 'op', ro...  3.97 us
    ppermute x3, starting transfers between devices, shards(): lax.ppermute(outer[-1] + zero[0, 0] if step == 1 else outer[-1], 'op', ro...  3.24 us
    unnamed x8, local copies, waits for them, and re-layouts  3.19 us
    ppermute x2, waiting for transfers between devices, shifted(): return lax.ppermute(block, axis, route)  2.4 us
  transfers between devices with their start and end apart: 14, of which 7 were waited for; matrix products, arithmetic and copies ran while one was open for 0% of the time, Pallas kernels for 34%

profile of v7, /device:TPU:1, one launch (start us, length us, event | category | flops | bytes accessed | tf_op | source)
XLA Modules:
  0.0 58.9 jit_solution(13338048108079387448)
XLA Ops:
  0.0 1.0 %fusion = (f32[2,64,256]{2,1,0:T(8,128)S(1)}, f32[2,64,256]{2,1,0:T(8,128)S(1)}) fusion(f32[4,64,256]{2,1,0:T(8,128)} %param.5), kind=kLoop, calls=%fused_computation.5 | loop fusion | bytes 524288 | tf_op jit(solution)/shard_map/slice | solution.py:172
  1.0 2.2 %collective-permute-start.3 = (f32[2,64,256]{2,1,0:T(8,128)S(1)}, f32[2,64,256]{2,1,0:T(8,128)S(1)}, u32[]{:S(2)}, u32[]{:S(2)}) collective-permute-start(f32[2,64,256]{2,1,0:T(8,128)S(1)} %get-tuple-element.35.refs_0_), channel_id=1, source_target_pairs={{0,4},{4,12},{12,8},{8,0},{1,5},{5,13},{13,9},{9,1},{2,6},{6,14},{... | collective-permute-start | bytes 393224 | tf_op jit(solution)/shard_map/ppermute | solution.py:174
  3.2 2.3 %collective-permute-start = (f32[2,64,256]{2,1,0:T(8,128)S(1)}, f32[2,64,256]{2,1,0:T(8,128)S(1)}, u32[]{:S(2)}, u32[]{:S(2)}) collective-permute-start(f32[2,64,256]{2,1,0:T(8,128)S(1)} %get-tuple-element.36.refs_0_), channel_id=1, source_target_pairs={{0,4},{4,12},{12,8},{8,0},{1,5},{5,13},{13,9},{9,1},{2,6},{6,14},{... | collective-permute-start | bytes 393224 | tf_op jit(solution)/shard_map/ppermute | solution.py:175
  5.5 0.0 copy-start.1
  5.5 1.6 %copy-done.1 = f32[8,256,256]{2,1,0:T(8,128)S(1)} copy-done((f32[8,256,256]{2,1,0:T(8,128)S(1)}, f32[8,256,256]{2,1,0:T(8,128)}, u32[]{:S(2)}) %copy-start.1) | copy-done | bytes 2097176
  7.1 0.0 copy-start.2
  7.1 1.6 %copy-done.2 = f32[8,256,256]{2,1,0:T(8,128)S(1)} copy-done((f32[8,256,256]{2,1,0:T(8,128)S(1)}, f32[8,256,256]{2,1,0:T(8,128)}, u32[]{:S(2)}) %copy-start.2) | copy-done | bytes 2097176
  8.7 1.1 %prepare.1 = (bf16[4,8,64,768]{3,2,1,0:T(8,128)(2,1)S(1)}, bf16[8,768,256]{2,1,0:T(8,128)(2,1)S(1)}, f32[1,128]{1,0:T(1,128)S(1)}) custom-call(f32[8,256,256]{2,1,0:T(8,128)S(1)} %copy-done.1, f32[8,256,256]{2,1,0:T(8,128)S(1)} %copy-done.2), custom_call_target="tpu_custom_call" | custom-call | flops 3221225472 | bytes 1048576 | tf_op jit(solution)/shard_map/prepare/pallas_call | solution.py:146
  9.8 0.5 collective-permute-done.refs_1_
  10.3 0.4 collective-permute-start.1
  10.6 0.0 collective-permute-done.3.refs_1_
  10.7 3.1 %collective-permute-start.4 = (f32[2,64,256]{2,1,0:T(8,128)S(1)}, f32[2,64,256]{2,1,0:T(8,128)S(1)}, u32[]{:S(2)}, u32[]{:S(2)}) collective-permute-start(f32[2,64,256]{2,1,0:T(8,128)S(1)} %broadcast_add_fusion), channel_id=1, source_target_pairs={{0,4},{4,12},{12,8},{8,0},{1,5},{5,13},{13,9},{9,1},{2,6},{6,14},{... | collective-permute-start | bytes 393224 | tf_op jit(solution)/shard_map/ppermute | solution.py:174
  13.8 1.3 %collective-permute-done.1.refs_2_ = f32[2,64,256]{2,1,0:T(8,128)S(1)} collective-permute-done((f32[2,64,256]{2,1,0:T(8,128)S(1)}, f32[2,64,256]{2,1,0:T(8,128)S(1)}, u32[]{:S(2)}, u32[]{:S(2)}) %collective-permute-start.1) | collective-permute-done | bytes 131104 | tf_op jit(solution)/shard_map/ppermute | solution.py:175
  15.0 0.6 collective-permute-start.2
  15.6 2.2 %collective-permute-done.4.refs_2_ = f32[2,64,256]{2,1,0:T(8,128)S(1)} collective-permute-done((f32[2,64,256]{2,1,0:T(8,128)S(1)}, f32[2,64,256]{2,1,0:T(8,128)S(1)}, u32[]{:S(2)}, u32[]{:S(2)}) %collective-permute-start.4) | collective-permute-done | bytes 131104 | tf_op jit(solution)/shard_map/ppermute | solution.py:174
  17.8 0.6 collective-permute-start.5
  18.4 2.3 %collective-permute-done.2.refs_3_ = f32[2,64,256]{2,1,0:T(8,128)S(1)} collective-permute-done((f32[2,64,256]{2,1,0:T(8,128)S(1)}, f32[2,64,256]{2,1,0:T(8,128)S(1)}, u32[]{:S(2)}, u32[]{:S(2)}) %collective-permute-start.2) | collective-permute-done | bytes 131104 | tf_op jit(solution)/shard_map/ppermute | solution.py:175
  20.7 6.5 %collective-permute-start.6 = (f32[4,64,256]{2,1,0:T(8,128)S(1)}, f32[4,64,256]{2,1,0:T(8,128)S(1)}, u32[]{:S(2)}, u32[]{:S(2)}) collective-permute-start(f32[4,64,256]{2,1,0:T(8,128)S(1)} %pad_maximum_fusion), channel_id=1, source_target_pairs={{0,1},{1,2},{2,3},{4,5},{5,6},{6,7},{8,9},{9,10},{10,11},{12,13},{... | collective-permute-start | bytes 786440 | tf_op jit(solution)/shard_map/ppermute | solution.py:18
  27.2 0.0 copy-start.3
  27.2 1.9 %collective-permute-start.7 = (f32[4,64,256]{2,1,0:T(8,128)S(1)}, f32[4,64,256]{2,1,0:T(8,128)S(1)}, u32[]{:S(2)}, u32[]{:S(2)}) collective-permute-start(f32[4,64,256]{2,1,0:T(8,128)S(1)} %pad_maximum_fusion.1), channel_id=1, source_target_pairs={{1,0},{2,1},{3,2},{5,4},{6,5},{7,6},{9,8},{10,9},{11,10},{13,12},{... | collective-permute-start | bytes 786440 | tf_op jit(solution)/shard_map/ppermute | solution.py:18
  29.2 0.2 assemble.1.outer
  29.4 0.0 collective-permute-done.5.refs_3_
  29.4 0.0 copy-done.3
  29.4 0.0 copy-start
  29.4 1.7 %own.1 = (bf16[2,768,256]{2,1,0:T(8,128)(2,1)S(1)}, bf16[4,512,256]{2,1,0:T(8,128)(2,1)S(1)}, bf16[4,512,256]{2,1,0:T(8,128)(2,1)S(1)}) custom-call(s32[8,16]{1,0:T(8,128)S(1)} %copy-done.3, bf16[2,768,256]{2,1,0:T(8,128)(2,1)S(1)} %assemble.1.outer, f32[2,64,256]{2,1,0:T(8,128)S(1)} %get-tuple-element.35.refs_0_, ...), custom_call_target="tpu_custom_call" | custom-call | flops 3221225472 | bytes 1048576 | tf_op jit(solution)/shard_map/own/pallas_call | solution.py:146
  31.1 0.0 copy-done
  31.1 1.1 %first_inner.1 = f32[2,64,256]{2,1,0:T(8,128)S(1)} custom-call(s32[8]{0:T(128)S(1)} %copy-done, bf16[4,512,256]{2,1,0:T(8,128)(2,1)S(1)} %get-tuple-element.22.high, bf16[4,512,256]{2,1,0:T(8,128)(2,1)S(1)} %get-tuple-element.23.low, bf16[8,768,256]{2,1,0:T(8,128)(2,1)S(1)} %get-tuple-element.26.right_parts), custom_call_target="tpu_custom_call" | custom-call | flops 805306368 | bytes 1048576 | tf_op jit(solution)/shard_map/first_inner/pallas_call | solution.py:146
  32.2 0.6 collective-permute-start.11
  32.8 0.0 collective-permute-done.6.above
  32.8 2.4 %collective-permute-done.7.below = f32[4,64,256]{2,1,0:T(8,128)S(1)} collective-permute-done((f32[4,64,256]{2,1,0:T(8,128)S(1)}, f32[4,64,256]{2,1,0:T(8,128)S(1)}, u32[]{:S(2)}, u32[]{:S(2)}) %collective-permute-start.7) | collective-permute-done | bytes 262176 | tf_op jit(solution)/shard_map/ppermute | solution.py:18
  35.2 1.3 %outside.1 = (bf16[2,768,256]{2,1,0:T(8,128)(2,1)S(1)}, bf16[2,512,256]{2,1,0:T(8,128)(2,1)S(1)}, bf16[2,512,256]{2,1,0:T(8,128)(2,1)S(1)}) custom-call(s32[8,16]{1,0:T(8,128)S(1)} %copy-done.3, f32[4,64,256]{2,1,0:T(8,128)S(1)} %collective-permute-done.6.above, f32[4,64,256]{2,1,0:T(8,128)S(1)} %collective-permute-done.7.below, ...), custom_call_target="tpu_custom_call" | custom-call | flops 1610612736 | bytes 1048576 | tf_op jit(solution)/shard_map/outside/pallas_call | solution.py:146
  36.5 1.1 %first_outer.1 = f32[2,64,256]{2,1,0:T(8,128)S(1)} custom-call(s32[8]{0:T(128)S(1)} %copy-done, bf16[4,512,256]{2,1,0:T(8,128)(2,1)S(1)} %get-tuple-element.22.high, bf16[4,512,256]{2,1,0:T(8,128)(2,1)S(1)} %get-tuple-element.23.low, bf16[2,512,256]{2,1,0:T(8,128)(2,1)S(1)} %get-tuple-element.24.end_high, ...), custom_call_target="tpu_custom_call" | custom-call | flops 805306368 | bytes 1048576 | tf_op jit(solution)/shard_map/first_outer/pallas_call | solution.py:146
  37.6 0.7 %collective-permute-start.8 = (f32[2,64,256]{2,1,0:T(8,128)S(1)}, f32[2,64,256]{2,1,0:T(8,128)S(1)}, u32[]{:S(2)}, u32[]{:S(2)}) collective-permute-start(f32[2,64,256]{2,1,0:T(8,128)S(1)} %first_outer.1), channel_id=1, source_target_pairs={{0,4},{4,12},{12,8},{8,0},{1,5},{5,13},{13,9},{9,1},{2,6},{6,14},{... | collective-permute-start | bytes 393224 | tf_op jit(solution)/shard_map/ppermute | solution.py:220
  38.4 4.5 %chunk.3 = (f32[2,64,256]{2,1,0:T(8,128)S(1)}, f32[2,64,256]{2,1,0:T(8,128)S(1)}) custom-call(s32[8]{0:T(128)S(1)} %copy-done, s32[8,16]{1,0:T(8,128)S(1)} %copy-done.3, bf16[2,768,256]{2,1,0:T(8,128)(2,1)S(1)} %assemble.1.outer, bf16[2,768,256]{2,1,0:T(8,128)(2,1)S(1)} %get-tuple-element.27.inner, bf16[2,768,256]{2,1,0:T(8,128)(2,1)S(1)} %get-tuple-element.28.outside, ...), custom_call_target="tpu_custom_call" | custom-call | flops 3221225472 | bytes 1048576 | tf_op jit(solution)/shard_map/chunk/pallas_call | solution.py:146
  42.9 0.0 collective-permute-done.11
  42.9 3.0 %collective-permute-start.12 = (f32[2,64,256]{2,1,0:T(8,128)S(1)}, f32[2,64,256]{2,1,0:T(8,128)S(1)}, u32[]{:S(2)}, u32[]{:S(2)}) collective-permute-start(f32[2,64,256]{2,1,0:T(8,128)S(1)} %add.34), channel_id=1, source_target_pairs={{0,4},{4,12},{12,8},{8,0},{1,5},{5,13},{13,9},{9,1},{2,6},{6,14},{... | collective-permute-start | bytes 393224 | tf_op jit(solution)/shard_map/ppermute | solution.py:219
  45.9 0.0 collective-permute-done.8
  45.9 0.1 collective-permute-start.9
  46.0 4.5 %chunk.4 = (f32[2,64,256]{2,1,0:T(8,128)S(1)}, f32[2,64,256]{2,1,0:T(8,128)S(1)}) custom-call(s32[8]{0:T(128)S(1)} %copy-done, s32[8,16]{1,0:T(8,128)S(1)} %copy-done.3, bf16[2,768,256]{2,1,0:T(8,128)(2,1)S(1)} %assemble.1.outer, bf16[2,768,256]{2,1,0:T(8,128)(2,1)S(1)} %get-tuple-element.27.inner, bf16[2,768,256]{2,1,0:T(8,128)(2,1)S(1)} %get-tuple-element.28.outside, ...), custom_call_target="tpu_custom_call" | custom-call | flops 3221225472 | bytes 1048576 | tf_op jit(solution)/shard_map/chunk/pallas_call | solution.py:146
  50.5 0.0 collective-permute-done.12
  50.6 0.8 %collective-permute-start.13 = (f32[2,64,256]{2,1,0:T(8,128)S(1)}, f32[2,64,256]{2,1,0:T(8,128)S(1)}, u32[]{:S(2)}, u32[]{:S(2)}) collective-permute-start(f32[2,64,256]{2,1,0:T(8,128)S(1)} %add.35), channel_id=1, source_target_pairs={{0,4},{4,12},{12,8},{8,0},{1,5},{5,13},{13,9},{9,1},{2,6},{6,14},{... | collective-permute-start | bytes 393224 | tf_op jit(solution)/shard_map/ppermute | solution.py:219
  51.3 0.0 collective-permute-done.9
  51.4 0.9 %collective-permute-start.10 = (f32[2,64,256]{2,1,0:T(8,128)S(1)}, f32[2,64,256]{2,1,0:T(8,128)S(1)}, u32[]{:S(2)}, u32[]{:S(2)}) collective-permute-start(f32[2,64,256]{2,1,0:T(8,128)S(1)} %add.32), channel_id=1, source_target_pairs={{0,4},{4,12},{12,8},{8,0},{1,5},{5,13},{13,9},{9,1},{2,6},{6,14},{... | collective-permute-start | bytes 393224 | tf_op jit(solution)/shard_map/ppermute | solution.py:220
  52.2 4.5 %chunk.5 = (f32[2,64,256]{2,1,0:T(8,128)S(1)}, f32[2,64,256]{2,1,0:T(8,128)S(1)}) custom-call(s32[8]{0:T(128)S(1)} %copy-done, s32[8,16]{1,0:T(8,128)S(1)} %copy-done.3, bf16[2,768,256]{2,1,0:T(8,128)(2,1)S(1)} %assemble.1.outer, bf16[2,768,256]{2,1,0:T(8,128)(2,1)S(1)} %get-tuple-element.27.inner, bf16[2,768,256]{2,1,0:T(8,128)(2,1)S(1)} %get-tuple-element.28.outside, ...), custom_call_target="tpu_custom_call" | custom-call | flops 3221225472 | bytes 1048576 | tf_op jit(solution)/shard_map/chunk/pallas_call | solution.py:146
  56.8 0.2 collective-permute-done.13
  57.0 1.1 %collective-permute-done.10 = f32[2,64,256]{2,1,0:T(8,128)S(1)} collective-permute-done((f32[2,64,256]{2,1,0:T(8,128)S(1)}, f32[2,64,256]{2,1,0:T(8,128)S(1)}, u32[]{:S(2)}, u32[]{:S(2)}) %collective-permute-start.10) | collective-permute-done | bytes 131104 | tf_op jit(solution)/shard_map/ppermute | solution.py:220
  58.2 0.7 %pad_maximum_fusion.2 = f32[4,64,256]{2,1,0:T(8,128)} fusion(f32[1,64,256]{2,1,0:T(8,128)S(1)} %get-tuple-element.38, f32[2,64,256]{2,1,0:T(8,128)S(1)} %add.36, f32[1,64,256]{2,1,0:T(8,128)S(1)} %get-tuple-element.37), kind=kLoop, calls=%fused_computation.2 | loop fusion | flops 131072 | bytes 524288 | tf_op jit(solution)/shard_map/concatenate | solution.py:221
  (15 shorter events, 0.3 us)
Async XLA Ops:
  1.0 9.6 %collective-permute-start.3 = (f32[2,64,256]{2,1,0:T(8,128)S(1)}, f32[2,64,256]{2,1,0:T(8,128)S(1)}, u32[]{:S(2)}, u32[]{:S(2)}) collective-permute-start(f32[2,64,256]{2,1,0:T(8,128)S(1)} %get-tuple-element.35.refs_0_), channel_id=1, source_target_pairs={{0,4},{4,12},{12,8},{8,0},{1,5},{5,13},{13,9},{9,1},{2,6},{6,14},{... | collective-permute-start | bytes 393224 | tf_op jit(solution)/shard_map/ppermute | solution.py:174
  3.2 7.0 %collective-permute-start = (f32[2,64,256]{2,1,0:T(8,128)S(1)}, f32[2,64,256]{2,1,0:T(8,128)S(1)}, u32[]{:S(2)}, u32[]{:S(2)}) collective-permute-start(f32[2,64,256]{2,1,0:T(8,128)S(1)} %get-tuple-element.36.refs_0_), channel_id=1, source_target_pairs={{0,4},{4,12},{12,8},{8,0},{1,5},{5,13},{13,9},{9,1},{2,6},{6,14},{... | collective-permute-start | bytes 393224 | tf_op jit(solution)/shard_map/ppermute | solution.py:175
  5.5 1.6 %copy-start.1 = (f32[8,256,256]{2,1,0:T(8,128)S(1)}, f32[8,256,256]{2,1,0:T(8,128)}, u32[]{:S(2)}) copy-start(f32[8,256,256]{2,1,0:T(8,128)} %left_ref.1) | copy-start | bytes 6291460
  7.1 1.6 %copy-start.2 = (f32[8,256,256]{2,1,0:T(8,128)S(1)}, f32[8,256,256]{2,1,0:T(8,128)}, u32[]{:S(2)}) copy-start(f32[8,256,256]{2,1,0:T(8,128)} %right_ref.1) | copy-start | bytes 6291460
  10.3 4.8 %collective-permute-start.1 = (f32[2,64,256]{2,1,0:T(8,128)S(1)}, f32[2,64,256]{2,1,0:T(8,128)S(1)}, u32[]{:S(2)}, u32[]{:S(2)}) collective-permute-start(f32[2,64,256]{2,1,0:T(8,128)S(1)} %broadcast_add_fusion.1), channel_id=1, source_target_pairs={{0,4},{4,12},{12,8},{8,0},{1,5},{5,13},{13,9},{9,1},{2,6},{6,14},{... | collective-permute-start | bytes 393224 | tf_op jit(solution)/shard_map/ppermute | solution.py:175
  10.7 7.1 %collective-permute-start.4 = (f32[2,64,256]{2,1,0:T(8,128)S(1)}, f32[2,64,256]{2,1,0:T(8,128)S(1)}, u32[]{:S(2)}, u32[]{:S(2)}) collective-permute-start(f32[2,64,256]{2,1,0:T(8,128)S(1)} %broadcast_add_fusion), channel_id=1, source_target_pairs={{0,4},{4,12},{12,8},{8,0},{1,5},{5,13},{13,9},{9,1},{2,6},{6,14},{... | collective-permute-start | bytes 393224 | tf_op jit(solution)/shard_map/ppermute | solution.py:174
  15.0 5.6 %collective-permute-start.2 = (f32[2,64,256]{2,1,0:T(8,128)S(1)}, f32[2,64,256]{2,1,0:T(8,128)S(1)}, u32[]{:S(2)}, u32[]{:S(2)}) collective-permute-start(f32[2,64,256]{2,1,0:T(8,128)S(1)} %collective-permute-done.1.refs_2_), channel_id=1, source_target_pairs={{0,4},{4,12},{12,8},{8,0},{1,5},{5,13},{13,9},{9,1},{2,6},{6,14},{... | collective-permute-start | bytes 393224 | tf_op jit(solution)/shard_map/ppermute | solution.py:175
  17.8 11.6 %collective-permute-start.5 = (f32[2,64,256]{2,1,0:T(8,128)S(1)}, f32[2,64,256]{2,1,0:T(8,128)S(1)}, u32[]{:S(2)}, u32[]{:S(2)}) collective-permute-start(f32[2,64,256]{2,1,0:T(8,128)S(1)} %collective-permute-done.4.refs_2_), channel_id=1, source_target_pairs={{0,4},{4,12},{12,8},{8,0},{1,5},{5,13},{13,9},{9,1},{2,6},{6,14},{... | collective-permute-start | bytes 393224 | tf_op jit(solution)/shard_map/ppermute | solution.py:174
  20.7 12.1 %collective-permute-start.6 = (f32[4,64,256]{2,1,0:T(8,128)S(1)}, f32[4,64,256]{2,1,0:T(8,128)S(1)}, u32[]{:S(2)}, u32[]{:S(2)}) collective-permute-start(f32[4,64,256]{2,1,0:T(8,128)S(1)} %pad_maximum_fusion), channel_id=1, source_target_pairs={{0,1},{1,2},{2,3},{4,5},{5,6},{6,7},{8,9},{9,10},{10,11},{12,13},{... | collective-permute-start | bytes 786440 | tf_op jit(solution)/shard_map/ppermute | solution.py:18
  27.2 2.1 %copy-start.3 = (s32[8,16]{1,0:T(8,128)S(1)}, s32[8,16]{1,0:T(8,128)}, u32[]{:S(2)}) copy-start(s32[8,16]{1,0:T(8,128)} %allowed_ref.9) | copy-start | bytes 1540
  27.2 8.0 %collective-permute-start.7 = (f32[4,64,256]{2,1,0:T(8,128)S(1)}, f32[4,64,256]{2,1,0:T(8,128)S(1)}, u32[]{:S(2)}, u32[]{:S(2)}) collective-permute-start(f32[4,64,256]{2,1,0:T(8,128)S(1)} %pad_maximum_fusion.1), channel_id=1, source_target_pairs={{1,0},{2,1},{3,2},{5,4},{6,5},{7,6},{9,8},{10,9},{11,10},{13,12},{... | collective-permute-start | bytes 786440 | tf_op jit(solution)/shard_map/ppermute | solution.py:18
  29.4 1.7 %copy-start = (s32[8]{0:T(128)S(1)}, s32[8]{0:T(128)}, u32[]{:S(2)}) copy-start(s32[8]{0:T(128)} %shifts_ref.9) | copy-start | bytes 100
  32.2 10.7 %collective-permute-start.11 = (f32[2,64,256]{2,1,0:T(8,128)S(1)}, f32[2,64,256]{2,1,0:T(8,128)S(1)}, u32[]{:S(2)}, u32[]{:S(2)}) collective-permute-start(f32[2,64,256]{2,1,0:T(8,128)S(1)} %first_inner.1), channel_id=1, source_target_pairs={{0,4},{4,12},{12,8},{8,0},{1,5},{5,13},{13,9},{9,1},{2,6},{6,14},{... | collective-permute-start | bytes 393224 | tf_op jit(solution)/shard_map/ppermute | solution.py:219
  37.6 8.3 %collective-permute-start.8 = (f32[2,64,256]{2,1,0:T(8,128)S(1)}, f32[2,64,256]{2,1,0:T(8,128)S(1)}, u32[]{:S(2)}, u32[]{:S(2)}) collective-permute-start(f32[2,64,256]{2,1,0:T(8,128)S(1)} %first_outer.1), channel_id=1, source_target_pairs={{0,4},{4,12},{12,8},{8,0},{1,5},{5,13},{13,9},{9,1},{2,6},{6,14},{... | collective-permute-start | bytes 393224 | tf_op jit(solution)/shard_map/ppermute | solution.py:220
  42.9 7.6 %collective-permute-start.12 = (f32[2,64,256]{2,1,0:T(8,128)S(1)}, f32[2,64,256]{2,1,0:T(8,128)S(1)}, u32[]{:S(2)}, u32[]{:S(2)}) collective-permute-start(f32[2,64,256]{2,1,0:T(8,128)S(1)} %add.34), channel_id=1, source_target_pairs={{0,4},{4,12},{12,8},{8,0},{1,5},{5,13},{13,9},{9,1},{2,6},{6,14},{... | collective-permute-start | bytes 393224 | tf_op jit(solution)/shard_map/ppermute | solution.py:219
  45.9 5.4 %collective-permute-start.9 = (f32[2,64,256]{2,1,0:T(8,128)S(1)}, f32[2,64,256]{2,1,0:T(8,128)S(1)}, u32[]{:S(2)}, u32[]{:S(2)}) collective-permute-start(f32[2,64,256]{2,1,0:T(8,128)S(1)} %add.31), channel_id=1, source_target_pairs={{0,4},{4,12},{12,8},{8,0},{1,5},{5,13},{13,9},{9,1},{2,6},{6,14},{... | collective-permute-start | bytes 393224 | tf_op jit(solution)/shard_map/ppermute | solution.py:220
  50.6 6.4 %collective-permute-start.13 = (f32[2,64,256]{2,1,0:T(8,128)S(1)}, f32[2,64,256]{2,1,0:T(8,128)S(1)}, u32[]{:S(2)}, u32[]{:S(2)}) collective-permute-start(f32[2,64,256]{2,1,0:T(8,128)S(1)} %add.35), channel_id=1, source_target_pairs={{0,4},{4,12},{12,8},{8,0},{1,5},{5,13},{13,9},{9,1},{2,6},{6,14},{... | collective-permute-start | bytes 393224 | tf_op jit(solution)/shard_map/ppermute | solution.py:219
  51.4 6.8 %collective-permute-start.10 = (f32[2,64,256]{2,1,0:T(8,128)S(1)}, f32[2,64,256]{2,1,0:T(8,128)S(1)}, u32[]{:S(2)}, u32[]{:S(2)}) collective-permute-start(f32[2,64,256]{2,1,0:T(8,128)S(1)} %add.32), channel_id=1, source_target_pairs={{0,4},{4,12},{12,8},{8,0},{1,5},{5,13},{13,9},{9,1},{2,6},{6,14},{... | collective-permute-start | bytes 393224 | tf_op jit(solution)/shard_map/ppermute | solution.py:220

commit v8 on v3

--- a/solution.py
+++ b/solution.py
@@ -105,33 +105,34 @@
         first_product(left, outside[i], allowed_ref, first - 1 + i * (nloc + 1), high.at[i], low.at[i])
 
 
-def second_product(targets, shifts_ref, high, low, right_hi, right_lo, out):
-    kops = shifts_ref.shape[0]
-    _, rows, width = out.shape
+def second_product(blocks_of, shifts_ref, high, low, right_hi, right_lo, out):
+    rows, width = out.shape[1:]
 
     def left(parts):
         columns = []
-        for k in range(kops):
-            shift, at = shifts_ref[k], slice(k * rows, (k + 1) * rows)
-            blocks = []
-            for t in targets:
-                below, same, above = [parts[t + d][at] for d in range(3)]
-                blocks.append(jnp.where(shift == 0, same, jnp.where(shift == 1, below, above)))
-            columns.append(jnp.concatenate(blocks))
+        for k in range(shifts_ref.shape[0]):
+            at = slice(k * rows, (k + 1) * rows)
+            columns.append(jnp.concatenate(blocks_of(parts, shifts_ref[k], at)))
         return jnp.concatenate(columns, axis=1)
 
-    out[...] = dot3((left(high), left(low)), (right_hi[...], right_lo[...])).reshape(len(targets), rows, width)
+    out[...] = dot3((left(high), left(low)), (right_hi[...], right_lo[...])).reshape(out.shape)
 
 
 def first_inner(nloc, shifts_ref, high, low, right_hi, right_lo, out):
-    own = [[None, *[ref.at[i] for i in range(nloc)], None] for ref in (high, low)]
-    second_product(range(1, nloc - 1), shifts_ref, *own, right_hi, right_lo, out)
+    def blocks_of(own, shift, at):
+        return [own[t - shift, at] for t in range(1, nloc - 1)]
+
+    second_product(blocks_of, shifts_ref, high, low, right_hi, right_lo, out)
 
 
 def first_outer(nloc, shifts_ref, high, low, end_high, end_low, right_hi, right_lo, out):
-    pairs = ((high, end_high), (low, end_low))
-    held = [[ends.at[0], *[ref.at[i] for i in range(nloc)], ends.at[1]] for ref, ends in pairs]
-    second_product((0, nloc - 1), shifts_ref, *held, right_hi, right_lo, out)
+    def blocks_of(parts, shift, at):
+        own, ends = parts
+        start = jnp.where(shift == 1, ends[0, at], own[jnp.maximum(-shift, 0), at])
+        end = jnp.where(shift == -1, ends[1, at], own[jnp.minimum(nloc - 1 - shift, nloc - 1), at])
+        return [start, end]
+
+    second_product(blocks_of, shifts_ref, (high, end_high), (low, end_low), right_hi, right_lo, out)
 
 
 def later_chunk(n, nloc, step, shifts_ref, allowed_ref, outer, inner, outside, left_parts, right_hi, right_lo, outer_out, inner_out, high, low):
@@ -140,9 +141,15 @@
     sources = [outside.at[0], outer.at[0], *[inner.at[i] for i in range(nloc - 2)], outer.at[1], outside.at[1]]
     for i, ref in enumerate(sources):
         first_product(left, ref[...], allowed_ref, first - 1 + i, high.at[i], low.at[i])
-    held = [[ref.at[i] for i in range(nloc + 2)] for ref in (high, low)]
-    second_product(range(1, nloc - 1), shifts_ref, *held, right_hi, right_lo, inner_out)
-    second_product((0, nloc - 1), shifts_ref, *held, right_hi, right_lo, outer_out)
+
+    def inner_blocks(parts, shift, at):
+        return [parts[t + 1 - shift, at] for t in range(1, nloc - 1)]
+
+    def outer_blocks(parts, shift, at):
+        return [parts[t + 1 - shift, at] for t in (0, nloc - 1)]
+
+    second_product(inner_blocks, shifts_ref, high, low, right_hi, right_lo, inner_out)
+    second_product(outer_blocks, shifts_ref, high, low, right_hi, right_lo, outer_out)
 
 
 def call(body, name, flops, out_shape, in_specs, operands, scratch=()):
@@ -172,10 +179,11 @@
         prepare, "prepare", 4 * kops * one, [parts, tall, tall, zero], [VMEM] * 2, [left_ops, right_ops]
     )
 
-    outer, inner = [psi[:: nloc - 1]], [psi[1 : nloc - 1]]
-    for step in range(n - 1):
+    blocks = [psi, lax.ppermute(psi, "op", route)]
+    outer, inner = [[b[:: nloc - 1] for b in blocks], [b[1 : nloc - 1] for b in blocks]]
+    for step in range(1, n - 1):
+        outer.append(lax.ppermute(outer[-1] + zero[0, 0] if step == 1 else outer[-1], "op", route))
         inner.append(lax.ppermute(inner[-1] + zero[0, 0] if step == 1 else inner[-1], "op", route))
-        outer.append(lax.ppermute(outer[-1] + zero[0, 0] if step == 1 else outer[-1], "op", route))
 
     above = shifted(jnp.concatenate([b[1:] for b in outer]), ("sec", "sub"), 1)
     below = shifted(jnp.concatenate([b[:1] for b in outer]), ("sec", "sub"), -1)

time: 58.3 us -> 55.8 us (0.957)
  waiting for transfers between devices: 16.3 us -> 13.1 us
  starting transfers between devices: 20.2 us -> 22.5 us
  local copies, waits for them, and re-layouts: 4.23 us -> 3.27 us
    ppermute x3 -> x2, waiting for transfers between devices: 8.07 us -> 3.62 us  [shards(): lax.ppermute(outer[-1] + zero[0, 0] if step == 1 else outer[-1], 'op', ro...]
    ppermute x0 -> x1, waiting for transfers between devices: none -> 2.94 us  [shards(): blocks = [psi, lax.ppermute(psi, 'op', route)]]
    ppermute x0 -> x1, starting transfers between devices: none -> 2.13 us  [shards(): blocks = [psi, lax.ppermute(psi, 'op', route)]]
    ppermute x3 -> x2, starting transfers between devices: 3 us -> 0.97 us  [shards(): lax.ppermute(outer[-1] + zero[0, 0] if step == 1 else outer[-1], 'op', ro...]
    ppermute x3 -> x2, waiting for transfers between devices: 3.62 us -> 2.18 us  [shards(): lax.ppermute(inner[-1] + zero[0, 0] if step == 1 else inner[-1], 'op', ro...]
    ppermute x3 -> x2, starting transfers between devices: 2.4 us -> 3.59 us  [shards(): lax.ppermute(inner[-1] + zero[0, 0] if step == 1 else inner[-1], 'op', ro...]
    slice x1, local copies, waits for them, and re-layouts: 0.99 us -> 0.02 us  [shards(): b[::nloc - 1]]
    ppermute x3, starting transfers between devices: 0.3 us -> 0.99 us  [shards(): result_outer = lax.ppermute(result_outer, 'op', route) + next_outer]
  transfers between devices with their start and end apart: 14 -> 13, of which waited for: 7 -> 7; matrix products, arithmetic and copies ran while one was open for 0% -> 0% of each run, Pallas kernels for 28% -> 28%
where the time goes in v8:
time: 55.8 us; the launch traced here: 55.6 us
  starting transfers between devices  22.5 us (40%)
  Pallas kernels  15.6 us (28%)
  waiting for transfers between devices  13.1 us (23%)
  local copies, waits for them, and re-layouts  3.27 us (6%)
  other arithmetic  0.95 us (2%)
    pallas_call x9, Pallas kernels, call(): pl.pallas_call(body, name=name, out_shape=out_shape, in_specs=in_specs, o...  15.6 us
    ppermute x2, starting transfers between devices, shifted(): return lax.ppermute(block, axis, route)  8.41 us
    ppermute x3, starting transfers between devices, shards(): result_inner = lax.ppermute(result_inner, 'op', route) + next_inner  6.4 us
    ppermute x2, waiting for transfers between devices, shards(): lax.ppermute(outer[-1] + zero[0, 0] if step == 1 else outer[-1], 'op', ro...  3.62 us
    ppermute x2, starting transfers between devices, shards(): lax.ppermute(inner[-1] + zero[0, 0] if step == 1 else inner[-1], 'op', ro...  3.59 us
    unnamed x10, local copies, waits for them, and re-layouts  3.2 us
    ppermute x1, waiting for transfers between devices, shards(): blocks = [psi, lax.ppermute(psi, 'op', route)]  2.94 us
    ppermute x2, waiting for transfers between devices, shifted(): return lax.ppermute(block, axis, route)  2.38 us
  transfers between devices with their start and end apart: 13, of which 7 were waited for; matrix products, arithmetic and copies ran while one was open for 0% of the time, Pallas kernels for 28%

profile of v8, /device:TPU:1, one launch (start us, length us, event | category | flops | bytes accessed | tf_op | source)
XLA Modules:
  0.0 55.6 jit_solution(7131514828988113591)
XLA Ops:
  0.0 2.1 %collective-permute-start = (f32[4,64,256]{2,1,0:T(8,128)}, f32[4,64,256]{2,1,0:T(8,128)S(1)}, u32[]{:S(2)}, u32[]{:S(2)}) collective-permute-start(f32[4,64,256]{2,1,0:T(8,128)} %param.5), channel_id=1, source_target_pairs={{0,4},{4,12},{12,8},{8,0},{1,5},{5,13},{13,9},{9,1},{2,6},{6,14},{... | collective-permute-start | bytes 786440 | tf_op jit(solution)/shard_map/ppermute | solution.py:182
  2.1 0.0 copy-start.1
  2.1 1.6 %copy-done.1 = f32[8,256,256]{2,1,0:T(8,128)S(1)} copy-done((f32[8,256,256]{2,1,0:T(8,128)S(1)}, f32[8,256,256]{2,1,0:T(8,128)}, u32[]{:S(2)}) %copy-start.1) | copy-done | bytes 2097176
  3.7 0.0 copy-start.2
  3.7 1.6 %copy-done.2 = f32[8,256,256]{2,1,0:T(8,128)S(1)} copy-done((f32[8,256,256]{2,1,0:T(8,128)S(1)}, f32[8,256,256]{2,1,0:T(8,128)}, u32[]{:S(2)}) %copy-start.2) | copy-done | bytes 2097176
  5.3 0.0 copy-start.4
  5.3 1.1 %prepare.1 = (bf16[4,8,64,768]{3,2,1,0:T(8,128)(2,1)S(1)}, bf16[2048,256]{1,0:T(8,128)(2,1)S(1)}, bf16[2048,256]{1,0:T(8,128)(2,1)S(1)}, f32[1,128]{1,0:T(1,128)S(1)}) custom-call(f32[8,256,256]{2,1,0:T(8,128)S(1)} %copy-done.1, f32[8,256,256]{2,1,0:T(8,128)S(1)} %copy-done.2), custom_call_target="tpu_custom_call" | custom-call | flops 3221225472 | bytes 1048576 | tf_op jit(solution)/shard_map/prepare/pallas_call | solution.py:156
  6.4 0.0 copy-done.4
  6.4 2.9 %collective-permute-done = f32[4,64,256]{2,1,0:T(8,128)S(1)} collective-permute-done((f32[4,64,256]{2,1,0:T(8,128)}, f32[4,64,256]{2,1,0:T(8,128)S(1)}, u32[]{:S(2)}, u32[]{:S(2)}) %collective-permute-start) | collective-permute-done | bytes 262176 | tf_op jit(solution)/shard_map/ppermute | solution.py:182
  9.4 0.1 broadcast_add_fusion
  9.5 0.4 collective-permute-start.3
  9.9 3.0 %collective-permute-start.1 = (f32[2,64,256]{2,1,0:T(8,128)S(1)}, f32[2,64,256]{2,1,0:T(8,128)S(1)}, u32[]{:S(2)}, u32[]{:S(2)}) collective-permute-start(f32[2,64,256]{2,1,0:T(8,128)S(1)} %get-tuple-element.40), channel_id=1, source_target_pairs={{0,4},{4,12},{12,8},{8,0},{1,5},{5,13},{13,9},{9,1},{2,6},{6,14},{... | collective-permute-start | bytes 393224 | tf_op jit(solution)/shard_map/ppermute | solution.py:186
  12.9 1.4 %collective-permute-done.3.refs_2_ = f32[2,64,256]{2,1,0:T(8,128)S(1)} collective-permute-done((f32[2,64,256]{2,1,0:T(8,128)S(1)}, f32[2,64,256]{2,1,0:T(8,128)S(1)}, u32[]{:S(2)}, u32[]{:S(2)}) %collective-permute-start.3) | collective-permute-done | bytes 131104 | tf_op jit(solution)/shard_map/ppermute | solution.py:185
  14.2 0.6 %collective-permute-start.4 = (f32[2,64,256]{2,1,0:T(8,128)S(1)}, f32[2,64,256]{2,1,0:T(8,128)S(1)}, u32[]{:S(2)}, u32[]{:S(2)}) collective-permute-start(f32[2,64,256]{2,1,0:T(8,128)S(1)} %collective-permute-done.3.refs_2_), channel_id=1, source_target_pairs={{0,4},{4,12},{12,8},{8,0},{1,5},{5,13},{13,9},{9,1},{2,6},{6,14},{... | collective-permute-start | bytes 393224 | tf_op jit(solution)/shard_map/ppermute | solution.py:185
  14.8 2.2 %collective-permute-done.1.refs_2_ = f32[2,64,256]{2,1,0:T(8,128)S(1)} collective-permute-done((f32[2,64,256]{2,1,0:T(8,128)S(1)}, f32[2,64,256]{2,1,0:T(8,128)S(1)}, u32[]{:S(2)}, u32[]{:S(2)}) %collective-permute-start.1) | collective-permute-done | bytes 131104 | tf_op jit(solution)/shard_map/ppermute | solution.py:186
  17.0 0.6 %collective-permute-start.2 = (f32[2,64,256]{2,1,0:T(8,128)S(1)}, f32[2,64,256]{2,1,0:T(8,128)S(1)}, u32[]{:S(2)}, u32[]{:S(2)}) collective-permute-start(f32[2,64,256]{2,1,0:T(8,128)S(1)} %collective-permute-done.1.refs_2_), channel_id=1, source_target_pairs={{0,4},{4,12},{12,8},{8,0},{1,5},{5,13},{13,9},{9,1},{2,6},{6,14},{... | collective-permute-start | bytes 393224 | tf_op jit(solution)/shard_map/ppermute | solution.py:186
  17.6 2.3 %collective-permute-done.4.refs_3_ = f32[2,64,256]{2,1,0:T(8,128)S(1)} collective-permute-done((f32[2,64,256]{2,1,0:T(8,128)S(1)}, f32[2,64,256]{2,1,0:T(8,128)S(1)}, u32[]{:S(2)}, u32[]{:S(2)}) %collective-permute-start.4) | collective-permute-done | bytes 131104 | tf_op jit(solution)/shard_map/ppermute | solution.py:185
  19.9 6.5 %collective-permute-start.5 = (f32[4,64,256]{2,1,0:T(8,128)S(1)}, f32[4,64,256]{2,1,0:T(8,128)S(1)}, u32[]{:S(2)}, u32[]{:S(2)}) collective-permute-start(f32[4,64,256]{2,1,0:T(8,128)S(1)} %pad_maximum_fusion), channel_id=1, source_target_pairs={{0,1},{1,2},{2,3},{4,5},{5,6},{6,7},{8,9},{9,10},{10,11},{12,13},{... | collective-permute-start | bytes 786440 | tf_op jit(solution)/shard_map/ppermute | solution.py:18
  26.4 0.0 copy-start.3
  26.4 1.9 %collective-permute-start.6 = (f32[4,64,256]{2,1,0:T(8,128)S(1)}, f32[4,64,256]{2,1,0:T(8,128)S(1)}, u32[]{:S(2)}, u32[]{:S(2)}) collective-permute-start(f32[4,64,256]{2,1,0:T(8,128)S(1)} %pad_maximum_fusion.1), channel_id=1, source_target_pairs={{1,0},{2,1},{3,2},{5,4},{6,5},{7,6},{9,8},{10,9},{11,10},{13,12},{... | collective-permute-start | bytes 786440 | tf_op jit(solution)/shard_map/ppermute | solution.py:18
  28.3 0.2 assemble.1.refs_4_.outer
  28.5 0.0 collective-permute-done.2.refs_3_
  28.6 0.0 copy-done.3
  28.6 0.0 copy-start
  28.6 1.7 %own.1 = (bf16[2,768,256]{2,1,0:T(8,128)(2,1)S(1)}, bf16[4,512,256]{2,1,0:T(8,128)(2,1)S(1)}, bf16[4,512,256]{2,1,0:T(8,128)(2,1)S(1)}) custom-call(s32[8,16]{1,0:T(8,128)S(1)} %copy-done.3, f32[2,64,256]{2,1,0:T(8,128)S(1)} %get-tuple-element.42.refs_0_, f32[2,64,256]{2,1,0:T(8,128)S(1)} %get-tuple-element.39.refs_1_, ...), custom_call_target="tpu_custom_call" | custom-call | flops 3221225472 | bytes 1048576 | tf_op jit(solution)/shard_map/own/pallas_call | solution.py:156
  30.3 0.0 copy-done
  30.3 1.1 %first_inner.1 = f32[2,64,256]{2,1,0:T(8,128)S(1)} custom-call(s32[8]{0:T(128)S(1)} %copy-done, bf16[4,512,256]{2,1,0:T(8,128)(2,1)S(1)} %get-tuple-element.23.high, bf16[4,512,256]{2,1,0:T(8,128)(2,1)S(1)} %get-tuple-element.24.low, bf16[2048,256]{1,0:T(8,128)(2,1)S(1)} %get-tuple-element.27.right_hi, bf16[2048,256]{1,0:T(8,128)(2,1)S(1)} %get-tuple-element.28.right_lo), custom_call_target="tpu_custom_call" | custom-call | flops 805306368 | bytes 1048576 | tf_op jit(solution)/shard_map/first_inner/pallas_call | solution.py:156
  31.4 0.6 %collective-permute-start.10 = (f32[2,64,256]{2,1,0:T(8,128)S(1)}, f32[2,64,256]{2,1,0:T(8,128)S(1)}, u32[]{:S(2)}, u32[]{:S(2)}) collective-permute-start(f32[2,64,256]{2,1,0:T(8,128)S(1)} %first_inner.1), channel_id=1, source_target_pairs={{0,4},{4,12},{12,8},{8,0},{1,5},{5,13},{13,9},{9,1},{2,6},{6,14},{... | collective-permute-start | bytes 393224 | tf_op jit(solution)/shard_map/ppermute | solution.py:230
  32.0 0.0 collective-permute-done.5.above
  32.0 2.4 %collective-permute-done.6.below = f32[4,64,256]{2,1,0:T(8,128)S(1)} collective-permute-done((f32[4,64,256]{2,1,0:T(8,128)S(1)}, f32[4,64,256]{2,1,0:T(8,128)S(1)}, u32[]{:S(2)}, u32[]{:S(2)}) %collective-permute-start.6) | collective-permute-done | bytes 262176 | tf_op jit(solution)/shard_map/ppermute | solution.py:18
  34.4 1.3 %outside.1 = (bf16[2,768,256]{2,1,0:T(8,128)(2,1)S(1)}, bf16[2,512,256]{2,1,0:T(8,128)(2,1)S(1)}, bf16[2,512,256]{2,1,0:T(8,128)(2,1)S(1)}) custom-call(s32[8,16]{1,0:T(8,128)S(1)} %copy-done.3, f32[4,64,256]{2,1,0:T(8,128)S(1)} %collective-permute-done.5.above, f32[4,64,256]{2,1,0:T(8,128)S(1)} %collective-permute-done.6.below, ...), custom_call_target="tpu_custom_call" | custom-call | flops 1610612736 | bytes 1048576 | tf_op jit(solution)/shard_map/outside/pallas_call | solution.py:156
  35.7 1.2 %first_outer.1 = f32[2,64,256]{2,1,0:T(8,128)S(1)} custom-call(s32[8]{0:T(128)S(1)} %copy-done, bf16[4,512,256]{2,1,0:T(8,128)(2,1)S(1)} %get-tuple-element.23.high, bf16[4,512,256]{2,1,0:T(8,128)(2,1)S(1)} %get-tuple-element.24.low, bf16[2,512,256]{2,1,0:T(8,128)(2,1)S(1)} %get-tuple-element.25.end_high, ...), custom_call_target="tpu_custom_call" | custom-call | flops 805306368 | bytes 1048576 | tf_op jit(solution)/shard_map/first_outer/pallas_call | solution.py:156
  36.9 0.7 %collective-permute-start.7 = (f32[2,64,256]{2,1,0:T(8,128)S(1)}, f32[2,64,256]{2,1,0:T(8,128)S(1)}, u32[]{:S(2)}, u32[]{:S(2)}) collective-permute-start(f32[2,64,256]{2,1,0:T(8,128)S(1)} %first_outer.1), channel_id=1, source_target_pairs={{0,4},{4,12},{12,8},{8,0},{1,5},{5,13},{13,9},{9,1},{2,6},{6,14},{... | collective-permute-start | bytes 393224 | tf_op jit(solution)/shard_map/ppermute | solution.py:231
  37.6 3.0 %chunk.3 = (f32[2,64,256]{2,1,0:T(8,128)S(1)}, f32[2,64,256]{2,1,0:T(8,128)S(1)}) custom-call(s32[8]{0:T(128)S(1)} %copy-done, s32[8,16]{1,0:T(8,128)S(1)} %copy-done.3, bf16[2,768,256]{2,1,0:T(8,128)(2,1)S(1)} %assemble.1.refs_4_.outer, bf16[2,768,256]{2,1,0:T(8,128)(2,1)S(1)} %get-tuple-element.29.inner, ...), custom_call_target="tpu_custom_call" | custom-call | flops 3221225472 | bytes 1048576 | tf_op jit(solution)/shard_map/chunk/pallas_call | solution.py:156
  40.7 0.0 collective-permute-done.10
  40.7 3.0 %collective-permute-start.11 = (f32[2,64,256]{2,1,0:T(8,128)S(1)}, f32[2,64,256]{2,1,0:T(8,128)S(1)}, u32[]{:S(2)}, u32[]{:S(2)}) collective-permute-start(f32[2,64,256]{2,1,0:T(8,128)S(1)} %add.34), channel_id=1, source_target_pairs={{0,4},{4,12},{12,8},{8,0},{1,5},{5,13},{13,9},{9,1},{2,6},{6,14},{... | collective-permute-start | bytes 393224 | tf_op jit(solution)/shard_map/ppermute | solution.py:230
  43.7 0.0 collective-permute-done.7
  43.7 0.2 collective-permute-start.8
  43.8 3.0 %chunk.4 = (f32[2,64,256]{2,1,0:T(8,128)S(1)}, f32[2,64,256]{2,1,0:T(8,128)S(1)}) custom-call(s32[8]{0:T(128)S(1)} %copy-done, s32[8,16]{1,0:T(8,128)S(1)} %copy-done.3, bf16[2,768,256]{2,1,0:T(8,128)(2,1)S(1)} %assemble.1.refs_4_.outer, bf16[2,768,256]{2,1,0:T(8,128)(2,1)S(1)} %get-tuple-element.29.inner, ...), custom_call_target="tpu_custom_call" | custom-call | flops 3221225472 | bytes 1048576 | tf_op jit(solution)/shard_map/chunk/pallas_call | solution.py:156
  46.9 0.3 collective-permute-done.11
  47.2 2.8 %collective-permute-start.12 = (f32[2,64,256]{2,1,0:T(8,128)S(1)}, f32[2,64,256]{2,1,0:T(8,128)S(1)}, u32[]{:S(2)}, u32[]{:S(2)}) collective-permute-start(f32[2,64,256]{2,1,0:T(8,128)S(1)} %add.35), channel_id=1, source_target_pairs={{0,4},{4,12},{12,8},{8,0},{1,5},{5,13},{13,9},{9,1},{2,6},{6,14},{... | collective-permute-start | bytes 393224 | tf_op jit(solution)/shard_map/ppermute | solution.py:230
  50.1 0.0 collective-permute-done.8
  50.1 0.1 collective-permute-start.9
  50.2 3.0 %chunk.5 = (f32[2,64,256]{2,1,0:T(8,128)S(1)}, f32[2,64,256]{2,1,0:T(8,128)S(1)}) custom-call(s32[8]{0:T(128)S(1)} %copy-done, s32[8,16]{1,0:T(8,128)S(1)} %copy-done.3, bf16[2,768,256]{2,1,0:T(8,128)(2,1)S(1)} %assemble.1.refs_4_.outer, bf16[2,768,256]{2,1,0:T(8,128)(2,1)S(1)} %get-tuple-element.29.inner, ...), custom_call_target="tpu_custom_call" | custom-call | flops 3221225472 | bytes 1048576 | tf_op jit(solution)/shard_map/chunk/pallas_call | solution.py:156
  53.2 0.0 collective-permute-done.12
  53.2 1.6 %collective-permute-done.9 = f32[2,64,256]{2,1,0:T(8,128)S(1)} collective-permute-done((f32[2,64,256]{2,1,0:T(8,128)S(1)}, f32[2,64,256]{2,1,0:T(8,128)S(1)}, u32[]{:S(2)}, u32[]{:S(2)}) %collective-permute-start.9) | collective-permute-done | bytes 131104 | tf_op jit(solution)/shard_map/ppermute | solution.py:231
  54.9 0.7 %pad_maximum_fusion.2 = f32[4,64,256]{2,1,0:T(8,128)} fusion(f32[1,64,256]{2,1,0:T(8,128)S(1)} %get-tuple-element.44, f32[2,64,256]{2,1,0:T(8,128)S(1)} %add.36, f32[1,64,256]{2,1,0:T(8,128)S(1)} %get-tuple-element.43), kind=kLoop, calls=%fused_computation.2 | loop fusion | flops 131072 | bytes 524288 | tf_op jit(solution)/shard_map/concatenate | solution.py:232
  (14 shorter events, 0.2 us)
Async XLA Ops:
  0.0 9.4 %collective-permute-start = (f32[4,64,256]{2,1,0:T(8,128)}, f32[4,64,256]{2,1,0:T(8,128)S(1)}, u32[]{:S(2)}, u32[]{:S(2)}) collective-permute-start(f32[4,64,256]{2,1,0:T(8,128)} %param.5), channel_id=1, source_target_pairs={{0,4},{4,12},{12,8},{8,0},{1,5},{5,13},{13,9},{9,1},{2,6},{6,14},{... | collective-permute-start | bytes 786440 | tf_op jit(solution)/shard_map/ppermute | solution.py:182
  2.1 1.6 %copy-start.1 = (f32[8,256,256]{2,1,0:T(8,128)S(1)}, f32[8,256,256]{2,1,0:T(8,128)}, u32[]{:S(2)}) copy-start(f32[8,256,256]{2,1,0:T(8,128)} %left_ref.1) | copy-start | bytes 6291460
  3.7 1.6 %copy-start.2 = (f32[8,256,256]{2,1,0:T(8,128)S(1)}, f32[8,256,256]{2,1,0:T(8,128)}, u32[]{:S(2)}) copy-start(f32[8,256,256]{2,1,0:T(8,128)} %right_ref.1) | copy-start | bytes 6291460
  5.3 1.1 %copy-start.4 = (f32[4,64,256]{2,1,0:T(8,128)S(1)}, f32[4,64,256]{2,1,0:T(8,128)}, u32[]{:S(2)}) copy-start(f32[4,64,256]{2,1,0:T(8,128)} %param.5) | copy-start | bytes 786436
  9.5 4.8 %collective-permute-start.3 = (f32[2,64,256]{2,1,0:T(8,128)S(1)}, f32[2,64,256]{2,1,0:T(8,128)S(1)}, u32[]{:S(2)}, u32[]{:S(2)}) collective-permute-start(f32[2,64,256]{2,1,0:T(8,128)S(1)} %get-tuple-element.37), channel_id=1, source_target_pairs={{0,4},{4,12},{12,8},{8,0},{1,5},{5,13},{13,9},{9,1},{2,6},{6,14},{... | collective-permute-start | bytes 393224 | tf_op jit(solution)/shard_map/ppermute | solution.py:185
  9.9 7.1 %collective-permute-start.1 = (f32[2,64,256]{2,1,0:T(8,128)S(1)}, f32[2,64,256]{2,1,0:T(8,128)S(1)}, u32[]{:S(2)}, u32[]{:S(2)}) collective-permute-start(f32[2,64,256]{2,1,0:T(8,128)S(1)} %get-tuple-element.40), channel_id=1, source_target_pairs={{0,4},{4,12},{12,8},{8,0},{1,5},{5,13},{13,9},{9,1},{2,6},{6,14},{... | collective-permute-start | bytes 393224 | tf_op jit(solution)/shard_map/ppermute | solution.py:186
  14.2 5.6 %collective-permute-start.4 = (f32[2,64,256]{2,1,0:T(8,128)S(1)}, f32[2,64,256]{2,1,0:T(8,128)S(1)}, u32[]{:S(2)}, u32[]{:S(2)}) collective-permute-start(f32[2,64,256]{2,1,0:T(8,128)S(1)} %collective-permute-done.3.refs_2_), channel_id=1, source_target_pairs={{0,4},{4,12},{12,8},{8,0},{1,5},{5,13},{13,9},{9,1},{2,6},{6,14},{... | collective-permute-start | bytes 393224 | tf_op jit(solution)/shard_map/ppermute | solution.py:185
  17.0 11.6 %collective-permute-start.2 = (f32[2,64,256]{2,1,0:T(8,128)S(1)}, f32[2,64,256]{2,1,0:T(8,128)S(1)}, u32[]{:S(2)}, u32[]{:S(2)}) collective-permute-start(f32[2,64,256]{2,1,0:T(8,128)S(1)} %collective-permute-done.1.refs_2_), channel_id=1, source_target_pairs={{0,4},{4,12},{12,8},{8,0},{1,5},{5,13},{13,9},{9,1},{2,6},{6,14},{... | collective-permute-start | bytes 393224 | tf_op jit(solution)/shard_map/ppermute | solution.py:186
  19.9 12.1 %collective-permute-start.5 = (f32[4,64,256]{2,1,0:T(8,128)S(1)}, f32[4,64,256]{2,1,0:T(8,128)S(1)}, u32[]{:S(2)}, u32[]{:S(2)}) collective-permute-start(f32[4,64,256]{2,1,0:T(8,128)S(1)} %pad_maximum_fusion), channel_id=1, source_target_pairs={{0,1},{1,2},{2,3},{4,5},{5,6},{6,7},{8,9},{9,10},{10,11},{12,13},{... | collective-permute-start | bytes 786440 | tf_op jit(solution)/shard_map/ppermute | solution.py:18
  26.4 2.1 %copy-start.3 = (s32[8,16]{1,0:T(8,128)S(1)}, s32[8,16]{1,0:T(8,128)}, u32[]{:S(2)}) copy-start(s32[8,16]{1,0:T(8,128)} %allowed_ref.9) | copy-start | bytes 1540
  26.4 8.0 %collective-permute-start.6 = (f32[4,64,256]{2,1,0:T(8,128)S(1)}, f32[4,64,256]{2,1,0:T(8,128)S(1)}, u32[]{:S(2)}, u32[]{:S(2)}) collective-permute-start(f32[4,64,256]{2,1,0:T(8,128)S(1)} %pad_maximum_fusion.1), channel_id=1, source_target_pairs={{1,0},{2,1},{3,2},{5,4},{6,5},{7,6},{9,8},{10,9},{11,10},{13,12},{... | collective-permute-start | bytes 786440 | tf_op jit(solution)/shard_map/ppermute | solution.py:18
  28.6 1.7 %copy-start = (s32[8]{0:T(128)S(1)}, s32[8]{0:T(128)}, u32[]{:S(2)}) copy-start(s32[8]{0:T(128)} %shifts_ref.9) | copy-start | bytes 100
  31.4 9.2 %collective-permute-start.10 = (f32[2,64,256]{2,1,0:T(8,128)S(1)}, f32[2,64,256]{2,1,0:T(8,128)S(1)}, u32[]{:S(2)}, u32[]{:S(2)}) collective-permute-start(f32[2,64,256]{2,1,0:T(8,128)S(1)} %first_inner.1), channel_id=1, source_target_pairs={{0,4},{4,12},{12,8},{8,0},{1,5},{5,13},{13,9},{9,1},{2,6},{6,14},{... | collective-permute-start | bytes 393224 | tf_op jit(solution)/shard_map/ppermute | solution.py:230
  36.9 6.8 %collective-permute-start.7 = (f32[2,64,256]{2,1,0:T(8,128)S(1)}, f32[2,64,256]{2,1,0:T(8,128)S(1)}, u32[]{:S(2)}, u32[]{:S(2)}) collective-permute-start(f32[2,64,256]{2,1,0:T(8,128)S(1)} %first_outer.1), channel_id=1, source_target_pairs={{0,4},{4,12},{12,8},{8,0},{1,5},{5,13},{13,9},{9,1},{2,6},{6,14},{... | collective-permute-start | bytes 393224 | tf_op jit(solution)/shard_map/ppermute | solution.py:231
  40.7 6.5 %collective-permute-start.11 = (f32[2,64,256]{2,1,0:T(8,128)S(1)}, f32[2,64,256]{2,1,0:T(8,128)S(1)}, u32[]{:S(2)}, u32[]{:S(2)}) collective-permute-start(f32[2,64,256]{2,1,0:T(8,128)S(1)} %add.34), channel_id=1, source_target_pairs={{0,4},{4,12},{12,8},{8,0},{1,5},{5,13},{13,9},{9,1},{2,6},{6,14},{... | collective-permute-start | bytes 393224 | tf_op jit(solution)/shard_map/ppermute | solution.py:230
  43.7 6.4 %collective-permute-start.8 = (f32[2,64,256]{2,1,0:T(8,128)S(1)}, f32[2,64,256]{2,1,0:T(8,128)S(1)}, u32[]{:S(2)}, u32[]{:S(2)}) collective-permute-start(f32[2,64,256]{2,1,0:T(8,128)S(1)} %add.31), channel_id=1, source_target_pairs={{0,4},{4,12},{12,8},{8,0},{1,5},{5,13},{13,9},{9,1},{2,6},{6,14},{... | collective-permute-start | bytes 393224 | tf_op jit(solution)/shard_map/ppermute | solution.py:231
  47.2 6.0 %collective-permute-start.12 = (f32[2,64,256]{2,1,0:T(8,128)S(1)}, f32[2,64,256]{2,1,0:T(8,128)S(1)}, u32[]{:S(2)}, u32[]{:S(2)}) collective-permute-start(f32[2,64,256]{2,1,0:T(8,128)S(1)} %add.35), channel_id=1, source_target_pairs={{0,4},{4,12},{12,8},{8,0},{1,5},{5,13},{13,9},{9,1},{2,6},{6,14},{... | collective-permute-start | bytes 393224 | tf_op jit(solution)/shard_map/ppermute | solution.py:230
  50.1 4.8 %collective-permute-start.9 = (f32[2,64,256]{2,1,0:T(8,128)S(1)}, f32[2,64,256]{2,1,0:T(8,128)S(1)}, u32[]{:S(2)}, u32[]{:S(2)}) collective-permute-start(f32[2,64,256]{2,1,0:T(8,128)S(1)} %add.32), channel_id=1, source_target_pairs={{0,4},{4,12},{12,8},{8,0},{1,5},{5,13},{13,9},{9,1},{2,6},{6,14},{... | collective-permute-start | bytes 393224 | tf_op jit(solution)/shard_map/ppermute | solution.py:231

commit v9 on v8

--- a/solution.py
+++ b/solution.py
@@ -28,6 +28,18 @@
     place = jnp.where(me == 0, 0, jnp.where(lax.rem(me, 2) == 1, (me + 1) // 2, n - me // 2))
     at = lax.rem(place - steps_back + 2 * n, n)
     return jnp.where(at == 0, 0, jnp.where(at <= n // 2, 2 * at - 1, 2 * (n - at)))
+
+
+def on_line(n):
+    return n == 4
+
+
+def block_owner(n, j):
+    return jnp.bitwise_xor(lax.axis_index("op"), j) if on_line(n) else ring_place(n, j)
+
+
+def chunk_target(n, step):
+    return jnp.bitwise_xor(lax.axis_index("op"), n - 1 - step) if on_line(n) else ring_place(n, step + 1)
 
 
 def split(x):
@@ -60,7 +72,7 @@
 def place_rows(n, target, blocks):
     for j, block in enumerate(blocks):
         rows = block.shape[-2]
-        target[..., pl.ds(pl.multiple_of(ring_place(n, j) * rows, rows), rows), :] = block
+        target[..., pl.ds(pl.multiple_of(block_owner(n, j) * rows, rows), rows), :] = block
 
 
 def assemble(n, *refs):
@@ -81,7 +93,7 @@
 
 
 def chunk_left(n, step, left_parts):
-    return left_parts[ring_place(n, step + 1)].reshape(-1, left_parts.shape[-1])
+    return left_parts[chunk_target(n, step)].reshape(-1, left_parts.shape[-1])
 
 
 def own_sectors(n, allowed_ref, *refs):
@@ -105,8 +117,7 @@
         first_product(left, outside[i], allowed_ref, first - 1 + i * (nloc + 1), high.at[i], low.at[i])
 
 
-def second_product(blocks_of, shifts_ref, high, low, right_hi, right_lo, out):
-    rows, width = out.shape[1:]
+def second_product(blocks_of, shifts_ref, high, low, right_hi, right_lo, rows):
 
     def left(parts):
         columns = []
@@ -115,14 +126,15 @@
             columns.append(jnp.concatenate(blocks_of(parts, shifts_ref[k], at)))
         return jnp.concatenate(columns, axis=1)
 
-    out[...] = dot3((left(high), left(low)), (right_hi[...], right_lo[...])).reshape(out.shape)
+    total = dot3((left(high), left(low)), (right_hi[...], right_lo[...]))
+    return total.reshape(-1, rows, total.shape[1])
 
 
 def first_inner(nloc, shifts_ref, high, low, right_hi, right_lo, out):
     def blocks_of(own, shift, at):
         return [own[t - shift, at] for t in range(1, nloc - 1)]
 
-    second_product(blocks_of, shifts_ref, high, low, right_hi, right_lo, out)
+    out[...] = second_product(blocks_of, shifts_ref, high, low, right_hi, right_lo, out.shape[1])
 
 
 def first_outer(nloc, shifts_ref, high, low, end_high, end_low, right_hi, right_lo, out):
@@ -132,10 +144,11 @@
         end = jnp.where(shift == -1, ends[1, at], own[jnp.minimum(nloc - 1 - shift, nloc - 1), at])
         return [start, end]
 
-    second_product(blocks_of, shifts_ref, (high, end_high), (low, end_low), right_hi, right_lo, out)
-
-
-def later_chunk(n, nloc, step, shifts_ref, allowed_ref, outer, inner, outside, left_parts, right_hi, right_lo, outer_out, inner_out, high, low):
+    out[...] = second_product(blocks_of, shifts_ref, (high, end_high), (low, end_low), right_hi, right_lo, out.shape[1])
+
+
+def later_chunk(n, nloc, step, shifts_ref, allowed_ref, outer, inner, outside, left_parts, right_hi, right_lo, *refs):
+    out, high, low = refs[-3:]
     left = chunk_left(n, step, left_parts)
     first = lax.axis_index(("sec", "sub")) * nloc
     sources = [outside.at[0], outer.at[0], *[inner.at[i] for i in range(nloc - 2)], outer.at[1], outside.at[1]]
@@ -148,8 +161,9 @@
     def outer_blocks(parts, shift, at):
         return [parts[t + 1 - shift, at] for t in (0, nloc - 1)]
 
-    second_product(inner_blocks, shifts_ref, high, low, right_hi, right_lo, inner_out)
-    second_product(outer_blocks, shifts_ref, high, low, right_hi, right_lo, outer_out)
+    out[1 : nloc - 1] = second_product(inner_blocks, shifts_ref, high, low, right_hi, right_lo, out.shape[1])
+    ends = second_product(outer_blocks, shifts_ref, high, low, right_hi, right_lo, out.shape[1])
+    out[0], out[nloc - 1] = ends[0], ends[1]
 
 
 def call(body, name, flops, out_shape, in_specs, operands, scratch=()):
@@ -165,11 +179,51 @@
     )(*operands)
 
 
+INWARDS, ACROSS, OUTWARDS, PAIRS = [(0, 1), (3, 2)], [(1, 2), (2, 1)], [(1, 0), (2, 3)], [(0, 1), (1, 0), (2, 3), (3, 2)]
+
+
+def gather(n, psi, zero):
+    nloc = psi.shape[0]
+    halves = [lambda b: b[:: nloc - 1], lambda b: b[1 : nloc - 1]]
+    if not on_line(n):
+        blocks = [psi]
+        for _ in range(n - 1):
+            blocks.append(lax.ppermute(blocks[-1], "op", ring_route(n)))
+        return [[part(b) for b in blocks] for part in halves]
+    one = lax.ppermute(psi, "op", PAIRS)
+    three = lax.ppermute(psi, "op", ACROSS)
+    far = lax.ppermute(one + zero, "op", ACROSS)
+    two = far + lax.ppermute(three + zero, "op", OUTWARDS)
+    three, far = [lax.optimization_barrier([part(b) for part in halves]) for b in (three, far)]
+    last = [t + lax.ppermute(f, "op", OUTWARDS) for t, f in zip(three, far)]
+    return [[part(psi), part(one), part(two), end] for part, end in zip(halves, last)]
+
+
+def joined(outer, inner):
+    return jnp.concatenate([outer[:1], inner, outer[1:]])
+
+
+def scatter(n, outer, inner, mine):
+    first = joined(outer, inner)
+    if not on_line(n):
+        result = first
+        for step in range(1, n):
+            result = lax.ppermute(result, "op", ring_route(n)) + mine(step)
+        return result
+    from_end = joined(lax.ppermute(outer, "op", INWARDS), lax.ppermute(inner, "op", INWARDS))
+    second = mine(1)
+    near = lax.ppermute(second, "op", INWARDS)
+    through = second + from_end
+    far = lax.ppermute(through, "op", ACROSS)
+    across = lax.ppermute(first + near, "op", ACROSS)
+    pair = lax.ppermute(mine(2, through) + far, "op", PAIRS)
+    return mine(3) + across + pair
+
+
 def shards(psi, left_ops, right_ops, shifts, allowed):
     nloc, rows, width = psi.shape
     kops = left_ops.shape[0]
     n = lax.axis_size("op")
-    route = ring_route(n)
     one = 6 * width**3
 
     tall = jax.ShapeDtypeStruct((kops * width, width), BF16)
@@ -179,12 +233,7 @@
         prepare, "prepare", 4 * kops * one, [parts, tall, tall, zero], [VMEM] * 2, [left_ops, right_ops]
     )
 
-    blocks = [psi, lax.ppermute(psi, "op", route)]
-    outer, inner = [[b[:: nloc - 1] for b in blocks], [b[1 : nloc - 1] for b in blocks]]
-    for step in range(1, n - 1):
-        outer.append(lax.ppermute(outer[-1] + zero[0, 0] if step == 1 else outer[-1], "op", route))
-        inner.append(lax.ppermute(inner[-1] + zero[0, 0] if step == 1 else inner[-1], "op", route))
-
+    outer, inner = gather(n, psi, zero[0, 0])
     above = shifted(jnp.concatenate([b[1:] for b in outer]), ("sec", "sub"), 1)
     below = shifted(jnp.concatenate([b[:1] for b in outer]), ("sec", "sub"), -1)
 
@@ -217,19 +266,15 @@
         [SMEM] + [VMEM] * 6, [shifts, *own, *ends, right_hi, right_lo],
     )
 
-    def mine(step):
+    def mine(step, *before):
         return call(
-            functools.partial(later_chunk, n, nloc, step), "chunk", 4 * nloc * kops * one // n, [chunk, chunk_inner],
-            [SMEM] * 2 + [VMEM] * 6,
-            [shifts, allowed, parts_outer, parts_inner, parts_outside, left_parts, right_hi, right_lo],
+            functools.partial(later_chunk, n, nloc, step), "chunk", 4 * nloc * kops * one // n,
+            jax.ShapeDtypeStruct((nloc, rows, width), F32), [SMEM] * 2 + [VMEM] * 6 + [pl.BlockSpec(memory_space=pl.ANY)] * len(before),
+            [shifts, allowed, parts_outer, parts_inner, parts_outside, left_parts, right_hi, right_lo, *before],
             [pltpu.VMEM((nloc + 2, kops * rows, width), BF16)] * 2,
         )
 
-    for step in range(1, n):
-        next_outer, next_inner = mine(step)
-        result_inner = lax.ppermute(result_inner, "op", route) + next_inner
-        result_outer = lax.ppermute(result_outer, "op", route) + next_outer
-    return jnp.concatenate([result_outer[:1], result_inner, result_outer[1:]])
+    return scatter(n, result_outer, result_inner, mine)
 
 
 def solution(mesh):

time: 55.8 us -> 59.9 us (1.073)
  starting transfers between devices: 22.5 us -> 25.7 us
    ppermute x11 -> x12, starting transfers between devices: 14.1 us -> 17.3 us  [the longest x1 4.52 us: scatter(): pair = lax.ppermute(mine(2, through) + far, 'op', PAIRS)]
    ppermute x11 -> x12, waiting for transfers between devices: 10.7 us -> 11.8 us  [the longest x1 5.98 us: gather(): two = far + lax.ppermute(three + zero, 'op', OUTWARDS)]
    add x7 -> x9, other arithmetic: 0.18 us -> 1.05 us  [the longest x1 0.76 us: scatter(): return mine(3) + across + pair]
    ppermute x2, waiting for transfers between devices: 2.38 us -> 1.54 us  [shifted(): return lax.ppermute(block, axis, route)]
    concatenate x1 -> x0, other arithmetic: 0.72 us -> none  [shards(): return jnp.concatenate([result_outer[:1], result_inner, result_outer[1:]])]
  transfers between devices with their start and end apart: 13 -> 14, of which waited for: 7 -> 5; matrix products, arithmetic and copies ran while one was open for 0% -> 1% of each run, Pallas kernels for 28% -> 26%
where the time goes in v9:
time: 59.9 us; the launch traced here: 59.5 us
  starting transfers between devices  25.7 us (43%)
  Pallas kernels  15.6 us (26%)
  waiting for transfers between devices  13.4 us (22%)
  local copies, waits for them, and re-layouts  3.35 us (6%)
  other arithmetic  1.1 us (2%)
    pallas_call x9, Pallas kernels, call(): pl.pallas_call(body, name=name, out_shape=out_shape, in_specs=in_specs, o...  15.6 us
    ppermute x2, starting transfers between devices, shifted(): return lax.ppermute(block, axis, route)  8.42 us
    ppermute x1, waiting for transfers between devices, gather(): two = far + lax.ppermute(three + zero, 'op', OUTWARDS)  5.98 us
    ppermute x1, starting transfers between devices, scatter(): pair = lax.ppermute(mine(2, through) + far, 'op', PAIRS)  4.52 us
    ppermute x2, waiting for transfers between devices, gather(): last = [t + lax.ppermute(f, 'op', OUTWARDS) for t, f in zip(three, far)]  3.83 us
    unnamed x10, local copies, waits for them, and re-layouts  3.19 us
    ppermute x2, starting transfers between devices, gather(): last = [t + lax.ppermute(f, 'op', OUTWARDS) for t, f in zip(three, far)]  2.58 us
    ppermute x1, starting transfers between devices, gather(): one = lax.ppermute(psi, 'op', PAIRS)  2.13 us
  transfers between devices with their start and end apart: 14, of which 5 were waited for; matrix products, arithmetic and copies ran while one was open for 1% of the time, Pallas kernels for 26%

profile of v9, /device:TPU:1, one launch (start us, length us, event | category | flops | bytes accessed | tf_op | source)
XLA Modules:
  0.0 59.5 jit_solution(15086215701588669259)
XLA Ops:
  0.0 2.1 %collective-permute-start = (f32[4,64,256]{2,1,0:T(8,128)}, f32[4,64,256]{2,1,0:T(8,128)S(1)}, u32[]{:S(2)}, u32[]{:S(2)}) collective-permute-start(f32[4,64,256]{2,1,0:T(8,128)} %param.5), channel_id=1, source_target_pairs={{0,4},{4,0},{8,12},{12,8},{1,5},{5,1},{9,13},{13,9},{2,6},{6,2},{1... | collective-permute-start | bytes 786440 | tf_op jit(solution)/shard_map/ppermute | solution.py:193
  2.1 0.7 %collective-permute-start.2 = (f32[4,64,256]{2,1,0:T(8,128)}, f32[4,64,256]{2,1,0:T(8,128)S(1)}, u32[]{:S(2)}, u32[]{:S(2)}) collective-permute-start(f32[4,64,256]{2,1,0:T(8,128)} %param.5), channel_id=1, source_target_pairs={{4,8},{8,4},{5,9},{9,5},{6,10},{10,6},{7,11},{11,7},{20,24},{24,20... | collective-permute-start | bytes 786440 | tf_op jit(solution)/shard_map/ppermute | solution.py:194
  2.8 0.0 copy-start.1
  2.8 1.6 %copy-done.1 = f32[8,256,256]{2,1,0:T(8,128)S(1)} copy-done((f32[8,256,256]{2,1,0:T(8,128)S(1)}, f32[8,256,256]{2,1,0:T(8,128)}, u32[]{:S(2)}) %copy-start.1) | copy-done | bytes 2097176
  4.4 1.6 %copy-done.2 = f32[8,256,256]{2,1,0:T(8,128)S(1)} copy-done((f32[8,256,256]{2,1,0:T(8,128)S(1)}, f32[8,256,256]{2,1,0:T(8,128)}, u32[]{:S(2)}) %copy-start.2) | copy-done | bytes 2097176
  6.0 1.1 %prepare.1 = (bf16[4,8,64,768]{3,2,1,0:T(8,128)(2,1)S(1)}, bf16[2048,256]{1,0:T(8,128)(2,1)S(1)}, bf16[2048,256]{1,0:T(8,128)(2,1)S(1)}, f32[1,128]{1,0:T(1,128)S(1)}) custom-call(f32[8,256,256]{2,1,0:T(8,128)S(1)} %copy-done.1, f32[8,256,256]{2,1,0:T(8,128)S(1)} %copy-done.2), custom_call_target="tpu_custom_call" | custom-call | flops 3221225472 | bytes 1048576 | tf_op jit(solution)/shard_map/prepare/pallas_call | solution.py:170
  7.1 0.0 copy-done.4
  7.1 1.3 %collective-permute-done = f32[4,64,256]{2,1,0:T(8,128)S(1)} collective-permute-done((f32[4,64,256]{2,1,0:T(8,128)}, f32[4,64,256]{2,1,0:T(8,128)S(1)}, u32[]{:S(2)}, u32[]{:S(2)}) %collective-permute-start) | collective-permute-done | bytes 262176 | tf_op jit(solution)/shard_map/ppermute | solution.py:193
  8.4 0.1 broadcast_add_fusion.1
  8.4 0.7 %collective-permute-start.1 = (f32[4,64,256]{2,1,0:T(8,128)S(1)}, f32[4,64,256]{2,1,0:T(8,128)S(1)}, u32[]{:S(2)}, u32[]{:S(2)}) collective-permute-start(f32[4,64,256]{2,1,0:T(8,128)S(1)} %broadcast_add_fusion.1), channel_id=1, source_target_pairs={{4,8},{8,4},{5,9},{9,5},{6,10},{10,6},{7,11},{11,7},{20,24},{24,20... | collective-permute-start | bytes 786440 | tf_op jit(solution)/shard_map/ppermute | solution.py:195
  9.1 0.0 collective-permute-done.2
  9.1 0.1 broadcast_add_fusion
  9.2 1.3 %collective-permute-start.3 = (f32[4,64,256]{2,1,0:T(8,128)S(1)}, f32[4,64,256]{2,1,0:T(8,128)S(1)}, u32[]{:S(2)}, u32[]{:S(2)}) collective-permute-start(f32[4,64,256]{2,1,0:T(8,128)S(1)} %broadcast_add_fusion), channel_id=1, source_target_pairs={{4,0},{8,12},{5,1},{9,13},{6,2},{10,14},{7,3},{11,15},{20,16},{24,... | collective-permute-start | bytes 786440 | tf_op jit(solution)/shard_map/ppermute | solution.py:196
  10.6 0.0 collective-permute-done.1
  10.6 1.3 %collective-permute-start.4 = (f32[2,64,256]{2,1,0:T(8,128)S(1)}, f32[2,64,256]{2,1,0:T(8,128)S(1)}, u32[]{:S(2)}, u32[]{:S(2)}) collective-permute-start(f32[2,64,256]{2,1,0:T(8,128)S(1)} %get-tuple-element.21), channel_id=1, source_target_pairs={{4,0},{8,12},{5,1},{9,13},{6,2},{10,14},{7,3},{11,15},{20,16},{24,... | collective-permute-start | bytes 393224 | tf_op jit(solution)/shard_map/ppermute | solution.py:198
  11.9 1.3 %collective-permute-start.5 = (f32[2,64,256]{2,1,0:T(8,128)S(1)}, f32[2,64,256]{2,1,0:T(8,128)S(1)}, u32[]{:S(2)}, u32[]{:S(2)}) collective-permute-start(f32[2,64,256]{2,1,0:T(8,128)S(1)} %get-tuple-element.23), channel_id=1, source_target_pairs={{4,0},{8,12},{5,1},{9,13},{6,2},{10,14},{7,3},{11,15},{20,16},{24,... | collective-permute-start | bytes 393224 | tf_op jit(solution)/shard_map/ppermute | solution.py:198
  13.2 6.0 %collective-permute-done.3 = f32[4,64,256]{2,1,0:T(8,128)S(1)} collective-permute-done((f32[4,64,256]{2,1,0:T(8,128)S(1)}, f32[4,64,256]{2,1,0:T(8,128)S(1)}, u32[]{:S(2)}, u32[]{:S(2)}) %collective-permute-start.3) | collective-permute-done | bytes 262176 | tf_op jit(solution)/shard_map/ppermute | solution.py:196
  19.3 3.8 %collective-permute-done.4 = f32[2,64,256]{2,1,0:T(8,128)S(1)} collective-permute-done((f32[2,64,256]{2,1,0:T(8,128)S(1)}, f32[2,64,256]{2,1,0:T(8,128)S(1)}, u32[]{:S(2)}, u32[]{:S(2)}) %collective-permute-start.4) | collective-permute-done | bytes 131104 | tf_op jit(solution)/shard_map/ppermute | solution.py:198
  23.1 0.0 copy-start.3
  23.1 0.2 assemble.1.refs_4_.outer
  23.4 6.5 %collective-permute-start.6 = (f32[4,64,256]{2,1,0:T(8,128)S(1)}, f32[4,64,256]{2,1,0:T(8,128)S(1)}, u32[]{:S(2)}, u32[]{:S(2)}) collective-permute-start(f32[4,64,256]{2,1,0:T(8,128)S(1)} %pad_maximum_fusion), channel_id=1, source_target_pairs={{0,1},{1,2},{2,3},{4,5},{5,6},{6,7},{8,9},{9,10},{10,11},{12,13},{... | collective-permute-start | bytes 786440 | tf_op jit(solution)/shard_map/ppermute | solution.py:18
  29.9 1.9 %collective-permute-start.7 = (f32[4,64,256]{2,1,0:T(8,128)S(1)}, f32[4,64,256]{2,1,0:T(8,128)S(1)}, u32[]{:S(2)}, u32[]{:S(2)}) collective-permute-start(f32[4,64,256]{2,1,0:T(8,128)S(1)} %pad_maximum_fusion.1), channel_id=1, source_target_pairs={{1,0},{2,1},{3,2},{5,4},{6,5},{7,6},{9,8},{10,9},{11,10},{13,12},{... | collective-permute-start | bytes 786440 | tf_op jit(solution)/shard_map/ppermute | solution.py:18
  31.8 0.0 collective-permute-done.5
  31.9 0.0 copy-done.3
  31.9 0.0 copy-start
  31.9 1.7 %own.1 = (bf16[2,768,256]{2,1,0:T(8,128)(2,1)S(1)}, bf16[4,512,256]{2,1,0:T(8,128)(2,1)S(1)}, bf16[4,512,256]{2,1,0:T(8,128)(2,1)S(1)}) custom-call(s32[8,16]{1,0:T(8,128)S(1)} %copy-done.3, f32[2,64,256]{2,1,0:T(8,128)S(1)} %get-tuple-element.37.refs_0_, f32[2,64,256]{2,1,0:T(8,128)S(1)} %get-tuple-element.35.refs_1_, ...), custom_call_target="tpu_custom_call" | custom-call | flops 3221225472 | bytes 1048576 | tf_op jit(solution)/shard_map/own/pallas_call | solution.py:170
  33.6 0.0 copy-done
  33.6 1.1 %first_inner.1 = f32[2,64,256]{2,1,0:T(8,128)S(1)} custom-call(s32[8]{0:T(128)S(1)} %copy-done, bf16[4,512,256]{2,1,0:T(8,128)(2,1)S(1)} %get-tuple-element.29.high, bf16[4,512,256]{2,1,0:T(8,128)(2,1)S(1)} %get-tuple-element.30.low, bf16[2048,256]{1,0:T(8,128)(2,1)S(1)} %get-tuple-element.27.right_hi, bf16[2048,256]{1,0:T(8,128)(2,1)S(1)} %get-tuple-element.28.right_lo), custom_call_target="tpu_custom_call" | custom-call | flops 805306368 | bytes 1048576 | tf_op jit(solution)/shard_map/first_inner/pallas_call | solution.py:170
  34.7 1.3 %collective-permute-start.11 = (f32[2,64,256]{2,1,0:T(8,128)S(1)}, f32[2,64,256]{2,1,0:T(8,128)S(1)}, u32[]{:S(2)}, u32[]{:S(2)}) collective-permute-start(f32[2,64,256]{2,1,0:T(8,128)S(1)} %first_inner.1), channel_id=1, source_target_pairs={{0,4},{12,8},{1,5},{13,9},{2,6},{14,10},{3,7},{15,11},{16,20},{28,... | collective-permute-start | bytes 393224 | tf_op jit(solution)/shard_map/ppermute | solution.py:213
  36.0 0.0 collective-permute-done.6.above
  36.0 1.5 %collective-permute-done.7.below = f32[4,64,256]{2,1,0:T(8,128)S(1)} collective-permute-done((f32[4,64,256]{2,1,0:T(8,128)S(1)}, f32[4,64,256]{2,1,0:T(8,128)S(1)}, u32[]{:S(2)}, u32[]{:S(2)}) %collective-permute-start.7) | collective-permute-done | bytes 262176 | tf_op jit(solution)/shard_map/ppermute | solution.py:18
  37.6 1.3 %outside.1 = (bf16[2,768,256]{2,1,0:T(8,128)(2,1)S(1)}, bf16[2,512,256]{2,1,0:T(8,128)(2,1)S(1)}, bf16[2,512,256]{2,1,0:T(8,128)(2,1)S(1)}) custom-call(s32[8,16]{1,0:T(8,128)S(1)} %copy-done.3, f32[4,64,256]{2,1,0:T(8,128)S(1)} %collective-permute-done.6.above, f32[4,64,256]{2,1,0:T(8,128)S(1)} %collective-permute-done.7.below, ...), custom_call_target="tpu_custom_call" | custom-call | flops 1610612736 | bytes 1048576 | tf_op jit(solution)/shard_map/outside/pallas_call | solution.py:170
  38.9 1.2 %first_outer.1 = f32[2,64,256]{2,1,0:T(8,128)S(1)} custom-call(s32[8]{0:T(128)S(1)} %copy-done, bf16[4,512,256]{2,1,0:T(8,128)(2,1)S(1)} %get-tuple-element.29.high, bf16[4,512,256]{2,1,0:T(8,128)(2,1)S(1)} %get-tuple-element.30.low, bf16[2,512,256]{2,1,0:T(8,128)(2,1)S(1)} %get-tuple-element.31.end_high, ...), custom_call_target="tpu_custom_call" | custom-call | flops 805306368 | bytes 1048576 | tf_op jit(solution)/shard_map/first_outer/pallas_call | solution.py:170
  40.0 1.5 %collective-permute-start.10 = (f32[2,64,256]{2,1,0:T(8,128)S(1)}, f32[2,64,256]{2,1,0:T(8,128)S(1)}, u32[]{:S(2)}, u32[]{:S(2)}) collective-permute-start(f32[2,64,256]{2,1,0:T(8,128)S(1)} %first_outer.1), channel_id=1, source_target_pairs={{0,4},{12,8},{1,5},{13,9},{2,6},{14,10},{3,7},{15,11},{16,20},{28,... | collective-permute-start | bytes 393224 | tf_op jit(solution)/shard_map/ppermute | solution.py:213
  41.5 3.0 %chunk.4 = f32[4,64,256]{2,1,0:T(8,128)S(1)} custom-call(s32[8]{0:T(128)S(1)} %copy-done, s32[8,16]{1,0:T(8,128)S(1)} %copy-done.3, bf16[2,768,256]{2,1,0:T(8,128)(2,1)S(1)} %assemble.1.refs_4_.outer, bf16[2,768,256]{2,1,0:T(8,128)(2,1)S(1)} %get-tuple-element.25.inner, bf16[2,768,256]{2,1,0:T(8,128)(2,1)S(1)} %get-tuple-element.26.outside, ...), custom_call_target="tpu_custom_call" | custom-call | flops 3221225472 | bytes 1048576 | tf_op jit(solution)/shard_map/chunk/pallas_call | solution.py:170
  44.5 1.3 %collective-permute-start.8 = (f32[4,64,256]{2,1,0:T(8,128)S(1)}, f32[4,64,256]{2,1,0:T(8,128)S(1)}, u32[]{:S(2)}, u32[]{:S(2)}) collective-permute-start(f32[4,64,256]{2,1,0:T(8,128)S(1)} %chunk.4), channel_id=1, source_target_pairs={{0,4},{12,8},{1,5},{13,9},{2,6},{14,10},{3,7},{15,11},{16,20},{28,... | collective-permute-start | bytes 786440 | tf_op jit(solution)/shard_map/ppermute | solution.py:215
  45.9 0.0 collective-permute-done.10
  45.9 0.0 collective-permute-done.11
  46.0 0.7 %collective-permute-start.12 = (f32[4,64,256]{2,1,0:T(8,128)S(1)}, f32[4,64,256]{2,1,0:T(8,128)S(1)}, u32[]{:S(2)}, u32[]{:S(2)}) collective-permute-start(f32[4,64,256]{2,1,0:T(8,128)S(1)} %maximum_add_fusion.1.refs_0_), channel_id=1, source_target_pairs={{4,8},{8,4},{5,9},{9,5},{6,10},{10,6},{7,11},{11,7},{20,24},{24,20... | collective-permute-start | bytes 786440 | tf_op jit(solution)/shard_map/ppermute | solution.py:217
  46.6 3.0 %chunk.5 = f32[4,64,256]{2,1,0:T(8,128)S(1)} custom-call(s32[8]{0:T(128)S(1)} %copy-done, s32[8,16]{1,0:T(8,128)S(1)} %copy-done.3, bf16[2,768,256]{2,1,0:T(8,128)(2,1)S(1)} %assemble.1.refs_4_.outer, bf16[2,768,256]{2,1,0:T(8,128)(2,1)S(1)} %get-tuple-element.25.inner, bf16[2,768,256]{2,1,0:T(8,128)(2,1)S(1)} %get-tuple-element.26.outside, ...), custom_call_target="tpu_custom_call" | custom-call | flops 3221225472 | bytes 1048576 | tf_op jit(solution)/shard_map/chunk/pallas_call | solution.py:170
  49.7 0.0 collective-permute-done.8
  49.7 0.7 %collective-permute-start.9 = (f32[4,64,256]{2,1,0:T(8,128)S(1)}, f32[4,64,256]{2,1,0:T(8,128)S(1)}, u32[]{:S(2)}, u32[]{:S(2)}) collective-permute-start(f32[4,64,256]{2,1,0:T(8,128)S(1)} %maximum_add_fusion), channel_id=1, source_target_pairs={{4,8},{8,4},{5,9},{9,5},{6,10},{10,6},{7,11},{11,7},{20,24},{24,20... | collective-permute-start | bytes 786440 | tf_op jit(solution)/shard_map/ppermute | solution.py:218
  50.4 0.0 collective-permute-done.12
  50.5 4.5 %collective-permute-start.13 = (f32[4,64,256]{2,1,0:T(8,128)S(1)}, f32[4,64,256]{2,1,0:T(8,128)S(1)}, u32[]{:S(2)}, u32[]{:S(2)}) collective-permute-start(f32[4,64,256]{2,1,0:T(8,128)S(1)} %add.43), channel_id=1, source_target_pairs={{0,4},{4,0},{8,12},{12,8},{1,5},{5,1},{9,13},{13,9},{2,6},{6,2},{1... | collective-permute-start | bytes 786440 | tf_op jit(solution)/shard_map/ppermute | solution.py:219
  55.0 3.0 %chunk.3 = f32[4,64,256]{2,1,0:T(8,128)S(1)} custom-call(s32[8]{0:T(128)S(1)} %copy-done, s32[8,16]{1,0:T(8,128)S(1)} %copy-done.3, bf16[2,768,256]{2,1,0:T(8,128)(2,1)S(1)} %assemble.1.refs_4_.outer, bf16[2,768,256]{2,1,0:T(8,128)(2,1)S(1)} %get-tuple-element.25.inner, bf16[2,768,256]{2,1,0:T(8,128)(2,1)S(1)} %get-tuple-element.26.outside, ...), custom_call_target="tpu_custom_call" | custom-call | flops 3221225472 | bytes 1048576 | tf_op jit(solution)/shard_map/chunk/pallas_call | solution.py:170
  58.0 0.0 collective-permute-done.9
  58.0 0.7 %collective-permute-done.13 = f32[4,64,256]{2,1,0:T(8,128)S(1)} collective-permute-done((f32[4,64,256]{2,1,0:T(8,128)S(1)}, f32[4,64,256]{2,1,0:T(8,128)S(1)}, u32[]{:S(2)}, u32[]{:S(2)}) %collective-permute-start.13) | collective-permute-done | bytes 262176 | tf_op jit(solution)/shard_map/ppermute | solution.py:219
  58.8 0.8 %add_add_fusion = f32[4,64,256]{2,1,0:T(8,128)} fusion(f32[4,64,256]{2,1,0:T(8,128)S(1)} %collective-permute-done.13, f32[4,64,256]{2,1,0:T(8,128)S(1)} %chunk.3, f32[4,64,256]{2,1,0:T(8,128)S(1)} %collective-permute-done.9), kind=kLoop, calls=%fused_computation.4 | loop fusion | flops 131072 | bytes 1048576 | tf_op jit(solution)/shard_map/add | solution.py:220
  (20 shorter events, 0.4 us)
Async XLA Ops:
  0.0 8.4 %collective-permute-start = (f32[4,64,256]{2,1,0:T(8,128)}, f32[4,64,256]{2,1,0:T(8,128)S(1)}, u32[]{:S(2)}, u32[]{:S(2)}) collective-permute-start(f32[4,64,256]{2,1,0:T(8,128)} %param.5), channel_id=1, source_target_pairs={{0,4},{4,0},{8,12},{12,8},{1,5},{5,1},{9,13},{13,9},{2,6},{6,2},{1... | collective-permute-start | bytes 786440 | tf_op jit(solution)/shard_map/ppermute | solution.py:193
  2.1 7.0 %collective-permute-start.2 = (f32[4,64,256]{2,1,0:T(8,128)}, f32[4,64,256]{2,1,0:T(8,128)S(1)}, u32[]{:S(2)}, u32[]{:S(2)}) collective-permute-start(f32[4,64,256]{2,1,0:T(8,128)} %param.5), channel_id=1, source_target_pairs={{4,8},{8,4},{5,9},{9,5},{6,10},{10,6},{7,11},{11,7},{20,24},{24,20... | collective-permute-start | bytes 786440 | tf_op jit(solution)/shard_map/ppermute | solution.py:194
  2.8 1.6 %copy-start.1 = (f32[8,256,256]{2,1,0:T(8,128)S(1)}, f32[8,256,256]{2,1,0:T(8,128)}, u32[]{:S(2)}) copy-start(f32[8,256,256]{2,1,0:T(8,128)} %left_ref.1) | copy-start | bytes 6291460
  4.4 1.6 %copy-start.2 = (f32[8,256,256]{2,1,0:T(8,128)S(1)}, f32[8,256,256]{2,1,0:T(8,128)}, u32[]{:S(2)}) copy-start(f32[8,256,256]{2,1,0:T(8,128)} %right_ref.1) | copy-start | bytes 6291460
  6.0 1.1 %copy-start.4 = (f32[4,64,256]{2,1,0:T(8,128)S(1)}, f32[4,64,256]{2,1,0:T(8,128)}, u32[]{:S(2)}) copy-start(f32[4,64,256]{2,1,0:T(8,128)} %param.5) | copy-start | bytes 786436
  8.4 2.1 %collective-permute-start.1 = (f32[4,64,256]{2,1,0:T(8,128)S(1)}, f32[4,64,256]{2,1,0:T(8,128)S(1)}, u32[]{:S(2)}, u32[]{:S(2)}) collective-permute-start(f32[4,64,256]{2,1,0:T(8,128)S(1)} %broadcast_add_fusion.1), channel_id=1, source_target_pairs={{4,8},{8,4},{5,9},{9,5},{6,10},{10,6},{7,11},{11,7},{20,24},{24,20... | collective-permute-start | bytes 786440 | tf_op jit(solution)/shard_map/ppermute | solution.py:195
  9.2 10.0 %collective-permute-start.3 = (f32[4,64,256]{2,1,0:T(8,128)S(1)}, f32[4,64,256]{2,1,0:T(8,128)S(1)}, u32[]{:S(2)}, u32[]{:S(2)}) collective-permute-start(f32[4,64,256]{2,1,0:T(8,128)S(1)} %broadcast_add_fusion), channel_id=1, source_target_pairs={{4,0},{8,12},{5,1},{9,13},{6,2},{10,14},{7,3},{11,15},{20,16},{24,... | collective-permute-start | bytes 786440 | tf_op jit(solution)/shard_map/ppermute | solution.py:196
  10.6 12.5 %collective-permute-start.4 = (f32[2,64,256]{2,1,0:T(8,128)S(1)}, f32[2,64,256]{2,1,0:T(8,128)S(1)}, u32[]{:S(2)}, u32[]{:S(2)}) collective-permute-start(f32[2,64,256]{2,1,0:T(8,128)S(1)} %get-tuple-element.21), channel_id=1, source_target_pairs={{4,0},{8,12},{5,1},{9,13},{6,2},{10,14},{7,3},{11,15},{20,16},{24,... | collective-permute-start | bytes 393224 | tf_op jit(solution)/shard_map/ppermute | solution.py:198
  11.9 19.9 %collective-permute-start.5 = (f32[2,64,256]{2,1,0:T(8,128)S(1)}, f32[2,64,256]{2,1,0:T(8,128)S(1)}, u32[]{:S(2)}, u32[]{:S(2)}) collective-permute-start(f32[2,64,256]{2,1,0:T(8,128)S(1)} %get-tuple-element.23), channel_id=1, source_target_pairs={{4,0},{8,12},{5,1},{9,13},{6,2},{10,14},{7,3},{11,15},{20,16},{24,... | collective-permute-start | bytes 393224 | tf_op jit(solution)/shard_map/ppermute | solution.py:198
  23.1 8.7 %copy-start.3 = (s32[8,16]{1,0:T(8,128)S(1)}, s32[8,16]{1,0:T(8,128)}, u32[]{:S(2)}) copy-start(s32[8,16]{1,0:T(8,128)} %allowed_ref.9) | copy-start | bytes 1540
  23.4 12.7 %collective-permute-start.6 = (f32[4,64,256]{2,1,0:T(8,128)S(1)}, f32[4,64,256]{2,1,0:T(8,128)S(1)}, u32[]{:S(2)}, u32[]{:S(2)}) collective-permute-start(f32[4,64,256]{2,1,0:T(8,128)S(1)} %pad_maximum_fusion), channel_id=1, source_target_pairs={{0,1},{1,2},{2,3},{4,5},{5,6},{6,7},{8,9},{9,10},{10,11},{12,13},{... | collective-permute-start | bytes 786440 | tf_op jit(solution)/shard_map/ppermute | solution.py:18
  29.9 7.7 %collective-permute-start.7 = (f32[4,64,256]{2,1,0:T(8,128)S(1)}, f32[4,64,256]{2,1,0:T(8,128)S(1)}, u32[]{:S(2)}, u32[]{:S(2)}) collective-permute-start(f32[4,64,256]{2,1,0:T(8,128)S(1)} %pad_maximum_fusion.1), channel_id=1, source_target_pairs={{1,0},{2,1},{3,2},{5,4},{6,5},{7,6},{9,8},{10,9},{11,10},{13,12},{... | collective-permute-start | bytes 786440 | tf_op jit(solution)/shard_map/ppermute | solution.py:18
  31.9 1.7 %copy-start = (s32[8]{0:T(128)S(1)}, s32[8]{0:T(128)}, u32[]{:S(2)}) copy-start(s32[8]{0:T(128)} %shifts_ref.9) | copy-start | bytes 100
  34.7 11.2 %collective-permute-start.11 = (f32[2,64,256]{2,1,0:T(8,128)S(1)}, f32[2,64,256]{2,1,0:T(8,128)S(1)}, u32[]{:S(2)}, u32[]{:S(2)}) collective-permute-start(f32[2,64,256]{2,1,0:T(8,128)S(1)} %first_inner.1), channel_id=1, source_target_pairs={{0,4},{12,8},{1,5},{13,9},{2,6},{14,10},{3,7},{15,11},{16,20},{28,... | collective-permute-start | bytes 393224 | tf_op jit(solution)/shard_map/ppermute | solution.py:213
  40.0 5.8 %collective-permute-start.10 = (f32[2,64,256]{2,1,0:T(8,128)S(1)}, f32[2,64,256]{2,1,0:T(8,128)S(1)}, u32[]{:S(2)}, u32[]{:S(2)}) collective-permute-start(f32[2,64,256]{2,1,0:T(8,128)S(1)} %first_outer.1), channel_id=1, source_target_pairs={{0,4},{12,8},{1,5},{13,9},{2,6},{14,10},{3,7},{15,11},{16,20},{28,... | collective-permute-start | bytes 393224 | tf_op jit(solution)/shard_map/ppermute | solution.py:213
  44.5 5.1 %collective-permute-start.8 = (f32[4,64,256]{2,1,0:T(8,128)S(1)}, f32[4,64,256]{2,1,0:T(8,128)S(1)}, u32[]{:S(2)}, u32[]{:S(2)}) collective-permute-start(f32[4,64,256]{2,1,0:T(8,128)S(1)} %chunk.4), channel_id=1, source_target_pairs={{0,4},{12,8},{1,5},{13,9},{2,6},{14,10},{3,7},{15,11},{16,20},{28,... | collective-permute-start | bytes 786440 | tf_op jit(solution)/shard_map/ppermute | solution.py:215
  46.0 4.5 %collective-permute-start.12 = (f32[4,64,256]{2,1,0:T(8,128)S(1)}, f32[4,64,256]{2,1,0:T(8,128)S(1)}, u32[]{:S(2)}, u32[]{:S(2)}) collective-permute-start(f32[4,64,256]{2,1,0:T(8,128)S(1)} %maximum_add_fusion.1.refs_0_), channel_id=1, source_target_pairs={{4,8},{8,4},{5,9},{9,5},{6,10},{10,6},{7,11},{11,7},{20,24},{24,20... | collective-permute-start | bytes 786440 | tf_op jit(solution)/shard_map/ppermute | solution.py:217
  49.7 8.3 %collective-permute-start.9 = (f32[4,64,256]{2,1,0:T(8,128)S(1)}, f32[4,64,256]{2,1,0:T(8,128)S(1)}, u32[]{:S(2)}, u32[]{:S(2)}) collective-permute-start(f32[4,64,256]{2,1,0:T(8,128)S(1)} %maximum_add_fusion), channel_id=1, source_target_pairs={{4,8},{8,4},{5,9},{9,5},{6,10},{10,6},{7,11},{11,7},{20,24},{24,20... | collective-permute-start | bytes 786440 | tf_op jit(solution)/shard_map/ppermute | solution.py:218
  50.5 8.3 %collective-permute-start.13 = (f32[4,64,256]{2,1,0:T(8,128)S(1)}, f32[4,64,256]{2,1,0:T(8,128)S(1)}, u32[]{:S(2)}, u32[]{:S(2)}) collective-permute-start(f32[4,64,256]{2,1,0:T(8,128)S(1)} %add.43), channel_id=1, source_target_pairs={{0,4},{4,0},{8,12},{12,8},{1,5},{5,1},{9,13},{13,9},{2,6},{6,2},{1... | collective-permute-start | bytes 786440 | tf_op jit(solution)/shard_map/ppermute | solution.py:219

commit v10 on v8

--- a/solution.py
+++ b/solution.py
@@ -12,10 +12,14 @@
 VMEM = pl.BlockSpec(memory_space=pltpu.VMEM)
 
 
-def shifted(block, axis, distance):
-    devices = range(lax.axis_size(axis))
-    route = [(i - distance, i) for i in devices if i - distance in devices]
-    return lax.ppermute(block, axis, route)
+def sector_group():
+    return lax.axis_index(("sec", "sub"))
+
+
+def swapped(block, odd):
+    groups = lax.axis_size(("sec", "sub"))
+    pairs = [(i, i + 1) for i in range(odd, groups - 1, 2)]
+    return lax.ppermute(block, ("sec", "sub"), pairs + [(j, i) for i, j in pairs])
 
 
 def ring_route(n):
@@ -89,17 +93,18 @@
     assemble(n, *refs[:n], inner, psi)
     left = chunk_left(n, 0, left_parts)
     nloc = high.shape[0]
-    first = lax.axis_index(("sec", "sub")) * nloc
+    first = sector_group() * nloc
     sources = [outer.at[0], *[inner.at[i] for i in range(nloc - 2)], outer.at[1]]
     for i, ref in enumerate(sources):
         first_product(left, ref[...], allowed_ref, first + i, high.at[i], low.at[i])
 
 
-def outside_sectors(n, nloc, allowed_ref, above, below, left_parts, outside, high, low, psi):
-    place_rows(n, psi.at[0], [above[j] for j in range(n)])
-    place_rows(n, psi.at[1], [below[j] for j in range(n)])
+def outside_sectors(n, nloc, allowed_ref, paired, apart, left_parts, outside, high, low, psi):
+    odd = lax.rem(sector_group(), 2)
+    place_rows(n, psi.at[odd], [apart[j] for j in range(n)])
+    place_rows(n, psi.at[1 - odd], [paired[j] for j in range(n)])
     left = chunk_left(n, 0, left_parts)
-    first = lax.axis_index(("sec", "sub")) * nloc
+    first = sector_group() * nloc
     for i in range(2):
         outside[i] = stacked(psi[i])
         first_product(left, outside[i], allowed_ref, first - 1 + i * (nloc + 1), high.at[i], low.at[i])
@@ -137,7 +142,7 @@
 
 def later_chunk(n, nloc, step, shifts_ref, allowed_ref, outer, inner, outside, left_parts, right_hi, right_lo, outer_out, inner_out, high, low):
     left = chunk_left(n, step, left_parts)
-    first = lax.axis_index(("sec", "sub")) * nloc
+    first = sector_group() * nloc
     sources = [outside.at[0], outer.at[0], *[inner.at[i] for i in range(nloc - 2)], outer.at[1], outside.at[1]]
     for i, ref in enumerate(sources):
         first_product(left, ref[...], allowed_ref, first - 1 + i, high.at[i], low.at[i])
@@ -185,8 +190,10 @@
         outer.append(lax.ppermute(outer[-1] + zero[0, 0] if step == 1 else outer[-1], "op", route))
         inner.append(lax.ppermute(inner[-1] + zero[0, 0] if step == 1 else inner[-1], "op", route))
 
-    above = shifted(jnp.concatenate([b[1:] for b in outer]), ("sec", "sub"), 1)
-    below = shifted(jnp.concatenate([b[:1] for b in outer]), ("sec", "sub"), -1)
+    even = lax.rem(sector_group(), 2) == 0
+    first_sector, last_sector = jnp.concatenate([b[:1] for b in outer]), jnp.concatenate([b[1:] for b in outer])
+    apart = swapped(jnp.where(even, first_sector, last_sector), 1)
+    paired = swapped(jnp.where(even, last_sector, first_sector), 0)
 
     def split_parts(sectors):
         return jax.ShapeDtypeStruct((sectors, 3 * width, width), BF16)
@@ -210,7 +217,7 @@
     )
     parts_outside, *ends = call(
         functools.partial(outside_sectors, n, nloc), "outside", 2 * kops * one, [split_parts(2), *products(2)],
-        [SMEM] + [VMEM] * 3, [allowed, above, below, left_parts], whole(2),
+        [SMEM] + [VMEM] * 3, [allowed, paired, apart, left_parts], whole(2),
     )
     result_outer = call(
         functools.partial(first_outer, nloc), "first_outer", nloc * kops * one // n, chunk,

time: 55.8 us -> 57.5 us (1.030)
  the two profiles are of different devices: /device:TPU:1 before, /device:TPU:0 now
where the time goes in v10:
time: 57.5 us; the launch traced here: 57.3 us
  starting transfers between devices  19.6 us (34%)
  waiting for transfers between devices  16 us (28%)
  Pallas kernels  15.6 us (27%)
  local copies, waits for them, and re-layouts  4.89 us (9%)
  other arithmetic  0.94 us (2%)
    pallas_call x9, Pallas kernels, call(): pl.pallas_call(body, name=name, out_shape=out_shape, in_specs=in_specs, o...  15.6 us
    ppermute x3, starting transfers between devices, shards(): result_outer = lax.ppermute(result_outer, 'op', route) + next_outer  5.97 us
    ppermute x3, waiting for transfers between devices, shards(): result_outer = lax.ppermute(result_outer, 'op', route) + next_outer  5.9 us
    ppermute x2, waiting for transfers between devices, shards(): lax.ppermute(outer[-1] + zero[0, 0] if step == 1 else outer[-1], 'op', ro...  4.9 us
    ppermute x2, starting transfers between devices, shards(): lax.ppermute(inner[-1] + zero[0, 0] if step == 1 else inner[-1], 'op', ro...  4.87 us
    unnamed x14, local copies, waits for them, and re-layouts  4.82 us
    ppermute x2, starting transfers between devices, swapped(): lax.ppermute(block, ('sec', 'sub'), pairs + [(j, i) for i, j in pairs])  3.12 us
    ppermute x1, starting transfers between devices, shards(): blocks = [psi, lax.ppermute(psi, 'op', route)]  3.02 us
  transfers between devices with their start and end apart: 13, of which 9 were waited for; matrix products, arithmetic and copies ran while one was open for 0% of the time, Pallas kernels for 27%

profile of v10, /device:TPU:0, one launch (start us, length us, event | category | flops | bytes accessed | tf_op | source)
XLA Modules:
  0.0 57.3 jit_solution(18210871071043836290)
XLA Ops:
  0.0 3.0 %collective-permute-start = (f32[4,64,256]{2,1,0:T(8,128)}, f32[4,64,256]{2,1,0:T(8,128)S(1)}, u32[]{:S(2)}, u32[]{:S(2)}) collective-permute-start(f32[4,64,256]{2,1,0:T(8,128)} %param.5), channel_id=1, source_target_pairs={{0,4},{4,12},{12,8},{8,0},{1,5},{5,13},{13,9},{9,1},{2,6},{6,14},{... | collective-permute-start | bytes 786440 | tf_op jit(solution)/shard_map/ppermute | solution.py:187
  3.0 1.6 %copy-done.1 = f32[8,256,256]{2,1,0:T(8,128)S(1)} copy-done((f32[8,256,256]{2,1,0:T(8,128)S(1)}, f32[8,256,256]{2,1,0:T(8,128)}, u32[]{:S(2)}) %copy-start.1) | copy-done | bytes 2097176
  4.6 1.6 %copy-done.2 = f32[8,256,256]{2,1,0:T(8,128)S(1)} copy-done((f32[8,256,256]{2,1,0:T(8,128)S(1)}, f32[8,256,256]{2,1,0:T(8,128)}, u32[]{:S(2)}) %copy-start.2) | copy-done | bytes 2097176
  6.2 1.1 %prepare.1 = (bf16[4,8,64,768]{3,2,1,0:T(8,128)(2,1)S(1)}, bf16[2048,256]{1,0:T(8,128)(2,1)S(1)}, bf16[2048,256]{1,0:T(8,128)(2,1)S(1)}, f32[1,128]{1,0:T(1,128)S(1)}) custom-call(f32[8,256,256]{2,1,0:T(8,128)S(1)} %copy-done.1, f32[8,256,256]{2,1,0:T(8,128)S(1)} %copy-done.2), custom_call_target="tpu_custom_call" | custom-call | flops 3221225472 | bytes 1048576 | tf_op jit(solution)/shard_map/prepare/pallas_call | solution.py:161
  7.3 0.0 copy-start.4
  7.3 1.6 %copy-done.4 = bf16[4,8,64,768]{3,2,1,0:T(8,128)(2,1)} copy-done((bf16[4,8,64,768]{3,2,1,0:T(8,128)(2,1)}, bf16[4,8,64,768]{3,2,1,0:T(8,128)(2,1)S(1)}, u32[]{:S(2)}) %copy-start.4) | copy-done | bytes 3145752
  8.9 0.0 copy-done.6
  9.0 1.6 %collective-permute-done = f32[4,64,256]{2,1,0:T(8,128)S(1)} collective-permute-done((f32[4,64,256]{2,1,0:T(8,128)}, f32[4,64,256]{2,1,0:T(8,128)S(1)}, u32[]{:S(2)}, u32[]{:S(2)}) %collective-permute-start) | collective-permute-done | bytes 262176 | tf_op jit(solution)/shard_map/ppermute | solution.py:187
  10.6 0.1 broadcast_add_fusion
  10.6 1.1 %collective-permute-start.3 = (f32[2,64,256]{2,1,0:T(8,128)S(1)}, f32[2,64,256]{2,1,0:T(8,128)S(1)}, u32[]{:S(2)}, u32[]{:S(2)}) collective-permute-start(f32[2,64,256]{2,1,0:T(8,128)S(1)} %get-tuple-element.39), channel_id=1, source_target_pairs={{0,4},{4,12},{12,8},{8,0},{1,5},{5,13},{13,9},{9,1},{2,6},{6,14},{... | collective-permute-start | bytes 393224 | tf_op jit(solution)/shard_map/ppermute | solution.py:190
  11.7 3.2 %collective-permute-start.1 = (f32[2,64,256]{2,1,0:T(8,128)S(1)}, f32[2,64,256]{2,1,0:T(8,128)S(1)}, u32[]{:S(2)}, u32[]{:S(2)}) collective-permute-start(f32[2,64,256]{2,1,0:T(8,128)S(1)} %get-tuple-element.42), channel_id=1, source_target_pairs={{0,4},{4,12},{12,8},{8,0},{1,5},{5,13},{13,9},{9,1},{2,6},{6,14},{... | collective-permute-start | bytes 393224 | tf_op jit(solution)/shard_map/ppermute | solution.py:191
  14.9 2.8 %collective-permute-done.3.refs_2_ = f32[2,64,256]{2,1,0:T(8,128)S(1)} collective-permute-done((f32[2,64,256]{2,1,0:T(8,128)S(1)}, f32[2,64,256]{2,1,0:T(8,128)S(1)}, u32[]{:S(2)}, u32[]{:S(2)}) %collective-permute-start.3) | collective-permute-done | bytes 131104 | tf_op jit(solution)/shard_map/ppermute | solution.py:190
  17.7 0.5 collective-permute-start.4
  18.2 1.7 %collective-permute-done.1.refs_2_ = f32[2,64,256]{2,1,0:T(8,128)S(1)} collective-permute-done((f32[2,64,256]{2,1,0:T(8,128)S(1)}, f32[2,64,256]{2,1,0:T(8,128)S(1)}, u32[]{:S(2)}, u32[]{:S(2)}) %collective-permute-start.1) | collective-permute-done | bytes 131104 | tf_op jit(solution)/shard_map/ppermute | solution.py:191
  19.9 1.7 %collective-permute-start.2 = (f32[2,64,256]{2,1,0:T(8,128)S(1)}, f32[2,64,256]{2,1,0:T(8,128)S(1)}, u32[]{:S(2)}, u32[]{:S(2)}) collective-permute-start(f32[2,64,256]{2,1,0:T(8,128)S(1)} %collective-permute-done.1.refs_2_), channel_id=1, source_target_pairs={{0,4},{4,12},{12,8},{8,0},{1,5},{5,13},{13,9},{9,1},{2,6},{6,14},{... | collective-permute-start | bytes 393224 | tf_op jit(solution)/shard_map/ppermute | solution.py:191
  21.6 2.1 %collective-permute-done.4.refs_3_ = f32[2,64,256]{2,1,0:T(8,128)S(1)} collective-permute-done((f32[2,64,256]{2,1,0:T(8,128)S(1)}, f32[2,64,256]{2,1,0:T(8,128)S(1)}, u32[]{:S(2)}, u32[]{:S(2)}) %collective-permute-start.4) | collective-permute-done | bytes 131104 | tf_op jit(solution)/shard_map/ppermute | solution.py:190
  23.8 0.7 %collective-permute-start.6 = (f32[4,64,256]{2,1,0:T(8,128)S(1)}, f32[4,64,256]{2,1,0:T(8,128)S(1)}, u32[]{:S(2)}, u32[]{:S(2)}) collective-permute-start(f32[4,64,256]{2,1,0:T(8,128)S(1)} %get-tuple-element.37), channel_id=1, source_target_pairs={{1,2},{2,1},{5,6},{6,5},{9,10},{10,9},{13,14},{14,13},{17,18},{18,... | collective-permute-start | bytes 786440 | tf_op jit(solution)/shard_map/ppermute | solution.py:22
  24.5 0.0 copy-start.3
  24.5 0.0 copy-start.5
  24.5 2.4 %collective-permute-start.5 = (f32[4,64,256]{2,1,0:T(8,128)S(1)}, f32[4,64,256]{2,1,0:T(8,128)S(1)}, u32[]{:S(2)}, u32[]{:S(2)}) collective-permute-start(f32[4,64,256]{2,1,0:T(8,128)S(1)} %get-tuple-element.38), channel_id=1, source_target_pairs={{0,1},{2,3},{1,0},{3,2},{4,5},{6,7},{5,4},{7,6},{8,9},{10,11},{9,8... | collective-permute-start | bytes 786440 | tf_op jit(solution)/shard_map/ppermute | solution.py:22
  26.9 0.2 assemble.1.refs_4_.outer
  27.1 0.0 collective-permute-done.2.refs_3_
  27.1 0.0 copy-done.3
  27.2 0.0 copy-done.5
  27.2 0.0 copy-start
  27.2 1.7 %own.1 = (bf16[2,768,256]{2,1,0:T(8,128)(2,1)S(1)}, bf16[4,512,256]{2,1,0:T(8,128)(2,1)S(1)}, bf16[4,512,256]{2,1,0:T(8,128)(2,1)S(1)}) custom-call(s32[8,16]{1,0:T(8,128)S(1)} %copy-done.3, f32[2,64,256]{2,1,0:T(8,128)S(1)} %get-tuple-element.44.refs_0_, f32[2,64,256]{2,1,0:T(8,128)S(1)} %get-tuple-element.41.refs_1_, ...), custom_call_target="tpu_custom_call" | custom-call | flops 3221225472 | bytes 1048576 | tf_op jit(solution)/shard_map/own/pallas_call | solution.py:161
  28.9 0.0 copy-done
  28.9 1.2 %first_inner.1 = f32[2,64,256]{2,1,0:T(8,128)S(1)} custom-call(s32[8]{0:T(128)S(1)} %copy-done, bf16[4,512,256]{2,1,0:T(8,128)(2,1)S(1)} %get-tuple-element.23.high, bf16[4,512,256]{2,1,0:T(8,128)(2,1)S(1)} %get-tuple-element.24.low, bf16[2048,256]{1,0:T(8,128)(2,1)S(1)} %get-tuple-element.27.right_hi, bf16[2048,256]{1,0:T(8,128)(2,1)S(1)} %get-tuple-element.28.right_lo), custom_call_target="tpu_custom_call" | custom-call | flops 805306368 | bytes 1048576 | tf_op jit(solution)/shard_map/first_inner/pallas_call | solution.py:161
  30.0 0.9 %collective-permute-start.10 = (f32[2,64,256]{2,1,0:T(8,128)S(1)}, f32[2,64,256]{2,1,0:T(8,128)S(1)}, u32[]{:S(2)}, u32[]{:S(2)}) collective-permute-start(f32[2,64,256]{2,1,0:T(8,128)S(1)} %first_inner.1), channel_id=1, source_target_pairs={{0,4},{4,12},{12,8},{8,0},{1,5},{5,13},{13,9},{9,1},{2,6},{6,14},{... | collective-permute-start | bytes 393224 | tf_op jit(solution)/shard_map/ppermute | solution.py:237
  30.9 0.0 collective-permute-done.6.apart
  30.9 0.0 collective-permute-done.5.paired
  30.9 1.3 %outside.1 = (bf16[2,768,256]{2,1,0:T(8,128)(2,1)S(1)}, bf16[2,512,256]{2,1,0:T(8,128)(2,1)S(1)}, bf16[2,512,256]{2,1,0:T(8,128)(2,1)S(1)}) custom-call(s32[8,16]{1,0:T(8,128)S(1)} %copy-done.3, f32[4,64,256]{2,1,0:T(8,128)S(1)} %collective-permute-done.5.paired, f32[4,64,256]{2,1,0:T(8,128)S(1)} %collective-permute-done.6.apart, ...), custom_call_target="tpu_custom_call" | custom-call | flops 1610612736 | bytes 1048576 | tf_op jit(solution)/shard_map/outside/pallas_call | solution.py:161
  32.2 1.2 %first_outer.1 = f32[2,64,256]{2,1,0:T(8,128)S(1)} custom-call(s32[8]{0:T(128)S(1)} %copy-done, bf16[4,512,256]{2,1,0:T(8,128)(2,1)S(1)} %get-tuple-element.23.high, bf16[4,512,256]{2,1,0:T(8,128)(2,1)S(1)} %get-tuple-element.24.low, bf16[2,512,256]{2,1,0:T(8,128)(2,1)S(1)} %get-tuple-element.25.end_high, ...), custom_call_target="tpu_custom_call" | custom-call | flops 805306368 | bytes 1048576 | tf_op jit(solution)/shard_map/first_outer/pallas_call | solution.py:161
  33.4 3.4 %collective-permute-start.7 = (f32[2,64,256]{2,1,0:T(8,128)S(1)}, f32[2,64,256]{2,1,0:T(8,128)S(1)}, u32[]{:S(2)}, u32[]{:S(2)}) collective-permute-start(f32[2,64,256]{2,1,0:T(8,128)S(1)} %first_outer.1), channel_id=1, source_target_pairs={{0,4},{4,12},{12,8},{8,0},{1,5},{5,13},{13,9},{9,1},{2,6},{6,14},{... | collective-permute-start | bytes 393224 | tf_op jit(solution)/shard_map/ppermute | solution.py:238
  36.8 3.0 %chunk.3 = (f32[2,64,256]{2,1,0:T(8,128)S(1)}, f32[2,64,256]{2,1,0:T(8,128)S(1)}) custom-call(s32[8]{0:T(128)S(1)} %copy-done, s32[8,16]{1,0:T(8,128)S(1)} %copy-done.3, bf16[2,768,256]{2,1,0:T(8,128)(2,1)S(1)} %assemble.1.refs_4_.outer, bf16[2,768,256]{2,1,0:T(8,128)(2,1)S(1)} %get-tuple-element.29.inner, ...), custom_call_target="tpu_custom_call" | custom-call | flops 3221225472 | bytes 1048576 | tf_op jit(solution)/shard_map/chunk/pallas_call | solution.py:161
  39.8 0.0 collective-permute-done.10
  39.9 0.1 collective-permute-start.11
  39.9 0.4 collective-permute-done.7
  40.4 2.5 %collective-permute-start.8 = (f32[2,64,256]{2,1,0:T(8,128)S(1)}, f32[2,64,256]{2,1,0:T(8,128)S(1)}, u32[]{:S(2)}, u32[]{:S(2)}) collective-permute-start(f32[2,64,256]{2,1,0:T(8,128)S(1)} %add.35), channel_id=1, source_target_pairs={{0,4},{4,12},{12,8},{8,0},{1,5},{5,13},{13,9},{9,1},{2,6},{6,14},{... | collective-permute-start | bytes 393224 | tf_op jit(solution)/shard_map/ppermute | solution.py:238
  42.9 3.0 %chunk.4 = (f32[2,64,256]{2,1,0:T(8,128)S(1)}, f32[2,64,256]{2,1,0:T(8,128)S(1)}) custom-call(s32[8]{0:T(128)S(1)} %copy-done, s32[8,16]{1,0:T(8,128)S(1)} %copy-done.3, bf16[2,768,256]{2,1,0:T(8,128)(2,1)S(1)} %assemble.1.refs_4_.outer, bf16[2,768,256]{2,1,0:T(8,128)(2,1)S(1)} %get-tuple-element.29.inner, ...), custom_call_target="tpu_custom_call" | custom-call | flops 3221225472 | bytes 1048576 | tf_op jit(solution)/shard_map/chunk/pallas_call | solution.py:161
  45.9 1.2 %collective-permute-done.11 = f32[2,64,256]{2,1,0:T(8,128)S(1)} collective-permute-done((f32[2,64,256]{2,1,0:T(8,128)S(1)}, f32[2,64,256]{2,1,0:T(8,128)S(1)}, u32[]{:S(2)}, u32[]{:S(2)}) %collective-permute-start.11) | collective-permute-done | bytes 131104 | tf_op jit(solution)/shard_map/ppermute | solution.py:237
  47.1 0.1 collective-permute-start.12
  47.2 2.7 %collective-permute-done.8 = f32[2,64,256]{2,1,0:T(8,128)S(1)} collective-permute-done((f32[2,64,256]{2,1,0:T(8,128)S(1)}, f32[2,64,256]{2,1,0:T(8,128)S(1)}, u32[]{:S(2)}, u32[]{:S(2)}) %collective-permute-start.8) | collective-permute-done | bytes 131104 | tf_op jit(solution)/shard_map/ppermute | solution.py:238
  50.0 0.1 collective-permute-start.9
  50.0 3.0 %chunk.5 = (f32[2,64,256]{2,1,0:T(8,128)S(1)}, f32[2,64,256]{2,1,0:T(8,128)S(1)}) custom-call(s32[8]{0:T(128)S(1)} %copy-done, s32[8,16]{1,0:T(8,128)S(1)} %copy-done.3, bf16[2,768,256]{2,1,0:T(8,128)(2,1)S(1)} %assemble.1.refs_4_.outer, bf16[2,768,256]{2,1,0:T(8,128)(2,1)S(1)} %get-tuple-element.29.inner, ...), custom_call_target="tpu_custom_call" | custom-call | flops 3221225472 | bytes 1048576 | tf_op jit(solution)/shard_map/chunk/pallas_call | solution.py:161
  53.0 0.7 %collective-permute-done.12 = f32[2,64,256]{2,1,0:T(8,128)S(1)} collective-permute-done((f32[2,64,256]{2,1,0:T(8,128)S(1)}, f32[2,64,256]{2,1,0:T(8,128)S(1)}, u32[]{:S(2)}, u32[]{:S(2)}) %collective-permute-start.12) | collective-permute-done | bytes 131104 | tf_op jit(solution)/shard_map/ppermute | solution.py:237
  53.8 2.7 %collective-permute-done.9 = f32[2,64,256]{2,1,0:T(8,128)S(1)} collective-permute-done((f32[2,64,256]{2,1,0:T(8,128)S(1)}, f32[2,64,256]{2,1,0:T(8,128)S(1)}, u32[]{:S(2)}, u32[]{:S(2)}) %collective-permute-start.9) | collective-permute-done | bytes 131104 | tf_op jit(solution)/shard_map/ppermute | solution.py:238
  56.6 0.7 %pad_maximum_fusion.2 = f32[4,64,256]{2,1,0:T(8,128)} fusion(f32[1,64,256]{2,1,0:T(8,128)S(1)} %get-tuple-element.46, f32[2,64,256]{2,1,0:T(8,128)S(1)} %add.40, f32[1,64,256]{2,1,0:T(8,128)S(1)} %get-tuple-element.45), kind=kLoop, calls=%fused_computation.2 | loop fusion | flops 131072 | bytes 524288 | tf_op jit(solution)/shard_map/concatenate | solution.py:239
  (16 shorter events, 0.2 us)
Async XLA Ops:
  0.0 10.5 %collective-permute-start = (f32[4,64,256]{2,1,0:T(8,128)}, f32[4,64,256]{2,1,0:T(8,128)S(1)}, u32[]{:S(2)}, u32[]{:S(2)}) collective-permute-start(f32[4,64,256]{2,1,0:T(8,128)} %param.5), channel_id=1, source_target_pairs={{0,4},{4,12},{12,8},{8,0},{1,5},{5,13},{13,9},{9,1},{2,6},{6,14},{... | collective-permute-start | bytes 786440 | tf_op jit(solution)/shard_map/ppermute | solution.py:187
  3.0 1.6 %copy-start.1 = (f32[8,256,256]{2,1,0:T(8,128)S(1)}, f32[8,256,256]{2,1,0:T(8,128)}, u32[]{:S(2)}) copy-start(f32[8,256,256]{2,1,0:T(8,128)} %left_ref.1) | copy-start | bytes 6291460
  4.6 1.6 %copy-start.2 = (f32[8,256,256]{2,1,0:T(8,128)S(1)}, f32[8,256,256]{2,1,0:T(8,128)}, u32[]{:S(2)}) copy-start(f32[8,256,256]{2,1,0:T(8,128)} %right_ref.1) | copy-start | bytes 6291460
  6.2 2.7 %copy-start.6 = (f32[4,64,256]{2,1,0:T(8,128)S(1)}, f32[4,64,256]{2,1,0:T(8,128)}, u32[]{:S(2)}) copy-start(f32[4,64,256]{2,1,0:T(8,128)} %param.5) | copy-start | bytes 786436
  7.3 1.6 %copy-start.4 = (bf16[4,8,64,768]{3,2,1,0:T(8,128)(2,1)}, bf16[4,8,64,768]{3,2,1,0:T(8,128)(2,1)S(1)}, u32[]{:S(2)}) copy-start(bf16[4,8,64,768]{3,2,1,0:T(8,128)(2,1)S(1)} %get-tuple-element.22.refs_5_.left_parts) | copy-start | bytes 9437188
  10.6 7.0 %collective-permute-start.3 = (f32[2,64,256]{2,1,0:T(8,128)S(1)}, f32[2,64,256]{2,1,0:T(8,128)S(1)}, u32[]{:S(2)}, u32[]{:S(2)}) collective-permute-start(f32[2,64,256]{2,1,0:T(8,128)S(1)} %get-tuple-element.39), channel_id=1, source_target_pairs={{0,4},{4,12},{12,8},{8,0},{1,5},{5,13},{13,9},{9,1},{2,6},{6,14},{... | collective-permute-start | bytes 393224 | tf_op jit(solution)/shard_map/ppermute | solution.py:190
  11.7 8.2 %collective-permute-start.1 = (f32[2,64,256]{2,1,0:T(8,128)S(1)}, f32[2,64,256]{2,1,0:T(8,128)S(1)}, u32[]{:S(2)}, u32[]{:S(2)}) collective-permute-start(f32[2,64,256]{2,1,0:T(8,128)S(1)} %get-tuple-element.42), channel_id=1, source_target_pairs={{0,4},{4,12},{12,8},{8,0},{1,5},{5,13},{13,9},{9,1},{2,6},{6,14},{... | collective-permute-start | bytes 393224 | tf_op jit(solution)/shard_map/ppermute | solution.py:191
  17.7 6.1 %collective-permute-start.4 = (f32[2,64,256]{2,1,0:T(8,128)S(1)}, f32[2,64,256]{2,1,0:T(8,128)S(1)}, u32[]{:S(2)}, u32[]{:S(2)}) collective-permute-start(f32[2,64,256]{2,1,0:T(8,128)S(1)} %collective-permute-done.3.refs_2_), channel_id=1, source_target_pairs={{0,4},{4,12},{12,8},{8,0},{1,5},{5,13},{13,9},{9,1},{2,6},{6,14},{... | collective-permute-start | bytes 393224 | tf_op jit(solution)/shard_map/ppermute | solution.py:190
  19.9 7.2 %collective-permute-start.2 = (f32[2,64,256]{2,1,0:T(8,128)S(1)}, f32[2,64,256]{2,1,0:T(8,128)S(1)}, u32[]{:S(2)}, u32[]{:S(2)}) collective-permute-start(f32[2,64,256]{2,1,0:T(8,128)S(1)} %collective-permute-done.1.refs_2_), channel_id=1, source_target_pairs={{0,4},{4,12},{12,8},{8,0},{1,5},{5,13},{13,9},{9,1},{2,6},{6,14},{... | collective-permute-start | bytes 393224 | tf_op jit(solution)/shard_map/ppermute | solution.py:191
  23.8 7.1 %collective-permute-start.6 = (f32[4,64,256]{2,1,0:T(8,128)S(1)}, f32[4,64,256]{2,1,0:T(8,128)S(1)}, u32[]{:S(2)}, u32[]{:S(2)}) collective-permute-start(f32[4,64,256]{2,1,0:T(8,128)S(1)} %get-tuple-element.37), channel_id=1, source_target_pairs={{1,2},{2,1},{5,6},{6,5},{9,10},{10,9},{13,14},{14,13},{17,18},{18,... | collective-permute-start | bytes 786440 | tf_op jit(solution)/shard_map/ppermute | solution.py:22
  24.5 2.7 %copy-start.3 = (s32[8,16]{1,0:T(8,128)S(1)}, s32[8,16]{1,0:T(8,128)}, u32[]{:S(2)}) copy-start(s32[8,16]{1,0:T(8,128)} %allowed_ref.9) | copy-start | bytes 1540
  24.5 2.7 %copy-start.5 = (bf16[4,8,64,768]{3,2,1,0:T(8,128)(2,1)S(1)}, bf16[4,8,64,768]{3,2,1,0:T(8,128)(2,1)}, u32[]{:S(2)}) copy-start(bf16[4,8,64,768]{3,2,1,0:T(8,128)(2,1)} %copy-done.4) | copy-start | bytes 9437188
  24.5 6.4 %collective-permute-start.5 = (f32[4,64,256]{2,1,0:T(8,128)S(1)}, f32[4,64,256]{2,1,0:T(8,128)S(1)}, u32[]{:S(2)}, u32[]{:S(2)}) collective-permute-start(f32[4,64,256]{2,1,0:T(8,128)S(1)} %get-tuple-element.38), channel_id=1, source_target_pairs={{0,1},{2,3},{1,0},{3,2},{4,5},{6,7},{5,4},{7,6},{8,9},{10,11},{9,8... | collective-permute-start | bytes 786440 | tf_op jit(solution)/shard_map/ppermute | solution.py:22
  27.2 1.7 %copy-start = (s32[8]{0:T(128)S(1)}, s32[8]{0:T(128)}, u32[]{:S(2)}) copy-start(s32[8]{0:T(128)} %shifts_ref.9) | copy-start | bytes 100
  30.0 9.8 %collective-permute-start.10 = (f32[2,64,256]{2,1,0:T(8,128)S(1)}, f32[2,64,256]{2,1,0:T(8,128)S(1)}, u32[]{:S(2)}, u32[]{:S(2)}) collective-permute-start(f32[2,64,256]{2,1,0:T(8,128)S(1)} %first_inner.1), channel_id=1, source_target_pairs={{0,4},{4,12},{12,8},{8,0},{1,5},{5,13},{13,9},{9,1},{2,6},{6,14},{... | collective-permute-start | bytes 393224 | tf_op jit(solution)/shard_map/ppermute | solution.py:237
  33.4 7.0 %collective-permute-start.7 = (f32[2,64,256]{2,1,0:T(8,128)S(1)}, f32[2,64,256]{2,1,0:T(8,128)S(1)}, u32[]{:S(2)}, u32[]{:S(2)}) collective-permute-start(f32[2,64,256]{2,1,0:T(8,128)S(1)} %first_outer.1), channel_id=1, source_target_pairs={{0,4},{4,12},{12,8},{8,0},{1,5},{5,13},{13,9},{9,1},{2,6},{6,14},{... | collective-permute-start | bytes 393224 | tf_op jit(solution)/shard_map/ppermute | solution.py:238
  39.9 7.3 %collective-permute-start.11 = (f32[2,64,256]{2,1,0:T(8,128)S(1)}, f32[2,64,256]{2,1,0:T(8,128)S(1)}, u32[]{:S(2)}, u32[]{:S(2)}) collective-permute-start(f32[2,64,256]{2,1,0:T(8,128)S(1)} %add.38), channel_id=1, source_target_pairs={{0,4},{4,12},{12,8},{8,0},{1,5},{5,13},{13,9},{9,1},{2,6},{6,14},{... | collective-permute-start | bytes 393224 | tf_op jit(solution)/shard_map/ppermute | solution.py:237
  40.4 9.5 %collective-permute-start.8 = (f32[2,64,256]{2,1,0:T(8,128)S(1)}, f32[2,64,256]{2,1,0:T(8,128)S(1)}, u32[]{:S(2)}, u32[]{:S(2)}) collective-permute-start(f32[2,64,256]{2,1,0:T(8,128)S(1)} %add.35), channel_id=1, source_target_pairs={{0,4},{4,12},{12,8},{8,0},{1,5},{5,13},{13,9},{9,1},{2,6},{6,14},{... | collective-permute-start | bytes 393224 | tf_op jit(solution)/shard_map/ppermute | solution.py:238
  47.1 6.6 %collective-permute-start.12 = (f32[2,64,256]{2,1,0:T(8,128)S(1)}, f32[2,64,256]{2,1,0:T(8,128)S(1)}, u32[]{:S(2)}, u32[]{:S(2)}) collective-permute-start(f32[2,64,256]{2,1,0:T(8,128)S(1)} %add.39), channel_id=1, source_target_pairs={{0,4},{4,12},{12,8},{8,0},{1,5},{5,13},{13,9},{9,1},{2,6},{6,14},{... | collective-permute-start | bytes 393224 | tf_op jit(solution)/shard_map/ppermute | solution.py:237
  50.0 6.6 %collective-permute-start.9 = (f32[2,64,256]{2,1,0:T(8,128)S(1)}, f32[2,64,256]{2,1,0:T(8,128)S(1)}, u32[]{:S(2)}, u32[]{:S(2)}) collective-permute-start(f32[2,64,256]{2,1,0:T(8,128)S(1)} %add.36), channel_id=1, source_target_pairs={{0,4},{4,12},{12,8},{8,0},{1,5},{5,13},{13,9},{9,1},{2,6},{6,14},{... | collective-permute-start | bytes 393224 | tf_op jit(solution)/shard_map/ppermute | solution.py:238

commit v11 on v8

--- a/solution.py
+++ b/solution.py
@@ -10,6 +10,7 @@
 F32, BF16 = jnp.float32, jnp.bfloat16
 SMEM = pl.BlockSpec(memory_space=pltpu.SMEM)
 VMEM = pl.BlockSpec(memory_space=pltpu.VMEM)
+ANY = pl.BlockSpec(memory_space=pl.ANY)
 
 
 def shifted(block, axis, distance):
@@ -95,7 +96,7 @@
         first_product(left, ref[...], allowed_ref, first + i, high.at[i], low.at[i])
 
 
-def outside_sectors(n, nloc, allowed_ref, above, below, left_parts, outside, high, low, psi):
+def outside_sectors(n, nloc, allowed_ref, above, below, left_parts, before, outside, high, low, psi):
     place_rows(n, psi.at[0], [above[j] for j in range(n)])
     place_rows(n, psi.at[1], [below[j] for j in range(n)])
     left = chunk_left(n, 0, left_parts)
@@ -118,14 +119,26 @@
     out[...] = dot3((left(high), left(low)), (right_hi[...], right_lo[...])).reshape(out.shape)
 
 
-def first_inner(nloc, shifts_ref, high, low, right_hi, right_lo, out):
+def inner_targets(nloc, shifts_ref, high, low, right_hi, right_lo, out):
     def blocks_of(own, shift, at):
         return [own[t - shift, at] for t in range(1, nloc - 1)]
 
     second_product(blocks_of, shifts_ref, high, low, right_hi, right_lo, out)
 
 
-def first_outer(nloc, shifts_ref, high, low, end_high, end_low, right_hi, right_lo, out):
+def first_inner(nloc, shifts_ref, high, low, right_hi, right_lo, out):
+    inner_targets(nloc, shifts_ref, high, low, right_hi, right_lo, out)
+
+
+def next_inner(n, nloc, shifts_ref, allowed_ref, outer, inner, left_parts, right_hi, right_lo, before, out, high, low):
+    left = chunk_left(n, 1, left_parts)
+    first = lax.axis_index(("sec", "sub")) * nloc
+    for i, ref in enumerate([outer.at[0], *[inner.at[i] for i in range(nloc - 2)], outer.at[1]]):
+        first_product(left, ref[...], allowed_ref, first + i, high.at[i], low.at[i])
+    inner_targets(nloc, shifts_ref, high, low, right_hi, right_lo, out)
+
+
+def outer_targets(nloc, shifts_ref, high, low, end_high, end_low, right_hi, right_lo, out):
     def blocks_of(parts, shift, at):
         own, ends = parts
         start = jnp.where(shift == 1, ends[0, at], own[jnp.maximum(-shift, 0), at])
@@ -133,6 +146,18 @@
         return [start, end]
 
     second_product(blocks_of, shifts_ref, (high, end_high), (low, end_low), right_hi, right_lo, out)
+
+
+def first_outer(nloc, shifts_ref, high, low, end_high, end_low, right_hi, right_lo, out):
+    outer_targets(nloc, shifts_ref, high, low, end_high, end_low, right_hi, right_lo, out)
+
+
+def next_outer(n, nloc, shifts_ref, allowed_ref, high, low, outside, left_parts, right_hi, right_lo, before, out, end_high, end_low):
+    left = chunk_left(n, 1, left_parts)
+    first = lax.axis_index(("sec", "sub")) * nloc
+    for i in range(2):
+        first_product(left, outside[i], allowed_ref, first - 1 + i * (nloc + 1), end_high.at[i], end_low.at[i])
+    outer_targets(nloc, shifts_ref, high, low, end_high, end_low, right_hi, right_lo, out)
 
 
 def later_chunk(n, nloc, step, shifts_ref, allowed_ref, outer, inner, outside, left_parts, right_hi, right_lo, outer_out, inner_out, high, low):
@@ -208,16 +233,30 @@
         functools.partial(first_inner, nloc), "first_inner", nloc * kops * one // n, chunk_inner,
         [SMEM] + [VMEM] * 4, [shifts, *own, right_hi, right_lo],
     )
+    next_inner_rows, *own_next = call(
+        functools.partial(next_inner, n, nloc), "next_inner", 2 * kops * one, [chunk_inner, *products(nloc)],
+        [SMEM] * 2 + [VMEM] * 5 + [ANY],
+        [shifts, allowed, parts_outer, parts_inner, left_parts, right_hi, right_lo, result_inner],
+    )
     parts_outside, *ends = call(
         functools.partial(outside_sectors, n, nloc), "outside", 2 * kops * one, [split_parts(2), *products(2)],
-        [SMEM] + [VMEM] * 3, [allowed, above, below, left_parts], whole(2),
+        [SMEM] + [VMEM] * 3 + [ANY], [allowed, above, below, left_parts, next_inner_rows], whole(2),
     )
     result_outer = call(
         functools.partial(first_outer, nloc), "first_outer", nloc * kops * one // n, chunk,
         [SMEM] + [VMEM] * 6, [shifts, *own, *ends, right_hi, right_lo],
     )
 
+    next_outer_rows = call(
+        functools.partial(next_outer, n, nloc), "next_outer", kops * one, chunk,
+        [SMEM] * 2 + [VMEM] * 6 + [ANY],
+        [shifts, allowed, *own_next, parts_outside, left_parts, right_hi, right_lo, result_outer],
+        [pltpu.VMEM((2, kops * rows, width), BF16)] * 2,
+    )
+
     def mine(step):
+        if step == 1:
+            return next_outer_rows, next_inner_rows
         return call(
             functools.partial(later_chunk, n, nloc, step), "chunk", 4 * nloc * kops * one // n, [chunk, chunk_inner],
             [SMEM] * 2 + [VMEM] * 6,
@@ -226,9 +265,9 @@
         )
 
     for step in range(1, n):
-        next_outer, next_inner = mine(step)
-        result_inner = lax.ppermute(result_inner, "op", route) + next_inner
-        result_outer = lax.ppermute(result_outer, "op", route) + next_outer
+        next_outer_chunk, next_inner_chunk = mine(step)
+        result_inner = lax.ppermute(result_inner, "op", route) + next_inner_chunk
+        result_outer = lax.ppermute(result_outer, "op", route) + next_outer_chunk
     return jnp.concatenate([result_outer[:1], result_inner, result_outer[1:]])
 
 

time: 55.8 us -> 57.3 us (1.027)
  Pallas kernels: 15.6 us -> 17.9 us
    ppermute x2, waiting for transfers between devices: 2.38 us -> 0.01 us  [shifted(): return lax.ppermute(block, axis, route)]
    pallas_call x9 -> x10, Pallas kernels: 15.6 us -> 17.9 us  [call(): pl.pallas_call(body, name=name, out_shape=out_shape, in_specs=in_specs, o...]
    ppermute x6, waiting for transfers between devices: 1.97 us -> 3.83 us  [the longest x3 1.98 us: shards(): result_inner = lax.ppermute(result_inner, 'op', route) + next_inner_chunk]
  transfers between devices with their start and end apart: 13 -> 13, of which waited for: 7 -> 7; matrix products, arithmetic and copies ran while one was open for 0% -> 0% of each run, Pallas kernels for 28% -> 31%
where the time goes in v11:
time: 57.3 us; the launch traced here: 57.1 us
  starting transfers between devices  22.2 us (39%)
  Pallas kernels  17.9 us (31%)
  waiting for transfers between devices  12.6 us (22%)
  local copies, waits for them, and re-layouts  3.27 us (6%)
  other arithmetic  0.94 us (2%)
    pallas_call x10, Pallas kernels, call(): pl.pallas_call(body, name=name, out_shape=out_shape, in_specs=in_specs, o...  17.9 us
    ppermute x2, starting transfers between devices, shifted(): return lax.ppermute(block, axis, route)  8.41 us
    ppermute x3, starting transfers between devices, shards(): result_outer = lax.ppermute(result_outer, 'op', route) + next_outer_chunk  5.79 us
    ppermute x2, waiting for transfers between devices, shards(): lax.ppermute(outer[-1] + zero[0, 0] if step == 1 else outer[-1], 'op', ro...  3.62 us
    ppermute x2, starting transfers between devices, shards(): lax.ppermute(inner[-1] + zero[0, 0] if step == 1 else inner[-1], 'op', ro...  3.59 us
    unnamed x10, local copies, waits for them, and re-layouts  3.2 us
    ppermute x1, waiting for transfers between devices, shards(): blocks = [psi, lax.ppermute(psi, 'op', route)]  2.94 us
    ppermute x2, waiting for transfers between devices, shards(): lax.ppermute(inner[-1] + zero[0, 0] if step == 1 else inner[-1], 'op', ro...  2.18 us
  transfers between devices with their start and end apart: 13, of which 7 were waited for; matrix products, arithmetic and copies ran while one was open for 0% of the time, Pallas kernels for 31%

profile of v11, /device:TPU:1, one launch (start us, length us, event | category | flops | bytes accessed | tf_op | source)
XLA Modules:
  0.0 57.1 jit_solution(3576629119259145724)
XLA Ops:
  0.0 2.1 %collective-permute-start = (f32[4,64,256]{2,1,0:T(8,128)}, f32[4,64,256]{2,1,0:T(8,128)S(1)}, u32[]{:S(2)}, u32[]{:S(2)}) collective-permute-start(f32[4,64,256]{2,1,0:T(8,128)} %param.5), channel_id=1, source_target_pairs={{0,4},{4,12},{12,8},{8,0},{1,5},{5,13},{13,9},{9,1},{2,6},{6,14},{... | collective-permute-start | bytes 786440 | tf_op jit(solution)/shard_map/ppermute | solution.py:207
  2.1 0.0 copy-start.2
  2.1 1.6 %copy-done.2 = f32[8,256,256]{2,1,0:T(8,128)S(1)} copy-done((f32[8,256,256]{2,1,0:T(8,128)S(1)}, f32[8,256,256]{2,1,0:T(8,128)}, u32[]{:S(2)}) %copy-start.2) | copy-done | bytes 2097176
  3.7 0.0 copy-start.3
  3.7 1.6 %copy-done.3 = f32[8,256,256]{2,1,0:T(8,128)S(1)} copy-done((f32[8,256,256]{2,1,0:T(8,128)S(1)}, f32[8,256,256]{2,1,0:T(8,128)}, u32[]{:S(2)}) %copy-start.3) | copy-done | bytes 2097176
  5.3 0.0 copy-start.4
  5.3 1.1 %prepare.1 = (bf16[4,8,64,768]{3,2,1,0:T(8,128)(2,1)S(1)}, bf16[2048,256]{1,0:T(8,128)(2,1)S(1)}, bf16[2048,256]{1,0:T(8,128)(2,1)S(1)}, f32[1,128]{1,0:T(1,128)S(1)}) custom-call(f32[8,256,256]{2,1,0:T(8,128)S(1)} %copy-done.2, f32[8,256,256]{2,1,0:T(8,128)S(1)} %copy-done.3), custom_call_target="tpu_custom_call" | custom-call | flops 3221225472 | bytes 1048576 | tf_op jit(solution)/shard_map/prepare/pallas_call | solution.py:181
  6.4 0.0 copy-done.4
  6.4 2.9 %collective-permute-done = f32[4,64,256]{2,1,0:T(8,128)S(1)} collective-permute-done((f32[4,64,256]{2,1,0:T(8,128)}, f32[4,64,256]{2,1,0:T(8,128)S(1)}, u32[]{:S(2)}, u32[]{:S(2)}) %collective-permute-start) | collective-permute-done | bytes 262176 | tf_op jit(solution)/shard_map/ppermute | solution.py:207
  9.4 0.1 broadcast_add_fusion
  9.5 0.4 collective-permute-start.3
  9.9 3.0 %collective-permute-start.1 = (f32[2,64,256]{2,1,0:T(8,128)S(1)}, f32[2,64,256]{2,1,0:T(8,128)S(1)}, u32[]{:S(2)}, u32[]{:S(2)}) collective-permute-start(f32[2,64,256]{2,1,0:T(8,128)S(1)} %get-tuple-element.42), channel_id=1, source_target_pairs={{0,4},{4,12},{12,8},{8,0},{1,5},{5,13},{13,9},{9,1},{2,6},{6,14},{... | collective-permute-start | bytes 393224 | tf_op jit(solution)/shard_map/ppermute | solution.py:211
  12.9 1.4 %collective-permute-done.3.refs_2_ = f32[2,64,256]{2,1,0:T(8,128)S(1)} collective-permute-done((f32[2,64,256]{2,1,0:T(8,128)S(1)}, f32[2,64,256]{2,1,0:T(8,128)S(1)}, u32[]{:S(2)}, u32[]{:S(2)}) %collective-permute-start.3) | collective-permute-done | bytes 131104 | tf_op jit(solution)/shard_map/ppermute | solution.py:210
  14.2 0.6 %collective-permute-start.4 = (f32[2,64,256]{2,1,0:T(8,128)S(1)}, f32[2,64,256]{2,1,0:T(8,128)S(1)}, u32[]{:S(2)}, u32[]{:S(2)}) collective-permute-start(f32[2,64,256]{2,1,0:T(8,128)S(1)} %collective-permute-done.3.refs_2_), channel_id=1, source_target_pairs={{0,4},{4,12},{12,8},{8,0},{1,5},{5,13},{13,9},{9,1},{2,6},{6,14},{... | collective-permute-start | bytes 393224 | tf_op jit(solution)/shard_map/ppermute | solution.py:210
  14.8 2.2 %collective-permute-done.1.refs_2_ = f32[2,64,256]{2,1,0:T(8,128)S(1)} collective-permute-done((f32[2,64,256]{2,1,0:T(8,128)S(1)}, f32[2,64,256]{2,1,0:T(8,128)S(1)}, u32[]{:S(2)}, u32[]{:S(2)}) %collective-permute-start.1) | collective-permute-done | bytes 131104 | tf_op jit(solution)/shard_map/ppermute | solution.py:211
  17.0 0.6 %collective-permute-start.2 = (f32[2,64,256]{2,1,0:T(8,128)S(1)}, f32[2,64,256]{2,1,0:T(8,128)S(1)}, u32[]{:S(2)}, u32[]{:S(2)}) collective-permute-start(f32[2,64,256]{2,1,0:T(8,128)S(1)} %collective-permute-done.1.refs_2_), channel_id=1, source_target_pairs={{0,4},{4,12},{12,8},{8,0},{1,5},{5,13},{13,9},{9,1},{2,6},{6,14},{... | collective-permute-start | bytes 393224 | tf_op jit(solution)/shard_map/ppermute | solution.py:211
  17.6 2.3 %collective-permute-done.4.refs_3_ = f32[2,64,256]{2,1,0:T(8,128)S(1)} collective-permute-done((f32[2,64,256]{2,1,0:T(8,128)S(1)}, f32[2,64,256]{2,1,0:T(8,128)S(1)}, u32[]{:S(2)}, u32[]{:S(2)}) %collective-permute-start.4) | collective-permute-done | bytes 131104 | tf_op jit(solution)/shard_map/ppermute | solution.py:210
  19.9 6.5 %collective-permute-start.5 = (f32[4,64,256]{2,1,0:T(8,128)S(1)}, f32[4,64,256]{2,1,0:T(8,128)S(1)}, u32[]{:S(2)}, u32[]{:S(2)}) collective-permute-start(f32[4,64,256]{2,1,0:T(8,128)S(1)} %pad_maximum_fusion), channel_id=1, source_target_pairs={{0,1},{1,2},{2,3},{4,5},{5,6},{6,7},{8,9},{9,10},{10,11},{12,13},{... | collective-permute-start | bytes 786440 | tf_op jit(solution)/shard_map/ppermute | solution.py:19
  26.4 0.0 copy-start
  26.4 1.9 %collective-permute-start.6 = (f32[4,64,256]{2,1,0:T(8,128)S(1)}, f32[4,64,256]{2,1,0:T(8,128)S(1)}, u32[]{:S(2)}, u32[]{:S(2)}) collective-permute-start(f32[4,64,256]{2,1,0:T(8,128)S(1)} %pad_maximum_fusion.1), channel_id=1, source_target_pairs={{1,0},{2,1},{3,2},{5,4},{6,5},{7,6},{9,8},{10,9},{11,10},{13,12},{... | collective-permute-start | bytes 786440 | tf_op jit(solution)/shard_map/ppermute | solution.py:19
  28.3 0.2 assemble.1.refs_4_.outer
  28.5 0.0 collective-permute-done.2.refs_3_
  28.6 0.0 copy-done
  28.6 0.0 copy-start.1
  28.6 1.7 %own.1 = (bf16[2,768,256]{2,1,0:T(8,128)(2,1)S(1)}, bf16[4,512,256]{2,1,0:T(8,128)(2,1)S(1)}, bf16[4,512,256]{2,1,0:T(8,128)(2,1)S(1)}) custom-call(s32[8,16]{1,0:T(8,128)S(1)} %copy-done, f32[2,64,256]{2,1,0:T(8,128)S(1)} %get-tuple-element.44.refs_0_, f32[2,64,256]{2,1,0:T(8,128)S(1)} %get-tuple-element.41.refs_1_, ...), custom_call_target="tpu_custom_call" | custom-call | flops 3221225472 | bytes 1048576 | tf_op jit(solution)/shard_map/own/pallas_call | solution.py:181
  30.3 0.0 copy-done.1
  30.3 1.2 %first_inner.1.before = f32[2,64,256]{2,1,0:T(8,128)S(1)} custom-call(s32[8]{0:T(128)S(1)} %copy-done.1, bf16[4,512,256]{2,1,0:T(8,128)(2,1)S(1)} %get-tuple-element.24.high, bf16[4,512,256]{2,1,0:T(8,128)(2,1)S(1)} %get-tuple-element.25.low, bf16[2048,256]{1,0:T(8,128)(2,1)S(1)} %get-tuple-element.27.right_hi, bf16[2048,256]{1,0:T(8,128)(2,1)S(1)} %get-tuple-element.28.right_lo), custom_call_target="tpu_custom_call" | custom-call | flops 805306368 | bytes 1048576 | tf_op jit(solution)/shard_map/first_inner/pallas_call | solution.py:181
  31.4 0.6 %collective-permute-start.10 = (f32[2,64,256]{2,1,0:T(8,128)S(1)}, f32[2,64,256]{2,1,0:T(8,128)S(1)}, u32[]{:S(2)}, u32[]{:S(2)}) collective-permute-start(f32[2,64,256]{2,1,0:T(8,128)S(1)} %first_inner.1.before), channel_id=1, source_target_pairs={{0,4},{4,12},{12,8},{8,0},{1,5},{5,13},{13,9},{9,1},{2,6},{6,14},{... | collective-permute-start | bytes 393224 | tf_op jit(solution)/shard_map/ppermute | solution.py:269
  32.0 2.9 %next_inner.1 = (f32[2,64,256]{2,1,0:T(8,128)S(1)}, bf16[4,512,256]{2,1,0:T(8,128)(2,1)S(1)}, bf16[4,512,256]{2,1,0:T(8,128)(2,1)S(1)}) custom-call(s32[8]{0:T(128)S(1)} %copy-done.1, s32[8,16]{1,0:T(8,128)S(1)} %copy-done, bf16[2,768,256]{2,1,0:T(8,128)(2,1)S(1)} %assemble.1.refs_4_.outer, bf16[2,768,256]{2,1,0:T(8,128)(2,1)S(1)} %get-tuple-element.26.inner, ...), custom_call_target="tpu_custom_call" | custom-call | flops 1610612736 | bytes 1048576 | tf_op jit(solution)/shard_map/next_inner/pallas_call | solution.py:181
  34.9 0.0 collective-permute-done.5.above
  34.9 0.0 collective-permute-done.6.below
  35.0 1.3 %outside.1 = (bf16[2,768,256]{2,1,0:T(8,128)(2,1)S(1)}, bf16[2,512,256]{2,1,0:T(8,128)(2,1)S(1)}, bf16[2,512,256]{2,1,0:T(8,128)(2,1)S(1)}) custom-call(s32[8,16]{1,0:T(8,128)S(1)} %copy-done, f32[4,64,256]{2,1,0:T(8,128)S(1)} %collective-permute-done.5.above, f32[4,64,256]{2,1,0:T(8,128)S(1)} %collective-permute-done.6.below, ...), custom_call_target="tpu_custom_call" | custom-call | flops 1610612736 | bytes 1048576 | tf_op jit(solution)/shard_map/outside/pallas_call | solution.py:181
  36.3 1.2 %first_outer.1.before = f32[2,64,256]{2,1,0:T(8,128)S(1)} custom-call(s32[8]{0:T(128)S(1)} %copy-done.1, bf16[4,512,256]{2,1,0:T(8,128)(2,1)S(1)} %get-tuple-element.24.high, bf16[4,512,256]{2,1,0:T(8,128)(2,1)S(1)} %get-tuple-element.25.low, bf16[2,512,256]{2,1,0:T(8,128)(2,1)S(1)} %get-tuple-element.30.end_high, ...), custom_call_target="tpu_custom_call" | custom-call | flops 805306368 | bytes 1048576 | tf_op jit(solution)/shard_map/first_outer/pallas_call | solution.py:181
  37.4 3.1 %collective-permute-start.7 = (f32[2,64,256]{2,1,0:T(8,128)S(1)}, f32[2,64,256]{2,1,0:T(8,128)S(1)}, u32[]{:S(2)}, u32[]{:S(2)}) collective-permute-start(f32[2,64,256]{2,1,0:T(8,128)S(1)} %first_outer.1.before), channel_id=1, source_target_pairs={{0,4},{4,12},{12,8},{8,0},{1,5},{5,13},{13,9},{9,1},{2,6},{6,14},{... | collective-permute-start | bytes 393224 | tf_op jit(solution)/shard_map/ppermute | solution.py:270
  40.6 0.0 collective-permute-done.10
  40.6 0.1 collective-permute-start.11
  40.7 2.4 %next_outer.1 = f32[2,64,256]{2,1,0:T(8,128)S(1)} custom-call(s32[8]{0:T(128)S(1)} %copy-done.1, s32[8,16]{1,0:T(8,128)S(1)} %copy-done, bf16[4,512,256]{2,1,0:T(8,128)(2,1)S(1)} %get-tuple-element.32.high, bf16[4,512,256]{2,1,0:T(8,128)(2,1)S(1)} %get-tuple-element.33.low, bf16[2,768,256]{2,1,0:T(8,128)(2,1)S(1)} %get-tuple-element.34.outside, ...), custom_call_target="tpu_custom_call" | custom-call | flops 805306368 | bytes 1048576 | tf_op jit(solution)/shard_map/next_outer/pallas_call | solution.py:181
  43.0 0.7 %collective-permute-done.7 = f32[2,64,256]{2,1,0:T(8,128)S(1)} collective-permute-done((f32[2,64,256]{2,1,0:T(8,128)S(1)}, f32[2,64,256]{2,1,0:T(8,128)S(1)}, u32[]{:S(2)}, u32[]{:S(2)}) %collective-permute-start.7) | collective-permute-done | bytes 131104 | tf_op jit(solution)/shard_map/ppermute | solution.py:270
  43.7 2.0 %collective-permute-start.8 = (f32[2,64,256]{2,1,0:T(8,128)S(1)}, f32[2,64,256]{2,1,0:T(8,128)S(1)}, u32[]{:S(2)}, u32[]{:S(2)}) collective-permute-start(f32[2,64,256]{2,1,0:T(8,128)S(1)} %add.31), channel_id=1, source_target_pairs={{0,4},{4,12},{12,8},{8,0},{1,5},{5,13},{13,9},{9,1},{2,6},{6,14},{... | collective-permute-start | bytes 393224 | tf_op jit(solution)/shard_map/ppermute | solution.py:270
  45.7 3.0 %chunk.2 = (f32[2,64,256]{2,1,0:T(8,128)S(1)}, f32[2,64,256]{2,1,0:T(8,128)S(1)}) custom-call(s32[8]{0:T(128)S(1)} %copy-done.1, s32[8,16]{1,0:T(8,128)S(1)} %copy-done, bf16[2,768,256]{2,1,0:T(8,128)(2,1)S(1)} %assemble.1.refs_4_.outer, bf16[2,768,256]{2,1,0:T(8,128)(2,1)S(1)} %get-tuple-element.26.inner, ...), custom_call_target="tpu_custom_call" | custom-call | flops 3221225472 | bytes 1048576 | tf_op jit(solution)/shard_map/chunk/pallas_call | solution.py:181
  48.7 0.0 collective-permute-done.11
  48.8 0.6 %collective-permute-start.12 = (f32[2,64,256]{2,1,0:T(8,128)S(1)}, f32[2,64,256]{2,1,0:T(8,128)S(1)}, u32[]{:S(2)}, u32[]{:S(2)}) collective-permute-start(f32[2,64,256]{2,1,0:T(8,128)S(1)} %add.35), channel_id=1, source_target_pairs={{0,4},{4,12},{12,8},{8,0},{1,5},{5,13},{13,9},{9,1},{2,6},{6,14},{... | collective-permute-start | bytes 393224 | tf_op jit(solution)/shard_map/ppermute | solution.py:269
  49.4 0.0 collective-permute-done.8
  49.4 0.7 %collective-permute-start.9 = (f32[2,64,256]{2,1,0:T(8,128)S(1)}, f32[2,64,256]{2,1,0:T(8,128)S(1)}, u32[]{:S(2)}, u32[]{:S(2)}) collective-permute-start(f32[2,64,256]{2,1,0:T(8,128)S(1)} %add.32), channel_id=1, source_target_pairs={{0,4},{4,12},{12,8},{8,0},{1,5},{5,13},{13,9},{9,1},{2,6},{6,14},{... | collective-permute-start | bytes 393224 | tf_op jit(solution)/shard_map/ppermute | solution.py:270
  50.1 3.0 %chunk.3 = (f32[2,64,256]{2,1,0:T(8,128)S(1)}, f32[2,64,256]{2,1,0:T(8,128)S(1)}) custom-call(s32[8]{0:T(128)S(1)} %copy-done.1, s32[8,16]{1,0:T(8,128)S(1)} %copy-done, bf16[2,768,256]{2,1,0:T(8,128)(2,1)S(1)} %assemble.1.refs_4_.outer, bf16[2,768,256]{2,1,0:T(8,128)(2,1)S(1)} %get-tuple-element.26.inner, ...), custom_call_target="tpu_custom_call" | custom-call | flops 3221225472 | bytes 1048576 | tf_op jit(solution)/shard_map/chunk/pallas_call | solution.py:181
  53.2 2.0 %collective-permute-done.12 = f32[2,64,256]{2,1,0:T(8,128)S(1)} collective-permute-done((f32[2,64,256]{2,1,0:T(8,128)S(1)}, f32[2,64,256]{2,1,0:T(8,128)S(1)}, u32[]{:S(2)}, u32[]{:S(2)}) %collective-permute-start.12) | collective-permute-done | bytes 131104 | tf_op jit(solution)/shard_map/ppermute | solution.py:269
  55.2 1.2 %collective-permute-done.9 = f32[2,64,256]{2,1,0:T(8,128)S(1)} collective-permute-done((f32[2,64,256]{2,1,0:T(8,128)S(1)}, f32[2,64,256]{2,1,0:T(8,128)S(1)}, u32[]{:S(2)}, u32[]{:S(2)}) %collective-permute-start.9) | collective-permute-done | bytes 131104 | tf_op jit(solution)/shard_map/ppermute | solution.py:270
  56.4 0.7 %pad_maximum_fusion.2 = f32[4,64,256]{2,1,0:T(8,128)} fusion(f32[1,64,256]{2,1,0:T(8,128)S(1)} %get-tuple-element.46, f32[2,64,256]{2,1,0:T(8,128)S(1)} %add.36, f32[1,64,256]{2,1,0:T(8,128)S(1)} %get-tuple-element.45), kind=kLoop, calls=%fused_computation.2 | loop fusion | flops 131072 | bytes 524288 | tf_op jit(solution)/shard_map/concatenate | solution.py:271
  (14 shorter events, 0.2 us)
Async XLA Ops:
  0.0 9.4 %collective-permute-start = (f32[4,64,256]{2,1,0:T(8,128)}, f32[4,64,256]{2,1,0:T(8,128)S(1)}, u32[]{:S(2)}, u32[]{:S(2)}) collective-permute-start(f32[4,64,256]{2,1,0:T(8,128)} %param.5), channel_id=1, source_target_pairs={{0,4},{4,12},{12,8},{8,0},{1,5},{5,13},{13,9},{9,1},{2,6},{6,14},{... | collective-permute-start | bytes 786440 | tf_op jit(solution)/shard_map/ppermute | solution.py:207
  2.1 1.6 %copy-start.2 = (f32[8,256,256]{2,1,0:T(8,128)S(1)}, f32[8,256,256]{2,1,0:T(8,128)}, u32[]{:S(2)}) copy-start(f32[8,256,256]{2,1,0:T(8,128)} %left_ref.1) | copy-start | bytes 6291460
  3.7 1.6 %copy-start.3 = (f32[8,256,256]{2,1,0:T(8,128)S(1)}, f32[8,256,256]{2,1,0:T(8,128)}, u32[]{:S(2)}) copy-start(f32[8,256,256]{2,1,0:T(8,128)} %right_ref.1) | copy-start | bytes 6291460
  5.3 1.1 %copy-start.4 = (f32[4,64,256]{2,1,0:T(8,128)S(1)}, f32[4,64,256]{2,1,0:T(8,128)}, u32[]{:S(2)}) copy-start(f32[4,64,256]{2,1,0:T(8,128)} %param.5) | copy-start | bytes 786436
  9.5 4.8 %collective-permute-start.3 = (f32[2,64,256]{2,1,0:T(8,128)S(1)}, f32[2,64,256]{2,1,0:T(8,128)S(1)}, u32[]{:S(2)}, u32[]{:S(2)}) collective-permute-start(f32[2,64,256]{2,1,0:T(8,128)S(1)} %get-tuple-element.39), channel_id=1, source_target_pairs={{0,4},{4,12},{12,8},{8,0},{1,5},{5,13},{13,9},{9,1},{2,6},{6,14},{... | collective-permute-start | bytes 393224 | tf_op jit(solution)/shard_map/ppermute | solution.py:210
  9.9 7.1 %collective-permute-start.1 = (f32[2,64,256]{2,1,0:T(8,128)S(1)}, f32[2,64,256]{2,1,0:T(8,128)S(1)}, u32[]{:S(2)}, u32[]{:S(2)}) collective-permute-start(f32[2,64,256]{2,1,0:T(8,128)S(1)} %get-tuple-element.42), channel_id=1, source_target_pairs={{0,4},{4,12},{12,8},{8,0},{1,5},{5,13},{13,9},{9,1},{2,6},{6,14},{... | collective-permute-start | bytes 393224 | tf_op jit(solution)/shard_map/ppermute | solution.py:211
  14.2 5.6 %collective-permute-start.4 = (f32[2,64,256]{2,1,0:T(8,128)S(1)}, f32[2,64,256]{2,1,0:T(8,128)S(1)}, u32[]{:S(2)}, u32[]{:S(2)}) collective-permute-start(f32[2,64,256]{2,1,0:T(8,128)S(1)} %collective-permute-done.3.refs_2_), channel_id=1, source_target_pairs={{0,4},{4,12},{12,8},{8,0},{1,5},{5,13},{13,9},{9,1},{2,6},{6,14},{... | collective-permute-start | bytes 393224 | tf_op jit(solution)/shard_map/ppermute | solution.py:210
  17.0 11.6 %collective-permute-start.2 = (f32[2,64,256]{2,1,0:T(8,128)S(1)}, f32[2,64,256]{2,1,0:T(8,128)S(1)}, u32[]{:S(2)}, u32[]{:S(2)}) collective-permute-start(f32[2,64,256]{2,1,0:T(8,128)S(1)} %collective-permute-done.1.refs_2_), channel_id=1, source_target_pairs={{0,4},{4,12},{12,8},{8,0},{1,5},{5,13},{13,9},{9,1},{2,6},{6,14},{... | collective-permute-start | bytes 393224 | tf_op jit(solution)/shard_map/ppermute | solution.py:211
  19.9 15.0 %collective-permute-start.5 = (f32[4,64,256]{2,1,0:T(8,128)S(1)}, f32[4,64,256]{2,1,0:T(8,128)S(1)}, u32[]{:S(2)}, u32[]{:S(2)}) collective-permute-start(f32[4,64,256]{2,1,0:T(8,128)S(1)} %pad_maximum_fusion), channel_id=1, source_target_pairs={{0,1},{1,2},{2,3},{4,5},{5,6},{6,7},{8,9},{9,10},{10,11},{12,13},{... | collective-permute-start | bytes 786440 | tf_op jit(solution)/shard_map/ppermute | solution.py:19
  26.4 2.1 %copy-start = (s32[8,16]{1,0:T(8,128)S(1)}, s32[8,16]{1,0:T(8,128)}, u32[]{:S(2)}) copy-start(s32[8,16]{1,0:T(8,128)} %allowed_ref.11) | copy-start | bytes 1540
  26.4 8.5 %collective-permute-start.6 = (f32[4,64,256]{2,1,0:T(8,128)S(1)}, f32[4,64,256]{2,1,0:T(8,128)S(1)}, u32[]{:S(2)}, u32[]{:S(2)}) collective-permute-start(f32[4,64,256]{2,1,0:T(8,128)S(1)} %pad_maximum_fusion.1), channel_id=1, source_target_pairs={{1,0},{2,1},{3,2},{5,4},{6,5},{7,6},{9,8},{10,9},{11,10},{13,12},{... | collective-permute-start | bytes 786440 | tf_op jit(solution)/shard_map/ppermute | solution.py:19
  28.6 1.7 %copy-start.1 = (s32[8]{0:T(128)S(1)}, s32[8]{0:T(128)}, u32[]{:S(2)}) copy-start(s32[8]{0:T(128)} %shifts_ref.11) | copy-start | bytes 100
  31.4 9.1 %collective-permute-start.10 = (f32[2,64,256]{2,1,0:T(8,128)S(1)}, f32[2,64,256]{2,1,0:T(8,128)S(1)}, u32[]{:S(2)}, u32[]{:S(2)}) collective-permute-start(f32[2,64,256]{2,1,0:T(8,128)S(1)} %first_inner.1.before), channel_id=1, source_target_pairs={{0,4},{4,12},{12,8},{8,0},{1,5},{5,13},{13,9},{9,1},{2,6},{6,14},{... | collective-permute-start | bytes 393224 | tf_op jit(solution)/shard_map/ppermute | solution.py:269
  37.4 6.2 %collective-permute-start.7 = (f32[2,64,256]{2,1,0:T(8,128)S(1)}, f32[2,64,256]{2,1,0:T(8,128)S(1)}, u32[]{:S(2)}, u32[]{:S(2)}) collective-permute-start(f32[2,64,256]{2,1,0:T(8,128)S(1)} %first_outer.1.before), channel_id=1, source_target_pairs={{0,4},{4,12},{12,8},{8,0},{1,5},{5,13},{13,9},{9,1},{2,6},{6,14},{... | collective-permute-start | bytes 393224 | tf_op jit(solution)/shard_map/ppermute | solution.py:270
  40.6 8.2 %collective-permute-start.11 = (f32[2,64,256]{2,1,0:T(8,128)S(1)}, f32[2,64,256]{2,1,0:T(8,128)S(1)}, u32[]{:S(2)}, u32[]{:S(2)}) collective-permute-start(f32[2,64,256]{2,1,0:T(8,128)S(1)} %add.34), channel_id=1, source_target_pairs={{0,4},{4,12},{12,8},{8,0},{1,5},{5,13},{13,9},{9,1},{2,6},{6,14},{... | collective-permute-start | bytes 393224 | tf_op jit(solution)/shard_map/ppermute | solution.py:269
  43.7 5.7 %collective-permute-start.8 = (f32[2,64,256]{2,1,0:T(8,128)S(1)}, f32[2,64,256]{2,1,0:T(8,128)S(1)}, u32[]{:S(2)}, u32[]{:S(2)}) collective-permute-start(f32[2,64,256]{2,1,0:T(8,128)S(1)} %add.31), channel_id=1, source_target_pairs={{0,4},{4,12},{12,8},{8,0},{1,5},{5,13},{13,9},{9,1},{2,6},{6,14},{... | collective-permute-start | bytes 393224 | tf_op jit(solution)/shard_map/ppermute | solution.py:270
  48.8 6.4 %collective-permute-start.12 = (f32[2,64,256]{2,1,0:T(8,128)S(1)}, f32[2,64,256]{2,1,0:T(8,128)S(1)}, u32[]{:S(2)}, u32[]{:S(2)}) collective-permute-start(f32[2,64,256]{2,1,0:T(8,128)S(1)} %add.35), channel_id=1, source_target_pairs={{0,4},{4,12},{12,8},{8,0},{1,5},{5,13},{13,9},{9,1},{2,6},{6,14},{... | collective-permute-start | bytes 393224 | tf_op jit(solution)/shard_map/ppermute | solution.py:269
  49.4 6.9 %collective-permute-start.9 = (f32[2,64,256]{2,1,0:T(8,128)S(1)}, f32[2,64,256]{2,1,0:T(8,128)S(1)}, u32[]{:S(2)}, u32[]{:S(2)}) collective-permute-start(f32[2,64,256]{2,1,0:T(8,128)S(1)} %add.32), channel_id=1, source_target_pairs={{0,4},{4,12},{12,8},{8,0},{1,5},{5,13},{13,9},{9,1},{2,6},{6,14},{... | collective-permute-start | bytes 393224 | tf_op jit(solution)/shard_map/ppermute | solution.py:270

commit v12 on v8

--- a/solution.py
+++ b/solution.py
@@ -95,44 +95,41 @@
         first_product(left, ref[...], allowed_ref, first + i, high.at[i], low.at[i])
 
 
-def outside_sectors(n, nloc, allowed_ref, above, below, left_parts, outside, high, low, psi):
+def second_product(blocks_of, shifts_ref, high, low, right_hi, right_lo, out):
+    rows, width = out.shape[1:]
+
+    def left(parts):
+        columns = []
+        for k in range(shifts_ref.shape[0]):
+            at = slice(k * rows, (k + 1) * rows)
+            columns.append(jnp.concatenate(blocks_of(parts, shifts_ref[k], at)))
+        return jnp.concatenate(columns, axis=1)
+
+    out[...] = dot3((left(high), left(low)), (right_hi[...], right_lo[...])).reshape(out.shape)
+
+
+def first_chunk(n, nloc, shifts_ref, allowed_ref, own_high, own_low, above, below, left_parts, right_hi, right_lo, *refs):
+    outer_out, inner_out, outside, end_high, end_low, psi = refs
     place_rows(n, psi.at[0], [above[j] for j in range(n)])
     place_rows(n, psi.at[1], [below[j] for j in range(n)])
     left = chunk_left(n, 0, left_parts)
     first = lax.axis_index(("sec", "sub")) * nloc
     for i in range(2):
         outside[i] = stacked(psi[i])
-        first_product(left, outside[i], allowed_ref, first - 1 + i * (nloc + 1), high.at[i], low.at[i])
-
-
-def second_product(blocks_of, shifts_ref, high, low, right_hi, right_lo, out):
-    rows, width = out.shape[1:]
-
-    def left(parts):
-        columns = []
-        for k in range(shifts_ref.shape[0]):
-            at = slice(k * rows, (k + 1) * rows)
-            columns.append(jnp.concatenate(blocks_of(parts, shifts_ref[k], at)))
-        return jnp.concatenate(columns, axis=1)
-
-    out[...] = dot3((left(high), left(low)), (right_hi[...], right_lo[...])).reshape(out.shape)
-
-
-def first_inner(nloc, shifts_ref, high, low, right_hi, right_lo, out):
-    def blocks_of(own, shift, at):
-        return [own[t - shift, at] for t in range(1, nloc - 1)]
-
-    second_product(blocks_of, shifts_ref, high, low, right_hi, right_lo, out)
-
-
-def first_outer(nloc, shifts_ref, high, low, end_high, end_low, right_hi, right_lo, out):
-    def blocks_of(parts, shift, at):
+        first_product(left, outside[i], allowed_ref, first - 1 + i * (nloc + 1), end_high.at[i], end_low.at[i])
+
+    def inner_blocks(parts, shift, at):
+        return [parts[0][t - shift, at] for t in range(1, nloc - 1)]
+
+    def outer_blocks(parts, shift, at):
         own, ends = parts
         start = jnp.where(shift == 1, ends[0, at], own[jnp.maximum(-shift, 0), at])
         end = jnp.where(shift == -1, ends[1, at], own[jnp.minimum(nloc - 1 - shift, nloc - 1), at])
         return [start, end]
 
-    second_product(blocks_of, shifts_ref, (high, end_high), (low, end_low), right_hi, right_lo, out)
+    high, low = (own_high, end_high), (own_low, end_low)
+    second_product(inner_blocks, shifts_ref, high, low, right_hi, right_lo, inner_out)
+    second_product(outer_blocks, shifts_ref, high, low, right_hi, right_lo, outer_out)
 
 
 def later_chunk(n, nloc, step, shifts_ref, allowed_ref, outer, inner, outside, left_parts, right_hi, right_lo, outer_out, inner_out, high, low):
@@ -204,17 +201,10 @@
         functools.partial(own_sectors, n), "own", 4 * kops * one, [split_parts(nloc - 2), *products(nloc)],
         [SMEM] + [VMEM] * (n + 2), [allowed, *inner, parts_outer, left_parts], whole(nloc - 2),
     )
-    result_inner = call(
-        functools.partial(first_inner, nloc), "first_inner", nloc * kops * one // n, chunk_inner,
-        [SMEM] + [VMEM] * 4, [shifts, *own, right_hi, right_lo],
-    )
-    parts_outside, *ends = call(
-        functools.partial(outside_sectors, n, nloc), "outside", 2 * kops * one, [split_parts(2), *products(2)],
-        [SMEM] + [VMEM] * 3, [allowed, above, below, left_parts], whole(2),
-    )
-    result_outer = call(
-        functools.partial(first_outer, nloc), "first_outer", nloc * kops * one // n, chunk,
-        [SMEM] + [VMEM] * 6, [shifts, *own, *ends, right_hi, right_lo],
+    result_outer, result_inner, parts_outside = call(
+        functools.partial(first_chunk, n, nloc), "first_chunk", 2 * kops * one, [chunk, chunk_inner, split_parts(2)],
+        [SMEM] * 2 + [VMEM] * 7, [shifts, allowed, *own, above, below, left_parts, right_hi, right_lo],
+        [pltpu.VMEM((2, kops * rows, width), BF16)] * 2 + whole(2),
     )
 
     def mine(step):

time: 55.8 us -> 59 us (1.057); the launches traced: 55.6 us -> 58.2 us
  waiting for transfers between devices: 13.1 us -> 17.5 us
  Pallas kernels: 15.6 us -> 14.3 us
  starting transfers between devices: 22.5 us -> 21.9 us
    ppermute x3, waiting for transfers between devices: 0.33 us -> 2.25 us  [shards(): result_inner = lax.ppermute(result_inner, 'op', route) + next_inner]
    ppermute x2, waiting for transfers between devices: 2.38 us -> 3.84 us  [shifted(): return lax.ppermute(block, axis, route)]
    pallas_call x9 -> x7, Pallas kernels: 15.6 us -> 14.3 us  [call(): pl.pallas_call(body, name=name, out_shape=out_shape, in_specs=in_specs, o...]
    ppermute x3, waiting for transfers between devices: 1.64 us -> 2.67 us  [shards(): result_outer = lax.ppermute(result_outer, 'op', route) + next_outer]
  transfers between devices with their start and end apart: 13 -> 13, of which waited for: 7 -> 8; matrix products, arithmetic and copies ran while one was open for 0% -> 0% of each run, Pallas kernels for 28% -> 21%
where the time goes in v12:
time: 59 us; the launch traced here: 58.2 us
  starting transfers between devices  21.9 us (37%)
  waiting for transfers between devices  17.5 us (30%)
  Pallas kernels  14.3 us (24%)
  local copies, waits for them, and re-layouts  3.27 us (6%)
  other arithmetic  0.94 us (2%)
    pallas_call x7, Pallas kernels, call(): pl.pallas_call(body, name=name, out_shape=out_shape, in_specs=in_specs, o...  14.3 us
    ppermute x2, starting transfers between devices, shifted(): return lax.ppermute(block, axis, route)  8.41 us
    ppermute x3, starting transfers between devices, shards(): result_inner = lax.ppermute(result_inner, 'op', route) + next_inner  6.08 us
    ppermute x2, waiting for transfers between devices, shifted(): return lax.ppermute(block, axis, route)  3.84 us
    ppermute x2, waiting for transfers between devices, shards(): lax.ppermute(outer[-1] + zero[0, 0] if step == 1 else outer[-1], 'op', ro...  3.62 us
    ppermute x2, starting transfers between devices, shards(): lax.ppermute(inner[-1] + zero[0, 0] if step == 1 else inner[-1], 'op', ro...  3.59 us
    unnamed x10, local copies, waits for them, and re-layouts  3.2 us
    ppermute x1, waiting for transfers between devices, shards(): blocks = [psi, lax.ppermute(psi, 'op', route)]  2.94 us
  transfers between devices with their start and end apart: 13, of which 8 were waited for; matrix products, arithmetic and copies ran while one was open for 0% of the time, Pallas kernels for 21%

profile of v12, /device:TPU:1, one launch (start us, length us, event | category | flops | bytes accessed | tf_op | source)
XLA Modules:
  0.0 58.2 jit_solution(2019849450302508783)
XLA Ops:
  0.0 2.1 %collective-permute-start = (f32[4,64,256]{2,1,0:T(8,128)}, f32[4,64,256]{2,1,0:T(8,128)S(1)}, u32[]{:S(2)}, u32[]{:S(2)}) collective-permute-start(f32[4,64,256]{2,1,0:T(8,128)} %param.5), channel_id=1, source_target_pairs={{0,4},{4,12},{12,8},{8,0},{1,5},{5,13},{13,9},{9,1},{2,6},{6,14},{... | collective-permute-start | bytes 786440 | tf_op jit(solution)/shard_map/ppermute | solution.py:179
  2.1 0.0 copy-start.2
  2.1 1.6 %copy-done.2 = f32[8,256,256]{2,1,0:T(8,128)S(1)} copy-done((f32[8,256,256]{2,1,0:T(8,128)S(1)}, f32[8,256,256]{2,1,0:T(8,128)}, u32[]{:S(2)}) %copy-start.2) | copy-done | bytes 2097176
  3.7 0.0 copy-start.3
  3.7 1.6 %copy-done.3 = f32[8,256,256]{2,1,0:T(8,128)S(1)} copy-done((f32[8,256,256]{2,1,0:T(8,128)S(1)}, f32[8,256,256]{2,1,0:T(8,128)}, u32[]{:S(2)}) %copy-start.3) | copy-done | bytes 2097176
  5.3 0.0 copy-start.4
  5.3 1.1 %prepare.1 = (bf16[4,8,64,768]{3,2,1,0:T(8,128)(2,1)S(1)}, bf16[2048,256]{1,0:T(8,128)(2,1)S(1)}, bf16[2048,256]{1,0:T(8,128)(2,1)S(1)}, f32[1,128]{1,0:T(1,128)S(1)}) custom-call(f32[8,256,256]{2,1,0:T(8,128)S(1)} %copy-done.2, f32[8,256,256]{2,1,0:T(8,128)S(1)} %copy-done.3), custom_call_target="tpu_custom_call" | custom-call | flops 3221225472 | bytes 1048576 | tf_op jit(solution)/shard_map/prepare/pallas_call | solution.py:153
  6.4 0.0 copy-done.4
  6.4 2.9 %collective-permute-done = f32[4,64,256]{2,1,0:T(8,128)S(1)} collective-permute-done((f32[4,64,256]{2,1,0:T(8,128)}, f32[4,64,256]{2,1,0:T(8,128)S(1)}, u32[]{:S(2)}, u32[]{:S(2)}) %collective-permute-start) | collective-permute-done | bytes 262176 | tf_op jit(solution)/shard_map/ppermute | solution.py:179
  9.4 0.1 broadcast_add_fusion
  9.5 0.4 collective-permute-start.3
  9.9 3.0 %collective-permute-start.1 = (f32[2,64,256]{2,1,0:T(8,128)S(1)}, f32[2,64,256]{2,1,0:T(8,128)S(1)}, u32[]{:S(2)}, u32[]{:S(2)}) collective-permute-start(f32[2,64,256]{2,1,0:T(8,128)S(1)} %get-tuple-element.40), channel_id=1, source_target_pairs={{0,4},{4,12},{12,8},{8,0},{1,5},{5,13},{13,9},{9,1},{2,6},{6,14},{... | collective-permute-start | bytes 393224 | tf_op jit(solution)/shard_map/ppermute | solution.py:183
  12.9 1.4 %collective-permute-done.3.refs_2_ = f32[2,64,256]{2,1,0:T(8,128)S(1)} collective-permute-done((f32[2,64,256]{2,1,0:T(8,128)S(1)}, f32[2,64,256]{2,1,0:T(8,128)S(1)}, u32[]{:S(2)}, u32[]{:S(2)}) %collective-permute-start.3) | collective-permute-done | bytes 131104 | tf_op jit(solution)/shard_map/ppermute | solution.py:182
  14.2 0.6 collective-permute-start.4
  14.8 2.2 %collective-permute-done.1.refs_2_ = f32[2,64,256]{2,1,0:T(8,128)S(1)} collective-permute-done((f32[2,64,256]{2,1,0:T(8,128)S(1)}, f32[2,64,256]{2,1,0:T(8,128)S(1)}, u32[]{:S(2)}, u32[]{:S(2)}) %collective-permute-start.1) | collective-permute-done | bytes 131104 | tf_op jit(solution)/shard_map/ppermute | solution.py:183
  17.0 0.6 %collective-permute-start.2 = (f32[2,64,256]{2,1,0:T(8,128)S(1)}, f32[2,64,256]{2,1,0:T(8,128)S(1)}, u32[]{:S(2)}, u32[]{:S(2)}) collective-permute-start(f32[2,64,256]{2,1,0:T(8,128)S(1)} %collective-permute-done.1.refs_2_), channel_id=1, source_target_pairs={{0,4},{4,12},{12,8},{8,0},{1,5},{5,13},{13,9},{9,1},{2,6},{6,14},{... | collective-permute-start | bytes 393224 | tf_op jit(solution)/shard_map/ppermute | solution.py:183
  17.6 2.3 %collective-permute-done.4.refs_3_ = f32[2,64,256]{2,1,0:T(8,128)S(1)} collective-permute-done((f32[2,64,256]{2,1,0:T(8,128)S(1)}, f32[2,64,256]{2,1,0:T(8,128)S(1)}, u32[]{:S(2)}, u32[]{:S(2)}) %collective-permute-start.4) | collective-permute-done | bytes 131104 | tf_op jit(solution)/shard_map/ppermute | solution.py:182
  19.9 6.5 %collective-permute-start.5 = (f32[4,64,256]{2,1,0:T(8,128)S(1)}, f32[4,64,256]{2,1,0:T(8,128)S(1)}, u32[]{:S(2)}, u32[]{:S(2)}) collective-permute-start(f32[4,64,256]{2,1,0:T(8,128)S(1)} %pad_maximum_fusion), channel_id=1, source_target_pairs={{0,1},{1,2},{2,3},{4,5},{5,6},{6,7},{8,9},{9,10},{10,11},{12,13},{... | collective-permute-start | bytes 786440 | tf_op jit(solution)/shard_map/ppermute | solution.py:18
  26.4 0.0 copy-start
  26.4 1.9 %collective-permute-start.6 = (f32[4,64,256]{2,1,0:T(8,128)S(1)}, f32[4,64,256]{2,1,0:T(8,128)S(1)}, u32[]{:S(2)}, u32[]{:S(2)}) collective-permute-start(f32[4,64,256]{2,1,0:T(8,128)S(1)} %pad_maximum_fusion.1), channel_id=1, source_target_pairs={{1,0},{2,1},{3,2},{5,4},{6,5},{7,6},{9,8},{10,9},{11,10},{13,12},{... | collective-permute-start | bytes 786440 | tf_op jit(solution)/shard_map/ppermute | solution.py:18
  28.4 0.2 assemble.1.refs_4_.outer
  28.5 0.0 collective-permute-done.2.refs_3_
  28.6 0.0 copy-done
  28.6 0.0 copy-start.1
  28.6 1.7 %own.1 = (bf16[2,768,256]{2,1,0:T(8,128)(2,1)S(1)}, bf16[4,512,256]{2,1,0:T(8,128)(2,1)S(1)}, bf16[4,512,256]{2,1,0:T(8,128)(2,1)S(1)}) custom-call(s32[8,16]{1,0:T(8,128)S(1)} %copy-done, f32[2,64,256]{2,1,0:T(8,128)S(1)} %get-tuple-element.42.refs_0_, f32[2,64,256]{2,1,0:T(8,128)S(1)} %get-tuple-element.39.refs_1_, ...), custom_call_target="tpu_custom_call" | custom-call | flops 3221225472 | bytes 1048576 | tf_op jit(solution)/shard_map/own/pallas_call | solution.py:153
  30.3 0.0 collective-permute-done.5.above
  30.3 3.8 %collective-permute-done.6.below = f32[4,64,256]{2,1,0:T(8,128)S(1)} collective-permute-done((f32[4,64,256]{2,1,0:T(8,128)S(1)}, f32[4,64,256]{2,1,0:T(8,128)S(1)}, u32[]{:S(2)}, u32[]{:S(2)}) %collective-permute-start.6) | collective-permute-done | bytes 262176 | tf_op jit(solution)/shard_map/ppermute | solution.py:18
  34.1 0.0 copy-done.1
  34.1 2.3 %first_chunk.1 = (f32[2,64,256]{2,1,0:T(8,128)S(1)}, f32[2,64,256]{2,1,0:T(8,128)S(1)}, bf16[2,768,256]{2,1,0:T(8,128)(2,1)S(1)}) custom-call(s32[8]{0:T(128)S(1)} %copy-done.1, s32[8,16]{1,0:T(8,128)S(1)} %copy-done, bf16[4,512,256]{2,1,0:T(8,128)(2,1)S(1)} %get-tuple-element.23.own_high, bf16[4,512,256]{2,1,0:T(8,128)(2,1)S(1)} %get-tuple-element.24.own_low, ...), custom_call_target="tpu_custom_call" | custom-call | flops 1610612736 | bytes 1048576 | tf_op jit(solution)/shard_map/first_chunk/pallas_call | solution.py:153
  36.4 0.6 %collective-permute-start.7 = (f32[2,64,256]{2,1,0:T(8,128)S(1)}, f32[2,64,256]{2,1,0:T(8,128)S(1)}, u32[]{:S(2)}, u32[]{:S(2)}) collective-permute-start(f32[2,64,256]{2,1,0:T(8,128)S(1)} %get-tuple-element.27), channel_id=1, source_target_pairs={{0,4},{4,12},{12,8},{8,0},{1,5},{5,13},{13,9},{9,1},{2,6},{6,14},{... | collective-permute-start | bytes 393224 | tf_op jit(solution)/shard_map/ppermute | solution.py:221
  37.0 3.1 %collective-permute-start.10 = (f32[2,64,256]{2,1,0:T(8,128)S(1)}, f32[2,64,256]{2,1,0:T(8,128)S(1)}, u32[]{:S(2)}, u32[]{:S(2)}) collective-permute-start(f32[2,64,256]{2,1,0:T(8,128)S(1)} %get-tuple-element.33), channel_id=1, source_target_pairs={{0,4},{4,12},{12,8},{8,0},{1,5},{5,13},{13,9},{9,1},{2,6},{6,14},{... | collective-permute-start | bytes 393224 | tf_op jit(solution)/shard_map/ppermute | solution.py:220
  40.0 3.0 %chunk.3 = (f32[2,64,256]{2,1,0:T(8,128)S(1)}, f32[2,64,256]{2,1,0:T(8,128)S(1)}) custom-call(s32[8]{0:T(128)S(1)} %copy-done.1, s32[8,16]{1,0:T(8,128)S(1)} %copy-done, bf16[2,768,256]{2,1,0:T(8,128)(2,1)S(1)} %assemble.1.refs_4_.outer, bf16[2,768,256]{2,1,0:T(8,128)(2,1)S(1)} %get-tuple-element.28.inner, ...), custom_call_target="tpu_custom_call" | custom-call | flops 3221225472 | bytes 1048576 | tf_op jit(solution)/shard_map/chunk/pallas_call | solution.py:153
  43.1 0.0 collective-permute-done.7
  43.1 0.1 collective-permute-start.8
  43.2 3.0 %chunk.4 = (f32[2,64,256]{2,1,0:T(8,128)S(1)}, f32[2,64,256]{2,1,0:T(8,128)S(1)}) custom-call(s32[8]{0:T(128)S(1)} %copy-done.1, s32[8,16]{1,0:T(8,128)S(1)} %copy-done, bf16[2,768,256]{2,1,0:T(8,128)(2,1)S(1)} %assemble.1.refs_4_.outer, bf16[2,768,256]{2,1,0:T(8,128)(2,1)S(1)} %get-tuple-element.28.inner, ...), custom_call_target="tpu_custom_call" | custom-call | flops 3221225472 | bytes 1048576 | tf_op jit(solution)/shard_map/chunk/pallas_call | solution.py:153
  46.3 0.0 collective-permute-done.10
  46.3 1.7 %collective-permute-start.11 = (f32[2,64,256]{2,1,0:T(8,128)S(1)}, f32[2,64,256]{2,1,0:T(8,128)S(1)}, u32[]{:S(2)}, u32[]{:S(2)}) collective-permute-start(f32[2,64,256]{2,1,0:T(8,128)S(1)} %add.34), channel_id=1, source_target_pairs={{0,4},{4,12},{12,8},{8,0},{1,5},{5,13},{13,9},{9,1},{2,6},{6,14},{... | collective-permute-start | bytes 393224 | tf_op jit(solution)/shard_map/ppermute | solution.py:220
  48.0 1.5 %collective-permute-done.8 = f32[2,64,256]{2,1,0:T(8,128)S(1)} collective-permute-done((f32[2,64,256]{2,1,0:T(8,128)S(1)}, f32[2,64,256]{2,1,0:T(8,128)S(1)}, u32[]{:S(2)}, u32[]{:S(2)}) %collective-permute-start.8) | collective-permute-done | bytes 131104 | tf_op jit(solution)/shard_map/ppermute | solution.py:221
  49.5 0.1 collective-permute-start.9
  49.6 3.0 %chunk.5 = (f32[2,64,256]{2,1,0:T(8,128)S(1)}, f32[2,64,256]{2,1,0:T(8,128)S(1)}) custom-call(s32[8]{0:T(128)S(1)} %copy-done.1, s32[8,16]{1,0:T(8,128)S(1)} %copy-done, bf16[2,768,256]{2,1,0:T(8,128)(2,1)S(1)} %assemble.1.refs_4_.outer, bf16[2,768,256]{2,1,0:T(8,128)(2,1)S(1)} %get-tuple-element.28.inner, ...), custom_call_target="tpu_custom_call" | custom-call | flops 3221225472 | bytes 1048576 | tf_op jit(solution)/shard_map/chunk/pallas_call | solution.py:153
  52.6 0.0 collective-permute-done.11
  52.7 1.4 %collective-permute-start.12 = (f32[2,64,256]{2,1,0:T(8,128)S(1)}, f32[2,64,256]{2,1,0:T(8,128)S(1)}, u32[]{:S(2)}, u32[]{:S(2)}) collective-permute-start(f32[2,64,256]{2,1,0:T(8,128)S(1)} %add.35), channel_id=1, source_target_pairs={{0,4},{4,12},{12,8},{8,0},{1,5},{5,13},{13,9},{9,1},{2,6},{6,14},{... | collective-permute-start | bytes 393224 | tf_op jit(solution)/shard_map/ppermute | solution.py:220
  54.0 1.1 %collective-permute-done.9 = f32[2,64,256]{2,1,0:T(8,128)S(1)} collective-permute-done((f32[2,64,256]{2,1,0:T(8,128)S(1)}, f32[2,64,256]{2,1,0:T(8,128)S(1)}, u32[]{:S(2)}, u32[]{:S(2)}) %collective-permute-start.9) | collective-permute-done | bytes 131104 | tf_op jit(solution)/shard_map/ppermute | solution.py:221
  55.2 2.2 %collective-permute-done.12 = f32[2,64,256]{2,1,0:T(8,128)S(1)} collective-permute-done((f32[2,64,256]{2,1,0:T(8,128)S(1)}, f32[2,64,256]{2,1,0:T(8,128)S(1)}, u32[]{:S(2)}, u32[]{:S(2)}) %collective-permute-start.12) | collective-permute-done | bytes 131104 | tf_op jit(solution)/shard_map/ppermute | solution.py:220
  57.5 0.7 %pad_maximum_fusion.2 = f32[4,64,256]{2,1,0:T(8,128)} fusion(f32[1,64,256]{2,1,0:T(8,128)S(1)} %get-tuple-element.44, f32[2,64,256]{2,1,0:T(8,128)S(1)} %add.36, f32[1,64,256]{2,1,0:T(8,128)S(1)} %get-tuple-element.43), kind=kLoop, calls=%fused_computation.2 | loop fusion | flops 131072 | bytes 524288 | tf_op jit(solution)/shard_map/concatenate | solution.py:222
  (14 shorter events, 0.2 us)
Async XLA Ops:
  0.0 9.4 %collective-permute-start = (f32[4,64,256]{2,1,0:T(8,128)}, f32[4,64,256]{2,1,0:T(8,128)S(1)}, u32[]{:S(2)}, u32[]{:S(2)}) collective-permute-start(f32[4,64,256]{2,1,0:T(8,128)} %param.5), channel_id=1, source_target_pairs={{0,4},{4,12},{12,8},{8,0},{1,5},{5,13},{13,9},{9,1},{2,6},{6,14},{... | collective-permute-start | bytes 786440 | tf_op jit(solution)/shard_map/ppermute | solution.py:179
  2.1 1.6 %copy-start.2 = (f32[8,256,256]{2,1,0:T(8,128)S(1)}, f32[8,256,256]{2,1,0:T(8,128)}, u32[]{:S(2)}) copy-start(f32[8,256,256]{2,1,0:T(8,128)} %left_ref.1) | copy-start | bytes 6291460
  3.7 1.6 %copy-start.3 = (f32[8,256,256]{2,1,0:T(8,128)S(1)}, f32[8,256,256]{2,1,0:T(8,128)}, u32[]{:S(2)}) copy-start(f32[8,256,256]{2,1,0:T(8,128)} %right_ref.1) | copy-start | bytes 6291460
  5.3 1.1 %copy-start.4 = (f32[4,64,256]{2,1,0:T(8,128)S(1)}, f32[4,64,256]{2,1,0:T(8,128)}, u32[]{:S(2)}) copy-start(f32[4,64,256]{2,1,0:T(8,128)} %param.5) | copy-start | bytes 786436
  9.5 4.8 %collective-permute-start.3 = (f32[2,64,256]{2,1,0:T(8,128)S(1)}, f32[2,64,256]{2,1,0:T(8,128)S(1)}, u32[]{:S(2)}, u32[]{:S(2)}) collective-permute-start(f32[2,64,256]{2,1,0:T(8,128)S(1)} %get-tuple-element.37), channel_id=1, source_target_pairs={{0,4},{4,12},{12,8},{8,0},{1,5},{5,13},{13,9},{9,1},{2,6},{6,14},{... | collective-permute-start | bytes 393224 | tf_op jit(solution)/shard_map/ppermute | solution.py:182
  9.9 7.1 %collective-permute-start.1 = (f32[2,64,256]{2,1,0:T(8,128)S(1)}, f32[2,64,256]{2,1,0:T(8,128)S(1)}, u32[]{:S(2)}, u32[]{:S(2)}) collective-permute-start(f32[2,64,256]{2,1,0:T(8,128)S(1)} %get-tuple-element.40), channel_id=1, source_target_pairs={{0,4},{4,12},{12,8},{8,0},{1,5},{5,13},{13,9},{9,1},{2,6},{6,14},{... | collective-permute-start | bytes 393224 | tf_op jit(solution)/shard_map/ppermute | solution.py:183
  14.2 5.6 %collective-permute-start.4 = (f32[2,64,256]{2,1,0:T(8,128)S(1)}, f32[2,64,256]{2,1,0:T(8,128)S(1)}, u32[]{:S(2)}, u32[]{:S(2)}) collective-permute-start(f32[2,64,256]{2,1,0:T(8,128)S(1)} %collective-permute-done.3.refs_2_), channel_id=1, source_target_pairs={{0,4},{4,12},{12,8},{8,0},{1,5},{5,13},{13,9},{9,1},{2,6},{6,14},{... | collective-permute-start | bytes 393224 | tf_op jit(solution)/shard_map/ppermute | solution.py:182
  17.0 11.6 %collective-permute-start.2 = (f32[2,64,256]{2,1,0:T(8,128)S(1)}, f32[2,64,256]{2,1,0:T(8,128)S(1)}, u32[]{:S(2)}, u32[]{:S(2)}) collective-permute-start(f32[2,64,256]{2,1,0:T(8,128)S(1)} %collective-permute-done.1.refs_2_), channel_id=1, source_target_pairs={{0,4},{4,12},{12,8},{8,0},{1,5},{5,13},{13,9},{9,1},{2,6},{6,14},{... | collective-permute-start | bytes 393224 | tf_op jit(solution)/shard_map/ppermute | solution.py:183
  19.9 10.4 %collective-permute-start.5 = (f32[4,64,256]{2,1,0:T(8,128)S(1)}, f32[4,64,256]{2,1,0:T(8,128)S(1)}, u32[]{:S(2)}, u32[]{:S(2)}) collective-permute-start(f32[4,64,256]{2,1,0:T(8,128)S(1)} %pad_maximum_fusion), channel_id=1, source_target_pairs={{0,1},{1,2},{2,3},{4,5},{5,6},{6,7},{8,9},{9,10},{10,11},{12,13},{... | collective-permute-start | bytes 786440 | tf_op jit(solution)/shard_map/ppermute | solution.py:18
  26.4 2.1 %copy-start = (s32[8,16]{1,0:T(8,128)S(1)}, s32[8,16]{1,0:T(8,128)}, u32[]{:S(2)}) copy-start(s32[8,16]{1,0:T(8,128)} %allowed_ref.9) | copy-start | bytes 1540
  26.4 7.7 %collective-permute-start.6 = (f32[4,64,256]{2,1,0:T(8,128)S(1)}, f32[4,64,256]{2,1,0:T(8,128)S(1)}, u32[]{:S(2)}, u32[]{:S(2)}) collective-permute-start(f32[4,64,256]{2,1,0:T(8,128)S(1)} %pad_maximum_fusion.1), channel_id=1, source_target_pairs={{1,0},{2,1},{3,2},{5,4},{6,5},{7,6},{9,8},{10,9},{11,10},{13,12},{... | collective-permute-start | bytes 786440 | tf_op jit(solution)/shard_map/ppermute | solution.py:18
  28.6 5.5 %copy-start.1 = (s32[8]{0:T(128)S(1)}, s32[8]{0:T(128)}, u32[]{:S(2)}) copy-start(s32[8]{0:T(128)} %shifts_ref.7) | copy-start | bytes 100
  36.4 6.7 %collective-permute-start.7 = (f32[2,64,256]{2,1,0:T(8,128)S(1)}, f32[2,64,256]{2,1,0:T(8,128)S(1)}, u32[]{:S(2)}, u32[]{:S(2)}) collective-permute-start(f32[2,64,256]{2,1,0:T(8,128)S(1)} %get-tuple-element.27), channel_id=1, source_target_pairs={{0,4},{4,12},{12,8},{8,0},{1,5},{5,13},{13,9},{9,1},{2,6},{6,14},{... | collective-permute-start | bytes 393224 | tf_op jit(solution)/shard_map/ppermute | solution.py:221
  37.0 9.3 %collective-permute-start.10 = (f32[2,64,256]{2,1,0:T(8,128)S(1)}, f32[2,64,256]{2,1,0:T(8,128)S(1)}, u32[]{:S(2)}, u32[]{:S(2)}) collective-permute-start(f32[2,64,256]{2,1,0:T(8,128)S(1)} %get-tuple-element.33), channel_id=1, source_target_pairs={{0,4},{4,12},{12,8},{8,0},{1,5},{5,13},{13,9},{9,1},{2,6},{6,14},{... | collective-permute-start | bytes 393224 | tf_op jit(solution)/shard_map/ppermute | solution.py:220
  43.1 6.4 %collective-permute-start.8 = (f32[2,64,256]{2,1,0:T(8,128)S(1)}, f32[2,64,256]{2,1,0:T(8,128)S(1)}, u32[]{:S(2)}, u32[]{:S(2)}) collective-permute-start(f32[2,64,256]{2,1,0:T(8,128)S(1)} %add.31), channel_id=1, source_target_pairs={{0,4},{4,12},{12,8},{8,0},{1,5},{5,13},{13,9},{9,1},{2,6},{6,14},{... | collective-permute-start | bytes 393224 | tf_op jit(solution)/shard_map/ppermute | solution.py:221
  46.3 6.3 %collective-permute-start.11 = (f32[2,64,256]{2,1,0:T(8,128)S(1)}, f32[2,64,256]{2,1,0:T(8,128)S(1)}, u32[]{:S(2)}, u32[]{:S(2)}) collective-permute-start(f32[2,64,256]{2,1,0:T(8,128)S(1)} %add.34), channel_id=1, source_target_pairs={{0,4},{4,12},{12,8},{8,0},{1,5},{5,13},{13,9},{9,1},{2,6},{6,14},{... | collective-permute-start | bytes 393224 | tf_op jit(solution)/shard_map/ppermute | solution.py:220
  49.5 5.6 %collective-permute-start.9 = (f32[2,64,256]{2,1,0:T(8,128)S(1)}, f32[2,64,256]{2,1,0:T(8,128)S(1)}, u32[]{:S(2)}, u32[]{:S(2)}) collective-permute-start(f32[2,64,256]{2,1,0:T(8,128)S(1)} %add.32), channel_id=1, source_target_pairs={{0,4},{4,12},{12,8},{8,0},{1,5},{5,13},{13,9},{9,1},{2,6},{6,14},{... | collective-permute-start | bytes 393224 | tf_op jit(solution)/shard_map/ppermute | solution.py:221
  52.7 4.8 %collective-permute-start.12 = (f32[2,64,256]{2,1,0:T(8,128)S(1)}, f32[2,64,256]{2,1,0:T(8,128)S(1)}, u32[]{:S(2)}, u32[]{:S(2)}) collective-permute-start(f32[2,64,256]{2,1,0:T(8,128)S(1)} %add.35), channel_id=1, source_target_pairs={{0,4},{4,12},{12,8},{8,0},{1,5},{5,13},{13,9},{9,1},{2,6},{6,14},{... | collective-permute-start | bytes 393224 | tf_op jit(solution)/shard_map/ppermute | solution.py:220

commit v13 on v12

--- a/solution.py
+++ b/solution.py
@@ -132,7 +132,8 @@
     second_product(outer_blocks, shifts_ref, high, low, right_hi, right_lo, outer_out)
 
 
-def later_chunk(n, nloc, step, shifts_ref, allowed_ref, outer, inner, outside, left_parts, right_hi, right_lo, outer_out, inner_out, high, low):
+def later_chunk(n, nloc, step, shifts_ref, allowed_ref, outer, inner, outside, left_parts, right_hi, right_lo, *refs):
+    outer_out, inner_out, high, low = refs[-4:]
     left = chunk_left(n, step, left_parts)
     first = lax.axis_index(("sec", "sub")) * nloc
     sources = [outside.at[0], outer.at[0], *[inner.at[i] for i in range(nloc - 2)], outer.at[1], outside.at[1]]
@@ -207,18 +208,19 @@
         [pltpu.VMEM((2, kops * rows, width), BF16)] * 2 + whole(2),
     )
 
-    def mine(step):
+    def mine(step, *before):
         return call(
             functools.partial(later_chunk, n, nloc, step), "chunk", 4 * nloc * kops * one // n, [chunk, chunk_inner],
-            [SMEM] * 2 + [VMEM] * 6,
-            [shifts, allowed, parts_outer, parts_inner, parts_outside, left_parts, right_hi, right_lo],
+            [SMEM] * 2 + [VMEM] * 6 + [pl.BlockSpec(memory_space=pl.ANY)] * len(before),
+            [shifts, allowed, parts_outer, parts_inner, parts_outside, left_parts, right_hi, right_lo, *before],
             [pltpu.VMEM((nloc + 2, kops * rows, width), BF16)] * 2,
         )
 
     for step in range(1, n):
-        next_outer, next_inner = mine(step)
-        result_inner = lax.ppermute(result_inner, "op", route) + next_inner
-        result_outer = lax.ppermute(result_outer, "op", route) + next_outer
+        moved_outer, moved_inner = lax.ppermute(result_outer, "op", route), lax.ppermute(result_inner, "op", route)
+        before = [result_outer, result_inner] if step < n - 1 else [moved_inner]
+        next_outer, next_inner = mine(step, *before)
+        result_outer, result_inner = moved_outer + next_outer, moved_inner + next_inner
     return jnp.concatenate([result_outer[:1], result_inner, result_outer[1:]])
 
 

time: 59 us -> 59.3 us (level)
  starting transfers between devices: 21.9 us -> 23.1 us
    ppermute x6, starting transfers between devices: 6.85 us -> 8.01 us  [the longest x3 4.09 us: shards(): lax.ppermute(result_inner, 'op', route)]
  transfers between devices with their start and end apart: 13 -> 13, of which waited for: 8 -> 7; matrix products, arithmetic and copies ran while one was open for 0% -> 0% of each run, Pallas kernels for 21% -> 20%
where the time goes in v13:
time: 59.3 us; the launch traced here: 59 us
  starting transfers between devices  23.1 us (39%)
  waiting for transfers between devices  17.2 us (29%)
  Pallas kernels  14.2 us (24%)
  local copies, waits for them, and re-layouts  3.27 us (6%)
  other arithmetic  0.94 us (2%)
    pallas_call x7, Pallas kernels, call(): pl.pallas_call(body, name=name, out_shape=out_shape, in_specs=in_specs, o...  14.2 us
    ppermute x2, starting transfers between devices, shifted(): return lax.ppermute(block, axis, route)  8.41 us
    ppermute x3, starting transfers between devices, shards(): lax.ppermute(result_inner, 'op', route)  4.09 us
    ppermute x3, starting transfers between devices, shards(): lax.ppermute(result_outer, 'op', route)  3.92 us
    ppermute x2, waiting for transfers between devices, shifted(): return lax.ppermute(block, axis, route)  3.84 us
    ppermute x3, waiting for transfers between devices, shards(): lax.ppermute(result_inner, 'op', route)  3.71 us
    ppermute x2, waiting for transfers between devices, shards(): lax.ppermute(outer[-1] + zero[0, 0] if step == 1 else outer[-1], 'op', ro...  3.62 us
    ppermute x2, starting transfers between devices, shards(): lax.ppermute(inner[-1] + zero[0, 0] if step == 1 else inner[-1], 'op', ro...  3.59 us
  transfers between devices with their start and end apart: 13, of which 7 were waited for; matrix products, arithmetic and copies ran while one was open for 0% of the time, Pallas kernels for 20%

profile of v13, /device:TPU:1, one launch (start us, length us, event | category | flops | bytes accessed | tf_op | source)
XLA Modules:
  0.0 59.0 jit_solution(1110097747875034795)
XLA Ops:
  0.0 2.1 %collective-permute-start = (f32[4,64,256]{2,1,0:T(8,128)}, f32[4,64,256]{2,1,0:T(8,128)S(1)}, u32[]{:S(2)}, u32[]{:S(2)}) collective-permute-start(f32[4,64,256]{2,1,0:T(8,128)} %param.5), channel_id=1, source_target_pairs={{0,4},{4,12},{12,8},{8,0},{1,5},{5,13},{13,9},{9,1},{2,6},{6,14},{... | collective-permute-start | bytes 786440 | tf_op jit(solution)/shard_map/ppermute | solution.py:180
  2.1 0.0 copy-start.2
  2.1 1.6 %copy-done.2 = f32[8,256,256]{2,1,0:T(8,128)S(1)} copy-done((f32[8,256,256]{2,1,0:T(8,128)S(1)}, f32[8,256,256]{2,1,0:T(8,128)}, u32[]{:S(2)}) %copy-start.2) | copy-done | bytes 2097176
  3.7 0.0 copy-start.3
  3.7 1.6 %copy-done.3 = f32[8,256,256]{2,1,0:T(8,128)S(1)} copy-done((f32[8,256,256]{2,1,0:T(8,128)S(1)}, f32[8,256,256]{2,1,0:T(8,128)}, u32[]{:S(2)}) %copy-start.3) | copy-done | bytes 2097176
  5.3 0.0 copy-start.4
  5.3 1.1 %prepare.1 = (bf16[4,8,64,768]{3,2,1,0:T(8,128)(2,1)S(1)}, bf16[2048,256]{1,0:T(8,128)(2,1)S(1)}, bf16[2048,256]{1,0:T(8,128)(2,1)S(1)}, f32[1,128]{1,0:T(1,128)S(1)}) custom-call(f32[8,256,256]{2,1,0:T(8,128)S(1)} %copy-done.2, f32[8,256,256]{2,1,0:T(8,128)S(1)} %copy-done.3), custom_call_target="tpu_custom_call" | custom-call | flops 3221225472 | bytes 1048576 | tf_op jit(solution)/shard_map/prepare/pallas_call | solution.py:154
  6.4 0.0 copy-done.4
  6.4 2.9 %collective-permute-done = f32[4,64,256]{2,1,0:T(8,128)S(1)} collective-permute-done((f32[4,64,256]{2,1,0:T(8,128)}, f32[4,64,256]{2,1,0:T(8,128)S(1)}, u32[]{:S(2)}, u32[]{:S(2)}) %collective-permute-start) | collective-permute-done | bytes 262176 | tf_op jit(solution)/shard_map/ppermute | solution.py:180
  9.4 0.1 broadcast_add_fusion
  9.5 0.4 collective-permute-start.3
  9.9 3.0 %collective-permute-start.1 = (f32[2,64,256]{2,1,0:T(8,128)S(1)}, f32[2,64,256]{2,1,0:T(8,128)S(1)}, u32[]{:S(2)}, u32[]{:S(2)}) collective-permute-start(f32[2,64,256]{2,1,0:T(8,128)S(1)} %get-tuple-element.40), channel_id=1, source_target_pairs={{0,4},{4,12},{12,8},{8,0},{1,5},{5,13},{13,9},{9,1},{2,6},{6,14},{... | collective-permute-start | bytes 393224 | tf_op jit(solution)/shard_map/ppermute | solution.py:184
  12.9 1.4 %collective-permute-done.3.refs_2_ = f32[2,64,256]{2,1,0:T(8,128)S(1)} collective-permute-done((f32[2,64,256]{2,1,0:T(8,128)S(1)}, f32[2,64,256]{2,1,0:T(8,128)S(1)}, u32[]{:S(2)}, u32[]{:S(2)}) %collective-permute-start.3) | collective-permute-done | bytes 131104 | tf_op jit(solution)/shard_map/ppermute | solution.py:183
  14.2 0.6 collective-permute-start.4
  14.8 2.2 %collective-permute-done.1.refs_2_ = f32[2,64,256]{2,1,0:T(8,128)S(1)} collective-permute-done((f32[2,64,256]{2,1,0:T(8,128)S(1)}, f32[2,64,256]{2,1,0:T(8,128)S(1)}, u32[]{:S(2)}, u32[]{:S(2)}) %collective-permute-start.1) | collective-permute-done | bytes 131104 | tf_op jit(solution)/shard_map/ppermute | solution.py:184
  17.0 0.6 %collective-permute-start.2 = (f32[2,64,256]{2,1,0:T(8,128)S(1)}, f32[2,64,256]{2,1,0:T(8,128)S(1)}, u32[]{:S(2)}, u32[]{:S(2)}) collective-permute-start(f32[2,64,256]{2,1,0:T(8,128)S(1)} %collective-permute-done.1.refs_2_), channel_id=1, source_target_pairs={{0,4},{4,12},{12,8},{8,0},{1,5},{5,13},{13,9},{9,1},{2,6},{6,14},{... | collective-permute-start | bytes 393224 | tf_op jit(solution)/shard_map/ppermute | solution.py:184
  17.6 2.3 %collective-permute-done.4.refs_3_ = f32[2,64,256]{2,1,0:T(8,128)S(1)} collective-permute-done((f32[2,64,256]{2,1,0:T(8,128)S(1)}, f32[2,64,256]{2,1,0:T(8,128)S(1)}, u32[]{:S(2)}, u32[]{:S(2)}) %collective-permute-start.4) | collective-permute-done | bytes 131104 | tf_op jit(solution)/shard_map/ppermute | solution.py:183
  19.9 6.5 %collective-permute-start.5 = (f32[4,64,256]{2,1,0:T(8,128)S(1)}, f32[4,64,256]{2,1,0:T(8,128)S(1)}, u32[]{:S(2)}, u32[]{:S(2)}) collective-permute-start(f32[4,64,256]{2,1,0:T(8,128)S(1)} %pad_maximum_fusion), channel_id=1, source_target_pairs={{0,1},{1,2},{2,3},{4,5},{5,6},{6,7},{8,9},{9,10},{10,11},{12,13},{... | collective-permute-start | bytes 786440 | tf_op jit(solution)/shard_map/ppermute | solution.py:18
  26.4 0.0 copy-start
  26.4 1.9 %collective-permute-start.6 = (f32[4,64,256]{2,1,0:T(8,128)S(1)}, f32[4,64,256]{2,1,0:T(8,128)S(1)}, u32[]{:S(2)}, u32[]{:S(2)}) collective-permute-start(f32[4,64,256]{2,1,0:T(8,128)S(1)} %pad_maximum_fusion.1), channel_id=1, source_target_pairs={{1,0},{2,1},{3,2},{5,4},{6,5},{7,6},{9,8},{10,9},{11,10},{13,12},{... | collective-permute-start | bytes 786440 | tf_op jit(solution)/shard_map/ppermute | solution.py:18
  28.4 0.2 assemble.1.refs_4_.outer
  28.5 0.0 collective-permute-done.2.refs_3_
  28.6 0.0 copy-done
  28.6 0.0 copy-start.1
  28.6 1.7 %own.1 = (bf16[2,768,256]{2,1,0:T(8,128)(2,1)S(1)}, bf16[4,512,256]{2,1,0:T(8,128)(2,1)S(1)}, bf16[4,512,256]{2,1,0:T(8,128)(2,1)S(1)}) custom-call(s32[8,16]{1,0:T(8,128)S(1)} %copy-done, f32[2,64,256]{2,1,0:T(8,128)S(1)} %get-tuple-element.42.refs_0_, f32[2,64,256]{2,1,0:T(8,128)S(1)} %get-tuple-element.39.refs_1_, ...), custom_call_target="tpu_custom_call" | custom-call | flops 3221225472 | bytes 1048576 | tf_op jit(solution)/shard_map/own/pallas_call | solution.py:154
  30.3 0.0 collective-permute-done.5.above
  30.3 3.8 %collective-permute-done.6.below = f32[4,64,256]{2,1,0:T(8,128)S(1)} collective-permute-done((f32[4,64,256]{2,1,0:T(8,128)S(1)}, f32[4,64,256]{2,1,0:T(8,128)S(1)}, u32[]{:S(2)}, u32[]{:S(2)}) %collective-permute-start.6) | collective-permute-done | bytes 262176 | tf_op jit(solution)/shard_map/ppermute | solution.py:18
  34.1 0.0 copy-done.1
  34.1 2.3 %first_chunk.1 = (f32[2,64,256]{2,1,0:T(8,128)S(1)}, f32[2,64,256]{2,1,0:T(8,128)S(1)}, bf16[2,768,256]{2,1,0:T(8,128)(2,1)S(1)}) custom-call(s32[8]{0:T(128)S(1)} %copy-done.1, s32[8,16]{1,0:T(8,128)S(1)} %copy-done, bf16[4,512,256]{2,1,0:T(8,128)(2,1)S(1)} %get-tuple-element.23.own_high, bf16[4,512,256]{2,1,0:T(8,128)(2,1)S(1)} %get-tuple-element.24.own_low, ...), custom_call_target="tpu_custom_call" | custom-call | flops 1610612736 | bytes 1048576 | tf_op jit(solution)/shard_map/first_chunk/pallas_call | solution.py:154
  36.4 0.6 %collective-permute-start.7 = (f32[2,64,256]{2,1,0:T(8,128)S(1)}, f32[2,64,256]{2,1,0:T(8,128)S(1)}, u32[]{:S(2)}, u32[]{:S(2)}) collective-permute-start(f32[2,64,256]{2,1,0:T(8,128)S(1)} %get-tuple-element.27.refs_0_), channel_id=1, source_target_pairs={{0,4},{4,12},{12,8},{8,0},{1,5},{5,13},{13,9},{9,1},{2,6},{6,14},{... | collective-permute-start | bytes 393224 | tf_op jit(solution)/shard_map/ppermute | solution.py:220
  37.0 3.1 %collective-permute-start.9 = (f32[2,64,256]{2,1,0:T(8,128)S(1)}, f32[2,64,256]{2,1,0:T(8,128)S(1)}, u32[]{:S(2)}, u32[]{:S(2)}) collective-permute-start(f32[2,64,256]{2,1,0:T(8,128)S(1)} %get-tuple-element.30.refs_1_), channel_id=1, source_target_pairs={{0,4},{4,12},{12,8},{8,0},{1,5},{5,13},{13,9},{9,1},{2,6},{6,14},{... | collective-permute-start | bytes 393224 | tf_op jit(solution)/shard_map/ppermute | solution.py:220
  40.0 3.0 %chunk.3 = (f32[2,64,256]{2,1,0:T(8,128)S(1)}, f32[2,64,256]{2,1,0:T(8,128)S(1)}) custom-call(s32[8]{0:T(128)S(1)} %copy-done.1, s32[8,16]{1,0:T(8,128)S(1)} %copy-done, bf16[2,768,256]{2,1,0:T(8,128)(2,1)S(1)} %assemble.1.refs_4_.outer, bf16[2,768,256]{2,1,0:T(8,128)(2,1)S(1)} %get-tuple-element.28.inner, ...), custom_call_target="tpu_custom_call" | custom-call | flops 3221225472 | bytes 1048576 | tf_op jit(solution)/shard_map/chunk/pallas_call | solution.py:154
  43.1 0.0 collective-permute-done.9
  43.1 0.8 %collective-permute-start.11 = (f32[2,64,256]{2,1,0:T(8,128)S(1)}, f32[2,64,256]{2,1,0:T(8,128)S(1)}, u32[]{:S(2)}, u32[]{:S(2)}) collective-permute-start(f32[2,64,256]{2,1,0:T(8,128)S(1)} %add.32.refs_1_), channel_id=1, source_target_pairs={{0,4},{4,12},{12,8},{8,0},{1,5},{5,13},{13,9},{9,1},{2,6},{6,14},{... | collective-permute-start | bytes 393224 | tf_op jit(solution)/shard_map/ppermute | solution.py:220
  43.9 0.0 collective-permute-done.7
  44.0 2.4 %collective-permute-start.8 = (f32[2,64,256]{2,1,0:T(8,128)S(1)}, f32[2,64,256]{2,1,0:T(8,128)S(1)}, u32[]{:S(2)}, u32[]{:S(2)}) collective-permute-start(f32[2,64,256]{2,1,0:T(8,128)S(1)} %add.31.refs_0_), channel_id=1, source_target_pairs={{0,4},{4,12},{12,8},{8,0},{1,5},{5,13},{13,9},{9,1},{2,6},{6,14},{... | collective-permute-start | bytes 393224 | tf_op jit(solution)/shard_map/ppermute | solution.py:220
  46.3 3.0 %chunk.4 = (f32[2,64,256]{2,1,0:T(8,128)S(1)}, f32[2,64,256]{2,1,0:T(8,128)S(1)}) custom-call(s32[8]{0:T(128)S(1)} %copy-done.1, s32[8,16]{1,0:T(8,128)S(1)} %copy-done, bf16[2,768,256]{2,1,0:T(8,128)(2,1)S(1)} %assemble.1.refs_4_.outer, bf16[2,768,256]{2,1,0:T(8,128)(2,1)S(1)} %get-tuple-element.28.inner, ...), custom_call_target="tpu_custom_call" | custom-call | flops 3221225472 | bytes 1048576 | tf_op jit(solution)/shard_map/chunk/pallas_call | solution.py:154
  49.3 0.0 collective-permute-done.11
  49.4 0.2 collective-permute-start.12
  49.6 0.9 %collective-permute-done.8 = f32[2,64,256]{2,1,0:T(8,128)S(1)} collective-permute-done((f32[2,64,256]{2,1,0:T(8,128)S(1)}, f32[2,64,256]{2,1,0:T(8,128)S(1)}, u32[]{:S(2)}, u32[]{:S(2)}) %collective-permute-start.8) | collective-permute-done | bytes 131104 | tf_op jit(solution)/shard_map/ppermute | solution.py:220
  50.5 1.0 %collective-permute-start.10 = (f32[2,64,256]{2,1,0:T(8,128)S(1)}, f32[2,64,256]{2,1,0:T(8,128)S(1)}, u32[]{:S(2)}, u32[]{:S(2)}) collective-permute-start(f32[2,64,256]{2,1,0:T(8,128)S(1)} %add.33), channel_id=1, source_target_pairs={{0,4},{4,12},{12,8},{8,0},{1,5},{5,13},{13,9},{9,1},{2,6},{6,14},{... | collective-permute-start | bytes 393224 | tf_op jit(solution)/shard_map/ppermute | solution.py:220
  51.5 3.7 %collective-permute-done.12.refs_0_ = f32[2,64,256]{2,1,0:T(8,128)S(1)} collective-permute-done((f32[2,64,256]{2,1,0:T(8,128)S(1)}, f32[2,64,256]{2,1,0:T(8,128)S(1)}, u32[]{:S(2)}, u32[]{:S(2)}) %collective-permute-start.12) | collective-permute-done | bytes 131104 | tf_op jit(solution)/shard_map/ppermute | solution.py:220
  55.2 3.0 %chunk.5 = (f32[2,64,256]{2,1,0:T(8,128)S(1)}, f32[2,64,256]{2,1,0:T(8,128)S(1)}) custom-call(s32[8]{0:T(128)S(1)} %copy-done.1, s32[8,16]{1,0:T(8,128)S(1)} %copy-done, bf16[2,768,256]{2,1,0:T(8,128)(2,1)S(1)} %assemble.1.refs_4_.outer, bf16[2,768,256]{2,1,0:T(8,128)(2,1)S(1)} %get-tuple-element.28.inner, ...), custom_call_target="tpu_custom_call" | custom-call | flops 3221225472 | bytes 1048576 | tf_op jit(solution)/shard_map/chunk/pallas_call | solution.py:154
  58.2 0.0 collective-permute-done.10
  58.3 0.7 %pad_maximum_fusion.2 = f32[4,64,256]{2,1,0:T(8,128)} fusion(f32[1,64,256]{2,1,0:T(8,128)S(1)} %get-tuple-element.44, f32[2,64,256]{2,1,0:T(8,128)S(1)} %add.36, f32[1,64,256]{2,1,0:T(8,128)S(1)} %get-tuple-element.43), kind=kLoop, calls=%fused_computation.2 | loop fusion | flops 131072 | bytes 524288 | tf_op jit(solution)/shard_map/concatenate | solution.py:224
  (14 shorter events, 0.2 us)
Async XLA Ops:
  0.0 9.4 %collective-permute-start = (f32[4,64,256]{2,1,0:T(8,128)}, f32[4,64,256]{2,1,0:T(8,128)S(1)}, u32[]{:S(2)}, u32[]{:S(2)}) collective-permute-start(f32[4,64,256]{2,1,0:T(8,128)} %param.5), channel_id=1, source_target_pairs={{0,4},{4,12},{12,8},{8,0},{1,5},{5,13},{13,9},{9,1},{2,6},{6,14},{... | collective-permute-start | bytes 786440 | tf_op jit(solution)/shard_map/ppermute | solution.py:180
  2.1 1.6 %copy-start.2 = (f32[8,256,256]{2,1,0:T(8,128)S(1)}, f32[8,256,256]{2,1,0:T(8,128)}, u32[]{:S(2)}) copy-start(f32[8,256,256]{2,1,0:T(8,128)} %left_ref.1) | copy-start | bytes 6291460
  3.7 1.6 %copy-start.3 = (f32[8,256,256]{2,1,0:T(8,128)S(1)}, f32[8,256,256]{2,1,0:T(8,128)}, u32[]{:S(2)}) copy-start(f32[8,256,256]{2,1,0:T(8,128)} %right_ref.1) | copy-start | bytes 6291460
  5.3 1.1 %copy-start.4 = (f32[4,64,256]{2,1,0:T(8,128)S(1)}, f32[4,64,256]{2,1,0:T(8,128)}, u32[]{:S(2)}) copy-start(f32[4,64,256]{2,1,0:T(8,128)} %param.5) | copy-start | bytes 786436
  9.5 4.8 %collective-permute-start.3 = (f32[2,64,256]{2,1,0:T(8,128)S(1)}, f32[2,64,256]{2,1,0:T(8,128)S(1)}, u32[]{:S(2)}, u32[]{:S(2)}) collective-permute-start(f32[2,64,256]{2,1,0:T(8,128)S(1)} %get-tuple-element.37), channel_id=1, source_target_pairs={{0,4},{4,12},{12,8},{8,0},{1,5},{5,13},{13,9},{9,1},{2,6},{6,14},{... | collective-permute-start | bytes 393224 | tf_op jit(solution)/shard_map/ppermute | solution.py:183
  9.9 7.1 %collective-permute-start.1 = (f32[2,64,256]{2,1,0:T(8,128)S(1)}, f32[2,64,256]{2,1,0:T(8,128)S(1)}, u32[]{:S(2)}, u32[]{:S(2)}) collective-permute-start(f32[2,64,256]{2,1,0:T(8,128)S(1)} %get-tuple-element.40), channel_id=1, source_target_pairs={{0,4},{4,12},{12,8},{8,0},{1,5},{5,13},{13,9},{9,1},{2,6},{6,14},{... | collective-permute-start | bytes 393224 | tf_op jit(solution)/shard_map/ppermute | solution.py:184
  14.2 5.6 %collective-permute-start.4 = (f32[2,64,256]{2,1,0:T(8,128)S(1)}, f32[2,64,256]{2,1,0:T(8,128)S(1)}, u32[]{:S(2)}, u32[]{:S(2)}) collective-permute-start(f32[2,64,256]{2,1,0:T(8,128)S(1)} %collective-permute-done.3.refs_2_), channel_id=1, source_target_pairs={{0,4},{4,12},{12,8},{8,0},{1,5},{5,13},{13,9},{9,1},{2,6},{6,14},{... | collective-permute-start | bytes 393224 | tf_op jit(solution)/shard_map/ppermute | solution.py:183
  17.0 11.6 %collective-permute-start.2 = (f32[2,64,256]{2,1,0:T(8,128)S(1)}, f32[2,64,256]{2,1,0:T(8,128)S(1)}, u32[]{:S(2)}, u32[]{:S(2)}) collective-permute-start(f32[2,64,256]{2,1,0:T(8,128)S(1)} %collective-permute-done.1.refs_2_), channel_id=1, source_target_pairs={{0,4},{4,12},{12,8},{8,0},{1,5},{5,13},{13,9},{9,1},{2,6},{6,14},{... | collective-permute-start | bytes 393224 | tf_op jit(solution)/shard_map/ppermute | solution.py:184
  19.9 10.4 %collective-permute-start.5 = (f32[4,64,256]{2,1,0:T(8,128)S(1)}, f32[4,64,256]{2,1,0:T(8,128)S(1)}, u32[]{:S(2)}, u32[]{:S(2)}) collective-permute-start(f32[4,64,256]{2,1,0:T(8,128)S(1)} %pad_maximum_fusion), channel_id=1, source_target_pairs={{0,1},{1,2},{2,3},{4,5},{5,6},{6,7},{8,9},{9,10},{10,11},{12,13},{... | collective-permute-start | bytes 786440 | tf_op jit(solution)/shard_map/ppermute | solution.py:18
  26.4 2.1 %copy-start = (s32[8,16]{1,0:T(8,128)S(1)}, s32[8,16]{1,0:T(8,128)}, u32[]{:S(2)}) copy-start(s32[8,16]{1,0:T(8,128)} %allowed_ref.9) | copy-start | bytes 1540
  26.4 7.7 %collective-permute-start.6 = (f32[4,64,256]{2,1,0:T(8,128)S(1)}, f32[4,64,256]{2,1,0:T(8,128)S(1)}, u32[]{:S(2)}, u32[]{:S(2)}) collective-permute-start(f32[4,64,256]{2,1,0:T(8,128)S(1)} %pad_maximum_fusion.1), channel_id=1, source_target_pairs={{1,0},{2,1},{3,2},{5,4},{6,5},{7,6},{9,8},{10,9},{11,10},{13,12},{... | collective-permute-start | bytes 786440 | tf_op jit(solution)/shard_map/ppermute | solution.py:18
  28.6 5.5 %copy-start.1 = (s32[8]{0:T(128)S(1)}, s32[8]{0:T(128)}, u32[]{:S(2)}) copy-start(s32[8]{0:T(128)} %shifts_ref.7) | copy-start | bytes 100
  36.4 7.6 %collective-permute-start.7 = (f32[2,64,256]{2,1,0:T(8,128)S(1)}, f32[2,64,256]{2,1,0:T(8,128)S(1)}, u32[]{:S(2)}, u32[]{:S(2)}) collective-permute-start(f32[2,64,256]{2,1,0:T(8,128)S(1)} %get-tuple-element.27.refs_0_), channel_id=1, source_target_pairs={{0,4},{4,12},{12,8},{8,0},{1,5},{5,13},{13,9},{9,1},{2,6},{6,14},{... | collective-permute-start | bytes 393224 | tf_op jit(solution)/shard_map/ppermute | solution.py:220
  37.0 6.1 %collective-permute-start.9 = (f32[2,64,256]{2,1,0:T(8,128)S(1)}, f32[2,64,256]{2,1,0:T(8,128)S(1)}, u32[]{:S(2)}, u32[]{:S(2)}) collective-permute-start(f32[2,64,256]{2,1,0:T(8,128)S(1)} %get-tuple-element.30.refs_1_), channel_id=1, source_target_pairs={{0,4},{4,12},{12,8},{8,0},{1,5},{5,13},{13,9},{9,1},{2,6},{6,14},{... | collective-permute-start | bytes 393224 | tf_op jit(solution)/shard_map/ppermute | solution.py:220
  43.1 6.2 %collective-permute-start.11 = (f32[2,64,256]{2,1,0:T(8,128)S(1)}, f32[2,64,256]{2,1,0:T(8,128)S(1)}, u32[]{:S(2)}, u32[]{:S(2)}) collective-permute-start(f32[2,64,256]{2,1,0:T(8,128)S(1)} %add.32.refs_1_), channel_id=1, source_target_pairs={{0,4},{4,12},{12,8},{8,0},{1,5},{5,13},{13,9},{9,1},{2,6},{6,14},{... | collective-permute-start | bytes 393224 | tf_op jit(solution)/shard_map/ppermute | solution.py:220
  44.0 6.5 %collective-permute-start.8 = (f32[2,64,256]{2,1,0:T(8,128)S(1)}, f32[2,64,256]{2,1,0:T(8,128)S(1)}, u32[]{:S(2)}, u32[]{:S(2)}) collective-permute-start(f32[2,64,256]{2,1,0:T(8,128)S(1)} %add.31.refs_0_), channel_id=1, source_target_pairs={{0,4},{4,12},{12,8},{8,0},{1,5},{5,13},{13,9},{9,1},{2,6},{6,14},{... | collective-permute-start | bytes 393224 | tf_op jit(solution)/shard_map/ppermute | solution.py:220
  49.4 5.8 %collective-permute-start.12 = (f32[2,64,256]{2,1,0:T(8,128)S(1)}, f32[2,64,256]{2,1,0:T(8,128)S(1)}, u32[]{:S(2)}, u32[]{:S(2)}) collective-permute-start(f32[2,64,256]{2,1,0:T(8,128)S(1)} %add.34), channel_id=1, source_target_pairs={{0,4},{4,12},{12,8},{8,0},{1,5},{5,13},{13,9},{9,1},{2,6},{6,14},{... | collective-permute-start | bytes 393224 | tf_op jit(solution)/shard_map/ppermute | solution.py:220
  50.5 7.7 %collective-permute-start.10 = (f32[2,64,256]{2,1,0:T(8,128)S(1)}, f32[2,64,256]{2,1,0:T(8,128)S(1)}, u32[]{:S(2)}, u32[]{:S(2)}) collective-permute-start(f32[2,64,256]{2,1,0:T(8,128)S(1)} %add.33), channel_id=1, source_target_pairs={{0,4},{4,12},{12,8},{8,0},{1,5},{5,13},{13,9},{9,1},{2,6},{6,14},{... | collective-permute-start | bytes 393224 | tf_op jit(solution)/shard_map/ppermute | solution.py:220

commit v14 on v13

--- a/solution.py
+++ b/solution.py
@@ -216,6 +216,7 @@
             [pltpu.VMEM((nloc + 2, kops * rows, width), BF16)] * 2,
         )
 
+    result_outer = result_outer + 0 * result_inner[:1]
     for step in range(1, n):
         moved_outer, moved_inner = lax.ppermute(result_outer, "op", route), lax.ppermute(result_inner, "op", route)
         before = [result_outer, result_inner] if step < n - 1 else [moved_inner]

time: 59.3 us -> 58.1 us (0.980)
  waiting for transfers between devices: 17.2 us -> 15.7 us
    ppermute x3, starting transfers between devices: 4.09 us -> 2.82 us  [shards(): lax.ppermute(result_inner, 'op', route)]
    ppermute x3, starting transfers between devices: 3.92 us -> 5.14 us  [shards(): lax.ppermute(result_outer, 'op', route)]
    ppermute x3, waiting for transfers between devices: 0.93 us -> 0.01 us  [shards(): lax.ppermute(result_outer, 'op', route)]
  transfers between devices with their start and end apart: 13 -> 13, of which waited for: 7 -> 6; matrix products, arithmetic and copies ran while one was open for 0% -> 0% of each run, Pallas kernels for 20% -> 21%
where the time goes in v14:
time: 58.1 us; the launch traced here: 57.5 us
  starting transfers between devices  23 us (40%)
  waiting for transfers between devices  15.7 us (27%)
  Pallas kernels  14.3 us (25%)
  local copies, waits for them, and re-layouts  3.27 us (6%)
  other arithmetic  0.96 us (2%)
    pallas_call x7, Pallas kernels, call(): pl.pallas_call(body, name=name, out_shape=out_shape, in_specs=in_specs, o...  14.3 us
    ppermute x2, starting transfers between devices, shifted(): return lax.ppermute(block, axis, route)  8.41 us
    ppermute x3, starting transfers between devices, shards(): lax.ppermute(result_outer, 'op', route)  5.14 us
    ppermute x2, waiting for transfers between devices, shifted(): return lax.ppermute(block, axis, route)  3.84 us
    ppermute x2, waiting for transfers between devices, shards(): lax.ppermute(outer[-1] + zero[0, 0] if step == 1 else outer[-1], 'op', ro...  3.62 us
    ppermute x2, starting transfers between devices, shards(): lax.ppermute(inner[-1] + zero[0, 0] if step == 1 else inner[-1], 'op', ro...  3.59 us
    unnamed x10, local copies, waits for them, and re-layouts  3.2 us
    ppermute x3, waiting for transfers between devices, shards(): lax.ppermute(result_inner, 'op', route)  3.15 us
  transfers between devices with their start and end apart: 13, of which 6 were waited for; matrix products, arithmetic and copies ran while one was open for 0% of the time, Pallas kernels for 21%

profile of v14, /device:TPU:1, one launch (start us, length us, event | category | flops | bytes accessed | tf_op | source)
XLA Modules:
  0.0 57.5 jit_solution(16360313093534550521)
XLA Ops:
  0.0 2.1 %collective-permute-start = (f32[4,64,256]{2,1,0:T(8,128)}, f32[4,64,256]{2,1,0:T(8,128)S(1)}, u32[]{:S(2)}, u32[]{:S(2)}) collective-permute-start(f32[4,64,256]{2,1,0:T(8,128)} %param.5), channel_id=1, source_target_pairs={{0,4},{4,12},{12,8},{8,0},{1,5},{5,13},{13,9},{9,1},{2,6},{6,14},{... | collective-permute-start | bytes 786440 | tf_op jit(solution)/shard_map/ppermute | solution.py:180
  2.1 0.0 copy-start.2
  2.1 1.6 %copy-done.2 = f32[8,256,256]{2,1,0:T(8,128)S(1)} copy-done((f32[8,256,256]{2,1,0:T(8,128)S(1)}, f32[8,256,256]{2,1,0:T(8,128)}, u32[]{:S(2)}) %copy-start.2) | copy-done | bytes 2097176
  3.7 0.0 copy-start.3
  3.7 1.6 %copy-done.3 = f32[8,256,256]{2,1,0:T(8,128)S(1)} copy-done((f32[8,256,256]{2,1,0:T(8,128)S(1)}, f32[8,256,256]{2,1,0:T(8,128)}, u32[]{:S(2)}) %copy-start.3) | copy-done | bytes 2097176
  5.3 0.0 copy-start.4
  5.3 1.1 %prepare.1 = (bf16[4,8,64,768]{3,2,1,0:T(8,128)(2,1)S(1)}, bf16[2048,256]{1,0:T(8,128)(2,1)S(1)}, bf16[2048,256]{1,0:T(8,128)(2,1)S(1)}, f32[1,128]{1,0:T(1,128)S(1)}) custom-call(f32[8,256,256]{2,1,0:T(8,128)S(1)} %copy-done.2, f32[8,256,256]{2,1,0:T(8,128)S(1)} %copy-done.3), custom_call_target="tpu_custom_call" | custom-call | flops 3221225472 | bytes 1048576 | tf_op jit(solution)/shard_map/prepare/pallas_call | solution.py:154
  6.4 0.0 copy-done.4
  6.4 2.9 %collective-permute-done = f32[4,64,256]{2,1,0:T(8,128)S(1)} collective-permute-done((f32[4,64,256]{2,1,0:T(8,128)}, f32[4,64,256]{2,1,0:T(8,128)S(1)}, u32[]{:S(2)}, u32[]{:S(2)}) %collective-permute-start) | collective-permute-done | bytes 262176 | tf_op jit(solution)/shard_map/ppermute | solution.py:180
  9.4 0.1 broadcast_add_fusion.1
  9.5 0.4 collective-permute-start.3
  9.9 3.0 %collective-permute-start.1 = (f32[2,64,256]{2,1,0:T(8,128)S(1)}, f32[2,64,256]{2,1,0:T(8,128)S(1)}, u32[]{:S(2)}, u32[]{:S(2)}) collective-permute-start(f32[2,64,256]{2,1,0:T(8,128)S(1)} %get-tuple-element.40), channel_id=1, source_target_pairs={{0,4},{4,12},{12,8},{8,0},{1,5},{5,13},{13,9},{9,1},{2,6},{6,14},{... | collective-permute-start | bytes 393224 | tf_op jit(solution)/shard_map/ppermute | solution.py:184
  12.9 1.4 %collective-permute-done.3.refs_2_ = f32[2,64,256]{2,1,0:T(8,128)S(1)} collective-permute-done((f32[2,64,256]{2,1,0:T(8,128)S(1)}, f32[2,64,256]{2,1,0:T(8,128)S(1)}, u32[]{:S(2)}, u32[]{:S(2)}) %collective-permute-start.3) | collective-permute-done | bytes 131104 | tf_op jit(solution)/shard_map/ppermute | solution.py:183
  14.2 0.6 collective-permute-start.4
  14.8 2.2 %collective-permute-done.1.refs_2_ = f32[2,64,256]{2,1,0:T(8,128)S(1)} collective-permute-done((f32[2,64,256]{2,1,0:T(8,128)S(1)}, f32[2,64,256]{2,1,0:T(8,128)S(1)}, u32[]{:S(2)}, u32[]{:S(2)}) %collective-permute-start.1) | collective-permute-done | bytes 131104 | tf_op jit(solution)/shard_map/ppermute | solution.py:184
  17.0 0.6 %collective-permute-start.2 = (f32[2,64,256]{2,1,0:T(8,128)S(1)}, f32[2,64,256]{2,1,0:T(8,128)S(1)}, u32[]{:S(2)}, u32[]{:S(2)}) collective-permute-start(f32[2,64,256]{2,1,0:T(8,128)S(1)} %collective-permute-done.1.refs_2_), channel_id=1, source_target_pairs={{0,4},{4,12},{12,8},{8,0},{1,5},{5,13},{13,9},{9,1},{2,6},{6,14},{... | collective-permute-start | bytes 393224 | tf_op jit(solution)/shard_map/ppermute | solution.py:184
  17.6 2.3 %collective-permute-done.4.refs_3_ = f32[2,64,256]{2,1,0:T(8,128)S(1)} collective-permute-done((f32[2,64,256]{2,1,0:T(8,128)S(1)}, f32[2,64,256]{2,1,0:T(8,128)S(1)}, u32[]{:S(2)}, u32[]{:S(2)}) %collective-permute-start.4) | collective-permute-done | bytes 131104 | tf_op jit(solution)/shard_map/ppermute | solution.py:183
  19.9 6.5 %collective-permute-start.5 = (f32[4,64,256]{2,1,0:T(8,128)S(1)}, f32[4,64,256]{2,1,0:T(8,128)S(1)}, u32[]{:S(2)}, u32[]{:S(2)}) collective-permute-start(f32[4,64,256]{2,1,0:T(8,128)S(1)} %pad_maximum_fusion), channel_id=1, source_target_pairs={{0,1},{1,2},{2,3},{4,5},{5,6},{6,7},{8,9},{9,10},{10,11},{12,13},{... | collective-permute-start | bytes 786440 | tf_op jit(solution)/shard_map/ppermute | solution.py:18
  26.4 0.0 copy-start
  26.4 1.9 %collective-permute-start.6 = (f32[4,64,256]{2,1,0:T(8,128)S(1)}, f32[4,64,256]{2,1,0:T(8,128)S(1)}, u32[]{:S(2)}, u32[]{:S(2)}) collective-permute-start(f32[4,64,256]{2,1,0:T(8,128)S(1)} %pad_maximum_fusion.1), channel_id=1, source_target_pairs={{1,0},{2,1},{3,2},{5,4},{6,5},{7,6},{9,8},{10,9},{11,10},{13,12},{... | collective-permute-start | bytes 786440 | tf_op jit(solution)/shard_map/ppermute | solution.py:18
  28.4 0.2 assemble.1.refs_4_.outer
  28.5 0.0 collective-permute-done.2.refs_3_
  28.6 0.0 copy-done
  28.6 0.0 copy-start.1
  28.6 1.7 %own.1 = (bf16[2,768,256]{2,1,0:T(8,128)(2,1)S(1)}, bf16[4,512,256]{2,1,0:T(8,128)(2,1)S(1)}, bf16[4,512,256]{2,1,0:T(8,128)(2,1)S(1)}) custom-call(s32[8,16]{1,0:T(8,128)S(1)} %copy-done, f32[2,64,256]{2,1,0:T(8,128)S(1)} %get-tuple-element.42.refs_0_, f32[2,64,256]{2,1,0:T(8,128)S(1)} %get-tuple-element.39.refs_1_, ...), custom_call_target="tpu_custom_call" | custom-call | flops 3221225472 | bytes 1048576 | tf_op jit(solution)/shard_map/own/pallas_call | solution.py:154
  30.3 0.0 collective-permute-done.5.above
  30.3 3.8 %collective-permute-done.6.below = f32[4,64,256]{2,1,0:T(8,128)S(1)} collective-permute-done((f32[4,64,256]{2,1,0:T(8,128)S(1)}, f32[4,64,256]{2,1,0:T(8,128)S(1)}, u32[]{:S(2)}, u32[]{:S(2)}) %collective-permute-start.6) | collective-permute-done | bytes 262176 | tf_op jit(solution)/shard_map/ppermute | solution.py:18
  34.1 0.0 copy-done.1
  34.1 2.3 %first_chunk.1 = (f32[2,64,256]{2,1,0:T(8,128)S(1)}, f32[2,64,256]{2,1,0:T(8,128)S(1)}, bf16[2,768,256]{2,1,0:T(8,128)(2,1)S(1)}) custom-call(s32[8]{0:T(128)S(1)} %copy-done.1, s32[8,16]{1,0:T(8,128)S(1)} %copy-done, bf16[4,512,256]{2,1,0:T(8,128)(2,1)S(1)} %get-tuple-element.23.own_high, bf16[4,512,256]{2,1,0:T(8,128)(2,1)S(1)} %get-tuple-element.24.own_low, ...), custom_call_target="tpu_custom_call" | custom-call | flops 1610612736 | bytes 1048576 | tf_op jit(solution)/shard_map/first_chunk/pallas_call | solution.py:154
  36.4 0.6 %collective-permute-start.9 = (f32[2,64,256]{2,1,0:T(8,128)S(1)}, f32[2,64,256]{2,1,0:T(8,128)S(1)}, u32[]{:S(2)}, u32[]{:S(2)}) collective-permute-start(f32[2,64,256]{2,1,0:T(8,128)S(1)} %get-tuple-element.28.refs_1_), channel_id=1, source_target_pairs={{0,4},{4,12},{12,8},{8,0},{1,5},{5,13},{13,9},{9,1},{2,6},{6,14},{... | collective-permute-start | bytes 393224 | tf_op jit(solution)/shard_map/ppermute | solution.py:221
  37.0 3.1 %collective-permute-start.7 = (f32[2,64,256]{2,1,0:T(8,128)S(1)}, f32[2,64,256]{2,1,0:T(8,128)S(1)}, u32[]{:S(2)}, u32[]{:S(2)}) collective-permute-start(f32[2,64,256]{2,1,0:T(8,128)S(1)} %broadcast_add_fusion.refs_0_), channel_id=1, source_target_pairs={{0,4},{4,12},{12,8},{8,0},{1,5},{5,13},{13,9},{9,1},{2,6},{6,14},{... | collective-permute-start | bytes 393224 | tf_op jit(solution)/shard_map/ppermute | solution.py:221
  40.1 3.0 %chunk.3 = (f32[2,64,256]{2,1,0:T(8,128)S(1)}, f32[2,64,256]{2,1,0:T(8,128)S(1)}) custom-call(s32[8]{0:T(128)S(1)} %copy-done.1, s32[8,16]{1,0:T(8,128)S(1)} %copy-done, bf16[2,768,256]{2,1,0:T(8,128)(2,1)S(1)} %assemble.1.refs_4_.outer, bf16[2,768,256]{2,1,0:T(8,128)(2,1)S(1)} %get-tuple-element.29.inner, ...), custom_call_target="tpu_custom_call" | custom-call | flops 3221225472 | bytes 1048576 | tf_op jit(solution)/shard_map/chunk/pallas_call | solution.py:154
  43.2 0.0 collective-permute-done.9
  43.2 0.1 collective-permute-start.11
  43.3 0.0 collective-permute-done.7
  43.3 1.8 %collective-permute-start.8 = (f32[2,64,256]{2,1,0:T(8,128)S(1)}, f32[2,64,256]{2,1,0:T(8,128)S(1)}, u32[]{:S(2)}, u32[]{:S(2)}) collective-permute-start(f32[2,64,256]{2,1,0:T(8,128)S(1)} %add.44.refs_0_), channel_id=1, source_target_pairs={{0,4},{4,12},{12,8},{8,0},{1,5},{5,13},{13,9},{9,1},{2,6},{6,14},{... | collective-permute-start | bytes 393224 | tf_op jit(solution)/shard_map/ppermute | solution.py:221
  45.1 3.0 %chunk.4 = (f32[2,64,256]{2,1,0:T(8,128)S(1)}, f32[2,64,256]{2,1,0:T(8,128)S(1)}) custom-call(s32[8]{0:T(128)S(1)} %copy-done.1, s32[8,16]{1,0:T(8,128)S(1)} %copy-done, bf16[2,768,256]{2,1,0:T(8,128)(2,1)S(1)} %assemble.1.refs_4_.outer, bf16[2,768,256]{2,1,0:T(8,128)(2,1)S(1)} %get-tuple-element.29.inner, ...), custom_call_target="tpu_custom_call" | custom-call | flops 3221225472 | bytes 1048576 | tf_op jit(solution)/shard_map/chunk/pallas_call | solution.py:154
  48.1 0.0 collective-permute-done.11
  48.1 2.2 %collective-permute-start.12 = (f32[2,64,256]{2,1,0:T(8,128)S(1)}, f32[2,64,256]{2,1,0:T(8,128)S(1)}, u32[]{:S(2)}, u32[]{:S(2)}) collective-permute-start(f32[2,64,256]{2,1,0:T(8,128)S(1)} %add.47), channel_id=1, source_target_pairs={{0,4},{4,12},{12,8},{8,0},{1,5},{5,13},{13,9},{9,1},{2,6},{6,14},{... | collective-permute-start | bytes 393224 | tf_op jit(solution)/shard_map/ppermute | solution.py:221
  50.3 0.0 collective-permute-done.8
  50.3 0.3 collective-permute-start.10
  50.5 3.1 %collective-permute-done.12.refs_0_ = f32[2,64,256]{2,1,0:T(8,128)S(1)} collective-permute-done((f32[2,64,256]{2,1,0:T(8,128)S(1)}, f32[2,64,256]{2,1,0:T(8,128)S(1)}, u32[]{:S(2)}, u32[]{:S(2)}) %collective-permute-start.12) | collective-permute-done | bytes 131104 | tf_op jit(solution)/shard_map/ppermute | solution.py:221
  53.7 3.0 %chunk.5 = (f32[2,64,256]{2,1,0:T(8,128)S(1)}, f32[2,64,256]{2,1,0:T(8,128)S(1)}) custom-call(s32[8]{0:T(128)S(1)} %copy-done.1, s32[8,16]{1,0:T(8,128)S(1)} %copy-done, bf16[2,768,256]{2,1,0:T(8,128)(2,1)S(1)} %assemble.1.refs_4_.outer, bf16[2,768,256]{2,1,0:T(8,128)(2,1)S(1)} %get-tuple-element.29.inner, ...), custom_call_target="tpu_custom_call" | custom-call | flops 3221225472 | bytes 1048576 | tf_op jit(solution)/shard_map/chunk/pallas_call | solution.py:154
  56.7 0.0 collective-permute-done.10
  56.8 0.7 %pad_maximum_fusion.2 = f32[4,64,256]{2,1,0:T(8,128)} fusion(f32[1,64,256]{2,1,0:T(8,128)S(1)} %get-tuple-element.44, f32[2,64,256]{2,1,0:T(8,128)S(1)} %add.49, f32[1,64,256]{2,1,0:T(8,128)S(1)} %get-tuple-element.43), kind=kLoop, calls=%fused_computation.2 | loop fusion | flops 131072 | bytes 524288 | tf_op jit(solution)/shard_map/concatenate | solution.py:225
  (16 shorter events, 0.2 us)
Async XLA Ops:
  0.0 9.4 %collective-permute-start = (f32[4,64,256]{2,1,0:T(8,128)}, f32[4,64,256]{2,1,0:T(8,128)S(1)}, u32[]{:S(2)}, u32[]{:S(2)}) collective-permute-start(f32[4,64,256]{2,1,0:T(8,128)} %param.5), channel_id=1, source_target_pairs={{0,4},{4,12},{12,8},{8,0},{1,5},{5,13},{13,9},{9,1},{2,6},{6,14},{... | collective-permute-start | bytes 786440 | tf_op jit(solution)/shard_map/ppermute | solution.py:180
  2.1 1.6 %copy-start.2 = (f32[8,256,256]{2,1,0:T(8,128)S(1)}, f32[8,256,256]{2,1,0:T(8,128)}, u32[]{:S(2)}) copy-start(f32[8,256,256]{2,1,0:T(8,128)} %left_ref.1) | copy-start | bytes 6291460
  3.7 1.6 %copy-start.3 = (f32[8,256,256]{2,1,0:T(8,128)S(1)}, f32[8,256,256]{2,1,0:T(8,128)}, u32[]{:S(2)}) copy-start(f32[8,256,256]{2,1,0:T(8,128)} %right_ref.1) | copy-start | bytes 6291460
  5.3 1.1 %copy-start.4 = (f32[4,64,256]{2,1,0:T(8,128)S(1)}, f32[4,64,256]{2,1,0:T(8,128)}, u32[]{:S(2)}) copy-start(f32[4,64,256]{2,1,0:T(8,128)} %param.5) | copy-start | bytes 786436
  9.5 4.8 %collective-permute-start.3 = (f32[2,64,256]{2,1,0:T(8,128)S(1)}, f32[2,64,256]{2,1,0:T(8,128)S(1)}, u32[]{:S(2)}, u32[]{:S(2)}) collective-permute-start(f32[2,64,256]{2,1,0:T(8,128)S(1)} %get-tuple-element.37), channel_id=1, source_target_pairs={{0,4},{4,12},{12,8},{8,0},{1,5},{5,13},{13,9},{9,1},{2,6},{6,14},{... | collective-permute-start | bytes 393224 | tf_op jit(solution)/shard_map/ppermute | solution.py:183
  9.9 7.1 %collective-permute-start.1 = (f32[2,64,256]{2,1,0:T(8,128)S(1)}, f32[2,64,256]{2,1,0:T(8,128)S(1)}, u32[]{:S(2)}, u32[]{:S(2)}) collective-permute-start(f32[2,64,256]{2,1,0:T(8,128)S(1)} %get-tuple-element.40), channel_id=1, source_target_pairs={{0,4},{4,12},{12,8},{8,0},{1,5},{5,13},{13,9},{9,1},{2,6},{6,14},{... | collective-permute-start | bytes 393224 | tf_op jit(solution)/shard_map/ppermute | solution.py:184
  14.2 5.6 %collective-permute-start.4 = (f32[2,64,256]{2,1,0:T(8,128)S(1)}, f32[2,64,256]{2,1,0:T(8,128)S(1)}, u32[]{:S(2)}, u32[]{:S(2)}) collective-permute-start(f32[2,64,256]{2,1,0:T(8,128)S(1)} %collective-permute-done.3.refs_2_), channel_id=1, source_target_pairs={{0,4},{4,12},{12,8},{8,0},{1,5},{5,13},{13,9},{9,1},{2,6},{6,14},{... | collective-permute-start | bytes 393224 | tf_op jit(solution)/shard_map/ppermute | solution.py:183
  17.0 11.6 %collective-permute-start.2 = (f32[2,64,256]{2,1,0:T(8,128)S(1)}, f32[2,64,256]{2,1,0:T(8,128)S(1)}, u32[]{:S(2)}, u32[]{:S(2)}) collective-permute-start(f32[2,64,256]{2,1,0:T(8,128)S(1)} %collective-permute-done.1.refs_2_), channel_id=1, source_target_pairs={{0,4},{4,12},{12,8},{8,0},{1,5},{5,13},{13,9},{9,1},{2,6},{6,14},{... | collective-permute-start | bytes 393224 | tf_op jit(solution)/shard_map/ppermute | solution.py:184
  19.9 10.4 %collective-permute-start.5 = (f32[4,64,256]{2,1,0:T(8,128)S(1)}, f32[4,64,256]{2,1,0:T(8,128)S(1)}, u32[]{:S(2)}, u32[]{:S(2)}) collective-permute-start(f32[4,64,256]{2,1,0:T(8,128)S(1)} %pad_maximum_fusion), channel_id=1, source_target_pairs={{0,1},{1,2},{2,3},{4,5},{5,6},{6,7},{8,9},{9,10},{10,11},{12,13},{... | collective-permute-start | bytes 786440 | tf_op jit(solution)/shard_map/ppermute | solution.py:18
  26.4 2.1 %copy-start = (s32[8,16]{1,0:T(8,128)S(1)}, s32[8,16]{1,0:T(8,128)}, u32[]{:S(2)}) copy-start(s32[8,16]{1,0:T(8,128)} %allowed_ref.9) | copy-start | bytes 1540
  26.4 7.7 %collective-permute-start.6 = (f32[4,64,256]{2,1,0:T(8,128)S(1)}, f32[4,64,256]{2,1,0:T(8,128)S(1)}, u32[]{:S(2)}, u32[]{:S(2)}) collective-permute-start(f32[4,64,256]{2,1,0:T(8,128)S(1)} %pad_maximum_fusion.1), channel_id=1, source_target_pairs={{1,0},{2,1},{3,2},{5,4},{6,5},{7,6},{9,8},{10,9},{11,10},{13,12},{... | collective-permute-start | bytes 786440 | tf_op jit(solution)/shard_map/ppermute | solution.py:18
  28.6 5.5 %copy-start.1 = (s32[8]{0:T(128)S(1)}, s32[8]{0:T(128)}, u32[]{:S(2)}) copy-start(s32[8]{0:T(128)} %shifts_ref.7) | copy-start | bytes 100
  36.4 6.8 %collective-permute-start.9 = (f32[2,64,256]{2,1,0:T(8,128)S(1)}, f32[2,64,256]{2,1,0:T(8,128)S(1)}, u32[]{:S(2)}, u32[]{:S(2)}) collective-permute-start(f32[2,64,256]{2,1,0:T(8,128)S(1)} %get-tuple-element.28.refs_1_), channel_id=1, source_target_pairs={{0,4},{4,12},{12,8},{8,0},{1,5},{5,13},{13,9},{9,1},{2,6},{6,14},{... | collective-permute-start | bytes 393224 | tf_op jit(solution)/shard_map/ppermute | solution.py:221
  37.0 6.3 %collective-permute-start.7 = (f32[2,64,256]{2,1,0:T(8,128)S(1)}, f32[2,64,256]{2,1,0:T(8,128)S(1)}, u32[]{:S(2)}, u32[]{:S(2)}) collective-permute-start(f32[2,64,256]{2,1,0:T(8,128)S(1)} %broadcast_add_fusion.refs_0_), channel_id=1, source_target_pairs={{0,4},{4,12},{12,8},{8,0},{1,5},{5,13},{13,9},{9,1},{2,6},{6,14},{... | collective-permute-start | bytes 393224 | tf_op jit(solution)/shard_map/ppermute | solution.py:221
  43.2 4.9 %collective-permute-start.11 = (f32[2,64,256]{2,1,0:T(8,128)S(1)}, f32[2,64,256]{2,1,0:T(8,128)S(1)}, u32[]{:S(2)}, u32[]{:S(2)}) collective-permute-start(f32[2,64,256]{2,1,0:T(8,128)S(1)} %add.45.refs_1_), channel_id=1, source_target_pairs={{0,4},{4,12},{12,8},{8,0},{1,5},{5,13},{13,9},{9,1},{2,6},{6,14},{... | collective-permute-start | bytes 393224 | tf_op jit(solution)/shard_map/ppermute | solution.py:221
  43.3 7.0 %collective-permute-start.8 = (f32[2,64,256]{2,1,0:T(8,128)S(1)}, f32[2,64,256]{2,1,0:T(8,128)S(1)}, u32[]{:S(2)}, u32[]{:S(2)}) collective-permute-start(f32[2,64,256]{2,1,0:T(8,128)S(1)} %add.44.refs_0_), channel_id=1, source_target_pairs={{0,4},{4,12},{12,8},{8,0},{1,5},{5,13},{13,9},{9,1},{2,6},{6,14},{... | collective-permute-start | bytes 393224 | tf_op jit(solution)/shard_map/ppermute | solution.py:221
  48.1 5.6 %collective-permute-start.12 = (f32[2,64,256]{2,1,0:T(8,128)S(1)}, f32[2,64,256]{2,1,0:T(8,128)S(1)}, u32[]{:S(2)}, u32[]{:S(2)}) collective-permute-start(f32[2,64,256]{2,1,0:T(8,128)S(1)} %add.47), channel_id=1, source_target_pairs={{0,4},{4,12},{12,8},{8,0},{1,5},{5,13},{13,9},{9,1},{2,6},{6,14},{... | collective-permute-start | bytes 393224 | tf_op jit(solution)/shard_map/ppermute | solution.py:221
  50.3 6.4 %collective-permute-start.10 = (f32[2,64,256]{2,1,0:T(8,128)S(1)}, f32[2,64,256]{2,1,0:T(8,128)S(1)}, u32[]{:S(2)}, u32[]{:S(2)}) collective-permute-start(f32[2,64,256]{2,1,0:T(8,128)S(1)} %add.46), channel_id=1, source_target_pairs={{0,4},{4,12},{12,8},{8,0},{1,5},{5,13},{13,9},{9,1},{2,6},{6,14},{... | collective-permute-start | bytes 393224 | tf_op jit(solution)/shard_map/ppermute | solution.py:221

commit v15 on v14

--- a/solution.py
+++ b/solution.py
@@ -219,7 +219,7 @@
     result_outer = result_outer + 0 * result_inner[:1]
     for step in range(1, n):
         moved_outer, moved_inner = lax.ppermute(result_outer, "op", route), lax.ppermute(result_inner, "op", route)
-        before = [result_outer, result_inner] if step < n - 1 else [moved_inner]
+        before = [] if step < n - 1 else [result_outer, result_inner]
         next_outer, next_inner = mine(step, *before)
         result_outer, result_inner = moved_outer + next_outer, moved_inner + next_inner
     return jnp.concatenate([result_outer[:1], result_inner, result_outer[1:]])

time: 58.1 us -> 57.8 us (level)
  the two profiles are of different devices: /device:TPU:1 before, /device:TPU:2 now
where the time goes in v15:
time: 57.8 us; the launch traced here: 57.6 us
  starting transfers between devices  24.5 us (42%)
  waiting for transfers between devices  14.4 us (25%)
  Pallas kernels  14.2 us (25%)
  local copies, waits for them, and re-layouts  3.27 us (6%)
  other arithmetic  0.96 us (2%)
    pallas_call x7, Pallas kernels, call(): pl.pallas_call(body, name=name, out_shape=out_shape, in_specs=in_specs, o...  14.2 us
    ppermute x3, starting transfers between devices, shards(): lax.ppermute(result_outer, 'op', route)  7.01 us
    ppermute x2, starting transfers between devices, shifted(): return lax.ppermute(block, axis, route)  5.56 us
    ppermute x2, starting transfers between devices, shards(): lax.ppermute(inner[-1] + zero[0, 0] if step == 1 else inner[-1], 'op', ro...  5.21 us
    ppermute x2, waiting for transfers between devices, shards(): lax.ppermute(outer[-1] + zero[0, 0] if step == 1 else outer[-1], 'op', ro...  4.17 us
    ppermute x3, starting transfers between devices, shards(): lax.ppermute(result_inner, 'op', route)  3.45 us
    ppermute x1, waiting for transfers between devices, shards(): blocks = [psi, lax.ppermute(psi, 'op', route)]  3.27 us
    unnamed x10, local copies, waits for them, and re-layouts  3.2 us
  transfers between devices with their start and end apart: 13, of which 10 were waited for; matrix products, arithmetic and copies ran while one was open for 0% of the time, Pallas kernels for 21%

profile of v15, /device:TPU:2, one launch (start us, length us, event | category | flops | bytes accessed | tf_op | source)
XLA Modules:
  0.0 57.6 jit_solution(17796519880739153084)
XLA Ops:
  0.0 1.6 %collective-permute-start = (f32[4,64,256]{2,1,0:T(8,128)}, f32[4,64,256]{2,1,0:T(8,128)S(1)}, u32[]{:S(2)}, u32[]{:S(2)}) collective-permute-start(f32[4,64,256]{2,1,0:T(8,128)} %param.5), channel_id=1, source_target_pairs={{0,4},{4,12},{12,8},{8,0},{1,5},{5,13},{13,9},{9,1},{2,6},{6,14},{... | collective-permute-start | bytes 786440 | tf_op jit(solution)/shard_map/ppermute | solution.py:180
  1.6 0.0 copy-start.2
  1.6 1.6 %copy-done.2 = f32[8,256,256]{2,1,0:T(8,128)S(1)} copy-done((f32[8,256,256]{2,1,0:T(8,128)S(1)}, f32[8,256,256]{2,1,0:T(8,128)}, u32[]{:S(2)}) %copy-start.2) | copy-done | bytes 2097176
  3.2 0.0 copy-start.3
  3.2 1.6 %copy-done.3 = f32[8,256,256]{2,1,0:T(8,128)S(1)} copy-done((f32[8,256,256]{2,1,0:T(8,128)S(1)}, f32[8,256,256]{2,1,0:T(8,128)}, u32[]{:S(2)}) %copy-start.3) | copy-done | bytes 2097176
  4.8 0.0 copy-start.4
  4.8 1.1 %prepare.1 = (bf16[4,8,64,768]{3,2,1,0:T(8,128)(2,1)S(1)}, bf16[2048,256]{1,0:T(8,128)(2,1)S(1)}, bf16[2048,256]{1,0:T(8,128)(2,1)S(1)}, f32[1,128]{1,0:T(1,128)S(1)}) custom-call(f32[8,256,256]{2,1,0:T(8,128)S(1)} %copy-done.2, f32[8,256,256]{2,1,0:T(8,128)S(1)} %copy-done.3), custom_call_target="tpu_custom_call" | custom-call | flops 3221225472 | bytes 1048576 | tf_op jit(solution)/shard_map/prepare/pallas_call | solution.py:154
  5.8 0.0 copy-done.4
  5.9 3.3 %collective-permute-done = f32[4,64,256]{2,1,0:T(8,128)S(1)} collective-permute-done((f32[4,64,256]{2,1,0:T(8,128)}, f32[4,64,256]{2,1,0:T(8,128)S(1)}, u32[]{:S(2)}, u32[]{:S(2)}) %collective-permute-start) | collective-permute-done | bytes 262176 | tf_op jit(solution)/shard_map/ppermute | solution.py:180
  9.2 0.1 broadcast_add_fusion.1
  9.2 0.9 %collective-permute-start.3 = (f32[2,64,256]{2,1,0:T(8,128)S(1)}, f32[2,64,256]{2,1,0:T(8,128)S(1)}, u32[]{:S(2)}, u32[]{:S(2)}) collective-permute-start(f32[2,64,256]{2,1,0:T(8,128)S(1)} %get-tuple-element.37), channel_id=1, source_target_pairs={{0,4},{4,12},{12,8},{8,0},{1,5},{5,13},{13,9},{9,1},{2,6},{6,14},{... | collective-permute-start | bytes 393224 | tf_op jit(solution)/shard_map/ppermute | solution.py:183
  10.2 3.3 %collective-permute-start.1 = (f32[2,64,256]{2,1,0:T(8,128)S(1)}, f32[2,64,256]{2,1,0:T(8,128)S(1)}, u32[]{:S(2)}, u32[]{:S(2)}) collective-permute-start(f32[2,64,256]{2,1,0:T(8,128)S(1)} %get-tuple-element.40), channel_id=1, source_target_pairs={{0,4},{4,12},{12,8},{8,0},{1,5},{5,13},{13,9},{9,1},{2,6},{6,14},{... | collective-permute-start | bytes 393224 | tf_op jit(solution)/shard_map/ppermute | solution.py:184
  13.5 2.5 %collective-permute-done.3.refs_2_ = f32[2,64,256]{2,1,0:T(8,128)S(1)} collective-permute-done((f32[2,64,256]{2,1,0:T(8,128)S(1)}, f32[2,64,256]{2,1,0:T(8,128)S(1)}, u32[]{:S(2)}, u32[]{:S(2)}) %collective-permute-start.3) | collective-permute-done | bytes 131104 | tf_op jit(solution)/shard_map/ppermute | solution.py:183
  16.0 0.8 %collective-permute-start.4 = (f32[2,64,256]{2,1,0:T(8,128)S(1)}, f32[2,64,256]{2,1,0:T(8,128)S(1)}, u32[]{:S(2)}, u32[]{:S(2)}) collective-permute-start(f32[2,64,256]{2,1,0:T(8,128)S(1)} %collective-permute-done.3.refs_2_), channel_id=1, source_target_pairs={{0,4},{4,12},{12,8},{8,0},{1,5},{5,13},{13,9},{9,1},{2,6},{6,14},{... | collective-permute-start | bytes 393224 | tf_op jit(solution)/shard_map/ppermute | solution.py:183
  16.7 1.5 %collective-permute-done.1.refs_2_ = f32[2,64,256]{2,1,0:T(8,128)S(1)} collective-permute-done((f32[2,64,256]{2,1,0:T(8,128)S(1)}, f32[2,64,256]{2,1,0:T(8,128)S(1)}, u32[]{:S(2)}, u32[]{:S(2)}) %collective-permute-start.1) | collective-permute-done | bytes 131104 | tf_op jit(solution)/shard_map/ppermute | solution.py:184
  18.2 1.9 %collective-permute-start.2 = (f32[2,64,256]{2,1,0:T(8,128)S(1)}, f32[2,64,256]{2,1,0:T(8,128)S(1)}, u32[]{:S(2)}, u32[]{:S(2)}) collective-permute-start(f32[2,64,256]{2,1,0:T(8,128)S(1)} %collective-permute-done.1.refs_2_), channel_id=1, source_target_pairs={{0,4},{4,12},{12,8},{8,0},{1,5},{5,13},{13,9},{9,1},{2,6},{6,14},{... | collective-permute-start | bytes 393224 | tf_op jit(solution)/shard_map/ppermute | solution.py:184
  20.1 1.7 %collective-permute-done.4.refs_3_ = f32[2,64,256]{2,1,0:T(8,128)S(1)} collective-permute-done((f32[2,64,256]{2,1,0:T(8,128)S(1)}, f32[2,64,256]{2,1,0:T(8,128)S(1)}, u32[]{:S(2)}, u32[]{:S(2)}) %collective-permute-start.4) | collective-permute-done | bytes 131104 | tf_op jit(solution)/shard_map/ppermute | solution.py:183
  21.9 1.9 %collective-permute-start.5 = (f32[4,64,256]{2,1,0:T(8,128)S(1)}, f32[4,64,256]{2,1,0:T(8,128)S(1)}, u32[]{:S(2)}, u32[]{:S(2)}) collective-permute-start(f32[4,64,256]{2,1,0:T(8,128)S(1)} %pad_maximum_fusion), channel_id=1, source_target_pairs={{0,1},{1,2},{2,3},{4,5},{5,6},{6,7},{8,9},{9,10},{10,11},{12,13},{... | collective-permute-start | bytes 786440 | tf_op jit(solution)/shard_map/ppermute | solution.py:18
  23.8 0.0 copy-start
  23.8 3.6 %collective-permute-start.6 = (f32[4,64,256]{2,1,0:T(8,128)S(1)}, f32[4,64,256]{2,1,0:T(8,128)S(1)}, u32[]{:S(2)}, u32[]{:S(2)}) collective-permute-start(f32[4,64,256]{2,1,0:T(8,128)S(1)} %pad_maximum_fusion.1), channel_id=1, source_target_pairs={{1,0},{2,1},{3,2},{5,4},{6,5},{7,6},{9,8},{10,9},{11,10},{13,12},{... | collective-permute-start | bytes 786440 | tf_op jit(solution)/shard_map/ppermute | solution.py:18
  27.5 0.2 assemble.1.refs_4_.outer
  27.7 0.0 collective-permute-done.2.refs_3_
  27.7 0.0 copy-done
  27.7 0.0 copy-start.1
  27.7 1.7 %own.1 = (bf16[2,768,256]{2,1,0:T(8,128)(2,1)S(1)}, bf16[4,512,256]{2,1,0:T(8,128)(2,1)S(1)}, bf16[4,512,256]{2,1,0:T(8,128)(2,1)S(1)}) custom-call(s32[8,16]{1,0:T(8,128)S(1)} %copy-done, f32[2,64,256]{2,1,0:T(8,128)S(1)} %get-tuple-element.42.refs_0_, f32[2,64,256]{2,1,0:T(8,128)S(1)} %get-tuple-element.39.refs_1_, ...), custom_call_target="tpu_custom_call" | custom-call | flops 3221225472 | bytes 1048576 | tf_op jit(solution)/shard_map/own/pallas_call | solution.py:154
  29.4 0.2 collective-permute-done.5.above
  29.6 1.8 %collective-permute-done.6.below = f32[4,64,256]{2,1,0:T(8,128)S(1)} collective-permute-done((f32[4,64,256]{2,1,0:T(8,128)S(1)}, f32[4,64,256]{2,1,0:T(8,128)S(1)}, u32[]{:S(2)}, u32[]{:S(2)}) %collective-permute-start.6) | collective-permute-done | bytes 262176 | tf_op jit(solution)/shard_map/ppermute | solution.py:18
  31.4 0.0 copy-done.1
  31.4 2.3 %first_chunk.1 = (f32[2,64,256]{2,1,0:T(8,128)S(1)}, f32[2,64,256]{2,1,0:T(8,128)S(1)}, bf16[2,768,256]{2,1,0:T(8,128)(2,1)S(1)}) custom-call(s32[8]{0:T(128)S(1)} %copy-done.1, s32[8,16]{1,0:T(8,128)S(1)} %copy-done, bf16[4,512,256]{2,1,0:T(8,128)(2,1)S(1)} %get-tuple-element.23.own_high, bf16[4,512,256]{2,1,0:T(8,128)(2,1)S(1)} %get-tuple-element.24.own_low, ...), custom_call_target="tpu_custom_call" | custom-call | flops 1610612736 | bytes 1048576 | tf_op jit(solution)/shard_map/first_chunk/pallas_call | solution.py:154
  33.6 0.9 %collective-permute-start.10 = (f32[2,64,256]{2,1,0:T(8,128)S(1)}, f32[2,64,256]{2,1,0:T(8,128)S(1)}, u32[]{:S(2)}, u32[]{:S(2)}) collective-permute-start(f32[2,64,256]{2,1,0:T(8,128)S(1)} %get-tuple-element.28), channel_id=1, source_target_pairs={{0,4},{4,12},{12,8},{8,0},{1,5},{5,13},{13,9},{9,1},{2,6},{6,14},{... | collective-permute-start | bytes 393224 | tf_op jit(solution)/shard_map/ppermute | solution.py:221
  34.5 3.4 %collective-permute-start.7 = (f32[2,64,256]{2,1,0:T(8,128)S(1)}, f32[2,64,256]{2,1,0:T(8,128)S(1)}, u32[]{:S(2)}, u32[]{:S(2)}) collective-permute-start(f32[2,64,256]{2,1,0:T(8,128)S(1)} %broadcast_add_fusion), channel_id=1, source_target_pairs={{0,4},{4,12},{12,8},{8,0},{1,5},{5,13},{13,9},{9,1},{2,6},{6,14},{... | collective-permute-start | bytes 393224 | tf_op jit(solution)/shard_map/ppermute | solution.py:221
  37.9 3.0 %chunk.3 = (f32[2,64,256]{2,1,0:T(8,128)S(1)}, f32[2,64,256]{2,1,0:T(8,128)S(1)}) custom-call(s32[8]{0:T(128)S(1)} %copy-done.1, s32[8,16]{1,0:T(8,128)S(1)} %copy-done, bf16[2,768,256]{2,1,0:T(8,128)(2,1)S(1)} %assemble.1.refs_4_.outer, bf16[2,768,256]{2,1,0:T(8,128)(2,1)S(1)} %get-tuple-element.29.inner, ...), custom_call_target="tpu_custom_call" | custom-call | flops 3221225472 | bytes 1048576 | tf_op jit(solution)/shard_map/chunk/pallas_call | solution.py:154
  41.0 0.0 collective-permute-done.10
  41.0 0.2 collective-permute-start.11
  41.2 0.5 collective-permute-done.7
  41.7 2.9 %collective-permute-start.8 = (f32[2,64,256]{2,1,0:T(8,128)S(1)}, f32[2,64,256]{2,1,0:T(8,128)S(1)}, u32[]{:S(2)}, u32[]{:S(2)}) collective-permute-start(f32[2,64,256]{2,1,0:T(8,128)S(1)} %add.44), channel_id=1, source_target_pairs={{0,4},{4,12},{12,8},{8,0},{1,5},{5,13},{13,9},{9,1},{2,6},{6,14},{... | collective-permute-start | bytes 393224 | tf_op jit(solution)/shard_map/ppermute | solution.py:221
  44.6 3.0 %chunk.4 = (f32[2,64,256]{2,1,0:T(8,128)S(1)}, f32[2,64,256]{2,1,0:T(8,128)S(1)}) custom-call(s32[8]{0:T(128)S(1)} %copy-done.1, s32[8,16]{1,0:T(8,128)S(1)} %copy-done, bf16[2,768,256]{2,1,0:T(8,128)(2,1)S(1)} %assemble.1.refs_4_.outer, bf16[2,768,256]{2,1,0:T(8,128)(2,1)S(1)} %get-tuple-element.29.inner, ...), custom_call_target="tpu_custom_call" | custom-call | flops 3221225472 | bytes 1048576 | tf_op jit(solution)/shard_map/chunk/pallas_call | solution.py:154
  47.7 0.4 collective-permute-done.11
  48.1 2.4 %collective-permute-start.12 = (f32[2,64,256]{2,1,0:T(8,128)S(1)}, f32[2,64,256]{2,1,0:T(8,128)S(1)}, u32[]{:S(2)}, u32[]{:S(2)}) collective-permute-start(f32[2,64,256]{2,1,0:T(8,128)S(1)} %add.47.refs_1_), channel_id=1, source_target_pairs={{0,4},{4,12},{12,8},{8,0},{1,5},{5,13},{13,9},{9,1},{2,6},{6,14},{... | collective-permute-start | bytes 393224 | tf_op jit(solution)/shard_map/ppermute | solution.py:221
  50.5 0.4 collective-permute-done.8
  50.9 0.7 %collective-permute-start.9 = (f32[2,64,256]{2,1,0:T(8,128)S(1)}, f32[2,64,256]{2,1,0:T(8,128)S(1)}, u32[]{:S(2)}, u32[]{:S(2)}) collective-permute-start(f32[2,64,256]{2,1,0:T(8,128)S(1)} %add.45.refs_0_), channel_id=1, source_target_pairs={{0,4},{4,12},{12,8},{8,0},{1,5},{5,13},{13,9},{9,1},{2,6},{6,14},{... | collective-permute-start | bytes 393224 | tf_op jit(solution)/shard_map/ppermute | solution.py:221
  51.6 3.0 %chunk.5 = (f32[2,64,256]{2,1,0:T(8,128)S(1)}, f32[2,64,256]{2,1,0:T(8,128)S(1)}) custom-call(s32[8]{0:T(128)S(1)} %copy-done.1, s32[8,16]{1,0:T(8,128)S(1)} %copy-done, bf16[2,768,256]{2,1,0:T(8,128)(2,1)S(1)} %assemble.1.refs_4_.outer, bf16[2,768,256]{2,1,0:T(8,128)(2,1)S(1)} %get-tuple-element.29.inner, ...), custom_call_target="tpu_custom_call" | custom-call | flops 3221225472 | bytes 1048576 | tf_op jit(solution)/shard_map/chunk/pallas_call | solution.py:154
  54.6 2.2 %collective-permute-done.9 = f32[2,64,256]{2,1,0:T(8,128)S(1)} collective-permute-done((f32[2,64,256]{2,1,0:T(8,128)S(1)}, f32[2,64,256]{2,1,0:T(8,128)S(1)}, u32[]{:S(2)}, u32[]{:S(2)}) %collective-permute-start.9) | collective-permute-done | bytes 131104 | tf_op jit(solution)/shard_map/ppermute | solution.py:221
  56.9 0.0 collective-permute-done.12
  56.9 0.7 %pad_maximum_fusion.2 = f32[4,64,256]{2,1,0:T(8,128)} fusion(f32[1,64,256]{2,1,0:T(8,128)S(1)} %get-tuple-element.44, f32[2,64,256]{2,1,0:T(8,128)S(1)} %add.49, f32[1,64,256]{2,1,0:T(8,128)S(1)} %get-tuple-element.43), kind=kLoop, calls=%fused_computation.2 | loop fusion | flops 131072 | bytes 524288 | tf_op jit(solution)/shard_map/concatenate | solution.py:225
  (16 shorter events, 0.2 us)
Async XLA Ops:
  0.0 9.2 %collective-permute-start = (f32[4,64,256]{2,1,0:T(8,128)}, f32[4,64,256]{2,1,0:T(8,128)S(1)}, u32[]{:S(2)}, u32[]{:S(2)}) collective-permute-start(f32[4,64,256]{2,1,0:T(8,128)} %param.5), channel_id=1, source_target_pairs={{0,4},{4,12},{12,8},{8,0},{1,5},{5,13},{13,9},{9,1},{2,6},{6,14},{... | collective-permute-start | bytes 786440 | tf_op jit(solution)/shard_map/ppermute | solution.py:180
  1.6 1.6 %copy-start.2 = (f32[8,256,256]{2,1,0:T(8,128)S(1)}, f32[8,256,256]{2,1,0:T(8,128)}, u32[]{:S(2)}) copy-start(f32[8,256,256]{2,1,0:T(8,128)} %left_ref.1) | copy-start | bytes 6291460
  3.2 1.6 %copy-start.3 = (f32[8,256,256]{2,1,0:T(8,128)S(1)}, f32[8,256,256]{2,1,0:T(8,128)}, u32[]{:S(2)}) copy-start(f32[8,256,256]{2,1,0:T(8,128)} %right_ref.1) | copy-start | bytes 6291460
  4.8 1.1 %copy-start.4 = (f32[4,64,256]{2,1,0:T(8,128)S(1)}, f32[4,64,256]{2,1,0:T(8,128)}, u32[]{:S(2)}) copy-start(f32[4,64,256]{2,1,0:T(8,128)} %param.5) | copy-start | bytes 786436
  9.2 6.7 %collective-permute-start.3 = (f32[2,64,256]{2,1,0:T(8,128)S(1)}, f32[2,64,256]{2,1,0:T(8,128)S(1)}, u32[]{:S(2)}, u32[]{:S(2)}) collective-permute-start(f32[2,64,256]{2,1,0:T(8,128)S(1)} %get-tuple-element.37), channel_id=1, source_target_pairs={{0,4},{4,12},{12,8},{8,0},{1,5},{5,13},{13,9},{9,1},{2,6},{6,14},{... | collective-permute-start | bytes 393224 | tf_op jit(solution)/shard_map/ppermute | solution.py:183
  10.2 8.0 %collective-permute-start.1 = (f32[2,64,256]{2,1,0:T(8,128)S(1)}, f32[2,64,256]{2,1,0:T(8,128)S(1)}, u32[]{:S(2)}, u32[]{:S(2)}) collective-permute-start(f32[2,64,256]{2,1,0:T(8,128)S(1)} %get-tuple-element.40), channel_id=1, source_target_pairs={{0,4},{4,12},{12,8},{8,0},{1,5},{5,13},{13,9},{9,1},{2,6},{6,14},{... | collective-permute-start | bytes 393224 | tf_op jit(solution)/shard_map/ppermute | solution.py:184
  16.0 5.9 %collective-permute-start.4 = (f32[2,64,256]{2,1,0:T(8,128)S(1)}, f32[2,64,256]{2,1,0:T(8,128)S(1)}, u32[]{:S(2)}, u32[]{:S(2)}) collective-permute-start(f32[2,64,256]{2,1,0:T(8,128)S(1)} %collective-permute-done.3.refs_2_), channel_id=1, source_target_pairs={{0,4},{4,12},{12,8},{8,0},{1,5},{5,13},{13,9},{9,1},{2,6},{6,14},{... | collective-permute-start | bytes 393224 | tf_op jit(solution)/shard_map/ppermute | solution.py:183
  18.2 9.5 %collective-permute-start.2 = (f32[2,64,256]{2,1,0:T(8,128)S(1)}, f32[2,64,256]{2,1,0:T(8,128)S(1)}, u32[]{:S(2)}, u32[]{:S(2)}) collective-permute-start(f32[2,64,256]{2,1,0:T(8,128)S(1)} %collective-permute-done.1.refs_2_), channel_id=1, source_target_pairs={{0,4},{4,12},{12,8},{8,0},{1,5},{5,13},{13,9},{9,1},{2,6},{6,14},{... | collective-permute-start | bytes 393224 | tf_op jit(solution)/shard_map/ppermute | solution.py:184
  21.9 7.7 %collective-permute-start.5 = (f32[4,64,256]{2,1,0:T(8,128)S(1)}, f32[4,64,256]{2,1,0:T(8,128)S(1)}, u32[]{:S(2)}, u32[]{:S(2)}) collective-permute-start(f32[4,64,256]{2,1,0:T(8,128)S(1)} %pad_maximum_fusion), channel_id=1, source_target_pairs={{0,1},{1,2},{2,3},{4,5},{5,6},{6,7},{8,9},{9,10},{10,11},{12,13},{... | collective-permute-start | bytes 786440 | tf_op jit(solution)/shard_map/ppermute | solution.py:18
  23.8 3.9 %copy-start = (s32[8,16]{1,0:T(8,128)S(1)}, s32[8,16]{1,0:T(8,128)}, u32[]{:S(2)}) copy-start(s32[8,16]{1,0:T(8,128)} %allowed_ref.9) | copy-start | bytes 1540
  23.8 7.5 %collective-permute-start.6 = (f32[4,64,256]{2,1,0:T(8,128)S(1)}, f32[4,64,256]{2,1,0:T(8,128)S(1)}, u32[]{:S(2)}, u32[]{:S(2)}) collective-permute-start(f32[4,64,256]{2,1,0:T(8,128)S(1)} %pad_maximum_fusion.1), channel_id=1, source_target_pairs={{1,0},{2,1},{3,2},{5,4},{6,5},{7,6},{9,8},{10,9},{11,10},{13,12},{... | collective-permute-start | bytes 786440 | tf_op jit(solution)/shard_map/ppermute | solution.py:18
  27.7 3.7 %copy-start.1 = (s32[8]{0:T(128)S(1)}, s32[8]{0:T(128)}, u32[]{:S(2)}) copy-start(s32[8]{0:T(128)} %shifts_ref.7) | copy-start | bytes 100
  33.6 7.3 %collective-permute-start.10 = (f32[2,64,256]{2,1,0:T(8,128)S(1)}, f32[2,64,256]{2,1,0:T(8,128)S(1)}, u32[]{:S(2)}, u32[]{:S(2)}) collective-permute-start(f32[2,64,256]{2,1,0:T(8,128)S(1)} %get-tuple-element.28), channel_id=1, source_target_pairs={{0,4},{4,12},{12,8},{8,0},{1,5},{5,13},{13,9},{9,1},{2,6},{6,14},{... | collective-permute-start | bytes 393224 | tf_op jit(solution)/shard_map/ppermute | solution.py:221
  34.5 7.2 %collective-permute-start.7 = (f32[2,64,256]{2,1,0:T(8,128)S(1)}, f32[2,64,256]{2,1,0:T(8,128)S(1)}, u32[]{:S(2)}, u32[]{:S(2)}) collective-permute-start(f32[2,64,256]{2,1,0:T(8,128)S(1)} %broadcast_add_fusion), channel_id=1, source_target_pairs={{0,4},{4,12},{12,8},{8,0},{1,5},{5,13},{13,9},{9,1},{2,6},{6,14},{... | collective-permute-start | bytes 393224 | tf_op jit(solution)/shard_map/ppermute | solution.py:221
  41.0 7.1 %collective-permute-start.11 = (f32[2,64,256]{2,1,0:T(8,128)S(1)}, f32[2,64,256]{2,1,0:T(8,128)S(1)}, u32[]{:S(2)}, u32[]{:S(2)}) collective-permute-start(f32[2,64,256]{2,1,0:T(8,128)S(1)} %add.46), channel_id=1, source_target_pairs={{0,4},{4,12},{12,8},{8,0},{1,5},{5,13},{13,9},{9,1},{2,6},{6,14},{... | collective-permute-start | bytes 393224 | tf_op jit(solution)/shard_map/ppermute | solution.py:221
  41.7 9.1 %collective-permute-start.8 = (f32[2,64,256]{2,1,0:T(8,128)S(1)}, f32[2,64,256]{2,1,0:T(8,128)S(1)}, u32[]{:S(2)}, u32[]{:S(2)}) collective-permute-start(f32[2,64,256]{2,1,0:T(8,128)S(1)} %add.44), channel_id=1, source_target_pairs={{0,4},{4,12},{12,8},{8,0},{1,5},{5,13},{13,9},{9,1},{2,6},{6,14},{... | collective-permute-start | bytes 393224 | tf_op jit(solution)/shard_map/ppermute | solution.py:221
  48.1 8.8 %collective-permute-start.12 = (f32[2,64,256]{2,1,0:T(8,128)S(1)}, f32[2,64,256]{2,1,0:T(8,128)S(1)}, u32[]{:S(2)}, u32[]{:S(2)}) collective-permute-start(f32[2,64,256]{2,1,0:T(8,128)S(1)} %add.47.refs_1_), channel_id=1, source_target_pairs={{0,4},{4,12},{12,8},{8,0},{1,5},{5,13},{13,9},{9,1},{2,6},{6,14},{... | collective-permute-start | bytes 393224 | tf_op jit(solution)/shard_map/ppermute | solution.py:221
  50.9 5.9 %collective-permute-start.9 = (f32[2,64,256]{2,1,0:T(8,128)S(1)}, f32[2,64,256]{2,1,0:T(8,128)S(1)}, u32[]{:S(2)}, u32[]{:S(2)}) collective-permute-start(f32[2,64,256]{2,1,0:T(8,128)S(1)} %add.45.refs_0_), channel_id=1, source_target_pairs={{0,4},{4,12},{12,8},{8,0},{1,5},{5,13},{13,9},{9,1},{2,6},{6,14},{... | collective-permute-start | bytes 393224 | tf_op jit(solution)/shard_map/ppermute | solution.py:221

commit v16 on v8

--- a/solution.py
+++ b/solution.py
@@ -20,13 +20,16 @@
 
 def ring_route(n):
     order = [0] + [i for i in range(n) if i % 2] + [i for i in reversed(range(1, n)) if i % 2 == 0]
-    return [(order[i], order[(i + 1) % n]) for i in range(n)]
+    cores = lax.axis_size("sub")
+    hops = [(order[i], order[(i + 1) % n]) for i in range(n)]
+    return [(hop[core % 2] * cores + core, hop[1 - core % 2] * cores + core) for hop in hops for core in range(cores)]
 
 
 def ring_place(n, steps_back):
     me = lax.axis_index("op")
     place = jnp.where(me == 0, 0, jnp.where(lax.rem(me, 2) == 1, (me + 1) // 2, n - me // 2))
-    at = lax.rem(place - steps_back + 2 * n, n)
+    steps = jnp.where(lax.rem(lax.axis_index("sub"), 2) == 0, steps_back, -steps_back)
+    at = lax.rem(place - steps + 2 * n, n)
     return jnp.where(at == 0, 0, jnp.where(at <= n // 2, 2 * at - 1, 2 * (n - at)))
 
 
@@ -57,10 +60,10 @@
     return jnp.concatenate([hi, lo, hi], axis=0)
 
 
-def place_rows(n, target, blocks):
+def place_rows(n, target, blocks, way=1):
     for j, block in enumerate(blocks):
         rows = block.shape[-2]
-        target[..., pl.ds(pl.multiple_of(ring_place(n, j) * rows, rows), rows), :] = block
+        target[..., pl.ds(pl.multiple_of(ring_place(n, way * j) * rows, rows), rows), :] = block
 
 
 def assemble(n, *refs):
@@ -96,8 +99,8 @@
 
 
 def outside_sectors(n, nloc, allowed_ref, above, below, left_parts, outside, high, low, psi):
-    place_rows(n, psi.at[0], [above[j] for j in range(n)])
-    place_rows(n, psi.at[1], [below[j] for j in range(n)])
+    place_rows(n, psi.at[0], [above[j] for j in range(n)], -1)
+    place_rows(n, psi.at[1], [below[j] for j in range(n)], -1)
     left = chunk_left(n, 0, left_parts)
     first = lax.axis_index(("sec", "sub")) * nloc
     for i in range(2):
@@ -179,11 +182,11 @@
         prepare, "prepare", 4 * kops * one, [parts, tall, tall, zero], [VMEM] * 2, [left_ops, right_ops]
     )
 
-    blocks = [psi, lax.ppermute(psi, "op", route)]
+    blocks = [psi, lax.ppermute(psi, ("op", "sub"), route)]
     outer, inner = [[b[:: nloc - 1] for b in blocks], [b[1 : nloc - 1] for b in blocks]]
     for step in range(1, n - 1):
-        outer.append(lax.ppermute(outer[-1] + zero[0, 0] if step == 1 else outer[-1], "op", route))
-        inner.append(lax.ppermute(inner[-1] + zero[0, 0] if step == 1 else inner[-1], "op", route))
+        outer.append(lax.ppermute(outer[-1] + zero[0, 0] if step == 1 else outer[-1], ("op", "sub"), route))
+        inner.append(lax.ppermute(inner[-1] + zero[0, 0] if step == 1 else inner[-1], ("op", "sub"), route))
 
     above = shifted(jnp.concatenate([b[1:] for b in outer]), ("sec", "sub"), 1)
     below = shifted(jnp.concatenate([b[:1] for b in outer]), ("sec", "sub"), -1)
@@ -227,8 +230,8 @@
 
     for step in range(1, n):
         next_outer, next_inner = mine(step)
-        result_inner = lax.ppermute(result_inner, "op", route) + next_inner
-        result_outer = lax.ppermute(result_outer, "op", route) + next_outer
+        result_inner = lax.ppermute(result_inner, ("op", "sub"), route) + next_inner
+        result_outer = lax.ppermute(result_outer, ("op", "sub"), route) + next_outer
     return jnp.concatenate([result_outer[:1], result_inner, result_outer[1:]])
 
 

time: 55.8 us -> 60.3 us (1.081)
  the two profiles are of different devices: /device:TPU:1 before, /device:TPU:0 now
where the time goes in v16:
time: 60.3 us; the launch traced here: 60 us
  starting transfers between devices  20.9 us (35%)
  waiting for transfers between devices  19 us (32%)
  Pallas kernels  15.6 us (26%)
  local copies, waits for them, and re-layouts  3.27 us (5%)
  other arithmetic  0.95 us (2%)
    pallas_call x9, Pallas kernels, call(): pl.pallas_call(body, name=name, out_shape=out_shape, in_specs=in_specs, o...  15.6 us
    ppermute x3, waiting for transfers between devices, shards(): result_outer = lax.ppermute(result_outer, ('op', 'sub'), route) + next_outer  8.19 us
    ppermute x2, starting transfers between devices, shards(): lax.ppermute(inner[-1] + zero[0, 0] if step == 1 else inner[-1], ('op', '...  5.48 us
    ppermute x3, starting transfers between devices, shards(): result_outer = lax.ppermute(result_outer, ('op', 'sub'), route) + next_outer  4.69 us
    ppermute x1, waiting for transfers between devices, shards(): blocks = [psi, lax.ppermute(psi, ('op', 'sub'), route)]  4.07 us
    ppermute x2, waiting for transfers between devices, shards(): lax.ppermute(outer[-1] + zero[0, 0] if step == 1 else outer[-1], ('op', '...  3.89 us
    unnamed x10, local copies, waits for them, and re-layouts  3.2 us
    ppermute x1, starting transfers between devices, shards(): blocks = [psi, lax.ppermute(psi, ('op', 'sub'), route)]  3.02 us
  transfers between devices with their start and end apart: 13, of which 7 were waited for; matrix products, arithmetic and copies ran while one was open for 0% of the time, Pallas kernels for 26%

profile of v16, /device:TPU:0, one launch (start us, length us, event | category | flops | bytes accessed | tf_op | source)
XLA Modules:
  0.0 60.0 jit_solution(755054112183698612)
XLA Ops:
  0.0 3.0 %collective-permute-start = (f32[4,64,256]{2,1,0:T(8,128)}, f32[4,64,256]{2,1,0:T(8,128)S(1)}, u32[]{:S(2)}, u32[]{:S(2)}) collective-permute-start(f32[4,64,256]{2,1,0:T(8,128)} %param.5), channel_id=1, source_target_pairs={{0,4},{5,1},{4,12},{13,5},{12,8},{9,13},{8,0},{1,9},{2,6},{7,3},{6... | collective-permute-start | bytes 786440 | tf_op jit(solution)/shard_map/ppermute | solution.py:185
  3.0 0.0 copy-start.1
  3.0 1.6 %copy-done.1 = f32[8,256,256]{2,1,0:T(8,128)S(1)} copy-done((f32[8,256,256]{2,1,0:T(8,128)S(1)}, f32[8,256,256]{2,1,0:T(8,128)}, u32[]{:S(2)}) %copy-start.1) | copy-done | bytes 2097176
  4.6 0.0 copy-start.2
  4.6 1.6 %copy-done.2 = f32[8,256,256]{2,1,0:T(8,128)S(1)} copy-done((f32[8,256,256]{2,1,0:T(8,128)S(1)}, f32[8,256,256]{2,1,0:T(8,128)}, u32[]{:S(2)}) %copy-start.2) | copy-done | bytes 2097176
  6.2 0.0 copy-start.4
  6.2 1.1 %prepare.1 = (bf16[4,8,64,768]{3,2,1,0:T(8,128)(2,1)S(1)}, bf16[2048,256]{1,0:T(8,128)(2,1)S(1)}, bf16[2048,256]{1,0:T(8,128)(2,1)S(1)}, f32[1,128]{1,0:T(1,128)S(1)}) custom-call(f32[8,256,256]{2,1,0:T(8,128)S(1)} %copy-done.1, f32[8,256,256]{2,1,0:T(8,128)S(1)} %copy-done.2), custom_call_target="tpu_custom_call" | custom-call | flops 3221225472 | bytes 1048576 | tf_op jit(solution)/shard_map/prepare/pallas_call | solution.py:159
  7.3 0.0 copy-done.4
  7.3 4.1 %collective-permute-done = f32[4,64,256]{2,1,0:T(8,128)S(1)} collective-permute-done((f32[4,64,256]{2,1,0:T(8,128)}, f32[4,64,256]{2,1,0:T(8,128)S(1)}, u32[]{:S(2)}, u32[]{:S(2)}) %collective-permute-start) | collective-permute-done | bytes 262176 | tf_op jit(solution)/shard_map/ppermute | solution.py:185
  11.4 0.1 broadcast_add_fusion
  11.5 0.9 %collective-permute-start.3 = (f32[2,64,256]{2,1,0:T(8,128)S(1)}, f32[2,64,256]{2,1,0:T(8,128)S(1)}, u32[]{:S(2)}, u32[]{:S(2)}) collective-permute-start(f32[2,64,256]{2,1,0:T(8,128)S(1)} %get-tuple-element.37), channel_id=1, source_target_pairs={{0,4},{5,1},{4,12},{13,5},{12,8},{9,13},{8,0},{1,9},{2,6},{7,3},{6... | collective-permute-start | bytes 393224 | tf_op jit(solution)/shard_map/ppermute | solution.py:188
  12.4 2.9 %collective-permute-start.1 = (f32[2,64,256]{2,1,0:T(8,128)S(1)}, f32[2,64,256]{2,1,0:T(8,128)S(1)}, u32[]{:S(2)}, u32[]{:S(2)}) collective-permute-start(f32[2,64,256]{2,1,0:T(8,128)S(1)} %get-tuple-element.40), channel_id=1, source_target_pairs={{0,4},{5,1},{4,12},{13,5},{12,8},{9,13},{8,0},{1,9},{2,6},{7,3},{6... | collective-permute-start | bytes 393224 | tf_op jit(solution)/shard_map/ppermute | solution.py:189
  15.4 2.8 %collective-permute-done.3.refs_2_ = f32[2,64,256]{2,1,0:T(8,128)S(1)} collective-permute-done((f32[2,64,256]{2,1,0:T(8,128)S(1)}, f32[2,64,256]{2,1,0:T(8,128)S(1)}, u32[]{:S(2)}, u32[]{:S(2)}) %collective-permute-start.3) | collective-permute-done | bytes 131104 | tf_op jit(solution)/shard_map/ppermute | solution.py:188
  18.1 1.2 %collective-permute-start.4 = (f32[2,64,256]{2,1,0:T(8,128)S(1)}, f32[2,64,256]{2,1,0:T(8,128)S(1)}, u32[]{:S(2)}, u32[]{:S(2)}) collective-permute-start(f32[2,64,256]{2,1,0:T(8,128)S(1)} %collective-permute-done.3.refs_2_), channel_id=1, source_target_pairs={{0,4},{5,1},{4,12},{13,5},{12,8},{9,13},{8,0},{1,9},{2,6},{7,3},{6... | collective-permute-start | bytes 393224 | tf_op jit(solution)/shard_map/ppermute | solution.py:188
  19.4 1.0 %collective-permute-done.1.refs_2_ = f32[2,64,256]{2,1,0:T(8,128)S(1)} collective-permute-done((f32[2,64,256]{2,1,0:T(8,128)S(1)}, f32[2,64,256]{2,1,0:T(8,128)S(1)}, u32[]{:S(2)}, u32[]{:S(2)}) %collective-permute-start.1) | collective-permute-done | bytes 131104 | tf_op jit(solution)/shard_map/ppermute | solution.py:189
  20.3 2.6 %collective-permute-start.2 = (f32[2,64,256]{2,1,0:T(8,128)S(1)}, f32[2,64,256]{2,1,0:T(8,128)S(1)}, u32[]{:S(2)}, u32[]{:S(2)}) collective-permute-start(f32[2,64,256]{2,1,0:T(8,128)S(1)} %collective-permute-done.1.refs_2_), channel_id=1, source_target_pairs={{0,4},{5,1},{4,12},{13,5},{12,8},{9,13},{8,0},{1,9},{2,6},{7,3},{6... | collective-permute-start | bytes 393224 | tf_op jit(solution)/shard_map/ppermute | solution.py:189
  22.9 1.1 %collective-permute-done.4.refs_3_ = f32[2,64,256]{2,1,0:T(8,128)S(1)} collective-permute-done((f32[2,64,256]{2,1,0:T(8,128)S(1)}, f32[2,64,256]{2,1,0:T(8,128)S(1)}, u32[]{:S(2)}, u32[]{:S(2)}) %collective-permute-start.4) | collective-permute-done | bytes 131104 | tf_op jit(solution)/shard_map/ppermute | solution.py:188
  24.1 1.3 %collective-permute-start.5 = (f32[4,64,256]{2,1,0:T(8,128)S(1)}, f32[4,64,256]{2,1,0:T(8,128)S(1)}, u32[]{:S(2)}, u32[]{:S(2)}) collective-permute-start(f32[4,64,256]{2,1,0:T(8,128)S(1)} %pad_maximum_fusion), channel_id=1, source_target_pairs={{0,1},{1,2},{2,3},{4,5},{5,6},{6,7},{8,9},{9,10},{10,11},{12,13},{... | collective-permute-start | bytes 786440 | tf_op jit(solution)/shard_map/ppermute | solution.py:18
  25.4 0.0 copy-start.3
  25.4 1.3 %collective-permute-start.6 = (f32[4,64,256]{2,1,0:T(8,128)S(1)}, f32[4,64,256]{2,1,0:T(8,128)S(1)}, u32[]{:S(2)}, u32[]{:S(2)}) collective-permute-start(f32[4,64,256]{2,1,0:T(8,128)S(1)} %pad_maximum_fusion.1), channel_id=1, source_target_pairs={{1,0},{2,1},{3,2},{5,4},{6,5},{7,6},{9,8},{10,9},{11,10},{13,12},{... | collective-permute-start | bytes 786440 | tf_op jit(solution)/shard_map/ppermute | solution.py:18
  26.7 0.2 assemble.1.refs_4_.outer
  26.9 0.0 collective-permute-done.2.refs_3_
  26.9 0.0 copy-done.3
  26.9 0.0 copy-start
  26.9 1.7 %own.1 = (bf16[2,768,256]{2,1,0:T(8,128)(2,1)S(1)}, bf16[4,512,256]{2,1,0:T(8,128)(2,1)S(1)}, bf16[4,512,256]{2,1,0:T(8,128)(2,1)S(1)}) custom-call(s32[8,16]{1,0:T(8,128)S(1)} %copy-done.3, f32[2,64,256]{2,1,0:T(8,128)S(1)} %get-tuple-element.42.refs_0_, f32[2,64,256]{2,1,0:T(8,128)S(1)} %get-tuple-element.39.refs_1_, ...), custom_call_target="tpu_custom_call" | custom-call | flops 3221225472 | bytes 1048576 | tf_op jit(solution)/shard_map/own/pallas_call | solution.py:159
  28.6 0.0 copy-done
  28.6 1.2 %first_inner.1 = f32[2,64,256]{2,1,0:T(8,128)S(1)} custom-call(s32[8]{0:T(128)S(1)} %copy-done, bf16[4,512,256]{2,1,0:T(8,128)(2,1)S(1)} %get-tuple-element.23.high, bf16[4,512,256]{2,1,0:T(8,128)(2,1)S(1)} %get-tuple-element.24.low, bf16[2048,256]{1,0:T(8,128)(2,1)S(1)} %get-tuple-element.27.right_hi, bf16[2048,256]{1,0:T(8,128)(2,1)S(1)} %get-tuple-element.28.right_lo), custom_call_target="tpu_custom_call" | custom-call | flops 805306368 | bytes 1048576 | tf_op jit(solution)/shard_map/first_inner/pallas_call | solution.py:159
  29.8 2.2 %collective-permute-start.10 = (f32[2,64,256]{2,1,0:T(8,128)S(1)}, f32[2,64,256]{2,1,0:T(8,128)S(1)}, u32[]{:S(2)}, u32[]{:S(2)}) collective-permute-start(f32[2,64,256]{2,1,0:T(8,128)S(1)} %first_inner.1), channel_id=1, source_target_pairs={{0,4},{5,1},{4,12},{13,5},{12,8},{9,13},{8,0},{1,9},{2,6},{7,3},{6... | collective-permute-start | bytes 393224 | tf_op jit(solution)/shard_map/ppermute | solution.py:233
  31.9 0.0 collective-permute-done.5.above
  32.0 0.0 collective-permute-done.6.below
  32.0 1.3 %outside.1 = (bf16[2,768,256]{2,1,0:T(8,128)(2,1)S(1)}, bf16[2,512,256]{2,1,0:T(8,128)(2,1)S(1)}, bf16[2,512,256]{2,1,0:T(8,128)(2,1)S(1)}) custom-call(s32[8,16]{1,0:T(8,128)S(1)} %copy-done.3, f32[4,64,256]{2,1,0:T(8,128)S(1)} %collective-permute-done.5.above, f32[4,64,256]{2,1,0:T(8,128)S(1)} %collective-permute-done.6.below, ...), custom_call_target="tpu_custom_call" | custom-call | flops 1610612736 | bytes 1048576 | tf_op jit(solution)/shard_map/outside/pallas_call | solution.py:159
  33.3 1.2 %first_outer.1 = f32[2,64,256]{2,1,0:T(8,128)S(1)} custom-call(s32[8]{0:T(128)S(1)} %copy-done, bf16[4,512,256]{2,1,0:T(8,128)(2,1)S(1)} %get-tuple-element.23.high, bf16[4,512,256]{2,1,0:T(8,128)(2,1)S(1)} %get-tuple-element.24.low, bf16[2,512,256]{2,1,0:T(8,128)(2,1)S(1)} %get-tuple-element.25.end_high, ...), custom_call_target="tpu_custom_call" | custom-call | flops 805306368 | bytes 1048576 | tf_op jit(solution)/shard_map/first_outer/pallas_call | solution.py:159
  34.4 3.4 %collective-permute-start.7 = (f32[2,64,256]{2,1,0:T(8,128)S(1)}, f32[2,64,256]{2,1,0:T(8,128)S(1)}, u32[]{:S(2)}, u32[]{:S(2)}) collective-permute-start(f32[2,64,256]{2,1,0:T(8,128)S(1)} %first_outer.1), channel_id=1, source_target_pairs={{0,4},{5,1},{4,12},{13,5},{12,8},{9,13},{8,0},{1,9},{2,6},{7,3},{6... | collective-permute-start | bytes 393224 | tf_op jit(solution)/shard_map/ppermute | solution.py:234
  37.9 3.0 %chunk.3 = (f32[2,64,256]{2,1,0:T(8,128)S(1)}, f32[2,64,256]{2,1,0:T(8,128)S(1)}) custom-call(s32[8]{0:T(128)S(1)} %copy-done, s32[8,16]{1,0:T(8,128)S(1)} %copy-done.3, bf16[2,768,256]{2,1,0:T(8,128)(2,1)S(1)} %assemble.1.refs_4_.outer, bf16[2,768,256]{2,1,0:T(8,128)(2,1)S(1)} %get-tuple-element.29.inner, ...), custom_call_target="tpu_custom_call" | custom-call | flops 3221225472 | bytes 1048576 | tf_op jit(solution)/shard_map/chunk/pallas_call | solution.py:159
  40.9 0.0 collective-permute-done.10
  40.9 0.8 %collective-permute-start.11 = (f32[2,64,256]{2,1,0:T(8,128)S(1)}, f32[2,64,256]{2,1,0:T(8,128)S(1)}, u32[]{:S(2)}, u32[]{:S(2)}) collective-permute-start(f32[2,64,256]{2,1,0:T(8,128)S(1)} %add.34), channel_id=1, source_target_pairs={{0,4},{5,1},{4,12},{13,5},{12,8},{9,13},{8,0},{1,9},{2,6},{7,3},{6... | collective-permute-start | bytes 393224 | tf_op jit(solution)/shard_map/ppermute | solution.py:233
  41.7 0.0 collective-permute-done.7
  41.7 1.2 %collective-permute-start.8 = (f32[2,64,256]{2,1,0:T(8,128)S(1)}, f32[2,64,256]{2,1,0:T(8,128)S(1)}, u32[]{:S(2)}, u32[]{:S(2)}) collective-permute-start(f32[2,64,256]{2,1,0:T(8,128)S(1)} %add.31), channel_id=1, source_target_pairs={{0,4},{5,1},{4,12},{13,5},{12,8},{9,13},{8,0},{1,9},{2,6},{7,3},{6... | collective-permute-start | bytes 393224 | tf_op jit(solution)/shard_map/ppermute | solution.py:234
  42.9 3.0 %chunk.4 = (f32[2,64,256]{2,1,0:T(8,128)S(1)}, f32[2,64,256]{2,1,0:T(8,128)S(1)}) custom-call(s32[8]{0:T(128)S(1)} %copy-done, s32[8,16]{1,0:T(8,128)S(1)} %copy-done.3, bf16[2,768,256]{2,1,0:T(8,128)(2,1)S(1)} %assemble.1.refs_4_.outer, bf16[2,768,256]{2,1,0:T(8,128)(2,1)S(1)} %get-tuple-element.29.inner, ...), custom_call_target="tpu_custom_call" | custom-call | flops 3221225472 | bytes 1048576 | tf_op jit(solution)/shard_map/chunk/pallas_call | solution.py:159
  45.9 1.9 %collective-permute-done.11 = f32[2,64,256]{2,1,0:T(8,128)S(1)} collective-permute-done((f32[2,64,256]{2,1,0:T(8,128)S(1)}, f32[2,64,256]{2,1,0:T(8,128)S(1)}, u32[]{:S(2)}, u32[]{:S(2)}) %collective-permute-start.11) | collective-permute-done | bytes 131104 | tf_op jit(solution)/shard_map/ppermute | solution.py:233
  47.9 0.1 collective-permute-start.12
  47.9 3.7 %collective-permute-done.8 = f32[2,64,256]{2,1,0:T(8,128)S(1)} collective-permute-done((f32[2,64,256]{2,1,0:T(8,128)S(1)}, f32[2,64,256]{2,1,0:T(8,128)S(1)}, u32[]{:S(2)}, u32[]{:S(2)}) %collective-permute-start.8) | collective-permute-done | bytes 131104 | tf_op jit(solution)/shard_map/ppermute | solution.py:234
  51.6 0.1 collective-permute-start.9
  51.7 3.0 %chunk.5 = (f32[2,64,256]{2,1,0:T(8,128)S(1)}, f32[2,64,256]{2,1,0:T(8,128)S(1)}) custom-call(s32[8]{0:T(128)S(1)} %copy-done, s32[8,16]{1,0:T(8,128)S(1)} %copy-done.3, bf16[2,768,256]{2,1,0:T(8,128)(2,1)S(1)} %assemble.1.refs_4_.outer, bf16[2,768,256]{2,1,0:T(8,128)(2,1)S(1)} %get-tuple-element.29.inner, ...), custom_call_target="tpu_custom_call" | custom-call | flops 3221225472 | bytes 1048576 | tf_op jit(solution)/shard_map/chunk/pallas_call | solution.py:159
  54.7 0.0 collective-permute-done.12
  54.8 4.5 %collective-permute-done.9 = f32[2,64,256]{2,1,0:T(8,128)S(1)} collective-permute-done((f32[2,64,256]{2,1,0:T(8,128)S(1)}, f32[2,64,256]{2,1,0:T(8,128)S(1)}, u32[]{:S(2)}, u32[]{:S(2)}) %collective-permute-start.9) | collective-permute-done | bytes 131104 | tf_op jit(solution)/shard_map/ppermute | solution.py:234
  59.3 0.7 %pad_maximum_fusion.2 = f32[4,64,256]{2,1,0:T(8,128)} fusion(f32[1,64,256]{2,1,0:T(8,128)S(1)} %get-tuple-element.44, f32[2,64,256]{2,1,0:T(8,128)S(1)} %add.36, f32[1,64,256]{2,1,0:T(8,128)S(1)} %get-tuple-element.43), kind=kLoop, calls=%fused_computation.2 | loop fusion | flops 131072 | bytes 524288 | tf_op jit(solution)/shard_map/concatenate | solution.py:235
  (14 shorter events, 0.2 us)
Async XLA Ops:
  0.0 11.4 %collective-permute-start = (f32[4,64,256]{2,1,0:T(8,128)}, f32[4,64,256]{2,1,0:T(8,128)S(1)}, u32[]{:S(2)}, u32[]{:S(2)}) collective-permute-start(f32[4,64,256]{2,1,0:T(8,128)} %param.5), channel_id=1, source_target_pairs={{0,4},{5,1},{4,12},{13,5},{12,8},{9,13},{8,0},{1,9},{2,6},{7,3},{6... | collective-permute-start | bytes 786440 | tf_op jit(solution)/shard_map/ppermute | solution.py:185
  3.0 1.6 %copy-start.1 = (f32[8,256,256]{2,1,0:T(8,128)S(1)}, f32[8,256,256]{2,1,0:T(8,128)}, u32[]{:S(2)}) copy-start(f32[8,256,256]{2,1,0:T(8,128)} %left_ref.1) | copy-start | bytes 6291460
  4.6 1.6 %copy-start.2 = (f32[8,256,256]{2,1,0:T(8,128)S(1)}, f32[8,256,256]{2,1,0:T(8,128)}, u32[]{:S(2)}) copy-start(f32[8,256,256]{2,1,0:T(8,128)} %right_ref.1) | copy-start | bytes 6291460
  6.2 1.1 %copy-start.4 = (f32[4,64,256]{2,1,0:T(8,128)S(1)}, f32[4,64,256]{2,1,0:T(8,128)}, u32[]{:S(2)}) copy-start(f32[4,64,256]{2,1,0:T(8,128)} %param.5) | copy-start | bytes 786436
  11.5 6.7 %collective-permute-start.3 = (f32[2,64,256]{2,1,0:T(8,128)S(1)}, f32[2,64,256]{2,1,0:T(8,128)S(1)}, u32[]{:S(2)}, u32[]{:S(2)}) collective-permute-start(f32[2,64,256]{2,1,0:T(8,128)S(1)} %get-tuple-element.37), channel_id=1, source_target_pairs={{0,4},{5,1},{4,12},{13,5},{12,8},{9,13},{8,0},{1,9},{2,6},{7,3},{6... | collective-permute-start | bytes 393224 | tf_op jit(solution)/shard_map/ppermute | solution.py:188
  12.4 7.9 %collective-permute-start.1 = (f32[2,64,256]{2,1,0:T(8,128)S(1)}, f32[2,64,256]{2,1,0:T(8,128)S(1)}, u32[]{:S(2)}, u32[]{:S(2)}) collective-permute-start(f32[2,64,256]{2,1,0:T(8,128)S(1)} %get-tuple-element.40), channel_id=1, source_target_pairs={{0,4},{5,1},{4,12},{13,5},{12,8},{9,13},{8,0},{1,9},{2,6},{7,3},{6... | collective-permute-start | bytes 393224 | tf_op jit(solution)/shard_map/ppermute | solution.py:189
  18.1 5.9 %collective-permute-start.4 = (f32[2,64,256]{2,1,0:T(8,128)S(1)}, f32[2,64,256]{2,1,0:T(8,128)S(1)}, u32[]{:S(2)}, u32[]{:S(2)}) collective-permute-start(f32[2,64,256]{2,1,0:T(8,128)S(1)} %collective-permute-done.3.refs_2_), channel_id=1, source_target_pairs={{0,4},{5,1},{4,12},{13,5},{12,8},{9,13},{8,0},{1,9},{2,6},{7,3},{6... | collective-permute-start | bytes 393224 | tf_op jit(solution)/shard_map/ppermute | solution.py:188
  20.3 6.6 %collective-permute-start.2 = (f32[2,64,256]{2,1,0:T(8,128)S(1)}, f32[2,64,256]{2,1,0:T(8,128)S(1)}, u32[]{:S(2)}, u32[]{:S(2)}) collective-permute-start(f32[2,64,256]{2,1,0:T(8,128)S(1)} %collective-permute-done.1.refs_2_), channel_id=1, source_target_pairs={{0,4},{5,1},{4,12},{13,5},{12,8},{9,13},{8,0},{1,9},{2,6},{7,3},{6... | collective-permute-start | bytes 393224 | tf_op jit(solution)/shard_map/ppermute | solution.py:189
  24.1 7.9 %collective-permute-start.5 = (f32[4,64,256]{2,1,0:T(8,128)S(1)}, f32[4,64,256]{2,1,0:T(8,128)S(1)}, u32[]{:S(2)}, u32[]{:S(2)}) collective-permute-start(f32[4,64,256]{2,1,0:T(8,128)S(1)} %pad_maximum_fusion), channel_id=1, source_target_pairs={{0,1},{1,2},{2,3},{4,5},{5,6},{6,7},{8,9},{9,10},{10,11},{12,13},{... | collective-permute-start | bytes 786440 | tf_op jit(solution)/shard_map/ppermute | solution.py:18
  25.4 1.5 %copy-start.3 = (s32[8,16]{1,0:T(8,128)S(1)}, s32[8,16]{1,0:T(8,128)}, u32[]{:S(2)}) copy-start(s32[8,16]{1,0:T(8,128)} %allowed_ref.9) | copy-start | bytes 1540
  25.4 6.5 %collective-permute-start.6 = (f32[4,64,256]{2,1,0:T(8,128)S(1)}, f32[4,64,256]{2,1,0:T(8,128)S(1)}, u32[]{:S(2)}, u32[]{:S(2)}) collective-permute-start(f32[4,64,256]{2,1,0:T(8,128)S(1)} %pad_maximum_fusion.1), channel_id=1, source_target_pairs={{1,0},{2,1},{3,2},{5,4},{6,5},{7,6},{9,8},{10,9},{11,10},{13,12},{... | collective-permute-start | bytes 786440 | tf_op jit(solution)/shard_map/ppermute | solution.py:18
  26.9 1.7 %copy-start = (s32[8]{0:T(128)S(1)}, s32[8]{0:T(128)}, u32[]{:S(2)}) copy-start(s32[8]{0:T(128)} %shifts_ref.9) | copy-start | bytes 100
  29.8 11.1 %collective-permute-start.10 = (f32[2,64,256]{2,1,0:T(8,128)S(1)}, f32[2,64,256]{2,1,0:T(8,128)S(1)}, u32[]{:S(2)}, u32[]{:S(2)}) collective-permute-start(f32[2,64,256]{2,1,0:T(8,128)S(1)} %first_inner.1), channel_id=1, source_target_pairs={{0,4},{5,1},{4,12},{13,5},{12,8},{9,13},{8,0},{1,9},{2,6},{7,3},{6... | collective-permute-start | bytes 393224 | tf_op jit(solution)/shard_map/ppermute | solution.py:233
  34.4 7.3 %collective-permute-start.7 = (f32[2,64,256]{2,1,0:T(8,128)S(1)}, f32[2,64,256]{2,1,0:T(8,128)S(1)}, u32[]{:S(2)}, u32[]{:S(2)}) collective-permute-start(f32[2,64,256]{2,1,0:T(8,128)S(1)} %first_outer.1), channel_id=1, source_target_pairs={{0,4},{5,1},{4,12},{13,5},{12,8},{9,13},{8,0},{1,9},{2,6},{7,3},{6... | collective-permute-start | bytes 393224 | tf_op jit(solution)/shard_map/ppermute | solution.py:234
  40.9 6.9 %collective-permute-start.11 = (f32[2,64,256]{2,1,0:T(8,128)S(1)}, f32[2,64,256]{2,1,0:T(8,128)S(1)}, u32[]{:S(2)}, u32[]{:S(2)}) collective-permute-start(f32[2,64,256]{2,1,0:T(8,128)S(1)} %add.34), channel_id=1, source_target_pairs={{0,4},{5,1},{4,12},{13,5},{12,8},{9,13},{8,0},{1,9},{2,6},{7,3},{6... | collective-permute-start | bytes 393224 | tf_op jit(solution)/shard_map/ppermute | solution.py:233
  41.7 9.9 %collective-permute-start.8 = (f32[2,64,256]{2,1,0:T(8,128)S(1)}, f32[2,64,256]{2,1,0:T(8,128)S(1)}, u32[]{:S(2)}, u32[]{:S(2)}) collective-permute-start(f32[2,64,256]{2,1,0:T(8,128)S(1)} %add.31), channel_id=1, source_target_pairs={{0,4},{5,1},{4,12},{13,5},{12,8},{9,13},{8,0},{1,9},{2,6},{7,3},{6... | collective-permute-start | bytes 393224 | tf_op jit(solution)/shard_map/ppermute | solution.py:234
  47.9 6.9 %collective-permute-start.12 = (f32[2,64,256]{2,1,0:T(8,128)S(1)}, f32[2,64,256]{2,1,0:T(8,128)S(1)}, u32[]{:S(2)}, u32[]{:S(2)}) collective-permute-start(f32[2,64,256]{2,1,0:T(8,128)S(1)} %add.35), channel_id=1, source_target_pairs={{0,4},{5,1},{4,12},{13,5},{12,8},{9,13},{8,0},{1,9},{2,6},{7,3},{6... | collective-permute-start | bytes 393224 | tf_op jit(solution)/shard_map/ppermute | solution.py:233
  51.6 7.6 %collective-permute-start.9 = (f32[2,64,256]{2,1,0:T(8,128)S(1)}, f32[2,64,256]{2,1,0:T(8,128)S(1)}, u32[]{:S(2)}, u32[]{:S(2)}) collective-permute-start(f32[2,64,256]{2,1,0:T(8,128)S(1)} %add.32), channel_id=1, source_target_pairs={{0,4},{5,1},{4,12},{13,5},{12,8},{9,13},{8,0},{1,9},{2,6},{7,3},{6... | collective-permute-start | bytes 393224 | tf_op jit(solution)/shard_map/ppermute | solution.py:234

commit v17 on v12

--- a/solution.py
+++ b/solution.py
@@ -84,8 +84,8 @@
     return left_parts[ring_place(n, step + 1)].reshape(-1, left_parts.shape[-1])
 
 
-def own_sectors(n, allowed_ref, *refs):
-    (outer, left_parts), (inner, high, low, psi) = refs[n : n + 2], refs[n + 2 :]
+def own_sectors(n, allowed_ref, outer, *refs):
+    left_parts, inner, high, low, psi = refs[n:]
     assemble(n, *refs[:n], inner, psi)
     left = chunk_left(n, 0, left_parts)
     nloc = high.shape[0]
@@ -108,8 +108,15 @@
     out[...] = dot3((left(high), left(low)), (right_hi[...], right_lo[...])).reshape(out.shape)
 
 
-def first_chunk(n, nloc, shifts_ref, allowed_ref, own_high, own_low, above, below, left_parts, right_hi, right_lo, *refs):
-    outer_out, inner_out, outside, end_high, end_low, psi = refs
+def first_inner(nloc, shifts_ref, high, low, right_hi, right_lo, out):
+    def blocks_of(own, shift, at):
+        return [own[t - shift, at] for t in range(1, nloc - 1)]
+
+    second_product(blocks_of, shifts_ref, high, low, right_hi, right_lo, out)
+
+
+def first_outer(n, nloc, shifts_ref, allowed_ref, own_high, own_low, above, below, left_parts, right_hi, right_lo, *refs):
+    out, outside, end_high, end_low, psi = refs
     place_rows(n, psi.at[0], [above[j] for j in range(n)])
     place_rows(n, psi.at[1], [below[j] for j in range(n)])
     left = chunk_left(n, 0, left_parts)
@@ -118,18 +125,13 @@
         outside[i] = stacked(psi[i])
         first_product(left, outside[i], allowed_ref, first - 1 + i * (nloc + 1), end_high.at[i], end_low.at[i])
 
-    def inner_blocks(parts, shift, at):
-        return [parts[0][t - shift, at] for t in range(1, nloc - 1)]
-
-    def outer_blocks(parts, shift, at):
+    def blocks_of(parts, shift, at):
         own, ends = parts
         start = jnp.where(shift == 1, ends[0, at], own[jnp.maximum(-shift, 0), at])
         end = jnp.where(shift == -1, ends[1, at], own[jnp.minimum(nloc - 1 - shift, nloc - 1), at])
         return [start, end]
 
-    high, low = (own_high, end_high), (own_low, end_low)
-    second_product(inner_blocks, shifts_ref, high, low, right_hi, right_lo, inner_out)
-    second_product(outer_blocks, shifts_ref, high, low, right_hi, right_lo, outer_out)
+    second_product(blocks_of, shifts_ref, (own_high, end_high), (own_low, end_low), right_hi, right_lo, out)
 
 
 def later_chunk(n, nloc, step, shifts_ref, allowed_ref, outer, inner, outside, left_parts, right_hi, right_lo, outer_out, inner_out, high, low):
@@ -199,10 +201,14 @@
     chunk_inner = jax.ShapeDtypeStruct((nloc - 2, rows, width), F32)
     parts_inner, *own = call(
         functools.partial(own_sectors, n), "own", 4 * kops * one, [split_parts(nloc - 2), *products(nloc)],
-        [SMEM] + [VMEM] * (n + 2), [allowed, *inner, parts_outer, left_parts], whole(nloc - 2),
-    )
-    result_outer, result_inner, parts_outside = call(
-        functools.partial(first_chunk, n, nloc), "first_chunk", 2 * kops * one, [chunk, chunk_inner, split_parts(2)],
+        [SMEM] + [VMEM] * (n + 2), [allowed, parts_outer, *inner, left_parts], whole(nloc - 2),
+    )
+    result_inner = call(
+        functools.partial(first_inner, nloc), "first_inner", nloc * kops * one // n, chunk_inner,
+        [SMEM] + [VMEM] * 4, [shifts, *own, right_hi, right_lo],
+    )
+    result_outer, parts_outside = call(
+        functools.partial(first_outer, n, nloc), "first_outer", 2 * kops * one, [chunk, split_parts(2)],
         [SMEM] * 2 + [VMEM] * 7, [shifts, allowed, *own, above, below, left_parts, right_hi, right_lo],
         [pltpu.VMEM((2, kops * rows, width), BF16)] * 2 + whole(2),
     )

time: 59 us -> 55.8 us (0.946); the launches traced: 58.2 us -> 55.6 us
  waiting for transfers between devices: 17.5 us -> 13 us
  Pallas kernels: 14.3 us -> 15.6 us
  starting transfers between devices: 21.9 us -> 22.5 us
    ppermute x3, waiting for transfers between devices: 2.25 us -> 0.3 us  [shards(): result_inner = lax.ppermute(result_inner, 'op', route) + next_inner]
    ppermute x2, waiting for transfers between devices: 3.84 us -> 2.41 us  [shifted(): return lax.ppermute(block, axis, route)]
    pallas_call x7 -> x8, Pallas kernels: 14.3 us -> 15.6 us  [call(): pl.pallas_call(body, name=name, out_shape=out_shape, in_specs=in_specs, o...]
    ppermute x3, waiting for transfers between devices: 2.67 us -> 1.59 us  [shards(): result_outer = lax.ppermute(result_outer, 'op', route) + next_outer]
  transfers between devices with their start and end apart: 13 -> 13, of which waited for: 8 -> 7; matrix products, arithmetic and copies ran while one was open for 0% -> 0% of each run, Pallas kernels for 21% -> 28%
where the time goes in v17:
time: 55.8 us; the launch traced here: 55.6 us
  starting transfers between devices  22.5 us (40%)
  Pallas kernels  15.6 us (28%)
  waiting for transfers between devices  13 us (23%)
  local copies, waits for them, and re-layouts  3.27 us (6%)
  other arithmetic  0.94 us (2%)
    pallas_call x8, Pallas kernels, call(): pl.pallas_call(body, name=name, out_shape=out_shape, in_specs=in_specs, o...  15.6 us
    ppermute x2, starting transfers between devices, shifted(): return lax.ppermute(block, axis, route)  8.41 us
    ppermute x3, starting transfers between devices, shards(): result_inner = lax.ppermute(result_inner, 'op', route) + next_inner  6.46 us
    ppermute x2, waiting for transfers between devices, shards(): lax.ppermute(outer[-1] + zero[0, 0] if step == 1 else outer[-1], 'op', ro...  3.62 us
    ppermute x2, starting transfers between devices, shards(): lax.ppermute(inner[-1] + zero[0, 0] if step == 1 else inner[-1], 'op', ro...  3.59 us
    unnamed x10, local copies, waits for them, and re-layouts  3.2 us
    ppermute x1, waiting for transfers between devices, shards(): blocks = [psi, lax.ppermute(psi, 'op', route)]  2.94 us
    ppermute x2, waiting for transfers between devices, shifted(): return lax.ppermute(block, axis, route)  2.41 us
  transfers between devices with their start and end apart: 13, of which 7 were waited for; matrix products, arithmetic and copies ran while one was open for 0% of the time, Pallas kernels for 28%

profile of v17, /device:TPU:1, one launch (start us, length us, event | category | flops | bytes accessed | tf_op | source)
XLA Modules:
  0.0 55.6 jit_solution(5195157269343064437)
XLA Ops:
  0.0 2.1 %collective-permute-start = (f32[4,64,256]{2,1,0:T(8,128)}, f32[4,64,256]{2,1,0:T(8,128)S(1)}, u32[]{:S(2)}, u32[]{:S(2)}) collective-permute-start(f32[4,64,256]{2,1,0:T(8,128)} %param.5), channel_id=1, source_target_pairs={{0,4},{4,12},{12,8},{8,0},{1,5},{5,13},{13,9},{9,1},{2,6},{6,14},{... | collective-permute-start | bytes 786440 | tf_op jit(solution)/shard_map/ppermute | solution.py:181
  2.1 0.0 copy-start.2
  2.1 1.6 %copy-done.2 = f32[8,256,256]{2,1,0:T(8,128)S(1)} copy-done((f32[8,256,256]{2,1,0:T(8,128)S(1)}, f32[8,256,256]{2,1,0:T(8,128)}, u32[]{:S(2)}) %copy-start.2) | copy-done | bytes 2097176
  3.7 0.0 copy-start.3
  3.7 1.6 %copy-done.3 = f32[8,256,256]{2,1,0:T(8,128)S(1)} copy-done((f32[8,256,256]{2,1,0:T(8,128)S(1)}, f32[8,256,256]{2,1,0:T(8,128)}, u32[]{:S(2)}) %copy-start.3) | copy-done | bytes 2097176
  5.3 0.0 copy-start.4
  5.3 1.1 %prepare.1 = (bf16[4,8,64,768]{3,2,1,0:T(8,128)(2,1)S(1)}, bf16[2048,256]{1,0:T(8,128)(2,1)S(1)}, bf16[2048,256]{1,0:T(8,128)(2,1)S(1)}, f32[1,128]{1,0:T(1,128)S(1)}) custom-call(f32[8,256,256]{2,1,0:T(8,128)S(1)} %copy-done.2, f32[8,256,256]{2,1,0:T(8,128)S(1)} %copy-done.3), custom_call_target="tpu_custom_call" | custom-call | flops 3221225472 | bytes 1048576 | tf_op jit(solution)/shard_map/prepare/pallas_call | solution.py:155
  6.4 0.0 copy-done.4
  6.4 2.9 %collective-permute-done = f32[4,64,256]{2,1,0:T(8,128)S(1)} collective-permute-done((f32[4,64,256]{2,1,0:T(8,128)}, f32[4,64,256]{2,1,0:T(8,128)S(1)}, u32[]{:S(2)}, u32[]{:S(2)}) %collective-permute-start) | collective-permute-done | bytes 262176 | tf_op jit(solution)/shard_map/ppermute | solution.py:181
  9.4 0.1 broadcast_add_fusion
  9.5 0.4 collective-permute-start.1
  9.9 3.0 %collective-permute-start.3 = (f32[2,64,256]{2,1,0:T(8,128)S(1)}, f32[2,64,256]{2,1,0:T(8,128)S(1)}, u32[]{:S(2)}, u32[]{:S(2)}) collective-permute-start(f32[2,64,256]{2,1,0:T(8,128)S(1)} %get-tuple-element.35), channel_id=1, source_target_pairs={{0,4},{4,12},{12,8},{8,0},{1,5},{5,13},{13,9},{9,1},{2,6},{6,14},{... | collective-permute-start | bytes 393224 | tf_op jit(solution)/shard_map/ppermute | solution.py:185
  12.9 1.4 %collective-permute-done.1.refs_2_ = f32[2,64,256]{2,1,0:T(8,128)S(1)} collective-permute-done((f32[2,64,256]{2,1,0:T(8,128)S(1)}, f32[2,64,256]{2,1,0:T(8,128)S(1)}, u32[]{:S(2)}, u32[]{:S(2)}) %collective-permute-start.1) | collective-permute-done | bytes 131104 | tf_op jit(solution)/shard_map/ppermute | solution.py:184
  14.2 0.6 %collective-permute-start.2 = (f32[2,64,256]{2,1,0:T(8,128)S(1)}, f32[2,64,256]{2,1,0:T(8,128)S(1)}, u32[]{:S(2)}, u32[]{:S(2)}) collective-permute-start(f32[2,64,256]{2,1,0:T(8,128)S(1)} %collective-permute-done.1.refs_2_), channel_id=1, source_target_pairs={{0,4},{4,12},{12,8},{8,0},{1,5},{5,13},{13,9},{9,1},{2,6},{6,14},{... | collective-permute-start | bytes 393224 | tf_op jit(solution)/shard_map/ppermute | solution.py:184
  14.8 2.2 %collective-permute-done.3.refs_2_ = f32[2,64,256]{2,1,0:T(8,128)S(1)} collective-permute-done((f32[2,64,256]{2,1,0:T(8,128)S(1)}, f32[2,64,256]{2,1,0:T(8,128)S(1)}, u32[]{:S(2)}, u32[]{:S(2)}) %collective-permute-start.3) | collective-permute-done | bytes 131104 | tf_op jit(solution)/shard_map/ppermute | solution.py:185
  17.0 0.6 %collective-permute-start.4 = (f32[2,64,256]{2,1,0:T(8,128)S(1)}, f32[2,64,256]{2,1,0:T(8,128)S(1)}, u32[]{:S(2)}, u32[]{:S(2)}) collective-permute-start(f32[2,64,256]{2,1,0:T(8,128)S(1)} %collective-permute-done.3.refs_2_), channel_id=1, source_target_pairs={{0,4},{4,12},{12,8},{8,0},{1,5},{5,13},{13,9},{9,1},{2,6},{6,14},{... | collective-permute-start | bytes 393224 | tf_op jit(solution)/shard_map/ppermute | solution.py:185
  17.6 2.3 %collective-permute-done.2.refs_3_ = f32[2,64,256]{2,1,0:T(8,128)S(1)} collective-permute-done((f32[2,64,256]{2,1,0:T(8,128)S(1)}, f32[2,64,256]{2,1,0:T(8,128)S(1)}, u32[]{:S(2)}, u32[]{:S(2)}) %collective-permute-start.2) | collective-permute-done | bytes 131104 | tf_op jit(solution)/shard_map/ppermute | solution.py:184
  19.9 6.5 %collective-permute-start.5 = (f32[4,64,256]{2,1,0:T(8,128)S(1)}, f32[4,64,256]{2,1,0:T(8,128)S(1)}, u32[]{:S(2)}, u32[]{:S(2)}) collective-permute-start(f32[4,64,256]{2,1,0:T(8,128)S(1)} %pad_maximum_fusion), channel_id=1, source_target_pairs={{0,1},{1,2},{2,3},{4,5},{5,6},{6,7},{8,9},{9,10},{10,11},{12,13},{... | collective-permute-start | bytes 786440 | tf_op jit(solution)/shard_map/ppermute | solution.py:18
  26.4 0.0 copy-start
  26.4 1.9 %collective-permute-start.6 = (f32[4,64,256]{2,1,0:T(8,128)S(1)}, f32[4,64,256]{2,1,0:T(8,128)S(1)}, u32[]{:S(2)}, u32[]{:S(2)}) collective-permute-start(f32[4,64,256]{2,1,0:T(8,128)S(1)} %pad_maximum_fusion.1), channel_id=1, source_target_pairs={{1,0},{2,1},{3,2},{5,4},{6,5},{7,6},{9,8},{10,9},{11,10},{13,12},{... | collective-permute-start | bytes 786440 | tf_op jit(solution)/shard_map/ppermute | solution.py:18
  28.3 0.2 assemble.1.outer
  28.5 0.0 collective-permute-done.4.refs_3_
  28.6 0.0 copy-done
  28.6 0.0 copy-start.1
  28.6 1.7 %own.1 = (bf16[2,768,256]{2,1,0:T(8,128)(2,1)S(1)}, bf16[4,512,256]{2,1,0:T(8,128)(2,1)S(1)}, bf16[4,512,256]{2,1,0:T(8,128)(2,1)S(1)}) custom-call(s32[8,16]{1,0:T(8,128)S(1)} %copy-done, bf16[2,768,256]{2,1,0:T(8,128)(2,1)S(1)} %assemble.1.outer, f32[2,64,256]{2,1,0:T(8,128)S(1)} %get-tuple-element.39.refs_0_, ...), custom_call_target="tpu_custom_call" | custom-call | flops 3221225472 | bytes 1048576 | tf_op jit(solution)/shard_map/own/pallas_call | solution.py:155
  30.3 0.0 copy-done.1
  30.3 1.1 %first_inner.1 = f32[2,64,256]{2,1,0:T(8,128)S(1)} custom-call(s32[8]{0:T(128)S(1)} %copy-done.1, bf16[4,512,256]{2,1,0:T(8,128)(2,1)S(1)} %get-tuple-element.22.own_high.high, bf16[4,512,256]{2,1,0:T(8,128)(2,1)S(1)} %get-tuple-element.23.own_low.low, bf16[2048,256]{1,0:T(8,128)(2,1)S(1)} %get-tuple-element.24.right_hi, ...), custom_call_target="tpu_custom_call" | custom-call | flops 805306368 | bytes 1048576 | tf_op jit(solution)/shard_map/first_inner/pallas_call | solution.py:155
  31.4 0.6 %collective-permute-start.10 = (f32[2,64,256]{2,1,0:T(8,128)S(1)}, f32[2,64,256]{2,1,0:T(8,128)S(1)}, u32[]{:S(2)}, u32[]{:S(2)}) collective-permute-start(f32[2,64,256]{2,1,0:T(8,128)S(1)} %first_inner.1), channel_id=1, source_target_pairs={{0,4},{4,12},{12,8},{8,0},{1,5},{5,13},{13,9},{9,1},{2,6},{6,14},{... | collective-permute-start | bytes 393224 | tf_op jit(solution)/shard_map/ppermute | solution.py:226
  32.0 0.0 collective-permute-done.5.above
  32.0 2.4 %collective-permute-done.6.below = f32[4,64,256]{2,1,0:T(8,128)S(1)} collective-permute-done((f32[4,64,256]{2,1,0:T(8,128)S(1)}, f32[4,64,256]{2,1,0:T(8,128)S(1)}, u32[]{:S(2)}, u32[]{:S(2)}) %collective-permute-start.6) | collective-permute-done | bytes 262176 | tf_op jit(solution)/shard_map/ppermute | solution.py:18
  34.4 2.4 %first_outer.1 = (f32[2,64,256]{2,1,0:T(8,128)S(1)}, bf16[2,768,256]{2,1,0:T(8,128)(2,1)S(1)}) custom-call(s32[8]{0:T(128)S(1)} %copy-done.1, s32[8,16]{1,0:T(8,128)S(1)} %copy-done, bf16[4,512,256]{2,1,0:T(8,128)(2,1)S(1)} %get-tuple-element.22.own_high.high, bf16[4,512,256]{2,1,0:T(8,128)(2,1)S(1)} %get-tuple-element.23.own_low.low, ...), custom_call_target="tpu_custom_call" | custom-call | flops 1610612736 | bytes 1048576 | tf_op jit(solution)/shard_map/first_outer/pallas_call | solution.py:155
  36.8 0.7 %collective-permute-start.7 = (f32[2,64,256]{2,1,0:T(8,128)S(1)}, f32[2,64,256]{2,1,0:T(8,128)S(1)}, u32[]{:S(2)}, u32[]{:S(2)}) collective-permute-start(f32[2,64,256]{2,1,0:T(8,128)S(1)} %get-tuple-element.26), channel_id=1, source_target_pairs={{0,4},{4,12},{12,8},{8,0},{1,5},{5,13},{13,9},{9,1},{2,6},{6,14},{... | collective-permute-start | bytes 393224 | tf_op jit(solution)/shard_map/ppermute | solution.py:227
  37.6 3.0 %chunk.3 = (f32[2,64,256]{2,1,0:T(8,128)S(1)}, f32[2,64,256]{2,1,0:T(8,128)S(1)}) custom-call(s32[8]{0:T(128)S(1)} %copy-done.1, s32[8,16]{1,0:T(8,128)S(1)} %copy-done, bf16[2,768,256]{2,1,0:T(8,128)(2,1)S(1)} %assemble.1.outer, bf16[2,768,256]{2,1,0:T(8,128)(2,1)S(1)} %get-tuple-element.27.inner, bf16[2,768,256]{2,1,0:T(8,128)(2,1)S(1)} %get-tuple-element.28.outside, ...), custom_call_target="tpu_custom_call" | custom-call | flops 3221225472 | bytes 1048576 | tf_op jit(solution)/shard_map/chunk/pallas_call | solution.py:155
  40.6 0.0 collective-permute-done.10
  40.6 3.0 %collective-permute-start.11 = (f32[2,64,256]{2,1,0:T(8,128)S(1)}, f32[2,64,256]{2,1,0:T(8,128)S(1)}, u32[]{:S(2)}, u32[]{:S(2)}) collective-permute-start(f32[2,64,256]{2,1,0:T(8,128)S(1)} %add.34), channel_id=1, source_target_pairs={{0,4},{4,12},{12,8},{8,0},{1,5},{5,13},{13,9},{9,1},{2,6},{6,14},{... | collective-permute-start | bytes 393224 | tf_op jit(solution)/shard_map/ppermute | solution.py:226
  43.6 0.0 collective-permute-done.7
  43.6 0.2 collective-permute-start.8
  43.8 3.0 %chunk.4 = (f32[2,64,256]{2,1,0:T(8,128)S(1)}, f32[2,64,256]{2,1,0:T(8,128)S(1)}) custom-call(s32[8]{0:T(128)S(1)} %copy-done.1, s32[8,16]{1,0:T(8,128)S(1)} %copy-done, bf16[2,768,256]{2,1,0:T(8,128)(2,1)S(1)} %assemble.1.outer, bf16[2,768,256]{2,1,0:T(8,128)(2,1)S(1)} %get-tuple-element.27.inner, bf16[2,768,256]{2,1,0:T(8,128)(2,1)S(1)} %get-tuple-element.28.outside, ...), custom_call_target="tpu_custom_call" | custom-call | flops 3221225472 | bytes 1048576 | tf_op jit(solution)/shard_map/chunk/pallas_call | solution.py:155
  46.8 0.3 collective-permute-done.11
  47.2 2.9 %collective-permute-start.12 = (f32[2,64,256]{2,1,0:T(8,128)S(1)}, f32[2,64,256]{2,1,0:T(8,128)S(1)}, u32[]{:S(2)}, u32[]{:S(2)}) collective-permute-start(f32[2,64,256]{2,1,0:T(8,128)S(1)} %add.35), channel_id=1, source_target_pairs={{0,4},{4,12},{12,8},{8,0},{1,5},{5,13},{13,9},{9,1},{2,6},{6,14},{... | collective-permute-start | bytes 393224 | tf_op jit(solution)/shard_map/ppermute | solution.py:226
  50.0 0.0 collective-permute-done.8
  50.1 0.1 collective-permute-start.9
  50.2 3.0 %chunk.5 = (f32[2,64,256]{2,1,0:T(8,128)S(1)}, f32[2,64,256]{2,1,0:T(8,128)S(1)}) custom-call(s32[8]{0:T(128)S(1)} %copy-done.1, s32[8,16]{1,0:T(8,128)S(1)} %copy-done, bf16[2,768,256]{2,1,0:T(8,128)(2,1)S(1)} %assemble.1.outer, bf16[2,768,256]{2,1,0:T(8,128)(2,1)S(1)} %get-tuple-element.27.inner, bf16[2,768,256]{2,1,0:T(8,128)(2,1)S(1)} %get-tuple-element.28.outside, ...), custom_call_target="tpu_custom_call" | custom-call | flops 3221225472 | bytes 1048576 | tf_op jit(solution)/shard_map/chunk/pallas_call | solution.py:155
  53.2 0.0 collective-permute-done.12
  53.2 1.6 %collective-permute-done.9 = f32[2,64,256]{2,1,0:T(8,128)S(1)} collective-permute-done((f32[2,64,256]{2,1,0:T(8,128)S(1)}, f32[2,64,256]{2,1,0:T(8,128)S(1)}, u32[]{:S(2)}, u32[]{:S(2)}) %collective-permute-start.9) | collective-permute-done | bytes 131104 | tf_op jit(solution)/shard_map/ppermute | solution.py:227
  54.9 0.7 %pad_maximum_fusion.2 = f32[4,64,256]{2,1,0:T(8,128)} fusion(f32[1,64,256]{2,1,0:T(8,128)S(1)} %get-tuple-element.42, f32[2,64,256]{2,1,0:T(8,128)S(1)} %add.36, f32[1,64,256]{2,1,0:T(8,128)S(1)} %get-tuple-element.41), kind=kLoop, calls=%fused_computation.2 | loop fusion | flops 131072 | bytes 524288 | tf_op jit(solution)/shard_map/concatenate | solution.py:228
  (14 shorter events, 0.2 us)
Async XLA Ops:
  0.0 9.4 %collective-permute-start = (f32[4,64,256]{2,1,0:T(8,128)}, f32[4,64,256]{2,1,0:T(8,128)S(1)}, u32[]{:S(2)}, u32[]{:S(2)}) collective-permute-start(f32[4,64,256]{2,1,0:T(8,128)} %param.5), channel_id=1, source_target_pairs={{0,4},{4,12},{12,8},{8,0},{1,5},{5,13},{13,9},{9,1},{2,6},{6,14},{... | collective-permute-start | bytes 786440 | tf_op jit(solution)/shard_map/ppermute | solution.py:181
  2.1 1.6 %copy-start.2 = (f32[8,256,256]{2,1,0:T(8,128)S(1)}, f32[8,256,256]{2,1,0:T(8,128)}, u32[]{:S(2)}) copy-start(f32[8,256,256]{2,1,0:T(8,128)} %left_ref.1) | copy-start | bytes 6291460
  3.7 1.6 %copy-start.3 = (f32[8,256,256]{2,1,0:T(8,128)S(1)}, f32[8,256,256]{2,1,0:T(8,128)}, u32[]{:S(2)}) copy-start(f32[8,256,256]{2,1,0:T(8,128)} %right_ref.1) | copy-start | bytes 6291460
  5.3 1.1 %copy-start.4 = (f32[4,64,256]{2,1,0:T(8,128)S(1)}, f32[4,64,256]{2,1,0:T(8,128)}, u32[]{:S(2)}) copy-start(f32[4,64,256]{2,1,0:T(8,128)} %param.5) | copy-start | bytes 786436
  9.5 4.8 %collective-permute-start.1 = (f32[2,64,256]{2,1,0:T(8,128)S(1)}, f32[2,64,256]{2,1,0:T(8,128)S(1)}, u32[]{:S(2)}, u32[]{:S(2)}) collective-permute-start(f32[2,64,256]{2,1,0:T(8,128)S(1)} %get-tuple-element.38), channel_id=1, source_target_pairs={{0,4},{4,12},{12,8},{8,0},{1,5},{5,13},{13,9},{9,1},{2,6},{6,14},{... | collective-permute-start | bytes 393224 | tf_op jit(solution)/shard_map/ppermute | solution.py:184
  9.9 7.1 %collective-permute-start.3 = (f32[2,64,256]{2,1,0:T(8,128)S(1)}, f32[2,64,256]{2,1,0:T(8,128)S(1)}, u32[]{:S(2)}, u32[]{:S(2)}) collective-permute-start(f32[2,64,256]{2,1,0:T(8,128)S(1)} %get-tuple-element.35), channel_id=1, source_target_pairs={{0,4},{4,12},{12,8},{8,0},{1,5},{5,13},{13,9},{9,1},{2,6},{6,14},{... | collective-permute-start | bytes 393224 | tf_op jit(solution)/shard_map/ppermute | solution.py:185
  14.2 5.6 %collective-permute-start.2 = (f32[2,64,256]{2,1,0:T(8,128)S(1)}, f32[2,64,256]{2,1,0:T(8,128)S(1)}, u32[]{:S(2)}, u32[]{:S(2)}) collective-permute-start(f32[2,64,256]{2,1,0:T(8,128)S(1)} %collective-permute-done.1.refs_2_), channel_id=1, source_target_pairs={{0,4},{4,12},{12,8},{8,0},{1,5},{5,13},{13,9},{9,1},{2,6},{6,14},{... | collective-permute-start | bytes 393224 | tf_op jit(solution)/shard_map/ppermute | solution.py:184
  17.0 11.6 %collective-permute-start.4 = (f32[2,64,256]{2,1,0:T(8,128)S(1)}, f32[2,64,256]{2,1,0:T(8,128)S(1)}, u32[]{:S(2)}, u32[]{:S(2)}) collective-permute-start(f32[2,64,256]{2,1,0:T(8,128)S(1)} %collective-permute-done.3.refs_2_), channel_id=1, source_target_pairs={{0,4},{4,12},{12,8},{8,0},{1,5},{5,13},{13,9},{9,1},{2,6},{6,14},{... | collective-permute-start | bytes 393224 | tf_op jit(solution)/shard_map/ppermute | solution.py:185
  19.9 12.1 %collective-permute-start.5 = (f32[4,64,256]{2,1,0:T(8,128)S(1)}, f32[4,64,256]{2,1,0:T(8,128)S(1)}, u32[]{:S(2)}, u32[]{:S(2)}) collective-permute-start(f32[4,64,256]{2,1,0:T(8,128)S(1)} %pad_maximum_fusion), channel_id=1, source_target_pairs={{0,1},{1,2},{2,3},{4,5},{5,6},{6,7},{8,9},{9,10},{10,11},{12,13},{... | collective-permute-start | bytes 786440 | tf_op jit(solution)/shard_map/ppermute | solution.py:18
  26.4 2.1 %copy-start = (s32[8,16]{1,0:T(8,128)S(1)}, s32[8,16]{1,0:T(8,128)}, u32[]{:S(2)}) copy-start(s32[8,16]{1,0:T(8,128)} %allowed_ref.9) | copy-start | bytes 1540
  26.4 8.0 %collective-permute-start.6 = (f32[4,64,256]{2,1,0:T(8,128)S(1)}, f32[4,64,256]{2,1,0:T(8,128)S(1)}, u32[]{:S(2)}, u32[]{:S(2)}) collective-permute-start(f32[4,64,256]{2,1,0:T(8,128)S(1)} %pad_maximum_fusion.1), channel_id=1, source_target_pairs={{1,0},{2,1},{3,2},{5,4},{6,5},{7,6},{9,8},{10,9},{11,10},{13,12},{... | collective-permute-start | bytes 786440 | tf_op jit(solution)/shard_map/ppermute | solution.py:18
  28.6 1.7 %copy-start.1 = (s32[8]{0:T(128)S(1)}, s32[8]{0:T(128)}, u32[]{:S(2)}) copy-start(s32[8]{0:T(128)} %shifts_ref.9) | copy-start | bytes 100
  31.4 9.2 %collective-permute-start.10 = (f32[2,64,256]{2,1,0:T(8,128)S(1)}, f32[2,64,256]{2,1,0:T(8,128)S(1)}, u32[]{:S(2)}, u32[]{:S(2)}) collective-permute-start(f32[2,64,256]{2,1,0:T(8,128)S(1)} %first_inner.1), channel_id=1, source_target_pairs={{0,4},{4,12},{12,8},{8,0},{1,5},{5,13},{13,9},{9,1},{2,6},{6,14},{... | collective-permute-start | bytes 393224 | tf_op jit(solution)/shard_map/ppermute | solution.py:226
  36.8 6.8 %collective-permute-start.7 = (f32[2,64,256]{2,1,0:T(8,128)S(1)}, f32[2,64,256]{2,1,0:T(8,128)S(1)}, u32[]{:S(2)}, u32[]{:S(2)}) collective-permute-start(f32[2,64,256]{2,1,0:T(8,128)S(1)} %get-tuple-element.26), channel_id=1, source_target_pairs={{0,4},{4,12},{12,8},{8,0},{1,5},{5,13},{13,9},{9,1},{2,6},{6,14},{... | collective-permute-start | bytes 393224 | tf_op jit(solution)/shard_map/ppermute | solution.py:227
  40.6 6.5 %collective-permute-start.11 = (f32[2,64,256]{2,1,0:T(8,128)S(1)}, f32[2,64,256]{2,1,0:T(8,128)S(1)}, u32[]{:S(2)}, u32[]{:S(2)}) collective-permute-start(f32[2,64,256]{2,1,0:T(8,128)S(1)} %add.34), channel_id=1, source_target_pairs={{0,4},{4,12},{12,8},{8,0},{1,5},{5,13},{13,9},{9,1},{2,6},{6,14},{... | collective-permute-start | bytes 393224 | tf_op jit(solution)/shard_map/ppermute | solution.py:226
  43.6 6.4 %collective-permute-start.8 = (f32[2,64,256]{2,1,0:T(8,128)S(1)}, f32[2,64,256]{2,1,0:T(8,128)S(1)}, u32[]{:S(2)}, u32[]{:S(2)}) collective-permute-start(f32[2,64,256]{2,1,0:T(8,128)S(1)} %add.31), channel_id=1, source_target_pairs={{0,4},{4,12},{12,8},{8,0},{1,5},{5,13},{13,9},{9,1},{2,6},{6,14},{... | collective-permute-start | bytes 393224 | tf_op jit(solution)/shard_map/ppermute | solution.py:227
  47.2 6.1 %collective-permute-start.12 = (f32[2,64,256]{2,1,0:T(8,128)S(1)}, f32[2,64,256]{2,1,0:T(8,128)S(1)}, u32[]{:S(2)}, u32[]{:S(2)}) collective-permute-start(f32[2,64,256]{2,1,0:T(8,128)S(1)} %add.35), channel_id=1, source_target_pairs={{0,4},{4,12},{12,8},{8,0},{1,5},{5,13},{13,9},{9,1},{2,6},{6,14},{... | collective-permute-start | bytes 393224 | tf_op jit(solution)/shard_map/ppermute | solution.py:226
  50.1 4.8 %collective-permute-start.9 = (f32[2,64,256]{2,1,0:T(8,128)S(1)}, f32[2,64,256]{2,1,0:T(8,128)S(1)}, u32[]{:S(2)}, u32[]{:S(2)}) collective-permute-start(f32[2,64,256]{2,1,0:T(8,128)S(1)} %add.32), channel_id=1, source_target_pairs={{0,4},{4,12},{12,8},{8,0},{1,5},{5,13},{13,9},{9,1},{2,6},{6,14},{... | collective-permute-start | bytes 393224 | tf_op jit(solution)/shard_map/ppermute | solution.py:227

commit v18 on v17

--- a/solution.py
+++ b/solution.py
@@ -72,12 +72,15 @@
 
 def first_product(left, parts, allowed_ref, source, high, low):
     kops, sectors = allowed_ref.shape
-    block = jnp.dot(left, parts, preferred_element_type=F32)
-    rows = block.shape[0] // kops
+    rows = left.shape[0] // kops
     source = jnp.clip(source, 0, sectors - 1)
-    for k in range(kops):
-        at = slice(k * rows, (k + 1) * rows)
-        high[at], low[at] = split(block[at] * allowed_ref[k, source].astype(F32))
+    some = max(kops // 2, 1)
+    for start in range(0, kops, some):
+        block = jnp.dot(left[start * rows : (start + some) * rows], parts, preferred_element_type=F32)
+        for k in range(start, min(start + some, kops)):
+            piece = block[(k - start) * rows : (k - start + 1) * rows]
+            at = slice(k * rows, (k + 1) * rows)
+            high[at], low[at] = split(piece * allowed_ref[k, source].astype(F32))
 
 
 def chunk_left(n, step, left_parts):

time: 55.8 us -> 55.8 us (level)
  no operation moved by 1% of the time
where the time goes in v18:
time: 55.8 us; the launch traced here: 55.5 us
  starting transfers between devices  22.7 us (41%)
  Pallas kernels  15.4 us (28%)
  waiting for transfers between devices  12.9 us (23%)
  local copies, waits for them, and re-layouts  3.27 us (6%)
  other arithmetic  0.94 us (2%)
    pallas_call x8, Pallas kernels, call(): pl.pallas_call(body, name=name, out_shape=out_shape, in_specs=in_specs, o...  15.4 us
    ppermute x2, starting transfers between devices, shifted(): return lax.ppermute(block, axis, route)  8.41 us
    ppermute x3, starting transfers between devices, shards(): result_inner = lax.ppermute(result_inner, 'op', route) + next_inner  6.54 us
    ppermute x2, waiting for transfers between devices, shards(): lax.ppermute(outer[-1] + zero[0, 0] if step == 1 else outer[-1], 'op', ro...  3.62 us
    ppermute x2, starting transfers between devices, shards(): lax.ppermute(inner[-1] + zero[0, 0] if step == 1 else inner[-1], 'op', ro...  3.59 us
    unnamed x10, local copies, waits for them, and re-layouts  3.2 us
    ppermute x1, waiting for transfers between devices, shards(): blocks = [psi, lax.ppermute(psi, 'op', route)]  2.94 us
    ppermute x2, waiting for transfers between devices, shifted(): return lax.ppermute(block, axis, route)  2.42 us
  transfers between devices with their start and end apart: 13, of which 7 were waited for; matrix products, arithmetic and copies ran while one was open for 0% of the time, Pallas kernels for 28%

profile of v18, /device:TPU:1, one launch (start us, length us, event | category | flops | bytes accessed | tf_op | source)
XLA Modules:
  0.0 55.5 jit_solution(17239317718711704625)
XLA Ops:
  0.0 2.1 %collective-permute-start = (f32[4,64,256]{2,1,0:T(8,128)}, f32[4,64,256]{2,1,0:T(8,128)S(1)}, u32[]{:S(2)}, u32[]{:S(2)}) collective-permute-start(f32[4,64,256]{2,1,0:T(8,128)} %param.5), channel_id=1, source_target_pairs={{0,4},{4,12},{12,8},{8,0},{1,5},{5,13},{13,9},{9,1},{2,6},{6,14},{... | collective-permute-start | bytes 786440 | tf_op jit(solution)/shard_map/ppermute | solution.py:184
  2.1 0.0 copy-start.2
  2.1 1.6 %copy-done.2 = f32[8,256,256]{2,1,0:T(8,128)S(1)} copy-done((f32[8,256,256]{2,1,0:T(8,128)S(1)}, f32[8,256,256]{2,1,0:T(8,128)}, u32[]{:S(2)}) %copy-start.2) | copy-done | bytes 2097176
  3.7 0.0 copy-start.3
  3.7 1.6 %copy-done.3 = f32[8,256,256]{2,1,0:T(8,128)S(1)} copy-done((f32[8,256,256]{2,1,0:T(8,128)S(1)}, f32[8,256,256]{2,1,0:T(8,128)}, u32[]{:S(2)}) %copy-start.3) | copy-done | bytes 2097176
  5.3 0.0 copy-start.4
  5.3 1.1 %prepare.1 = (bf16[4,8,64,768]{3,2,1,0:T(8,128)(2,1)S(1)}, bf16[2048,256]{1,0:T(8,128)(2,1)S(1)}, bf16[2048,256]{1,0:T(8,128)(2,1)S(1)}, f32[1,128]{1,0:T(1,128)S(1)}) custom-call(f32[8,256,256]{2,1,0:T(8,128)S(1)} %copy-done.2, f32[8,256,256]{2,1,0:T(8,128)S(1)} %copy-done.3), custom_call_target="tpu_custom_call" | custom-call | flops 3221225472 | bytes 1048576 | tf_op jit(solution)/shard_map/prepare/pallas_call | solution.py:158
  6.4 0.0 copy-done.4
  6.4 2.9 %collective-permute-done = f32[4,64,256]{2,1,0:T(8,128)S(1)} collective-permute-done((f32[4,64,256]{2,1,0:T(8,128)}, f32[4,64,256]{2,1,0:T(8,128)S(1)}, u32[]{:S(2)}, u32[]{:S(2)}) %collective-permute-start) | collective-permute-done | bytes 262176 | tf_op jit(solution)/shard_map/ppermute | solution.py:184
  9.4 0.1 broadcast_add_fusion
  9.5 0.4 collective-permute-start.1
  9.9 3.0 %collective-permute-start.3 = (f32[2,64,256]{2,1,0:T(8,128)S(1)}, f32[2,64,256]{2,1,0:T(8,128)S(1)}, u32[]{:S(2)}, u32[]{:S(2)}) collective-permute-start(f32[2,64,256]{2,1,0:T(8,128)S(1)} %get-tuple-element.35), channel_id=1, source_target_pairs={{0,4},{4,12},{12,8},{8,0},{1,5},{5,13},{13,9},{9,1},{2,6},{6,14},{... | collective-permute-start | bytes 393224 | tf_op jit(solution)/shard_map/ppermute | solution.py:188
  12.9 1.4 %collective-permute-done.1.refs_2_ = f32[2,64,256]{2,1,0:T(8,128)S(1)} collective-permute-done((f32[2,64,256]{2,1,0:T(8,128)S(1)}, f32[2,64,256]{2,1,0:T(8,128)S(1)}, u32[]{:S(2)}, u32[]{:S(2)}) %collective-permute-start.1) | collective-permute-done | bytes 131104 | tf_op jit(solution)/shard_map/ppermute | solution.py:187
  14.2 0.6 %collective-permute-start.2 = (f32[2,64,256]{2,1,0:T(8,128)S(1)}, f32[2,64,256]{2,1,0:T(8,128)S(1)}, u32[]{:S(2)}, u32[]{:S(2)}) collective-permute-start(f32[2,64,256]{2,1,0:T(8,128)S(1)} %collective-permute-done.1.refs_2_), channel_id=1, source_target_pairs={{0,4},{4,12},{12,8},{8,0},{1,5},{5,13},{13,9},{9,1},{2,6},{6,14},{... | collective-permute-start | bytes 393224 | tf_op jit(solution)/shard_map/ppermute | solution.py:187
  14.8 2.2 %collective-permute-done.3.refs_2_ = f32[2,64,256]{2,1,0:T(8,128)S(1)} collective-permute-done((f32[2,64,256]{2,1,0:T(8,128)S(1)}, f32[2,64,256]{2,1,0:T(8,128)S(1)}, u32[]{:S(2)}, u32[]{:S(2)}) %collective-permute-start.3) | collective-permute-done | bytes 131104 | tf_op jit(solution)/shard_map/ppermute | solution.py:188
  17.0 0.6 %collective-permute-start.4 = (f32[2,64,256]{2,1,0:T(8,128)S(1)}, f32[2,64,256]{2,1,0:T(8,128)S(1)}, u32[]{:S(2)}, u32[]{:S(2)}) collective-permute-start(f32[2,64,256]{2,1,0:T(8,128)S(1)} %collective-permute-done.3.refs_2_), channel_id=1, source_target_pairs={{0,4},{4,12},{12,8},{8,0},{1,5},{5,13},{13,9},{9,1},{2,6},{6,14},{... | collective-permute-start | bytes 393224 | tf_op jit(solution)/shard_map/ppermute | solution.py:188
  17.6 2.3 %collective-permute-done.2.refs_3_ = f32[2,64,256]{2,1,0:T(8,128)S(1)} collective-permute-done((f32[2,64,256]{2,1,0:T(8,128)S(1)}, f32[2,64,256]{2,1,0:T(8,128)S(1)}, u32[]{:S(2)}, u32[]{:S(2)}) %collective-permute-start.2) | collective-permute-done | bytes 131104 | tf_op jit(solution)/shard_map/ppermute | solution.py:187
  19.9 6.5 %collective-permute-start.5 = (f32[4,64,256]{2,1,0:T(8,128)S(1)}, f32[4,64,256]{2,1,0:T(8,128)S(1)}, u32[]{:S(2)}, u32[]{:S(2)}) collective-permute-start(f32[4,64,256]{2,1,0:T(8,128)S(1)} %pad_maximum_fusion), channel_id=1, source_target_pairs={{0,1},{1,2},{2,3},{4,5},{5,6},{6,7},{8,9},{9,10},{10,11},{12,13},{... | collective-permute-start | bytes 786440 | tf_op jit(solution)/shard_map/ppermute | solution.py:18
  26.4 0.0 copy-start
  26.4 1.9 %collective-permute-start.6 = (f32[4,64,256]{2,1,0:T(8,128)S(1)}, f32[4,64,256]{2,1,0:T(8,128)S(1)}, u32[]{:S(2)}, u32[]{:S(2)}) collective-permute-start(f32[4,64,256]{2,1,0:T(8,128)S(1)} %pad_maximum_fusion.1), channel_id=1, source_target_pairs={{1,0},{2,1},{3,2},{5,4},{6,5},{7,6},{9,8},{10,9},{11,10},{13,12},{... | collective-permute-start | bytes 786440 | tf_op jit(solution)/shard_map/ppermute | solution.py:18
  28.3 0.2 assemble.1.outer
  28.5 0.0 collective-permute-done.4.refs_3_
  28.6 0.0 copy-done
  28.6 0.0 copy-start.1
  28.6 1.7 %own.1 = (bf16[2,768,256]{2,1,0:T(8,128)(2,1)S(1)}, bf16[4,512,256]{2,1,0:T(8,128)(2,1)S(1)}, bf16[4,512,256]{2,1,0:T(8,128)(2,1)S(1)}) custom-call(s32[8,16]{1,0:T(8,128)S(1)} %copy-done, bf16[2,768,256]{2,1,0:T(8,128)(2,1)S(1)} %assemble.1.outer, f32[2,64,256]{2,1,0:T(8,128)S(1)} %get-tuple-element.39.refs_0_, ...), custom_call_target="tpu_custom_call" | custom-call | flops 3221225472 | bytes 1048576 | tf_op jit(solution)/shard_map/own/pallas_call | solution.py:158
  30.3 0.0 copy-done.1
  30.3 1.1 %first_inner.1 = f32[2,64,256]{2,1,0:T(8,128)S(1)} custom-call(s32[8]{0:T(128)S(1)} %copy-done.1, bf16[4,512,256]{2,1,0:T(8,128)(2,1)S(1)} %get-tuple-element.22.own_high.high, bf16[4,512,256]{2,1,0:T(8,128)(2,1)S(1)} %get-tuple-element.23.own_low.low, bf16[2048,256]{1,0:T(8,128)(2,1)S(1)} %get-tuple-element.24.right_hi, ...), custom_call_target="tpu_custom_call" | custom-call | flops 805306368 | bytes 1048576 | tf_op jit(solution)/shard_map/first_inner/pallas_call | solution.py:158
  31.4 0.6 %collective-permute-start.10 = (f32[2,64,256]{2,1,0:T(8,128)S(1)}, f32[2,64,256]{2,1,0:T(8,128)S(1)}, u32[]{:S(2)}, u32[]{:S(2)}) collective-permute-start(f32[2,64,256]{2,1,0:T(8,128)S(1)} %first_inner.1), channel_id=1, source_target_pairs={{0,4},{4,12},{12,8},{8,0},{1,5},{5,13},{13,9},{9,1},{2,6},{6,14},{... | collective-permute-start | bytes 393224 | tf_op jit(solution)/shard_map/ppermute | solution.py:229
  32.0 0.0 collective-permute-done.5.above
  32.0 2.4 %collective-permute-done.6.below = f32[4,64,256]{2,1,0:T(8,128)S(1)} collective-permute-done((f32[4,64,256]{2,1,0:T(8,128)S(1)}, f32[4,64,256]{2,1,0:T(8,128)S(1)}, u32[]{:S(2)}, u32[]{:S(2)}) %collective-permute-start.6) | collective-permute-done | bytes 262176 | tf_op jit(solution)/shard_map/ppermute | solution.py:18
  34.4 2.4 %first_outer.1 = (f32[2,64,256]{2,1,0:T(8,128)S(1)}, bf16[2,768,256]{2,1,0:T(8,128)(2,1)S(1)}) custom-call(s32[8]{0:T(128)S(1)} %copy-done.1, s32[8,16]{1,0:T(8,128)S(1)} %copy-done, bf16[4,512,256]{2,1,0:T(8,128)(2,1)S(1)} %get-tuple-element.22.own_high.high, bf16[4,512,256]{2,1,0:T(8,128)(2,1)S(1)} %get-tuple-element.23.own_low.low, ...), custom_call_target="tpu_custom_call" | custom-call | flops 1610612736 | bytes 1048576 | tf_op jit(solution)/shard_map/first_outer/pallas_call | solution.py:158
  36.8 0.7 %collective-permute-start.7 = (f32[2,64,256]{2,1,0:T(8,128)S(1)}, f32[2,64,256]{2,1,0:T(8,128)S(1)}, u32[]{:S(2)}, u32[]{:S(2)}) collective-permute-start(f32[2,64,256]{2,1,0:T(8,128)S(1)} %get-tuple-element.26), channel_id=1, source_target_pairs={{0,4},{4,12},{12,8},{8,0},{1,5},{5,13},{13,9},{9,1},{2,6},{6,14},{... | collective-permute-start | bytes 393224 | tf_op jit(solution)/shard_map/ppermute | solution.py:230
  37.5 3.0 %chunk.3 = (f32[2,64,256]{2,1,0:T(8,128)S(1)}, f32[2,64,256]{2,1,0:T(8,128)S(1)}) custom-call(s32[8]{0:T(128)S(1)} %copy-done.1, s32[8,16]{1,0:T(8,128)S(1)} %copy-done, bf16[2,768,256]{2,1,0:T(8,128)(2,1)S(1)} %assemble.1.outer, bf16[2,768,256]{2,1,0:T(8,128)(2,1)S(1)} %get-tuple-element.27.inner, bf16[2,768,256]{2,1,0:T(8,128)(2,1)S(1)} %get-tuple-element.28.outside, ...), custom_call_target="tpu_custom_call" | custom-call | flops 3221225472 | bytes 1048576 | tf_op jit(solution)/shard_map/chunk/pallas_call | solution.py:158
  40.5 0.0 collective-permute-done.10
  40.5 3.0 %collective-permute-start.11 = (f32[2,64,256]{2,1,0:T(8,128)S(1)}, f32[2,64,256]{2,1,0:T(8,128)S(1)}, u32[]{:S(2)}, u32[]{:S(2)}) collective-permute-start(f32[2,64,256]{2,1,0:T(8,128)S(1)} %add.34), channel_id=1, source_target_pairs={{0,4},{4,12},{12,8},{8,0},{1,5},{5,13},{13,9},{9,1},{2,6},{6,14},{... | collective-permute-start | bytes 393224 | tf_op jit(solution)/shard_map/ppermute | solution.py:229
  43.6 0.0 collective-permute-done.7
  43.6 0.2 collective-permute-start.8
  43.8 3.0 %chunk.4 = (f32[2,64,256]{2,1,0:T(8,128)S(1)}, f32[2,64,256]{2,1,0:T(8,128)S(1)}) custom-call(s32[8]{0:T(128)S(1)} %copy-done.1, s32[8,16]{1,0:T(8,128)S(1)} %copy-done, bf16[2,768,256]{2,1,0:T(8,128)(2,1)S(1)} %assemble.1.outer, bf16[2,768,256]{2,1,0:T(8,128)(2,1)S(1)} %get-tuple-element.27.inner, bf16[2,768,256]{2,1,0:T(8,128)(2,1)S(1)} %get-tuple-element.28.outside, ...), custom_call_target="tpu_custom_call" | custom-call | flops 3221225472 | bytes 1048576 | tf_op jit(solution)/shard_map/chunk/pallas_call | solution.py:158
  46.8 0.2 collective-permute-done.11
  47.1 2.9 %collective-permute-start.12 = (f32[2,64,256]{2,1,0:T(8,128)S(1)}, f32[2,64,256]{2,1,0:T(8,128)S(1)}, u32[]{:S(2)}, u32[]{:S(2)}) collective-permute-start(f32[2,64,256]{2,1,0:T(8,128)S(1)} %add.35), channel_id=1, source_target_pairs={{0,4},{4,12},{12,8},{8,0},{1,5},{5,13},{13,9},{9,1},{2,6},{6,14},{... | collective-permute-start | bytes 393224 | tf_op jit(solution)/shard_map/ppermute | solution.py:229
  50.0 0.0 collective-permute-done.8
  50.0 0.2 collective-permute-start.9
  50.2 3.0 %chunk.5 = (f32[2,64,256]{2,1,0:T(8,128)S(1)}, f32[2,64,256]{2,1,0:T(8,128)S(1)}) custom-call(s32[8]{0:T(128)S(1)} %copy-done.1, s32[8,16]{1,0:T(8,128)S(1)} %copy-done, bf16[2,768,256]{2,1,0:T(8,128)(2,1)S(1)} %assemble.1.outer, bf16[2,768,256]{2,1,0:T(8,128)(2,1)S(1)} %get-tuple-element.27.inner, bf16[2,768,256]{2,1,0:T(8,128)(2,1)S(1)} %get-tuple-element.28.outside, ...), custom_call_target="tpu_custom_call" | custom-call | flops 3221225472 | bytes 1048576 | tf_op jit(solution)/shard_map/chunk/pallas_call | solution.py:158
  53.2 0.0 collective-permute-done.12
  53.3 1.5 %collective-permute-done.9 = f32[2,64,256]{2,1,0:T(8,128)S(1)} collective-permute-done((f32[2,64,256]{2,1,0:T(8,128)S(1)}, f32[2,64,256]{2,1,0:T(8,128)S(1)}, u32[]{:S(2)}, u32[]{:S(2)}) %collective-permute-start.9) | collective-permute-done | bytes 131104 | tf_op jit(solution)/shard_map/ppermute | solution.py:230
  54.8 0.7 %pad_maximum_fusion.2 = f32[4,64,256]{2,1,0:T(8,128)} fusion(f32[1,64,256]{2,1,0:T(8,128)S(1)} %get-tuple-element.42, f32[2,64,256]{2,1,0:T(8,128)S(1)} %add.36, f32[1,64,256]{2,1,0:T(8,128)S(1)} %get-tuple-element.41), kind=kLoop, calls=%fused_computation.2 | loop fusion | flops 131072 | bytes 524288 | tf_op jit(solution)/shard_map/concatenate | solution.py:231
  (14 shorter events, 0.2 us)
Async XLA Ops:
  0.0 9.4 %collective-permute-start = (f32[4,64,256]{2,1,0:T(8,128)}, f32[4,64,256]{2,1,0:T(8,128)S(1)}, u32[]{:S(2)}, u32[]{:S(2)}) collective-permute-start(f32[4,64,256]{2,1,0:T(8,128)} %param.5), channel_id=1, source_target_pairs={{0,4},{4,12},{12,8},{8,0},{1,5},{5,13},{13,9},{9,1},{2,6},{6,14},{... | collective-permute-start | bytes 786440 | tf_op jit(solution)/shard_map/ppermute | solution.py:184
  2.1 1.6 %copy-start.2 = (f32[8,256,256]{2,1,0:T(8,128)S(1)}, f32[8,256,256]{2,1,0:T(8,128)}, u32[]{:S(2)}) copy-start(f32[8,256,256]{2,1,0:T(8,128)} %left_ref.1) | copy-start | bytes 6291460
  3.7 1.6 %copy-start.3 = (f32[8,256,256]{2,1,0:T(8,128)S(1)}, f32[8,256,256]{2,1,0:T(8,128)}, u32[]{:S(2)}) copy-start(f32[8,256,256]{2,1,0:T(8,128)} %right_ref.1) | copy-start | bytes 6291460
  5.3 1.1 %copy-start.4 = (f32[4,64,256]{2,1,0:T(8,128)S(1)}, f32[4,64,256]{2,1,0:T(8,128)}, u32[]{:S(2)}) copy-start(f32[4,64,256]{2,1,0:T(8,128)} %param.5) | copy-start | bytes 786436
  9.5 4.8 %collective-permute-start.1 = (f32[2,64,256]{2,1,0:T(8,128)S(1)}, f32[2,64,256]{2,1,0:T(8,128)S(1)}, u32[]{:S(2)}, u32[]{:S(2)}) collective-permute-start(f32[2,64,256]{2,1,0:T(8,128)S(1)} %get-tuple-element.38), channel_id=1, source_target_pairs={{0,4},{4,12},{12,8},{8,0},{1,5},{5,13},{13,9},{9,1},{2,6},{6,14},{... | collective-permute-start | bytes 393224 | tf_op jit(solution)/shard_map/ppermute | solution.py:187
  9.9 7.1 %collective-permute-start.3 = (f32[2,64,256]{2,1,0:T(8,128)S(1)}, f32[2,64,256]{2,1,0:T(8,128)S(1)}, u32[]{:S(2)}, u32[]{:S(2)}) collective-permute-start(f32[2,64,256]{2,1,0:T(8,128)S(1)} %get-tuple-element.35), channel_id=1, source_target_pairs={{0,4},{4,12},{12,8},{8,0},{1,5},{5,13},{13,9},{9,1},{2,6},{6,14},{... | collective-permute-start | bytes 393224 | tf_op jit(solution)/shard_map/ppermute | solution.py:188
  14.2 5.6 %collective-permute-start.2 = (f32[2,64,256]{2,1,0:T(8,128)S(1)}, f32[2,64,256]{2,1,0:T(8,128)S(1)}, u32[]{:S(2)}, u32[]{:S(2)}) collective-permute-start(f32[2,64,256]{2,1,0:T(8,128)S(1)} %collective-permute-done.1.refs_2_), channel_id=1, source_target_pairs={{0,4},{4,12},{12,8},{8,0},{1,5},{5,13},{13,9},{9,1},{2,6},{6,14},{... | collective-permute-start | bytes 393224 | tf_op jit(solution)/shard_map/ppermute | solution.py:187
  17.0 11.6 %collective-permute-start.4 = (f32[2,64,256]{2,1,0:T(8,128)S(1)}, f32[2,64,256]{2,1,0:T(8,128)S(1)}, u32[]{:S(2)}, u32[]{:S(2)}) collective-permute-start(f32[2,64,256]{2,1,0:T(8,128)S(1)} %collective-permute-done.3.refs_2_), channel_id=1, source_target_pairs={{0,4},{4,12},{12,8},{8,0},{1,5},{5,13},{13,9},{9,1},{2,6},{6,14},{... | collective-permute-start | bytes 393224 | tf_op jit(solution)/shard_map/ppermute | solution.py:188
  19.9 12.1 %collective-permute-start.5 = (f32[4,64,256]{2,1,0:T(8,128)S(1)}, f32[4,64,256]{2,1,0:T(8,128)S(1)}, u32[]{:S(2)}, u32[]{:S(2)}) collective-permute-start(f32[4,64,256]{2,1,0:T(8,128)S(1)} %pad_maximum_fusion), channel_id=1, source_target_pairs={{0,1},{1,2},{2,3},{4,5},{5,6},{6,7},{8,9},{9,10},{10,11},{12,13},{... | collective-permute-start | bytes 786440 | tf_op jit(solution)/shard_map/ppermute | solution.py:18
  26.4 2.1 %copy-start = (s32[8,16]{1,0:T(8,128)S(1)}, s32[8,16]{1,0:T(8,128)}, u32[]{:S(2)}) copy-start(s32[8,16]{1,0:T(8,128)} %allowed_ref.9) | copy-start | bytes 1540
  26.4 8.0 %collective-permute-start.6 = (f32[4,64,256]{2,1,0:T(8,128)S(1)}, f32[4,64,256]{2,1,0:T(8,128)S(1)}, u32[]{:S(2)}, u32[]{:S(2)}) collective-permute-start(f32[4,64,256]{2,1,0:T(8,128)S(1)} %pad_maximum_fusion.1), channel_id=1, source_target_pairs={{1,0},{2,1},{3,2},{5,4},{6,5},{7,6},{9,8},{10,9},{11,10},{13,12},{... | collective-permute-start | bytes 786440 | tf_op jit(solution)/shard_map/ppermute | solution.py:18
  28.6 1.7 %copy-start.1 = (s32[8]{0:T(128)S(1)}, s32[8]{0:T(128)}, u32[]{:S(2)}) copy-start(s32[8]{0:T(128)} %shifts_ref.9) | copy-start | bytes 100
  31.4 9.1 %collective-permute-start.10 = (f32[2,64,256]{2,1,0:T(8,128)S(1)}, f32[2,64,256]{2,1,0:T(8,128)S(1)}, u32[]{:S(2)}, u32[]{:S(2)}) collective-permute-start(f32[2,64,256]{2,1,0:T(8,128)S(1)} %first_inner.1), channel_id=1, source_target_pairs={{0,4},{4,12},{12,8},{8,0},{1,5},{5,13},{13,9},{9,1},{2,6},{6,14},{... | collective-permute-start | bytes 393224 | tf_op jit(solution)/shard_map/ppermute | solution.py:229
  36.8 6.8 %collective-permute-start.7 = (f32[2,64,256]{2,1,0:T(8,128)S(1)}, f32[2,64,256]{2,1,0:T(8,128)S(1)}, u32[]{:S(2)}, u32[]{:S(2)}) collective-permute-start(f32[2,64,256]{2,1,0:T(8,128)S(1)} %get-tuple-element.26), channel_id=1, source_target_pairs={{0,4},{4,12},{12,8},{8,0},{1,5},{5,13},{13,9},{9,1},{2,6},{6,14},{... | collective-permute-start | bytes 393224 | tf_op jit(solution)/shard_map/ppermute | solution.py:230
  40.5 6.5 %collective-permute-start.11 = (f32[2,64,256]{2,1,0:T(8,128)S(1)}, f32[2,64,256]{2,1,0:T(8,128)S(1)}, u32[]{:S(2)}, u32[]{:S(2)}) collective-permute-start(f32[2,64,256]{2,1,0:T(8,128)S(1)} %add.34), channel_id=1, source_target_pairs={{0,4},{4,12},{12,8},{8,0},{1,5},{5,13},{13,9},{9,1},{2,6},{6,14},{... | collective-permute-start | bytes 393224 | tf_op jit(solution)/shard_map/ppermute | solution.py:229
  43.6 6.4 %collective-permute-start.8 = (f32[2,64,256]{2,1,0:T(8,128)S(1)}, f32[2,64,256]{2,1,0:T(8,128)S(1)}, u32[]{:S(2)}, u32[]{:S(2)}) collective-permute-start(f32[2,64,256]{2,1,0:T(8,128)S(1)} %add.31), channel_id=1, source_target_pairs={{0,4},{4,12},{12,8},{8,0},{1,5},{5,13},{13,9},{9,1},{2,6},{6,14},{... | collective-permute-start | bytes 393224 | tf_op jit(solution)/shard_map/ppermute | solution.py:230
  47.1 6.2 %collective-permute-start.12 = (f32[2,64,256]{2,1,0:T(8,128)S(1)}, f32[2,64,256]{2,1,0:T(8,128)S(1)}, u32[]{:S(2)}, u32[]{:S(2)}) collective-permute-start(f32[2,64,256]{2,1,0:T(8,128)S(1)} %add.35), channel_id=1, source_target_pairs={{0,4},{4,12},{12,8},{8,0},{1,5},{5,13},{13,9},{9,1},{2,6},{6,14},{... | collective-permute-start | bytes 393224 | tf_op jit(solution)/shard_map/ppermute | solution.py:229
  50.0 4.8 %collective-permute-start.9 = (f32[2,64,256]{2,1,0:T(8,128)S(1)}, f32[2,64,256]{2,1,0:T(8,128)S(1)}, u32[]{:S(2)}, u32[]{:S(2)}) collective-permute-start(f32[2,64,256]{2,1,0:T(8,128)S(1)} %add.32), channel_id=1, source_target_pairs={{0,4},{4,12},{12,8},{8,0},{1,5},{5,13},{13,9},{9,1},{2,6},{6,14},{... | collective-permute-start | bytes 393224 | tf_op jit(solution)/shard_map/ppermute | solution.py:230

commit v19 on v15

--- a/solution.py
+++ b/solution.py
@@ -12,10 +12,14 @@
 VMEM = pl.BlockSpec(memory_space=pltpu.VMEM)
 
 
-def shifted(block, axis, distance):
-    devices = range(lax.axis_size(axis))
-    route = [(i - distance, i) for i in devices if i - distance in devices]
-    return lax.ppermute(block, axis, route)
+def sector_group():
+    return lax.axis_index(("sec", "sub"))
+
+
+def swapped(block, odd):
+    groups = lax.axis_size(("sec", "sub"))
+    pairs = [(i, i + 1) for i in range(odd, groups - 1, 2)]
+    return lax.ppermute(block, ("sec", "sub"), pairs + [(j, i) for i, j in pairs])
 
 
 def ring_route(n):
@@ -89,7 +93,7 @@
     assemble(n, *refs[:n], inner, psi)
     left = chunk_left(n, 0, left_parts)
     nloc = high.shape[0]
-    first = lax.axis_index(("sec", "sub")) * nloc
+    first = sector_group() * nloc
     sources = [outer.at[0], *[inner.at[i] for i in range(nloc - 2)], outer.at[1]]
     for i, ref in enumerate(sources):
         first_product(left, ref[...], allowed_ref, first + i, high.at[i], low.at[i])
@@ -108,12 +112,13 @@
     out[...] = dot3((left(high), left(low)), (right_hi[...], right_lo[...])).reshape(out.shape)
 
 
-def first_chunk(n, nloc, shifts_ref, allowed_ref, own_high, own_low, above, below, left_parts, right_hi, right_lo, *refs):
+def first_chunk(n, nloc, shifts_ref, allowed_ref, own_high, own_low, paired, apart, left_parts, right_hi, right_lo, *refs):
     outer_out, inner_out, outside, end_high, end_low, psi = refs
-    place_rows(n, psi.at[0], [above[j] for j in range(n)])
-    place_rows(n, psi.at[1], [below[j] for j in range(n)])
+    odd = lax.rem(sector_group(), 2)
+    place_rows(n, psi.at[odd], [apart[j] for j in range(n)])
+    place_rows(n, psi.at[1 - odd], [paired[j] for j in range(n)])
     left = chunk_left(n, 0, left_parts)
-    first = lax.axis_index(("sec", "sub")) * nloc
+    first = sector_group() * nloc
     for i in range(2):
         outside[i] = stacked(psi[i])
         first_product(left, outside[i], allowed_ref, first - 1 + i * (nloc + 1), end_high.at[i], end_low.at[i])
@@ -135,7 +140,7 @@
 def later_chunk(n, nloc, step, shifts_ref, allowed_ref, outer, inner, outside, left_parts, right_hi, right_lo, *refs):
     outer_out, inner_out, high, low = refs[-4:]
     left = chunk_left(n, step, left_parts)
-    first = lax.axis_index(("sec", "sub")) * nloc
+    first = sector_group() * nloc
     sources = [outside.at[0], outer.at[0], *[inner.at[i] for i in range(nloc - 2)], outer.at[1], outside.at[1]]
     for i, ref in enumerate(sources):
         first_product(left, ref[...], allowed_ref, first - 1 + i, high.at[i], low.at[i])
@@ -183,8 +188,10 @@
         outer.append(lax.ppermute(outer[-1] + zero[0, 0] if step == 1 else outer[-1], "op", route))
         inner.append(lax.ppermute(inner[-1] + zero[0, 0] if step == 1 else inner[-1], "op", route))
 
-    above = shifted(jnp.concatenate([b[1:] for b in outer]), ("sec", "sub"), 1)
-    below = shifted(jnp.concatenate([b[:1] for b in outer]), ("sec", "sub"), -1)
+    even = lax.rem(sector_group(), 2) == 0
+    first_sector, last_sector = jnp.concatenate([b[:1] for b in outer]), jnp.concatenate([b[1:] for b in outer])
+    apart = swapped(jnp.where(even, first_sector, last_sector), 1)
+    paired = swapped(jnp.where(even, last_sector, first_sector), 0)
 
     def split_parts(sectors):
         return jax.ShapeDtypeStruct((sectors, 3 * width, width), BF16)
@@ -204,7 +211,7 @@
     )
     result_outer, result_inner, parts_outside = call(
         functools.partial(first_chunk, n, nloc), "first_chunk", 2 * kops * one, [chunk, chunk_inner, split_parts(2)],
-        [SMEM] * 2 + [VMEM] * 7, [shifts, allowed, *own, above, below, left_parts, right_hi, right_lo],
+        [SMEM] * 2 + [VMEM] * 7, [shifts, allowed, *own, paired, apart, left_parts, right_hi, right_lo],
         [pltpu.VMEM((2, kops * rows, width), BF16)] * 2 + whole(2),
     )
 

time: 57.8 us -> 57.7 us (level)
  the two profiles are of different devices: /device:TPU:2 before, /device:TPU:1 now
where the time goes in v19:
time: 57.7 us; the launch traced here: 57.1 us
  starting transfers between devices  20.8 us (36%)
  Pallas kernels  14.2 us (25%)
  waiting for transfers between devices  14.2 us (25%)
  local copies, waits for them, and re-layouts  5.6 us (10%)
  other arithmetic  1.94 us (3%)
    pallas_call x7, Pallas kernels, call(): pl.pallas_call(body, name=name, out_shape=out_shape, in_specs=in_specs, o...  14.2 us
    ppermute x2, starting transfers between devices, swapped(): lax.ppermute(block, ('sec', 'sub'), pairs + [(j, i) for i, j in pairs])  6.73 us
    ppermute x3, waiting for transfers between devices, shards(): lax.ppermute(result_outer, 'op', route)  5.66 us
    unnamed x18, local copies, waits for them, and re-layouts  5.53 us
    ppermute x3, starting transfers between devices, shards(): lax.ppermute(result_outer, 'op', route)  5.26 us
    ppermute x2, waiting for transfers between devices, shards(): lax.ppermute(outer[-1] + zero[0, 0] if step == 1 else outer[-1], 'op', ro...  3.62 us
    ppermute x2, starting transfers between devices, shards(): lax.ppermute(inner[-1] + zero[0, 0] if step == 1 else inner[-1], 'op', ro...  2.71 us
    ppermute x2, waiting for transfers between devices, shards(): lax.ppermute(inner[-1] + zero[0, 0] if step == 1 else inner[-1], 'op', ro...  2.18 us
  transfers between devices with their start and end apart: 13, of which 8 were waited for; matrix products, arithmetic and copies ran while one was open for 0% of the time, Pallas kernels for 21%

profile of v19, /device:TPU:1, one launch (start us, length us, event | category | flops | bytes accessed | tf_op | source)
XLA Modules:
  0.0 57.1 jit_solution(12979879684981173729)
XLA Ops:
  0.0 2.1 %collective-permute-start = (f32[4,64,256]{2,1,0:T(8,128)}, f32[4,64,256]{2,1,0:T(8,128)}, u32[]{:S(2)}, u32[]{:S(2)}) collective-permute-start(f32[4,64,256]{2,1,0:T(8,128)} %param.5), channel_id=1, source_target_pairs={{0,4},{4,12},{12,8},{8,0},{1,5},{5,13},{13,9},{9,1},{2,6},{6,14},{... | collective-permute-start | bytes 786440 | tf_op jit(solution)/shard_map/ppermute | solution.py:185
  2.1 0.0 copy-start.6
  2.1 1.6 %copy-done.6 = f32[8,256,256]{2,1,0:T(8,128)S(1)} copy-done((f32[8,256,256]{2,1,0:T(8,128)S(1)}, f32[8,256,256]{2,1,0:T(8,128)}, u32[]{:S(2)}) %copy-start.6) | copy-done | bytes 2097176
  3.7 0.0 copy-start.7
  3.7 1.6 %copy-done.7 = f32[8,256,256]{2,1,0:T(8,128)S(1)} copy-done((f32[8,256,256]{2,1,0:T(8,128)S(1)}, f32[8,256,256]{2,1,0:T(8,128)}, u32[]{:S(2)}) %copy-start.7) | copy-done | bytes 2097176
  5.3 1.1 %prepare.1 = (bf16[4,8,64,768]{3,2,1,0:T(8,128)(2,1)S(1)}, bf16[2048,256]{1,0:T(8,128)(2,1)S(1)}, bf16[2048,256]{1,0:T(8,128)(2,1)S(1)}, f32[1,128]{1,0:T(1,128)S(1)}) custom-call(f32[8,256,256]{2,1,0:T(8,128)S(1)} %copy-done.6, f32[8,256,256]{2,1,0:T(8,128)S(1)} %copy-done.7), custom_call_target="tpu_custom_call" | custom-call | flops 3221225472 | bytes 1048576 | tf_op jit(solution)/shard_map/prepare/pallas_call | solution.py:159
  6.4 0.0 copy-start
  6.4 1.0 %copy-done = bf16[2048,256]{1,0:T(8,128)(2,1)} copy-done((bf16[2048,256]{1,0:T(8,128)(2,1)}, bf16[2048,256]{1,0:T(8,128)(2,1)S(1)}, u32[]{:S(2)}) %copy-start) | copy-done | bytes 1048600
  7.4 1.0 %copy-done.2 = bf16[2048,256]{1,0:T(8,128)(2,1)} copy-done((bf16[2048,256]{1,0:T(8,128)(2,1)}, bf16[2048,256]{1,0:T(8,128)(2,1)S(1)}, u32[]{:S(2)}) %copy-start.2) | copy-done | bytes 1048600
  8.3 0.0 copy-done.8
  8.4 1.1 %collective-permute-done = f32[4,64,256]{2,1,0:T(8,128)} collective-permute-done((f32[4,64,256]{2,1,0:T(8,128)}, f32[4,64,256]{2,1,0:T(8,128)}, u32[]{:S(2)}, u32[]{:S(2)}) %collective-permute-start) | collective-permute-done | bytes 262176 | tf_op jit(solution)/shard_map/ppermute | solution.py:185
  9.5 1.0 %broadcast_add_fusion.1 = (f32[2,64,256]{2,1,0:T(8,128)S(1)}, f32[2,64,256]{2,1,0:T(8,128)S(1)}, f32[2,64,256]{2,1,0:T(8,128)S(1)}, f32[2,64,256]{2,1,0:T(8,128)S(1)}) fusion(f32[]{:T(128)S(1)} %bitcast.4, f32[4,64,256]{2,1,0:T(8,128)} %collective-permute-done), kind=kLoop, calls=%fused_computation.7 | loop fusion | flops 65536 | bytes 786436 | tf_op jit(solution)/shard_map/add | solution.py:188
  10.5 1.3 %collective-permute-start.3 = (f32[2,64,256]{2,1,0:T(8,128)S(1)}, f32[2,64,256]{2,1,0:T(8,128)S(1)}, u32[]{:S(2)}, u32[]{:S(2)}) collective-permute-start(f32[2,64,256]{2,1,0:T(8,128)S(1)} %get-tuple-element.39), channel_id=1, source_target_pairs={{0,4},{4,12},{12,8},{8,0},{1,5},{5,13},{13,9},{9,1},{2,6},{6,14},{... | collective-permute-start | bytes 393224 | tf_op jit(solution)/shard_map/ppermute | solution.py:188
  11.8 2.1 %collective-permute-start.1 = (f32[2,64,256]{2,1,0:T(8,128)S(1)}, f32[2,64,256]{2,1,0:T(8,128)S(1)}, u32[]{:S(2)}, u32[]{:S(2)}) collective-permute-start(f32[2,64,256]{2,1,0:T(8,128)S(1)} %get-tuple-element.42), channel_id=1, source_target_pairs={{0,4},{4,12},{12,8},{8,0},{1,5},{5,13},{13,9},{9,1},{2,6},{6,14},{... | collective-permute-start | bytes 393224 | tf_op jit(solution)/shard_map/ppermute | solution.py:189
  13.9 1.4 %collective-permute-done.3.refs_2_ = f32[2,64,256]{2,1,0:T(8,128)S(1)} collective-permute-done((f32[2,64,256]{2,1,0:T(8,128)S(1)}, f32[2,64,256]{2,1,0:T(8,128)S(1)}, u32[]{:S(2)}, u32[]{:S(2)}) %collective-permute-start.3) | collective-permute-done | bytes 131104 | tf_op jit(solution)/shard_map/ppermute | solution.py:188
  15.3 0.6 %collective-permute-start.4 = (f32[2,64,256]{2,1,0:T(8,128)S(1)}, f32[2,64,256]{2,1,0:T(8,128)S(1)}, u32[]{:S(2)}, u32[]{:S(2)}) collective-permute-start(f32[2,64,256]{2,1,0:T(8,128)S(1)} %collective-permute-done.3.refs_2_), channel_id=1, source_target_pairs={{0,4},{4,12},{12,8},{8,0},{1,5},{5,13},{13,9},{9,1},{2,6},{6,14},{... | collective-permute-start | bytes 393224 | tf_op jit(solution)/shard_map/ppermute | solution.py:188
  15.9 2.2 %collective-permute-done.1.refs_2_ = f32[2,64,256]{2,1,0:T(8,128)S(1)} collective-permute-done((f32[2,64,256]{2,1,0:T(8,128)S(1)}, f32[2,64,256]{2,1,0:T(8,128)S(1)}, u32[]{:S(2)}, u32[]{:S(2)}) %collective-permute-start.1) | collective-permute-done | bytes 131104 | tf_op jit(solution)/shard_map/ppermute | solution.py:189
  18.1 0.6 %collective-permute-start.2 = (f32[2,64,256]{2,1,0:T(8,128)S(1)}, f32[2,64,256]{2,1,0:T(8,128)S(1)}, u32[]{:S(2)}, u32[]{:S(2)}) collective-permute-start(f32[2,64,256]{2,1,0:T(8,128)S(1)} %collective-permute-done.1.refs_2_), channel_id=1, source_target_pairs={{0,4},{4,12},{12,8},{8,0},{1,5},{5,13},{13,9},{9,1},{2,6},{6,14},{... | collective-permute-start | bytes 393224 | tf_op jit(solution)/shard_map/ppermute | solution.py:189
  18.7 2.3 %collective-permute-done.4.refs_3_ = f32[2,64,256]{2,1,0:T(8,128)S(1)} collective-permute-done((f32[2,64,256]{2,1,0:T(8,128)S(1)}, f32[2,64,256]{2,1,0:T(8,128)S(1)}, u32[]{:S(2)}, u32[]{:S(2)}) %collective-permute-start.4) | collective-permute-done | bytes 131104 | tf_op jit(solution)/shard_map/ppermute | solution.py:188
  21.0 6.7 %collective-permute-start.6 = (f32[4,64,256]{2,1,0:T(8,128)S(1)}, f32[4,64,256]{2,1,0:T(8,128)S(1)}, u32[]{:S(2)}, u32[]{:S(2)}) collective-permute-start(f32[4,64,256]{2,1,0:T(8,128)S(1)} %get-tuple-element.37), channel_id=1, source_target_pairs={{1,2},{2,1},{5,6},{6,5},{9,10},{10,9},{13,14},{14,13},{17,18},{18,... | collective-permute-start | bytes 786440 | tf_op jit(solution)/shard_map/ppermute | solution.py:22
  27.7 0.0 copy-start.4
  27.7 0.1 collective-permute-start.5
  27.7 0.2 assemble.1.refs_4_.outer
  27.9 0.0 collective-permute-done.2.refs_3_
  28.0 0.4 copy-done.4
  28.4 1.7 %own.1 = (bf16[2,768,256]{2,1,0:T(8,128)(2,1)S(1)}, bf16[4,512,256]{2,1,0:T(8,128)(2,1)S(1)}, bf16[4,512,256]{2,1,0:T(8,128)(2,1)S(1)}) custom-call(s32[8,16]{1,0:T(8,128)S(1)} %copy-done.4, f32[2,64,256]{2,1,0:T(8,128)S(1)} %get-tuple-element.44.refs_0_, f32[2,64,256]{2,1,0:T(8,128)S(1)} %get-tuple-element.41.refs_1_, ...), custom_call_target="tpu_custom_call" | custom-call | flops 3221225472 | bytes 1048576 | tf_op jit(solution)/shard_map/own/pallas_call | solution.py:159
  30.0 1.7 %collective-permute-done.6.apart = f32[4,64,256]{2,1,0:T(8,128)S(1)} collective-permute-done((f32[4,64,256]{2,1,0:T(8,128)S(1)}, f32[4,64,256]{2,1,0:T(8,128)S(1)}, u32[]{:S(2)}, u32[]{:S(2)}) %collective-permute-start.6) | collective-permute-done | bytes 262176 | tf_op jit(solution)/shard_map/ppermute | solution.py:22
  31.7 0.0 collective-permute-done.5.paired
  31.7 0.0 copy-done.1
  31.7 0.0 copy-done.3
  31.7 0.0 copy-done.5
  31.7 2.2 %first_chunk.1 = (f32[2,64,256]{2,1,0:T(8,128)S(1)}, f32[2,64,256]{2,1,0:T(8,128)S(1)}, bf16[2,768,256]{2,1,0:T(8,128)(2,1)S(1)}) custom-call(s32[8]{0:T(128)S(1)} %copy-done.5, s32[8,16]{1,0:T(8,128)S(1)} %copy-done.4, bf16[4,512,256]{2,1,0:T(8,128)(2,1)S(1)} %get-tuple-element.23.own_high, bf16[4,512,256]{2,1,0:T(8,128)(2,1)S(1)} %get-tuple-element.24.own_low, ...), custom_call_target="tpu_custom_call" | custom-call | flops 1610612736 | bytes 1048576 | tf_op jit(solution)/shard_map/first_chunk/pallas_call | solution.py:159
  34.0 0.4 collective-permute-start.10
  34.4 3.1 %collective-permute-start.7 = (f32[2,64,256]{2,1,0:T(8,128)S(1)}, f32[2,64,256]{2,1,0:T(8,128)S(1)}, u32[]{:S(2)}, u32[]{:S(2)}) collective-permute-start(f32[2,64,256]{2,1,0:T(8,128)S(1)} %broadcast_add_fusion), channel_id=1, source_target_pairs={{0,4},{4,12},{12,8},{8,0},{1,5},{5,13},{13,9},{9,1},{2,6},{6,14},{... | collective-permute-start | bytes 393224 | tf_op jit(solution)/shard_map/ppermute | solution.py:228
  37.5 3.0 %chunk.3 = (f32[2,64,256]{2,1,0:T(8,128)S(1)}, f32[2,64,256]{2,1,0:T(8,128)S(1)}) custom-call(s32[8]{0:T(128)S(1)} %copy-done.5, s32[8,16]{1,0:T(8,128)S(1)} %copy-done.4, bf16[2,768,256]{2,1,0:T(8,128)(2,1)S(1)} %assemble.1.refs_4_.outer, bf16[2,768,256]{2,1,0:T(8,128)(2,1)S(1)} %get-tuple-element.29.inner, ...), custom_call_target="tpu_custom_call" | custom-call | flops 3221225472 | bytes 1048576 | tf_op jit(solution)/shard_map/chunk/pallas_call | solution.py:159
  40.6 0.0 collective-permute-done.10
  40.6 0.3 collective-permute-start.11
  40.9 1.1 %collective-permute-done.7 = f32[2,64,256]{2,1,0:T(8,128)S(1)} collective-permute-done((f32[2,64,256]{2,1,0:T(8,128)S(1)}, f32[2,64,256]{2,1,0:T(8,128)S(1)}, u32[]{:S(2)}, u32[]{:S(2)}) %collective-permute-start.7) | collective-permute-done | bytes 131104 | tf_op jit(solution)/shard_map/ppermute | solution.py:228
  41.9 2.1 %collective-permute-start.8 = (f32[2,64,256]{2,1,0:T(8,128)S(1)}, f32[2,64,256]{2,1,0:T(8,128)S(1)}, u32[]{:S(2)}, u32[]{:S(2)}) collective-permute-start(f32[2,64,256]{2,1,0:T(8,128)S(1)} %add.48), channel_id=1, source_target_pairs={{0,4},{4,12},{12,8},{8,0},{1,5},{5,13},{13,9},{9,1},{2,6},{6,14},{... | collective-permute-start | bytes 393224 | tf_op jit(solution)/shard_map/ppermute | solution.py:228
  44.0 3.0 %chunk.4 = (f32[2,64,256]{2,1,0:T(8,128)S(1)}, f32[2,64,256]{2,1,0:T(8,128)S(1)}) custom-call(s32[8]{0:T(128)S(1)} %copy-done.5, s32[8,16]{1,0:T(8,128)S(1)} %copy-done.4, bf16[2,768,256]{2,1,0:T(8,128)(2,1)S(1)} %assemble.1.refs_4_.outer, bf16[2,768,256]{2,1,0:T(8,128)(2,1)S(1)} %get-tuple-element.29.inner, ...), custom_call_target="tpu_custom_call" | custom-call | flops 3221225472 | bytes 1048576 | tf_op jit(solution)/shard_map/chunk/pallas_call | solution.py:159
  47.1 0.0 collective-permute-done.11
  47.1 1.4 %collective-permute-start.12 = (f32[2,64,256]{2,1,0:T(8,128)S(1)}, f32[2,64,256]{2,1,0:T(8,128)S(1)}, u32[]{:S(2)}, u32[]{:S(2)}) collective-permute-start(f32[2,64,256]{2,1,0:T(8,128)S(1)} %add.51.refs_1_), channel_id=1, source_target_pairs={{0,4},{4,12},{12,8},{8,0},{1,5},{5,13},{13,9},{9,1},{2,6},{6,14},{... | collective-permute-start | bytes 393224 | tf_op jit(solution)/shard_map/ppermute | solution.py:228
  48.5 0.6 collective-permute-done.8
  49.1 0.1 collective-permute-start.9
  49.2 3.0 %chunk.5 = (f32[2,64,256]{2,1,0:T(8,128)S(1)}, f32[2,64,256]{2,1,0:T(8,128)S(1)}) custom-call(s32[8]{0:T(128)S(1)} %copy-done.5, s32[8,16]{1,0:T(8,128)S(1)} %copy-done.4, bf16[2,768,256]{2,1,0:T(8,128)(2,1)S(1)} %assemble.1.refs_4_.outer, bf16[2,768,256]{2,1,0:T(8,128)(2,1)S(1)} %get-tuple-element.29.inner, ...), custom_call_target="tpu_custom_call" | custom-call | flops 3221225472 | bytes 1048576 | tf_op jit(solution)/shard_map/chunk/pallas_call | solution.py:159
  52.2 4.0 %collective-permute-done.9 = f32[2,64,256]{2,1,0:T(8,128)S(1)} collective-permute-done((f32[2,64,256]{2,1,0:T(8,128)S(1)}, f32[2,64,256]{2,1,0:T(8,128)S(1)}, u32[]{:S(2)}, u32[]{:S(2)}) %collective-permute-start.9) | collective-permute-done | bytes 131104 | tf_op jit(solution)/shard_map/ppermute | solution.py:228
  56.3 0.0 collective-permute-done.12
  56.3 0.7 %pad_maximum_fusion.2 = f32[4,64,256]{2,1,0:T(8,128)} fusion(f32[1,64,256]{2,1,0:T(8,128)S(1)} %get-tuple-element.46, f32[2,64,256]{2,1,0:T(8,128)S(1)} %add.53, f32[1,64,256]{2,1,0:T(8,128)S(1)} %get-tuple-element.45), kind=kLoop, calls=%fused_computation.2 | loop fusion | flops 131072 | bytes 524288 | tf_op jit(solution)/shard_map/concatenate | solution.py:232
  (20 shorter events, 0.3 us)
Async XLA Ops:
  0.0 9.5 %collective-permute-start = (f32[4,64,256]{2,1,0:T(8,128)}, f32[4,64,256]{2,1,0:T(8,128)}, u32[]{:S(2)}, u32[]{:S(2)}) collective-permute-start(f32[4,64,256]{2,1,0:T(8,128)} %param.5), channel_id=1, source_target_pairs={{0,4},{4,12},{12,8},{8,0},{1,5},{5,13},{13,9},{9,1},{2,6},{6,14},{... | collective-permute-start | bytes 786440 | tf_op jit(solution)/shard_map/ppermute | solution.py:185
  2.1 1.6 %copy-start.6 = (f32[8,256,256]{2,1,0:T(8,128)S(1)}, f32[8,256,256]{2,1,0:T(8,128)}, u32[]{:S(2)}) copy-start(f32[8,256,256]{2,1,0:T(8,128)} %left_ref.1) | copy-start | bytes 6291460
  3.7 1.6 %copy-start.7 = (f32[8,256,256]{2,1,0:T(8,128)S(1)}, f32[8,256,256]{2,1,0:T(8,128)}, u32[]{:S(2)}) copy-start(f32[8,256,256]{2,1,0:T(8,128)} %right_ref.1) | copy-start | bytes 6291460
  5.3 3.0 %copy-start.8 = (f32[4,64,256]{2,1,0:T(8,128)S(1)}, f32[4,64,256]{2,1,0:T(8,128)}, u32[]{:S(2)}) copy-start(f32[4,64,256]{2,1,0:T(8,128)} %param.5) | copy-start | bytes 786436
  6.4 1.0 %copy-start = (bf16[2048,256]{1,0:T(8,128)(2,1)}, bf16[2048,256]{1,0:T(8,128)(2,1)S(1)}, u32[]{:S(2)}) copy-start(bf16[2048,256]{1,0:T(8,128)(2,1)S(1)} %get-tuple-element.25.right_hi) | copy-start | bytes 3145732
  7.4 1.0 %copy-start.2 = (bf16[2048,256]{1,0:T(8,128)(2,1)}, bf16[2048,256]{1,0:T(8,128)(2,1)S(1)}, u32[]{:S(2)}) copy-start(bf16[2048,256]{1,0:T(8,128)(2,1)S(1)} %get-tuple-element.26.right_lo) | copy-start | bytes 3145732
  10.5 4.8 %collective-permute-start.3 = (f32[2,64,256]{2,1,0:T(8,128)S(1)}, f32[2,64,256]{2,1,0:T(8,128)S(1)}, u32[]{:S(2)}, u32[]{:S(2)}) collective-permute-start(f32[2,64,256]{2,1,0:T(8,128)S(1)} %get-tuple-element.39), channel_id=1, source_target_pairs={{0,4},{4,12},{12,8},{8,0},{1,5},{5,13},{13,9},{9,1},{2,6},{6,14},{... | collective-permute-start | bytes 393224 | tf_op jit(solution)/shard_map/ppermute | solution.py:188
  11.8 6.3 %collective-permute-start.1 = (f32[2,64,256]{2,1,0:T(8,128)S(1)}, f32[2,64,256]{2,1,0:T(8,128)S(1)}, u32[]{:S(2)}, u32[]{:S(2)}) collective-permute-start(f32[2,64,256]{2,1,0:T(8,128)S(1)} %get-tuple-element.42), channel_id=1, source_target_pairs={{0,4},{4,12},{12,8},{8,0},{1,5},{5,13},{13,9},{9,1},{2,6},{6,14},{... | collective-permute-start | bytes 393224 | tf_op jit(solution)/shard_map/ppermute | solution.py:189
  15.3 5.6 %collective-permute-start.4 = (f32[2,64,256]{2,1,0:T(8,128)S(1)}, f32[2,64,256]{2,1,0:T(8,128)S(1)}, u32[]{:S(2)}, u32[]{:S(2)}) collective-permute-start(f32[2,64,256]{2,1,0:T(8,128)S(1)} %collective-permute-done.3.refs_2_), channel_id=1, source_target_pairs={{0,4},{4,12},{12,8},{8,0},{1,5},{5,13},{13,9},{9,1},{2,6},{6,14},{... | collective-permute-start | bytes 393224 | tf_op jit(solution)/shard_map/ppermute | solution.py:188
  18.1 9.9 %collective-permute-start.2 = (f32[2,64,256]{2,1,0:T(8,128)S(1)}, f32[2,64,256]{2,1,0:T(8,128)S(1)}, u32[]{:S(2)}, u32[]{:S(2)}) collective-permute-start(f32[2,64,256]{2,1,0:T(8,128)S(1)} %collective-permute-done.1.refs_2_), channel_id=1, source_target_pairs={{0,4},{4,12},{12,8},{8,0},{1,5},{5,13},{13,9},{9,1},{2,6},{6,14},{... | collective-permute-start | bytes 393224 | tf_op jit(solution)/shard_map/ppermute | solution.py:189
  21.0 10.7 %collective-permute-start.6 = (f32[4,64,256]{2,1,0:T(8,128)S(1)}, f32[4,64,256]{2,1,0:T(8,128)S(1)}, u32[]{:S(2)}, u32[]{:S(2)}) collective-permute-start(f32[4,64,256]{2,1,0:T(8,128)S(1)} %get-tuple-element.37), channel_id=1, source_target_pairs={{1,2},{2,1},{5,6},{6,5},{9,10},{10,9},{13,14},{14,13},{17,18},{18,... | collective-permute-start | bytes 786440 | tf_op jit(solution)/shard_map/ppermute | solution.py:22
  27.7 0.7 %copy-start.4 = (s32[8,16]{1,0:T(8,128)S(1)}, s32[8,16]{1,0:T(8,128)}, u32[]{:S(2)}) copy-start(s32[8,16]{1,0:T(8,128)} %allowed_ref.9) | copy-start | bytes 1540
  27.7 4.0 %collective-permute-start.5 = (f32[4,64,256]{2,1,0:T(8,128)S(1)}, f32[4,64,256]{2,1,0:T(8,128)S(1)}, u32[]{:S(2)}, u32[]{:S(2)}) collective-permute-start(f32[4,64,256]{2,1,0:T(8,128)S(1)} %get-tuple-element.38), channel_id=1, source_target_pairs={{0,1},{2,3},{1,0},{3,2},{4,5},{6,7},{5,4},{7,6},{8,9},{10,11},{9,8... | collective-permute-start | bytes 786440 | tf_op jit(solution)/shard_map/ppermute | solution.py:22
  28.3 3.4 %copy-start.1 = (bf16[2048,256]{1,0:T(8,128)(2,1)S(1)}, bf16[2048,256]{1,0:T(8,128)(2,1)}, u32[]{:S(2)}) copy-start(bf16[2048,256]{1,0:T(8,128)(2,1)} %copy-done) | copy-start | bytes 3145732
  28.3 3.4 %copy-start.3 = (bf16[2048,256]{1,0:T(8,128)(2,1)S(1)}, bf16[2048,256]{1,0:T(8,128)(2,1)}, u32[]{:S(2)}) copy-start(bf16[2048,256]{1,0:T(8,128)(2,1)} %copy-done.2) | copy-start | bytes 3145732
  28.4 3.4 %copy-start.5 = (s32[8]{0:T(128)S(1)}, s32[8]{0:T(128)}, u32[]{:S(2)}) copy-start(s32[8]{0:T(128)} %shifts_ref.7) | copy-start | bytes 100
  34.0 6.6 %collective-permute-start.10 = (f32[2,64,256]{2,1,0:T(8,128)S(1)}, f32[2,64,256]{2,1,0:T(8,128)S(1)}, u32[]{:S(2)}, u32[]{:S(2)}) collective-permute-start(f32[2,64,256]{2,1,0:T(8,128)S(1)} %get-tuple-element.28), channel_id=1, source_target_pairs={{0,4},{4,12},{12,8},{8,0},{1,5},{5,13},{13,9},{9,1},{2,6},{6,14},{... | collective-permute-start | bytes 393224 | tf_op jit(solution)/shard_map/ppermute | solution.py:228
  34.4 7.5 %collective-permute-start.7 = (f32[2,64,256]{2,1,0:T(8,128)S(1)}, f32[2,64,256]{2,1,0:T(8,128)S(1)}, u32[]{:S(2)}, u32[]{:S(2)}) collective-permute-start(f32[2,64,256]{2,1,0:T(8,128)S(1)} %broadcast_add_fusion), channel_id=1, source_target_pairs={{0,4},{4,12},{12,8},{8,0},{1,5},{5,13},{13,9},{9,1},{2,6},{6,14},{... | collective-permute-start | bytes 393224 | tf_op jit(solution)/shard_map/ppermute | solution.py:228
  40.6 6.5 %collective-permute-start.11 = (f32[2,64,256]{2,1,0:T(8,128)S(1)}, f32[2,64,256]{2,1,0:T(8,128)S(1)}, u32[]{:S(2)}, u32[]{:S(2)}) collective-permute-start(f32[2,64,256]{2,1,0:T(8,128)S(1)} %add.50), channel_id=1, source_target_pairs={{0,4},{4,12},{12,8},{8,0},{1,5},{5,13},{13,9},{9,1},{2,6},{6,14},{... | collective-permute-start | bytes 393224 | tf_op jit(solution)/shard_map/ppermute | solution.py:228
  41.9 7.2 %collective-permute-start.8 = (f32[2,64,256]{2,1,0:T(8,128)S(1)}, f32[2,64,256]{2,1,0:T(8,128)S(1)}, u32[]{:S(2)}, u32[]{:S(2)}) collective-permute-start(f32[2,64,256]{2,1,0:T(8,128)S(1)} %add.48), channel_id=1, source_target_pairs={{0,4},{4,12},{12,8},{8,0},{1,5},{5,13},{13,9},{9,1},{2,6},{6,14},{... | collective-permute-start | bytes 393224 | tf_op jit(solution)/shard_map/ppermute | solution.py:228
  47.1 9.2 %collective-permute-start.12 = (f32[2,64,256]{2,1,0:T(8,128)S(1)}, f32[2,64,256]{2,1,0:T(8,128)S(1)}, u32[]{:S(2)}, u32[]{:S(2)}) collective-permute-start(f32[2,64,256]{2,1,0:T(8,128)S(1)} %add.51.refs_1_), channel_id=1, source_target_pairs={{0,4},{4,12},{12,8},{8,0},{1,5},{5,13},{13,9},{9,1},{2,6},{6,14},{... | collective-permute-start | bytes 393224 | tf_op jit(solution)/shard_map/ppermute | solution.py:228
  49.1 7.1 %collective-permute-start.9 = (f32[2,64,256]{2,1,0:T(8,128)S(1)}, f32[2,64,256]{2,1,0:T(8,128)S(1)}, u32[]{:S(2)}, u32[]{:S(2)}) collective-permute-start(f32[2,64,256]{2,1,0:T(8,128)S(1)} %add.49.refs_0_), channel_id=1, source_target_pairs={{0,4},{4,12},{12,8},{8,0},{1,5},{5,13},{13,9},{9,1},{2,6},{6,14},{... | collective-permute-start | bytes 393224 | tf_op jit(solution)/shard_map/ppermute | solution.py:228

commit v20 on v17

--- a/solution.py
+++ b/solution.py
@@ -84,8 +84,8 @@
     return left_parts[ring_place(n, step + 1)].reshape(-1, left_parts.shape[-1])
 
 
-def own_sectors(n, allowed_ref, outer, *refs):
-    left_parts, inner, high, low, psi = refs[n:]
+def own_sectors(n, shifts_ref, allowed_ref, *refs):
+    (outer, left_parts, right_hi, right_lo), (inner, high, low, out, psi) = refs[n : n + 4], refs[n + 4 :]
     assemble(n, *refs[:n], inner, psi)
     left = chunk_left(n, 0, left_parts)
     nloc = high.shape[0]
@@ -94,6 +94,11 @@
     for i, ref in enumerate(sources):
         first_product(left, ref[...], allowed_ref, first + i, high.at[i], low.at[i])
 
+    def blocks_of(own, shift, at):
+        return [own[t - shift, at] for t in range(1, nloc - 1)]
+
+    second_product(blocks_of, shifts_ref, high, low, right_hi, right_lo, out)
+
 
 def second_product(blocks_of, shifts_ref, high, low, right_hi, right_lo, out):
     rows, width = out.shape[1:]
@@ -106,13 +111,6 @@
         return jnp.concatenate(columns, axis=1)
 
     out[...] = dot3((left(high), left(low)), (right_hi[...], right_lo[...])).reshape(out.shape)
-
-
-def first_inner(nloc, shifts_ref, high, low, right_hi, right_lo, out):
-    def blocks_of(own, shift, at):
-        return [own[t - shift, at] for t in range(1, nloc - 1)]
-
-    second_product(blocks_of, shifts_ref, high, low, right_hi, right_lo, out)
 
 
 def first_outer(n, nloc, shifts_ref, allowed_ref, own_high, own_low, above, below, left_parts, right_hi, right_lo, *refs):
@@ -199,13 +197,9 @@
 
     chunk = jax.ShapeDtypeStruct((2, rows, width), F32)
     chunk_inner = jax.ShapeDtypeStruct((nloc - 2, rows, width), F32)
-    parts_inner, *own = call(
-        functools.partial(own_sectors, n), "own", 4 * kops * one, [split_parts(nloc - 2), *products(nloc)],
-        [SMEM] + [VMEM] * (n + 2), [allowed, parts_outer, *inner, left_parts], whole(nloc - 2),
-    )
-    result_inner = call(
-        functools.partial(first_inner, nloc), "first_inner", nloc * kops * one // n, chunk_inner,
-        [SMEM] + [VMEM] * 4, [shifts, *own, right_hi, right_lo],
+    parts_inner, *own, result_inner = call(
+        functools.partial(own_sectors, n), "own", 4 * kops * one, [split_parts(nloc - 2), *products(nloc), chunk_inner],
+        [SMEM] * 2 + [VMEM] * (n + 4), [shifts, allowed, *inner, parts_outer, left_parts, right_hi, right_lo], whole(nloc - 2),
     )
     result_outer, parts_outside = call(
         functools.partial(first_outer, n, nloc), "first_outer", 2 * kops * one, [chunk, split_parts(2)],

time: 55.8 us -> 55.9 us (level)
    pallas_call x8 -> x7, Pallas kernels: 15.6 us -> 15.7 us  [call(): pl.pallas_call(body, name=name, out_shape=out_shape, in_specs=in_specs, o...]
where the time goes in v20:
time: 55.9 us; the launch traced here: 55.7 us
  starting transfers between devices  22.6 us (40%)
  Pallas kernels  15.7 us (28%)
  waiting for transfers between devices  13 us (23%)
  local copies, waits for them, and re-layouts  3.27 us (6%)
  other arithmetic  0.95 us (2%)
    pallas_call x7, Pallas kernels, call(): pl.pallas_call(body, name=name, out_shape=out_shape, in_specs=in_specs, o...  15.7 us
    ppermute x2, starting transfers between devices, shifted(): return lax.ppermute(block, axis, route)  8.41 us
    ppermute x3, starting transfers between devices, shards(): result_inner = lax.ppermute(result_inner, 'op', route) + next_inner  6.35 us
    ppermute x2, waiting for transfers between devices, shards(): lax.ppermute(outer[-1] + zero[0, 0] if step == 1 else outer[-1], 'op', ro...  3.62 us
    ppermute x2, starting transfers between devices, shards(): lax.ppermute(inner[-1] + zero[0, 0] if step == 1 else inner[-1], 'op', ro...  3.59 us
    unnamed x10, local copies, waits for them, and re-layouts  3.2 us
    ppermute x1, waiting for transfers between devices, shards(): blocks = [psi, lax.ppermute(psi, 'op', route)]  2.94 us
    ppermute x2, waiting for transfers between devices, shifted(): return lax.ppermute(block, axis, route)  2.31 us
  transfers between devices with their start and end apart: 13, of which 7 were waited for; matrix products, arithmetic and copies ran while one was open for 0% of the time, Pallas kernels for 28%

profile of v20, /device:TPU:1, one launch (start us, length us, event | category | flops | bytes accessed | tf_op | source)
XLA Modules:
  0.0 55.7 jit_solution(17413850246364449141)
XLA Ops:
  0.0 2.1 %collective-permute-start = (f32[4,64,256]{2,1,0:T(8,128)}, f32[4,64,256]{2,1,0:T(8,128)S(1)}, u32[]{:S(2)}, u32[]{:S(2)}) collective-permute-start(f32[4,64,256]{2,1,0:T(8,128)} %param.5), channel_id=1, source_target_pairs={{0,4},{4,12},{12,8},{8,0},{1,5},{5,13},{13,9},{9,1},{2,6},{6,14},{... | collective-permute-start | bytes 786440 | tf_op jit(solution)/shard_map/ppermute | solution.py:179
  2.1 0.0 copy-start.2
  2.1 1.6 %copy-done.2 = f32[8,256,256]{2,1,0:T(8,128)S(1)} copy-done((f32[8,256,256]{2,1,0:T(8,128)S(1)}, f32[8,256,256]{2,1,0:T(8,128)}, u32[]{:S(2)}) %copy-start.2) | copy-done | bytes 2097176
  3.7 0.0 copy-start.3
  3.7 1.6 %copy-done.3 = f32[8,256,256]{2,1,0:T(8,128)S(1)} copy-done((f32[8,256,256]{2,1,0:T(8,128)S(1)}, f32[8,256,256]{2,1,0:T(8,128)}, u32[]{:S(2)}) %copy-start.3) | copy-done | bytes 2097176
  5.3 0.0 copy-start.4
  5.3 1.1 %prepare.1 = (bf16[4,8,64,768]{3,2,1,0:T(8,128)(2,1)S(1)}, bf16[2048,256]{1,0:T(8,128)(2,1)S(1)}, bf16[2048,256]{1,0:T(8,128)(2,1)S(1)}, f32[1,128]{1,0:T(1,128)S(1)}) custom-call(f32[8,256,256]{2,1,0:T(8,128)S(1)} %copy-done.2, f32[8,256,256]{2,1,0:T(8,128)S(1)} %copy-done.3), custom_call_target="tpu_custom_call" | custom-call | flops 3221225472 | bytes 1048576 | tf_op jit(solution)/shard_map/prepare/pallas_call | solution.py:153
  6.4 0.0 copy-done.4
  6.4 2.9 %collective-permute-done = f32[4,64,256]{2,1,0:T(8,128)S(1)} collective-permute-done((f32[4,64,256]{2,1,0:T(8,128)}, f32[4,64,256]{2,1,0:T(8,128)S(1)}, u32[]{:S(2)}, u32[]{:S(2)}) %collective-permute-start) | collective-permute-done | bytes 262176 | tf_op jit(solution)/shard_map/ppermute | solution.py:179
  9.4 0.1 broadcast_add_fusion
  9.5 0.4 collective-permute-start.3
  9.9 3.0 %collective-permute-start.1 = (f32[2,64,256]{2,1,0:T(8,128)S(1)}, f32[2,64,256]{2,1,0:T(8,128)S(1)}, u32[]{:S(2)}, u32[]{:S(2)}) collective-permute-start(f32[2,64,256]{2,1,0:T(8,128)S(1)} %get-tuple-element.40), channel_id=1, source_target_pairs={{0,4},{4,12},{12,8},{8,0},{1,5},{5,13},{13,9},{9,1},{2,6},{6,14},{... | collective-permute-start | bytes 393224 | tf_op jit(solution)/shard_map/ppermute | solution.py:183
  12.9 1.4 %collective-permute-done.3.refs_2_ = f32[2,64,256]{2,1,0:T(8,128)S(1)} collective-permute-done((f32[2,64,256]{2,1,0:T(8,128)S(1)}, f32[2,64,256]{2,1,0:T(8,128)S(1)}, u32[]{:S(2)}, u32[]{:S(2)}) %collective-permute-start.3) | collective-permute-done | bytes 131104 | tf_op jit(solution)/shard_map/ppermute | solution.py:182
  14.2 0.6 %collective-permute-start.4 = (f32[2,64,256]{2,1,0:T(8,128)S(1)}, f32[2,64,256]{2,1,0:T(8,128)S(1)}, u32[]{:S(2)}, u32[]{:S(2)}) collective-permute-start(f32[2,64,256]{2,1,0:T(8,128)S(1)} %collective-permute-done.3.refs_2_), channel_id=1, source_target_pairs={{0,4},{4,12},{12,8},{8,0},{1,5},{5,13},{13,9},{9,1},{2,6},{6,14},{... | collective-permute-start | bytes 393224 | tf_op jit(solution)/shard_map/ppermute | solution.py:182
  14.8 2.2 %collective-permute-done.1.refs_2_ = f32[2,64,256]{2,1,0:T(8,128)S(1)} collective-permute-done((f32[2,64,256]{2,1,0:T(8,128)S(1)}, f32[2,64,256]{2,1,0:T(8,128)S(1)}, u32[]{:S(2)}, u32[]{:S(2)}) %collective-permute-start.1) | collective-permute-done | bytes 131104 | tf_op jit(solution)/shard_map/ppermute | solution.py:183
  17.0 0.6 %collective-permute-start.2 = (f32[2,64,256]{2,1,0:T(8,128)S(1)}, f32[2,64,256]{2,1,0:T(8,128)S(1)}, u32[]{:S(2)}, u32[]{:S(2)}) collective-permute-start(f32[2,64,256]{2,1,0:T(8,128)S(1)} %collective-permute-done.1.refs_2_), channel_id=1, source_target_pairs={{0,4},{4,12},{12,8},{8,0},{1,5},{5,13},{13,9},{9,1},{2,6},{6,14},{... | collective-permute-start | bytes 393224 | tf_op jit(solution)/shard_map/ppermute | solution.py:183
  17.6 2.3 %collective-permute-done.4.refs_3_ = f32[2,64,256]{2,1,0:T(8,128)S(1)} collective-permute-done((f32[2,64,256]{2,1,0:T(8,128)S(1)}, f32[2,64,256]{2,1,0:T(8,128)S(1)}, u32[]{:S(2)}, u32[]{:S(2)}) %collective-permute-start.4) | collective-permute-done | bytes 131104 | tf_op jit(solution)/shard_map/ppermute | solution.py:182
  19.9 6.5 %collective-permute-start.5 = (f32[4,64,256]{2,1,0:T(8,128)S(1)}, f32[4,64,256]{2,1,0:T(8,128)S(1)}, u32[]{:S(2)}, u32[]{:S(2)}) collective-permute-start(f32[4,64,256]{2,1,0:T(8,128)S(1)} %pad_maximum_fusion), channel_id=1, source_target_pairs={{0,1},{1,2},{2,3},{4,5},{5,6},{6,7},{8,9},{9,10},{10,11},{12,13},{... | collective-permute-start | bytes 786440 | tf_op jit(solution)/shard_map/ppermute | solution.py:18
  26.4 0.0 copy-start
  26.4 0.0 copy-start.1
  26.4 1.9 %collective-permute-start.6 = (f32[4,64,256]{2,1,0:T(8,128)S(1)}, f32[4,64,256]{2,1,0:T(8,128)S(1)}, u32[]{:S(2)}, u32[]{:S(2)}) collective-permute-start(f32[4,64,256]{2,1,0:T(8,128)S(1)} %pad_maximum_fusion.1), channel_id=1, source_target_pairs={{1,0},{2,1},{3,2},{5,4},{6,5},{7,6},{9,8},{10,9},{11,10},{13,12},{... | collective-permute-start | bytes 786440 | tf_op jit(solution)/shard_map/ppermute | solution.py:18
  28.4 0.2 assemble.1.refs_4_.outer
  28.6 0.0 collective-permute-done.2.refs_3_
  28.6 0.0 copy-done
  28.6 0.0 copy-done.1
  28.6 2.9 %own.1 = (bf16[2,768,256]{2,1,0:T(8,128)(2,1)S(1)}, bf16[4,512,256]{2,1,0:T(8,128)(2,1)S(1)}, bf16[4,512,256]{2,1,0:T(8,128)(2,1)S(1)}, f32[2,64,256]{2,1,0:T(8,128)S(1)}) custom-call(s32[8]{0:T(128)S(1)} %copy-done.1, s32[8,16]{1,0:T(8,128)S(1)} %copy-done, f32[2,64,256]{2,1,0:T(8,128)S(1)} %get-tuple-element.42.refs_0_, ...), custom_call_target="tpu_custom_call" | custom-call | flops 3221225472 | bytes 1048576 | tf_op jit(solution)/shard_map/own/pallas_call | solution.py:153
  31.5 0.6 %collective-permute-start.10 = (f32[2,64,256]{2,1,0:T(8,128)S(1)}, f32[2,64,256]{2,1,0:T(8,128)S(1)}, u32[]{:S(2)}, u32[]{:S(2)}) collective-permute-start(f32[2,64,256]{2,1,0:T(8,128)S(1)} %get-tuple-element.33), channel_id=1, source_target_pairs={{0,4},{4,12},{12,8},{8,0},{1,5},{5,13},{13,9},{9,1},{2,6},{6,14},{... | collective-permute-start | bytes 393224 | tf_op jit(solution)/shard_map/ppermute | solution.py:220
  32.1 0.0 collective-permute-done.5.above
  32.1 2.3 %collective-permute-done.6.below = f32[4,64,256]{2,1,0:T(8,128)S(1)} collective-permute-done((f32[4,64,256]{2,1,0:T(8,128)S(1)}, f32[4,64,256]{2,1,0:T(8,128)S(1)}, u32[]{:S(2)}, u32[]{:S(2)}) %collective-permute-start.6) | collective-permute-done | bytes 262176 | tf_op jit(solution)/shard_map/ppermute | solution.py:18
  34.4 2.5 %first_outer.1 = (f32[2,64,256]{2,1,0:T(8,128)S(1)}, bf16[2,768,256]{2,1,0:T(8,128)(2,1)S(1)}) custom-call(s32[8]{0:T(128)S(1)} %copy-done.1, s32[8,16]{1,0:T(8,128)S(1)} %copy-done, bf16[4,512,256]{2,1,0:T(8,128)(2,1)S(1)} %get-tuple-element.25.own_high, bf16[4,512,256]{2,1,0:T(8,128)(2,1)S(1)} %get-tuple-element.26.own_low, ...), custom_call_target="tpu_custom_call" | custom-call | flops 1610612736 | bytes 1048576 | tf_op jit(solution)/shard_map/first_outer/pallas_call | solution.py:153
  36.9 0.8 %collective-permute-start.7 = (f32[2,64,256]{2,1,0:T(8,128)S(1)}, f32[2,64,256]{2,1,0:T(8,128)S(1)}, u32[]{:S(2)}, u32[]{:S(2)}) collective-permute-start(f32[2,64,256]{2,1,0:T(8,128)S(1)} %get-tuple-element.27), channel_id=1, source_target_pairs={{0,4},{4,12},{12,8},{8,0},{1,5},{5,13},{13,9},{9,1},{2,6},{6,14},{... | collective-permute-start | bytes 393224 | tf_op jit(solution)/shard_map/ppermute | solution.py:221
  37.7 3.0 %chunk.3 = (f32[2,64,256]{2,1,0:T(8,128)S(1)}, f32[2,64,256]{2,1,0:T(8,128)S(1)}) custom-call(s32[8]{0:T(128)S(1)} %copy-done.1, s32[8,16]{1,0:T(8,128)S(1)} %copy-done, bf16[2,768,256]{2,1,0:T(8,128)(2,1)S(1)} %assemble.1.refs_4_.outer, bf16[2,768,256]{2,1,0:T(8,128)(2,1)S(1)} %get-tuple-element.28.inner, ...), custom_call_target="tpu_custom_call" | custom-call | flops 3221225472 | bytes 1048576 | tf_op jit(solution)/shard_map/chunk/pallas_call | solution.py:153
  40.7 0.0 collective-permute-done.10
  40.8 2.9 %collective-permute-start.11 = (f32[2,64,256]{2,1,0:T(8,128)S(1)}, f32[2,64,256]{2,1,0:T(8,128)S(1)}, u32[]{:S(2)}, u32[]{:S(2)}) collective-permute-start(f32[2,64,256]{2,1,0:T(8,128)S(1)} %add.34), channel_id=1, source_target_pairs={{0,4},{4,12},{12,8},{8,0},{1,5},{5,13},{13,9},{9,1},{2,6},{6,14},{... | collective-permute-start | bytes 393224 | tf_op jit(solution)/shard_map/ppermute | solution.py:220
  43.7 0.0 collective-permute-done.7
  43.7 0.2 collective-permute-start.8
  43.9 3.0 %chunk.4 = (f32[2,64,256]{2,1,0:T(8,128)S(1)}, f32[2,64,256]{2,1,0:T(8,128)S(1)}) custom-call(s32[8]{0:T(128)S(1)} %copy-done.1, s32[8,16]{1,0:T(8,128)S(1)} %copy-done, bf16[2,768,256]{2,1,0:T(8,128)(2,1)S(1)} %assemble.1.refs_4_.outer, bf16[2,768,256]{2,1,0:T(8,128)(2,1)S(1)} %get-tuple-element.28.inner, ...), custom_call_target="tpu_custom_call" | custom-call | flops 3221225472 | bytes 1048576 | tf_op jit(solution)/shard_map/chunk/pallas_call | solution.py:153
  47.0 0.3 collective-permute-done.11
  47.3 2.9 %collective-permute-start.12 = (f32[2,64,256]{2,1,0:T(8,128)S(1)}, f32[2,64,256]{2,1,0:T(8,128)S(1)}, u32[]{:S(2)}, u32[]{:S(2)}) collective-permute-start(f32[2,64,256]{2,1,0:T(8,128)S(1)} %add.35), channel_id=1, source_target_pairs={{0,4},{4,12},{12,8},{8,0},{1,5},{5,13},{13,9},{9,1},{2,6},{6,14},{... | collective-permute-start | bytes 393224 | tf_op jit(solution)/shard_map/ppermute | solution.py:220
  50.1 0.0 collective-permute-done.8
  50.2 0.1 collective-permute-start.9
  50.2 3.0 %chunk.5 = (f32[2,64,256]{2,1,0:T(8,128)S(1)}, f32[2,64,256]{2,1,0:T(8,128)S(1)}) custom-call(s32[8]{0:T(128)S(1)} %copy-done.1, s32[8,16]{1,0:T(8,128)S(1)} %copy-done, bf16[2,768,256]{2,1,0:T(8,128)(2,1)S(1)} %assemble.1.refs_4_.outer, bf16[2,768,256]{2,1,0:T(8,128)(2,1)S(1)} %get-tuple-element.28.inner, ...), custom_call_target="tpu_custom_call" | custom-call | flops 3221225472 | bytes 1048576 | tf_op jit(solution)/shard_map/chunk/pallas_call | solution.py:153
  53.3 0.0 collective-permute-done.12
  53.3 1.6 %collective-permute-done.9 = f32[2,64,256]{2,1,0:T(8,128)S(1)} collective-permute-done((f32[2,64,256]{2,1,0:T(8,128)S(1)}, f32[2,64,256]{2,1,0:T(8,128)S(1)}, u32[]{:S(2)}, u32[]{:S(2)}) %collective-permute-start.9) | collective-permute-done | bytes 131104 | tf_op jit(solution)/shard_map/ppermute | solution.py:221
  55.0 0.7 %pad_maximum_fusion.2 = f32[4,64,256]{2,1,0:T(8,128)} fusion(f32[1,64,256]{2,1,0:T(8,128)S(1)} %get-tuple-element.44, f32[2,64,256]{2,1,0:T(8,128)S(1)} %add.36, f32[1,64,256]{2,1,0:T(8,128)S(1)} %get-tuple-element.43), kind=kLoop, calls=%fused_computation.2 | loop fusion | flops 131072 | bytes 524288 | tf_op jit(solution)/shard_map/concatenate | solution.py:222
  (14 shorter events, 0.2 us)
Async XLA Ops:
  0.0 9.4 %collective-permute-start = (f32[4,64,256]{2,1,0:T(8,128)}, f32[4,64,256]{2,1,0:T(8,128)S(1)}, u32[]{:S(2)}, u32[]{:S(2)}) collective-permute-start(f32[4,64,256]{2,1,0:T(8,128)} %param.5), channel_id=1, source_target_pairs={{0,4},{4,12},{12,8},{8,0},{1,5},{5,13},{13,9},{9,1},{2,6},{6,14},{... | collective-permute-start | bytes 786440 | tf_op jit(solution)/shard_map/ppermute | solution.py:179
  2.1 1.6 %copy-start.2 = (f32[8,256,256]{2,1,0:T(8,128)S(1)}, f32[8,256,256]{2,1,0:T(8,128)}, u32[]{:S(2)}) copy-start(f32[8,256,256]{2,1,0:T(8,128)} %left_ref.1) | copy-start | bytes 6291460
  3.7 1.6 %copy-start.3 = (f32[8,256,256]{2,1,0:T(8,128)S(1)}, f32[8,256,256]{2,1,0:T(8,128)}, u32[]{:S(2)}) copy-start(f32[8,256,256]{2,1,0:T(8,128)} %right_ref.1) | copy-start | bytes 6291460
  5.3 1.1 %copy-start.4 = (f32[4,64,256]{2,1,0:T(8,128)S(1)}, f32[4,64,256]{2,1,0:T(8,128)}, u32[]{:S(2)}) copy-start(f32[4,64,256]{2,1,0:T(8,128)} %param.5) | copy-start | bytes 786436
  9.5 4.8 %collective-permute-start.3 = (f32[2,64,256]{2,1,0:T(8,128)S(1)}, f32[2,64,256]{2,1,0:T(8,128)S(1)}, u32[]{:S(2)}, u32[]{:S(2)}) collective-permute-start(f32[2,64,256]{2,1,0:T(8,128)S(1)} %get-tuple-element.37), channel_id=1, source_target_pairs={{0,4},{4,12},{12,8},{8,0},{1,5},{5,13},{13,9},{9,1},{2,6},{6,14},{... | collective-permute-start | bytes 393224 | tf_op jit(solution)/shard_map/ppermute | solution.py:182
  9.9 7.1 %collective-permute-start.1 = (f32[2,64,256]{2,1,0:T(8,128)S(1)}, f32[2,64,256]{2,1,0:T(8,128)S(1)}, u32[]{:S(2)}, u32[]{:S(2)}) collective-permute-start(f32[2,64,256]{2,1,0:T(8,128)S(1)} %get-tuple-element.40), channel_id=1, source_target_pairs={{0,4},{4,12},{12,8},{8,0},{1,5},{5,13},{13,9},{9,1},{2,6},{6,14},{... | collective-permute-start | bytes 393224 | tf_op jit(solution)/shard_map/ppermute | solution.py:183
  14.2 5.6 %collective-permute-start.4 = (f32[2,64,256]{2,1,0:T(8,128)S(1)}, f32[2,64,256]{2,1,0:T(8,128)S(1)}, u32[]{:S(2)}, u32[]{:S(2)}) collective-permute-start(f32[2,64,256]{2,1,0:T(8,128)S(1)} %collective-permute-done.3.refs_2_), channel_id=1, source_target_pairs={{0,4},{4,12},{12,8},{8,0},{1,5},{5,13},{13,9},{9,1},{2,6},{6,14},{... | collective-permute-start | bytes 393224 | tf_op jit(solution)/shard_map/ppermute | solution.py:182
  17.0 11.6 %collective-permute-start.2 = (f32[2,64,256]{2,1,0:T(8,128)S(1)}, f32[2,64,256]{2,1,0:T(8,128)S(1)}, u32[]{:S(2)}, u32[]{:S(2)}) collective-permute-start(f32[2,64,256]{2,1,0:T(8,128)S(1)} %collective-permute-done.1.refs_2_), channel_id=1, source_target_pairs={{0,4},{4,12},{12,8},{8,0},{1,5},{5,13},{13,9},{9,1},{2,6},{6,14},{... | collective-permute-start | bytes 393224 | tf_op jit(solution)/shard_map/ppermute | solution.py:183
  19.9 12.2 %collective-permute-start.5 = (f32[4,64,256]{2,1,0:T(8,128)S(1)}, f32[4,64,256]{2,1,0:T(8,128)S(1)}, u32[]{:S(2)}, u32[]{:S(2)}) collective-permute-start(f32[4,64,256]{2,1,0:T(8,128)S(1)} %pad_maximum_fusion), channel_id=1, source_target_pairs={{0,1},{1,2},{2,3},{4,5},{5,6},{6,7},{8,9},{9,10},{10,11},{12,13},{... | collective-permute-start | bytes 786440 | tf_op jit(solution)/shard_map/ppermute | solution.py:18
  26.4 2.2 %copy-start = (s32[8,16]{1,0:T(8,128)S(1)}, s32[8,16]{1,0:T(8,128)}, u32[]{:S(2)}) copy-start(s32[8,16]{1,0:T(8,128)} %allowed_ref.9) | copy-start | bytes 1540
  26.4 2.2 %copy-start.1 = (s32[8]{0:T(128)S(1)}, s32[8]{0:T(128)}, u32[]{:S(2)}) copy-start(s32[8]{0:T(128)} %shifts_ref.9) | copy-start | bytes 100
  26.4 8.0 %collective-permute-start.6 = (f32[4,64,256]{2,1,0:T(8,128)S(1)}, f32[4,64,256]{2,1,0:T(8,128)S(1)}, u32[]{:S(2)}, u32[]{:S(2)}) collective-permute-start(f32[4,64,256]{2,1,0:T(8,128)S(1)} %pad_maximum_fusion.1), channel_id=1, source_target_pairs={{1,0},{2,1},{3,2},{5,4},{6,5},{7,6},{9,8},{10,9},{11,10},{13,12},{... | collective-permute-start | bytes 786440 | tf_op jit(solution)/shard_map/ppermute | solution.py:18
  31.5 9.2 %collective-permute-start.10 = (f32[2,64,256]{2,1,0:T(8,128)S(1)}, f32[2,64,256]{2,1,0:T(8,128)S(1)}, u32[]{:S(2)}, u32[]{:S(2)}) collective-permute-start(f32[2,64,256]{2,1,0:T(8,128)S(1)} %get-tuple-element.33), channel_id=1, source_target_pairs={{0,4},{4,12},{12,8},{8,0},{1,5},{5,13},{13,9},{9,1},{2,6},{6,14},{... | collective-permute-start | bytes 393224 | tf_op jit(solution)/shard_map/ppermute | solution.py:220
  36.9 6.8 %collective-permute-start.7 = (f32[2,64,256]{2,1,0:T(8,128)S(1)}, f32[2,64,256]{2,1,0:T(8,128)S(1)}, u32[]{:S(2)}, u32[]{:S(2)}) collective-permute-start(f32[2,64,256]{2,1,0:T(8,128)S(1)} %get-tuple-element.27), channel_id=1, source_target_pairs={{0,4},{4,12},{12,8},{8,0},{1,5},{5,13},{13,9},{9,1},{2,6},{6,14},{... | collective-permute-start | bytes 393224 | tf_op jit(solution)/shard_map/ppermute | solution.py:221
  40.8 6.5 %collective-permute-start.11 = (f32[2,64,256]{2,1,0:T(8,128)S(1)}, f32[2,64,256]{2,1,0:T(8,128)S(1)}, u32[]{:S(2)}, u32[]{:S(2)}) collective-permute-start(f32[2,64,256]{2,1,0:T(8,128)S(1)} %add.34), channel_id=1, source_target_pairs={{0,4},{4,12},{12,8},{8,0},{1,5},{5,13},{13,9},{9,1},{2,6},{6,14},{... | collective-permute-start | bytes 393224 | tf_op jit(solution)/shard_map/ppermute | solution.py:220
  43.7 6.5 %collective-permute-start.8 = (f32[2,64,256]{2,1,0:T(8,128)S(1)}, f32[2,64,256]{2,1,0:T(8,128)S(1)}, u32[]{:S(2)}, u32[]{:S(2)}) collective-permute-start(f32[2,64,256]{2,1,0:T(8,128)S(1)} %add.31), channel_id=1, source_target_pairs={{0,4},{4,12},{12,8},{8,0},{1,5},{5,13},{13,9},{9,1},{2,6},{6,14},{... | collective-permute-start | bytes 393224 | tf_op jit(solution)/shard_map/ppermute | solution.py:221
  47.3 6.0 %collective-permute-start.12 = (f32[2,64,256]{2,1,0:T(8,128)S(1)}, f32[2,64,256]{2,1,0:T(8,128)S(1)}, u32[]{:S(2)}, u32[]{:S(2)}) collective-permute-start(f32[2,64,256]{2,1,0:T(8,128)S(1)} %add.35), channel_id=1, source_target_pairs={{0,4},{4,12},{12,8},{8,0},{1,5},{5,13},{13,9},{9,1},{2,6},{6,14},{... | collective-permute-start | bytes 393224 | tf_op jit(solution)/shard_map/ppermute | solution.py:220
  50.2 4.8 %collective-permute-start.9 = (f32[2,64,256]{2,1,0:T(8,128)S(1)}, f32[2,64,256]{2,1,0:T(8,128)S(1)}, u32[]{:S(2)}, u32[]{:S(2)}) collective-permute-start(f32[2,64,256]{2,1,0:T(8,128)S(1)} %add.32), channel_id=1, source_target_pairs={{0,4},{4,12},{12,8},{8,0},{1,5},{5,13},{13,9},{9,1},{2,6},{6,14},{... | collective-permute-start | bytes 393224 | tf_op jit(solution)/shard_map/ppermute | solution.py:221

commit v21 on v17

--- a/solution.py
+++ b/solution.py
@@ -72,7 +72,9 @@
 
 def first_product(left, parts, allowed_ref, source, high, low):
     kops, sectors = allowed_ref.shape
-    block = jnp.dot(left, parts, preferred_element_type=F32)
+    cut = 2 * parts.shape[0] // 3
+    block = jnp.dot(left[:, :cut], parts[:cut], preferred_element_type=F32)
+    block = block + jnp.dot(left[:, cut:], parts[cut:], preferred_element_type=F32)
     rows = block.shape[0] // kops
     source = jnp.clip(source, 0, sectors - 1)
     for k in range(kops):

time: 55.8 us -> 55.8 us (level)
  no operation moved by 1% of the time
where the time goes in v21:
time: 55.8 us; the launch traced here: 55.6 us
  starting transfers between devices  22.6 us (41%)
  Pallas kernels  15.5 us (28%)
  waiting for transfers between devices  13 us (23%)
  local copies, waits for them, and re-layouts  3.27 us (6%)
  other arithmetic  0.94 us (2%)
    pallas_call x8, Pallas kernels, call(): pl.pallas_call(body, name=name, out_shape=out_shape, in_specs=in_specs, o...  15.5 us
    ppermute x2, starting transfers between devices, shifted(): return lax.ppermute(block, axis, route)  8.41 us
    ppermute x3, starting transfers between devices, shards(): result_inner = lax.ppermute(result_inner, 'op', route) + next_inner  6.52 us
    ppermute x2, waiting for transfers between devices, shards(): lax.ppermute(outer[-1] + zero[0, 0] if step == 1 else outer[-1], 'op', ro...  3.62 us
    ppermute x2, starting transfers between devices, shards(): lax.ppermute(inner[-1] + zero[0, 0] if step == 1 else inner[-1], 'op', ro...  3.59 us
    unnamed x10, local copies, waits for them, and re-layouts  3.2 us
    ppermute x1, waiting for transfers between devices, shards(): blocks = [psi, lax.ppermute(psi, 'op', route)]  2.94 us
    ppermute x2, waiting for transfers between devices, shifted(): return lax.ppermute(block, axis, route)  2.44 us
  transfers between devices with their start and end apart: 13, of which 7 were waited for; matrix products, arithmetic and copies ran while one was open for 0% of the time, Pallas kernels for 28%

profile of v21, /device:TPU:1, one launch (start us, length us, event | category | flops | bytes accessed | tf_op | source)
XLA Modules:
  0.0 55.6 jit_solution(8420271749918835641)
XLA Ops:
  0.0 2.1 %collective-permute-start = (f32[4,64,256]{2,1,0:T(8,128)}, f32[4,64,256]{2,1,0:T(8,128)S(1)}, u32[]{:S(2)}, u32[]{:S(2)}) collective-permute-start(f32[4,64,256]{2,1,0:T(8,128)} %param.5), channel_id=1, source_target_pairs={{0,4},{4,12},{12,8},{8,0},{1,5},{5,13},{13,9},{9,1},{2,6},{6,14},{... | collective-permute-start | bytes 786440 | tf_op jit(solution)/shard_map/ppermute | solution.py:183
  2.1 0.0 copy-start.2
  2.1 1.6 %copy-done.2 = f32[8,256,256]{2,1,0:T(8,128)S(1)} copy-done((f32[8,256,256]{2,1,0:T(8,128)S(1)}, f32[8,256,256]{2,1,0:T(8,128)}, u32[]{:S(2)}) %copy-start.2) | copy-done | bytes 2097176
  3.7 0.0 copy-start.3
  3.7 1.6 %copy-done.3 = f32[8,256,256]{2,1,0:T(8,128)S(1)} copy-done((f32[8,256,256]{2,1,0:T(8,128)S(1)}, f32[8,256,256]{2,1,0:T(8,128)}, u32[]{:S(2)}) %copy-start.3) | copy-done | bytes 2097176
  5.3 0.0 copy-start.4
  5.3 1.1 %prepare.1 = (bf16[4,8,64,768]{3,2,1,0:T(8,128)(2,1)S(1)}, bf16[2048,256]{1,0:T(8,128)(2,1)S(1)}, bf16[2048,256]{1,0:T(8,128)(2,1)S(1)}, f32[1,128]{1,0:T(1,128)S(1)}) custom-call(f32[8,256,256]{2,1,0:T(8,128)S(1)} %copy-done.2, f32[8,256,256]{2,1,0:T(8,128)S(1)} %copy-done.3), custom_call_target="tpu_custom_call" | custom-call | flops 3221225472 | bytes 1048576 | tf_op jit(solution)/shard_map/prepare/pallas_call | solution.py:157
  6.4 0.0 copy-done.4
  6.4 2.9 %collective-permute-done = f32[4,64,256]{2,1,0:T(8,128)S(1)} collective-permute-done((f32[4,64,256]{2,1,0:T(8,128)}, f32[4,64,256]{2,1,0:T(8,128)S(1)}, u32[]{:S(2)}, u32[]{:S(2)}) %collective-permute-start) | collective-permute-done | bytes 262176 | tf_op jit(solution)/shard_map/ppermute | solution.py:183
  9.4 0.1 broadcast_add_fusion
  9.5 0.4 collective-permute-start.1
  9.9 3.0 %collective-permute-start.3 = (f32[2,64,256]{2,1,0:T(8,128)S(1)}, f32[2,64,256]{2,1,0:T(8,128)S(1)}, u32[]{:S(2)}, u32[]{:S(2)}) collective-permute-start(f32[2,64,256]{2,1,0:T(8,128)S(1)} %get-tuple-element.35), channel_id=1, source_target_pairs={{0,4},{4,12},{12,8},{8,0},{1,5},{5,13},{13,9},{9,1},{2,6},{6,14},{... | collective-permute-start | bytes 393224 | tf_op jit(solution)/shard_map/ppermute | solution.py:187
  12.9 1.4 %collective-permute-done.1.refs_2_ = f32[2,64,256]{2,1,0:T(8,128)S(1)} collective-permute-done((f32[2,64,256]{2,1,0:T(8,128)S(1)}, f32[2,64,256]{2,1,0:T(8,128)S(1)}, u32[]{:S(2)}, u32[]{:S(2)}) %collective-permute-start.1) | collective-permute-done | bytes 131104 | tf_op jit(solution)/shard_map/ppermute | solution.py:186
  14.2 0.6 %collective-permute-start.2 = (f32[2,64,256]{2,1,0:T(8,128)S(1)}, f32[2,64,256]{2,1,0:T(8,128)S(1)}, u32[]{:S(2)}, u32[]{:S(2)}) collective-permute-start(f32[2,64,256]{2,1,0:T(8,128)S(1)} %collective-permute-done.1.refs_2_), channel_id=1, source_target_pairs={{0,4},{4,12},{12,8},{8,0},{1,5},{5,13},{13,9},{9,1},{2,6},{6,14},{... | collective-permute-start | bytes 393224 | tf_op jit(solution)/shard_map/ppermute | solution.py:186
  14.8 2.2 %collective-permute-done.3.refs_2_ = f32[2,64,256]{2,1,0:T(8,128)S(1)} collective-permute-done((f32[2,64,256]{2,1,0:T(8,128)S(1)}, f32[2,64,256]{2,1,0:T(8,128)S(1)}, u32[]{:S(2)}, u32[]{:S(2)}) %collective-permute-start.3) | collective-permute-done | bytes 131104 | tf_op jit(solution)/shard_map/ppermute | solution.py:187
  17.0 0.6 %collective-permute-start.4 = (f32[2,64,256]{2,1,0:T(8,128)S(1)}, f32[2,64,256]{2,1,0:T(8,128)S(1)}, u32[]{:S(2)}, u32[]{:S(2)}) collective-permute-start(f32[2,64,256]{2,1,0:T(8,128)S(1)} %collective-permute-done.3.refs_2_), channel_id=1, source_target_pairs={{0,4},{4,12},{12,8},{8,0},{1,5},{5,13},{13,9},{9,1},{2,6},{6,14},{... | collective-permute-start | bytes 393224 | tf_op jit(solution)/shard_map/ppermute | solution.py:187
  17.6 2.3 %collective-permute-done.2.refs_3_ = f32[2,64,256]{2,1,0:T(8,128)S(1)} collective-permute-done((f32[2,64,256]{2,1,0:T(8,128)S(1)}, f32[2,64,256]{2,1,0:T(8,128)S(1)}, u32[]{:S(2)}, u32[]{:S(2)}) %collective-permute-start.2) | collective-permute-done | bytes 131104 | tf_op jit(solution)/shard_map/ppermute | solution.py:186
  19.9 6.5 %collective-permute-start.5 = (f32[4,64,256]{2,1,0:T(8,128)S(1)}, f32[4,64,256]{2,1,0:T(8,128)S(1)}, u32[]{:S(2)}, u32[]{:S(2)}) collective-permute-start(f32[4,64,256]{2,1,0:T(8,128)S(1)} %pad_maximum_fusion), channel_id=1, source_target_pairs={{0,1},{1,2},{2,3},{4,5},{5,6},{6,7},{8,9},{9,10},{10,11},{12,13},{... | collective-permute-start | bytes 786440 | tf_op jit(solution)/shard_map/ppermute | solution.py:18
  26.4 0.0 copy-start
  26.4 1.9 %collective-permute-start.6 = (f32[4,64,256]{2,1,0:T(8,128)S(1)}, f32[4,64,256]{2,1,0:T(8,128)S(1)}, u32[]{:S(2)}, u32[]{:S(2)}) collective-permute-start(f32[4,64,256]{2,1,0:T(8,128)S(1)} %pad_maximum_fusion.1), channel_id=1, source_target_pairs={{1,0},{2,1},{3,2},{5,4},{6,5},{7,6},{9,8},{10,9},{11,10},{13,12},{... | collective-permute-start | bytes 786440 | tf_op jit(solution)/shard_map/ppermute | solution.py:18
  28.3 0.2 assemble.1.outer
  28.5 0.0 collective-permute-done.4.refs_3_
  28.6 0.0 copy-done
  28.6 0.0 copy-start.1
  28.6 1.7 %own.1 = (bf16[2,768,256]{2,1,0:T(8,128)(2,1)S(1)}, bf16[4,512,256]{2,1,0:T(8,128)(2,1)S(1)}, bf16[4,512,256]{2,1,0:T(8,128)(2,1)S(1)}) custom-call(s32[8,16]{1,0:T(8,128)S(1)} %copy-done, bf16[2,768,256]{2,1,0:T(8,128)(2,1)S(1)} %assemble.1.outer, f32[2,64,256]{2,1,0:T(8,128)S(1)} %get-tuple-element.39.refs_0_, ...), custom_call_target="tpu_custom_call" | custom-call | flops 3221225472 | bytes 1048576 | tf_op jit(solution)/shard_map/own/pallas_call | solution.py:157
  30.2 0.0 copy-done.1
  30.2 1.1 %first_inner.1 = f32[2,64,256]{2,1,0:T(8,128)S(1)} custom-call(s32[8]{0:T(128)S(1)} %copy-done.1, bf16[4,512,256]{2,1,0:T(8,128)(2,1)S(1)} %get-tuple-element.22.own_high.high, bf16[4,512,256]{2,1,0:T(8,128)(2,1)S(1)} %get-tuple-element.23.own_low.low, bf16[2048,256]{1,0:T(8,128)(2,1)S(1)} %get-tuple-element.24.right_hi, ...), custom_call_target="tpu_custom_call" | custom-call | flops 805306368 | bytes 1048576 | tf_op jit(solution)/shard_map/first_inner/pallas_call | solution.py:157
  31.4 0.6 %collective-permute-start.10 = (f32[2,64,256]{2,1,0:T(8,128)S(1)}, f32[2,64,256]{2,1,0:T(8,128)S(1)}, u32[]{:S(2)}, u32[]{:S(2)}) collective-permute-start(f32[2,64,256]{2,1,0:T(8,128)S(1)} %first_inner.1), channel_id=1, source_target_pairs={{0,4},{4,12},{12,8},{8,0},{1,5},{5,13},{13,9},{9,1},{2,6},{6,14},{... | collective-permute-start | bytes 393224 | tf_op jit(solution)/shard_map/ppermute | solution.py:228
  32.0 0.0 collective-permute-done.5.above
  32.0 2.4 %collective-permute-done.6.below = f32[4,64,256]{2,1,0:T(8,128)S(1)} collective-permute-done((f32[4,64,256]{2,1,0:T(8,128)S(1)}, f32[4,64,256]{2,1,0:T(8,128)S(1)}, u32[]{:S(2)}, u32[]{:S(2)}) %collective-permute-start.6) | collective-permute-done | bytes 262176 | tf_op jit(solution)/shard_map/ppermute | solution.py:18
  34.4 2.4 %first_outer.1 = (f32[2,64,256]{2,1,0:T(8,128)S(1)}, bf16[2,768,256]{2,1,0:T(8,128)(2,1)S(1)}) custom-call(s32[8]{0:T(128)S(1)} %copy-done.1, s32[8,16]{1,0:T(8,128)S(1)} %copy-done, bf16[4,512,256]{2,1,0:T(8,128)(2,1)S(1)} %get-tuple-element.22.own_high.high, bf16[4,512,256]{2,1,0:T(8,128)(2,1)S(1)} %get-tuple-element.23.own_low.low, ...), custom_call_target="tpu_custom_call" | custom-call | flops 1610612736 | bytes 1048576 | tf_op jit(solution)/shard_map/first_outer/pallas_call | solution.py:157
  36.8 0.7 %collective-permute-start.7 = (f32[2,64,256]{2,1,0:T(8,128)S(1)}, f32[2,64,256]{2,1,0:T(8,128)S(1)}, u32[]{:S(2)}, u32[]{:S(2)}) collective-permute-start(f32[2,64,256]{2,1,0:T(8,128)S(1)} %get-tuple-element.26), channel_id=1, source_target_pairs={{0,4},{4,12},{12,8},{8,0},{1,5},{5,13},{13,9},{9,1},{2,6},{6,14},{... | collective-permute-start | bytes 393224 | tf_op jit(solution)/shard_map/ppermute | solution.py:229
  37.5 3.0 %chunk.3 = (f32[2,64,256]{2,1,0:T(8,128)S(1)}, f32[2,64,256]{2,1,0:T(8,128)S(1)}) custom-call(s32[8]{0:T(128)S(1)} %copy-done.1, s32[8,16]{1,0:T(8,128)S(1)} %copy-done, bf16[2,768,256]{2,1,0:T(8,128)(2,1)S(1)} %assemble.1.outer, bf16[2,768,256]{2,1,0:T(8,128)(2,1)S(1)} %get-tuple-element.27.inner, bf16[2,768,256]{2,1,0:T(8,128)(2,1)S(1)} %get-tuple-element.28.outside, ...), custom_call_target="tpu_custom_call" | custom-call | flops 3221225472 | bytes 1048576 | tf_op jit(solution)/shard_map/chunk/pallas_call | solution.py:157
  40.6 0.0 collective-permute-done.10
  40.6 3.0 %collective-permute-start.11 = (f32[2,64,256]{2,1,0:T(8,128)S(1)}, f32[2,64,256]{2,1,0:T(8,128)S(1)}, u32[]{:S(2)}, u32[]{:S(2)}) collective-permute-start(f32[2,64,256]{2,1,0:T(8,128)S(1)} %add.34), channel_id=1, source_target_pairs={{0,4},{4,12},{12,8},{8,0},{1,5},{5,13},{13,9},{9,1},{2,6},{6,14},{... | collective-permute-start | bytes 393224 | tf_op jit(solution)/shard_map/ppermute | solution.py:228
  43.6 0.0 collective-permute-done.7
  43.6 0.2 collective-permute-start.8
  43.8 3.0 %chunk.4 = (f32[2,64,256]{2,1,0:T(8,128)S(1)}, f32[2,64,256]{2,1,0:T(8,128)S(1)}) custom-call(s32[8]{0:T(128)S(1)} %copy-done.1, s32[8,16]{1,0:T(8,128)S(1)} %copy-done, bf16[2,768,256]{2,1,0:T(8,128)(2,1)S(1)} %assemble.1.outer, bf16[2,768,256]{2,1,0:T(8,128)(2,1)S(1)} %get-tuple-element.27.inner, bf16[2,768,256]{2,1,0:T(8,128)(2,1)S(1)} %get-tuple-element.28.outside, ...), custom_call_target="tpu_custom_call" | custom-call | flops 3221225472 | bytes 1048576 | tf_op jit(solution)/shard_map/chunk/pallas_call | solution.py:157
  46.8 0.3 collective-permute-done.11
  47.1 2.9 %collective-permute-start.12 = (f32[2,64,256]{2,1,0:T(8,128)S(1)}, f32[2,64,256]{2,1,0:T(8,128)S(1)}, u32[]{:S(2)}, u32[]{:S(2)}) collective-permute-start(f32[2,64,256]{2,1,0:T(8,128)S(1)} %add.35), channel_id=1, source_target_pairs={{0,4},{4,12},{12,8},{8,0},{1,5},{5,13},{13,9},{9,1},{2,6},{6,14},{... | collective-permute-start | bytes 393224 | tf_op jit(solution)/shard_map/ppermute | solution.py:228
  50.0 0.0 collective-permute-done.8
  50.0 0.2 collective-permute-start.9
  50.2 3.0 %chunk.5 = (f32[2,64,256]{2,1,0:T(8,128)S(1)}, f32[2,64,256]{2,1,0:T(8,128)S(1)}) custom-call(s32[8]{0:T(128)S(1)} %copy-done.1, s32[8,16]{1,0:T(8,128)S(1)} %copy-done, bf16[2,768,256]{2,1,0:T(8,128)(2,1)S(1)} %assemble.1.outer, bf16[2,768,256]{2,1,0:T(8,128)(2,1)S(1)} %get-tuple-element.27.inner, bf16[2,768,256]{2,1,0:T(8,128)(2,1)S(1)} %get-tuple-element.28.outside, ...), custom_call_target="tpu_custom_call" | custom-call | flops 3221225472 | bytes 1048576 | tf_op jit(solution)/shard_map/chunk/pallas_call | solution.py:157
  53.3 0.0 collective-permute-done.12
  53.3 1.5 %collective-permute-done.9 = f32[2,64,256]{2,1,0:T(8,128)S(1)} collective-permute-done((f32[2,64,256]{2,1,0:T(8,128)S(1)}, f32[2,64,256]{2,1,0:T(8,128)S(1)}, u32[]{:S(2)}, u32[]{:S(2)}) %collective-permute-start.9) | collective-permute-done | bytes 131104 | tf_op jit(solution)/shard_map/ppermute | solution.py:229
  54.9 0.7 %pad_maximum_fusion.2 = f32[4,64,256]{2,1,0:T(8,128)} fusion(f32[1,64,256]{2,1,0:T(8,128)S(1)} %get-tuple-element.42, f32[2,64,256]{2,1,0:T(8,128)S(1)} %add.36, f32[1,64,256]{2,1,0:T(8,128)S(1)} %get-tuple-element.41), kind=kLoop, calls=%fused_computation.2 | loop fusion | flops 131072 | bytes 524288 | tf_op jit(solution)/shard_map/concatenate | solution.py:230
  (14 shorter events, 0.2 us)
Async XLA Ops:
  0.0 9.4 %collective-permute-start = (f32[4,64,256]{2,1,0:T(8,128)}, f32[4,64,256]{2,1,0:T(8,128)S(1)}, u32[]{:S(2)}, u32[]{:S(2)}) collective-permute-start(f32[4,64,256]{2,1,0:T(8,128)} %param.5), channel_id=1, source_target_pairs={{0,4},{4,12},{12,8},{8,0},{1,5},{5,13},{13,9},{9,1},{2,6},{6,14},{... | collective-permute-start | bytes 786440 | tf_op jit(solution)/shard_map/ppermute | solution.py:183
  2.1 1.6 %copy-start.2 = (f32[8,256,256]{2,1,0:T(8,128)S(1)}, f32[8,256,256]{2,1,0:T(8,128)}, u32[]{:S(2)}) copy-start(f32[8,256,256]{2,1,0:T(8,128)} %left_ref.1) | copy-start | bytes 6291460
  3.7 1.6 %copy-start.3 = (f32[8,256,256]{2,1,0:T(8,128)S(1)}, f32[8,256,256]{2,1,0:T(8,128)}, u32[]{:S(2)}) copy-start(f32[8,256,256]{2,1,0:T(8,128)} %right_ref.1) | copy-start | bytes 6291460
  5.3 1.1 %copy-start.4 = (f32[4,64,256]{2,1,0:T(8,128)S(1)}, f32[4,64,256]{2,1,0:T(8,128)}, u32[]{:S(2)}) copy-start(f32[4,64,256]{2,1,0:T(8,128)} %param.5) | copy-start | bytes 786436
  9.5 4.8 %collective-permute-start.1 = (f32[2,64,256]{2,1,0:T(8,128)S(1)}, f32[2,64,256]{2,1,0:T(8,128)S(1)}, u32[]{:S(2)}, u32[]{:S(2)}) collective-permute-start(f32[2,64,256]{2,1,0:T(8,128)S(1)} %get-tuple-element.38), channel_id=1, source_target_pairs={{0,4},{4,12},{12,8},{8,0},{1,5},{5,13},{13,9},{9,1},{2,6},{6,14},{... | collective-permute-start | bytes 393224 | tf_op jit(solution)/shard_map/ppermute | solution.py:186
  9.9 7.1 %collective-permute-start.3 = (f32[2,64,256]{2,1,0:T(8,128)S(1)}, f32[2,64,256]{2,1,0:T(8,128)S(1)}, u32[]{:S(2)}, u32[]{:S(2)}) collective-permute-start(f32[2,64,256]{2,1,0:T(8,128)S(1)} %get-tuple-element.35), channel_id=1, source_target_pairs={{0,4},{4,12},{12,8},{8,0},{1,5},{5,13},{13,9},{9,1},{2,6},{6,14},{... | collective-permute-start | bytes 393224 | tf_op jit(solution)/shard_map/ppermute | solution.py:187
  14.2 5.6 %collective-permute-start.2 = (f32[2,64,256]{2,1,0:T(8,128)S(1)}, f32[2,64,256]{2,1,0:T(8,128)S(1)}, u32[]{:S(2)}, u32[]{:S(2)}) collective-permute-start(f32[2,64,256]{2,1,0:T(8,128)S(1)} %collective-permute-done.1.refs_2_), channel_id=1, source_target_pairs={{0,4},{4,12},{12,8},{8,0},{1,5},{5,13},{13,9},{9,1},{2,6},{6,14},{... | collective-permute-start | bytes 393224 | tf_op jit(solution)/shard_map/ppermute | solution.py:186
  17.0 11.6 %collective-permute-start.4 = (f32[2,64,256]{2,1,0:T(8,128)S(1)}, f32[2,64,256]{2,1,0:T(8,128)S(1)}, u32[]{:S(2)}, u32[]{:S(2)}) collective-permute-start(f32[2,64,256]{2,1,0:T(8,128)S(1)} %collective-permute-done.3.refs_2_), channel_id=1, source_target_pairs={{0,4},{4,12},{12,8},{8,0},{1,5},{5,13},{13,9},{9,1},{2,6},{6,14},{... | collective-permute-start | bytes 393224 | tf_op jit(solution)/shard_map/ppermute | solution.py:187
  19.9 12.1 %collective-permute-start.5 = (f32[4,64,256]{2,1,0:T(8,128)S(1)}, f32[4,64,256]{2,1,0:T(8,128)S(1)}, u32[]{:S(2)}, u32[]{:S(2)}) collective-permute-start(f32[4,64,256]{2,1,0:T(8,128)S(1)} %pad_maximum_fusion), channel_id=1, source_target_pairs={{0,1},{1,2},{2,3},{4,5},{5,6},{6,7},{8,9},{9,10},{10,11},{12,13},{... | collective-permute-start | bytes 786440 | tf_op jit(solution)/shard_map/ppermute | solution.py:18
  26.4 2.1 %copy-start = (s32[8,16]{1,0:T(8,128)S(1)}, s32[8,16]{1,0:T(8,128)}, u32[]{:S(2)}) copy-start(s32[8,16]{1,0:T(8,128)} %allowed_ref.9) | copy-start | bytes 1540
  26.4 8.0 %collective-permute-start.6 = (f32[4,64,256]{2,1,0:T(8,128)S(1)}, f32[4,64,256]{2,1,0:T(8,128)S(1)}, u32[]{:S(2)}, u32[]{:S(2)}) collective-permute-start(f32[4,64,256]{2,1,0:T(8,128)S(1)} %pad_maximum_fusion.1), channel_id=1, source_target_pairs={{1,0},{2,1},{3,2},{5,4},{6,5},{7,6},{9,8},{10,9},{11,10},{13,12},{... | collective-permute-start | bytes 786440 | tf_op jit(solution)/shard_map/ppermute | solution.py:18
  28.6 1.7 %copy-start.1 = (s32[8]{0:T(128)S(1)}, s32[8]{0:T(128)}, u32[]{:S(2)}) copy-start(s32[8]{0:T(128)} %shifts_ref.9) | copy-start | bytes 100
  31.4 9.2 %collective-permute-start.10 = (f32[2,64,256]{2,1,0:T(8,128)S(1)}, f32[2,64,256]{2,1,0:T(8,128)S(1)}, u32[]{:S(2)}, u32[]{:S(2)}) collective-permute-start(f32[2,64,256]{2,1,0:T(8,128)S(1)} %first_inner.1), channel_id=1, source_target_pairs={{0,4},{4,12},{12,8},{8,0},{1,5},{5,13},{13,9},{9,1},{2,6},{6,14},{... | collective-permute-start | bytes 393224 | tf_op jit(solution)/shard_map/ppermute | solution.py:228
  36.8 6.8 %collective-permute-start.7 = (f32[2,64,256]{2,1,0:T(8,128)S(1)}, f32[2,64,256]{2,1,0:T(8,128)S(1)}, u32[]{:S(2)}, u32[]{:S(2)}) collective-permute-start(f32[2,64,256]{2,1,0:T(8,128)S(1)} %get-tuple-element.26), channel_id=1, source_target_pairs={{0,4},{4,12},{12,8},{8,0},{1,5},{5,13},{13,9},{9,1},{2,6},{6,14},{... | collective-permute-start | bytes 393224 | tf_op jit(solution)/shard_map/ppermute | solution.py:229
  40.6 6.5 %collective-permute-start.11 = (f32[2,64,256]{2,1,0:T(8,128)S(1)}, f32[2,64,256]{2,1,0:T(8,128)S(1)}, u32[]{:S(2)}, u32[]{:S(2)}) collective-permute-start(f32[2,64,256]{2,1,0:T(8,128)S(1)} %add.34), channel_id=1, source_target_pairs={{0,4},{4,12},{12,8},{8,0},{1,5},{5,13},{13,9},{9,1},{2,6},{6,14},{... | collective-permute-start | bytes 393224 | tf_op jit(solution)/shard_map/ppermute | solution.py:228
  43.6 6.4 %collective-permute-start.8 = (f32[2,64,256]{2,1,0:T(8,128)S(1)}, f32[2,64,256]{2,1,0:T(8,128)S(1)}, u32[]{:S(2)}, u32[]{:S(2)}) collective-permute-start(f32[2,64,256]{2,1,0:T(8,128)S(1)} %add.31), channel_id=1, source_target_pairs={{0,4},{4,12},{12,8},{8,0},{1,5},{5,13},{13,9},{9,1},{2,6},{6,14},{... | collective-permute-start | bytes 393224 | tf_op jit(solution)/shard_map/ppermute | solution.py:229
  47.1 6.1 %collective-permute-start.12 = (f32[2,64,256]{2,1,0:T(8,128)S(1)}, f32[2,64,256]{2,1,0:T(8,128)S(1)}, u32[]{:S(2)}, u32[]{:S(2)}) collective-permute-start(f32[2,64,256]{2,1,0:T(8,128)S(1)} %add.35), channel_id=1, source_target_pairs={{0,4},{4,12},{12,8},{8,0},{1,5},{5,13},{13,9},{9,1},{2,6},{6,14},{... | collective-permute-start | bytes 393224 | tf_op jit(solution)/shard_map/ppermute | solution.py:228
  50.0 4.8 %collective-permute-start.9 = (f32[2,64,256]{2,1,0:T(8,128)S(1)}, f32[2,64,256]{2,1,0:T(8,128)S(1)}, u32[]{:S(2)}, u32[]{:S(2)}) collective-permute-start(f32[2,64,256]{2,1,0:T(8,128)S(1)} %add.32), channel_id=1, source_target_pairs={{0,4},{4,12},{12,8},{8,0},{1,5},{5,13},{13,9},{9,1},{2,6},{6,14},{... | collective-permute-start | bytes 393224 | tf_op jit(solution)/shard_map/ppermute | solution.py:229
